TPU v7x, 128 devices: a whole 4x4x4 slice. The times are simulated.
128 devices in a mesh: store: 32 (over y, x, core), frame: 4 (over z).
Axes of the slice: x: 4, y: 4, z: 4, core: 2. Of those that a mesh axis runs over, the one named last changes fastest.
Arguments:
- act: bfloat16 [16384, 2048], P(('store', 'frame')), may hold values from -6 to 6
- cache_rows: bfloat16 [16384, 128], P(('store', 'frame')), may hold values from -6 to 6
- row_dest: int32 [16384], P(('store', 'frame')), may hold values from 0 to 31, as said below
- time_index: int32 [32], P('store'), may hold values from 0 to 999
- w_embed: bfloat16 [64, 2048], replicated, may hold values from -0.75 to 0.75
- norm_gain: float32 [2048], replicated, may hold values from 0.5 to 8
- w_qkv: bfloat16 [3, 2048, 2048], P(None, None, 'frame'), may hold values from -0.125 to 0.125
- w_out_attn: bfloat16 [2048, 2048], P('frame'), may hold values from -0.125 to 0.125
- w_head: bfloat16 [2048, 64], replicated, may hold values from -0.125 to 0.125
Outputs:
- frame_loss: float32 [32, 4], P('store', 'frame')
- grad_qkv: float32 [3, 2048, 2048], P(None, None, 'frame')
- grad_out_attn: float32 [2048, 2048], P('frame')
Inputs may be any that keep to these rules, and one draw needn't show every extreme that they name: `row_dest`: over the devices of one frame index, each store index is named by exactly 128 rows. The rows of one device name any one store index at most 8 times, and some store index exactly 8 times.
All inputs are finite; a program needn't handle non-finite values.
Results may differ from a plain program's by a relative error of at most 0.02.
The roundings to bfloat16 on the way count: a program that leaves them out, or rounds other values in their place, can miss the bound.
Values may be sent and summed in bfloat16 or wider, within the bound.
No kernel may reach another device: no remote copies, remote signals or barrier semaphores. Data moves between devices by JAX's collectives and lax.ppermute only.
A program may use at most 128 MiB of HBM per device.

v0:
```python
import functools
import math

import jax
import jax.numpy as jnp
from jax import lax
from jax.experimental import pallas as pl
from jax.experimental.pallas import tpu as pltpu
from jax.sharding import Mesh, PartitionSpec as P

HEAD_DIM = 128
TIMESTEPS = 1000
UNUSED = 64.0
FIRST = ((0, 1), (0, 3), (0, 2), (1, 3), (1, 2))
f32 = jnp.float32
bf16 = jnp.bfloat16
HIGHEST = lax.Precision.HIGHEST
INV_ROOT = 1.0 / math.sqrt(HEAD_DIM)
NN = (((1,), (0,)), ((), ()))
NT = (((1,), (1,)), ((), ()))
TN = (((0,), (0,)), ((), ()))
ORDER = (0, 1, 3, 2)
SPOT = {r: i for i, r in enumerate(ORDER)}
VMEM = pl.BlockSpec(memory_space=pltpu.VMEM)
SMEM = pl.BlockSpec(memory_space=pltpu.SMEM)
HBM = pl.BlockSpec(memory_space=pltpu.HBM)
ANY = pl.BlockSpec(memory_space=pl.ANY)


def params(mib):
    return pltpu.CompilerParams(vmem_limit_bytes=mib << 20)


def cost(flops, moved):
    return pl.CostEstimate(flops=flops, bytes_accessed=moved, transcendentals=0)


TINY = cost(0, 1024)


def dot(a, b, dims=NN, precision=None):
    return lax.dot_general(a, b, dims, preferred_element_type=f32, precision=precision)


def shift(value, axis, offset):
    size = lax.axis_size(axis)
    return lax.ppermute(value, axis, [(i, (i + offset) % size) for i in range(size)])


def shape(dims, kind):
    return jax.ShapeDtypeStruct(dims, kind)


def bucket_kernel(rows, dest_row, out):
    dest_col = jnp.broadcast_to(dest_row[...].astype(f32), (128, 128)).T
    earlier = lax.broadcasted_iota(jnp.int32, (128, 128), 0) < lax.broadcasted_iota(
        jnp.int32, (128, 128), 1
    )
    same = jnp.where((dest_col == dest_row[...].astype(f32)) & earlier, 1.0, 0.0)
    slot = dest_row[...] * 8 + jnp.sum(same, axis=0, keepdims=True).astype(jnp.int32)
    hot = jnp.where(lax.broadcasted_iota(jnp.int32, (256, 128), 0) == slot, 1.0, 0.0)
    used = jnp.max(hot, axis=1, keepdims=True)
    moved = dot(hot.astype(bf16), rows[...]) + (1.0 - used) * UNUSED
    out[...] = moved.astype(bf16).reshape(16, 16, 128)


def prepare_kernel(place, w, w_out, head_t, w_t, mix, mix_t, held, out_rows, turned, sems, leave):
    start = pl.multiple_of(place[1] * 256, 256)
    loads = [
        pltpu.make_async_copy(w.at[j, :, pl.ds(start, 256)], held.at[j], sems.at[j]) for j in range(3)
    ]
    loads.append(pltpu.make_async_copy(w_out.at[pl.ds(start, 256)], out_rows, sems.at[3]))
    for load in loads:
        load.start()
    stores = []
    for j in range(3):
        loads[j].wait()
        for h in range(2):
            k = h * 3 + j
            turned[k] = held[j, :, h * 128 : h * 128 + 128].T
            stores.append(pltpu.make_async_copy(turned.at[k], w_t.at[pl.ds(k * 128, 128)], leave.at[k]))
            stores[-1].start()
    loads[3].wait()
    mix[...] = dot(out_rows[...], head_t[...], NT)
    mix_t[...] = dot(head_t[...], out_rows[...], NT)
    for store in stores:
        store.wait()


def sides_kernel(before, after, arrived, top, bottom, both, spread):
    top[...] = before[:64]
    bottom[...] = after[64:]
    both[0] = before[...]
    both[1] = after[...]
    for k in range(8):
        spread[k] = arrived[...]


def fetch_kernel(place, arrived, pairs):
    frame, core = place[0], place[1]
    slots = 512

    def rank_of(i):
        return ((i % 256) // 16) * 32 + (i // 256) * 16 + i % 16

    before = jnp.where(
        rank_of(lax.broadcasted_iota(jnp.int32, (slots, slots), 1))
        < rank_of(lax.broadcasted_iota(jnp.int32, (slots, slots), 0)),
        1.0,
        0.0,
    ).astype(bf16)
    half = (lax.broadcasted_iota(jnp.int32, (slots, 128), 0) // 8) % 2
    lane = lax.broadcasted_iota(jnp.int32, (slots, 128), 1).astype(f32)
    for i, r in enumerate(ORDER):
        from_frame = (frame + 4 - r) % 4
        rows = jnp.concatenate([arrived[from_frame], arrived[4 + from_frame]], axis=0)
        valid = jnp.broadcast_to(rows[:, 0:1].astype(f32), (slots, 128)) < 32.0
        for other in range(2):
            clip = core + other - 2 * core * other
            mine = jnp.where(valid & (half == clip), 1.0, 0.0)
            rank = dot(before, mine.astype(bf16))
            pick = jnp.where(rank == lane, mine, 0.0)
            pairs[2 * i + other] = dot(pick.astype(bf16), rows, TN).astype(bf16)


def lanes(i, other):
    return slice((2 * i + other) * 128, (2 * i + other) * 128 + 128)


def forward_kernel(moments, *refs):
    act, act_theirs, sides, sides_theirs, top, top_theirs, bottom, bottom_theirs = refs[:8]
    pairs, w_embed, gain, w_t_far, head_t, mix_t = refs[8:14]
    normed_far, proj_far, attended_far, probs, part_own, part_other = refs[14:20]
    w_t, normed, proj, attended, rest, sems = refs[20:]
    weights = pltpu.make_async_copy(w_t_far, w_t, sems.at[0])
    weights.start()
    work = [(0, 0, act[...]), (1, 0, act_theirs[...])]
    for side in range(2):
        work += [(2 + 2 * side, 0, sides[side]), (3 + 2 * side, 0, sides_theirs[side])]
    work += [(6, 0, top[...]), (6, 64, bottom[...]), (7, 0, top_theirs[...]), (7, 64, bottom_theirs[...])]
    for b, start, rows in work:
        pair = pairs[b, start : start + rows.shape[0]].astype(f32)
        t = moments[b % 2]
        noised = ((1.0 - t) * pair[:, :64] + t * pair[:, 64:]).astype(bf16)
        hidden = rows.astype(f32) + dot(noised, w_embed[...])
        scale = lax.rsqrt(jnp.mean(hidden * hidden, axis=1, keepdims=True) + 1e-06)
        first = b * 128 + start
        normed[first : first + rows.shape[0]] = (hidden * scale * gain[...]).astype(bf16)
        if b == 0:
            turned = pair.T
            own = dot(head_t[...].astype(f32), hidden, NT, HIGHEST)
            rest[...] = own - (turned[64:] - turned[:64])
    leave = [pltpu.make_async_copy(normed, normed_far, sems.at[1])]
    leave[0].start()
    weights.wait()
    for i in range(3):
        rows = slice(i * 256, i * 256 + 256)
        proj[rows] = dot(w_t[rows], normed[...], NT).astype(bf16)
    leave.append(pltpu.make_async_copy(proj, proj_far, sems.at[2]))
    leave[1].start()
    for h in range(2):
        for other in range(2):

            def read(j, f):
                row = h * 384 + j * 128
                return proj[row : row + 128, lanes(f, other)].astype(f32)

            keys = [read(1, g) for g in range(4)]
            values = [read(2, g) for g in range(4)]
            for f in range(4):
                query = read(0, f)
                scores = [jnp.sum(query * k, axis=0, keepdims=True) * INV_ROOT for k in keys]
                peak = jnp.maximum(jnp.maximum(scores[0], scores[1]), jnp.maximum(scores[2], scores[3]))
                powers = [jnp.exp(s - peak) for s in scores]
                whole = powers[0] + powers[1] + powers[2] + powers[3]
                prob = [p / whole for p in powers]
                rounded = [p.astype(bf16).astype(f32) for p in prob]
                out = rounded[0] * values[0]
                for g in range(1, 4):
                    out = out + rounded[g] * values[g]
                attended[h * 128 : h * 128 + 128, lanes(f, other)] = out.astype(bf16)
                for g in range(4):
                    probs[h * 2 + other, f * 4 + g : f * 4 + g + 1] = prob[g]
    leave.append(pltpu.make_async_copy(attended, attended_far, sems.at[3]))
    leave[2].start()
    for other, part in ((0, part_own), (1, part_other)):
        for f in range(4):
            value = dot(mix_t[...], attended[:, lanes(f, other)].astype(f32), NN, HIGHEST)
            if other == 0 and f == 0:
                value = value + rest[...]
            part[:, f * 128 : f * 128 + 128] = value
    for copy in leave:
        copy.wait()


def gradient_piece(delta, normed, factor, h, block, out):
    columns = pl.ds(pl.multiple_of(block * 512, 512), 512)
    out[:384] = dot(delta[h * 384 : h * 384 + 384], normed[:, columns]).astype(bf16)
    for i in range(4):
        out[384:, i * 128 : i * 128 + 128] = factor[i * 16 : i * 16 + 16]


def backward_kernel(place, error_own, error_other, probs, mix, proj_far, attended_far, normed_far, *refs):
    pieces, delta, own_factor = refs[:5], refs[5], refs[6]
    slope, grad, proj, attended, normed, sems = refs[7:]
    loads = [
        pltpu.make_async_copy(far, near, sems.at[k])
        for k, (far, near) in enumerate(((proj_far, proj), (attended_far, attended), (normed_far, normed)))
    ]
    for load in loads:
        load.start()
    for i in range(4):
        for other, error in ((0, error_own), (1, error_other)):
            slope[:, lanes(i, other)] = error[:, i * 128 : i * 128 + 128] * (2.0 / 32.0)
    grad[...] = dot(mix[...], slope[...], NN, HIGHEST)
    loads[0].wait()
    for h in range(2):
        for other in range(2):

            def read(j, f):
                row = h * 384 + j * 128
                return proj[row : row + 128, lanes(f, other)].astype(f32)

            def prob(f, g):
                return probs[h * 2 + other, f * 4 + g : f * 4 + g + 1]

            grads = [grad[h * 128 : h * 128 + 128, lanes(f, other)] for f in range(4)]
            score = [[None] * 4 for _ in range(4)]
            for f in range(4):
                dprob = [jnp.sum(grads[f] * read(2, g), axis=0, keepdims=True) for g in range(4)]
                mean = sum(dprob[g] * prob(f, g) for g in range(4))
                for g in range(4):
                    score[f][g] = prob(f, g) * (dprob[g] - mean) * INV_ROOT
            for g in range(4):
                value = sum(prob(f, g).astype(bf16).astype(f32) * grads[f] for f in range(4))
                query = sum(score[g][i] * read(1, i) for i in range(4))
                key = sum(score[f][g] * read(0, f) for f in range(4))
                for j, out in enumerate((query, key, value)):
                    row = h * 384 + j * 128
                    delta[row : row + 128, lanes(g, other)] = out.astype(bf16)
    loads[1].wait()
    for h in range(2):
        factor = dot(slope[...], attended[h * 128 : h * 128 + 128].astype(f32), NT, HIGHEST)
        own_factor[h] = factor.astype(bf16)
    loads[2].wait()
    for (h, o), out in zip(FIRST, pieces):
        gradient_piece(delta, normed, own_factor[h], h, (place[h] + o) % 4, out)


def late_kernel(place, delta, own_factor, normed_far, own_x, own_y, last, normed, sems):
    load = pltpu.make_async_copy(normed_far, normed, sems.at[0])
    load.start()
    load.wait()
    for (h, o), out in (((1, 1), last), ((0, 0), own_x), ((1, 0), own_y)):
        gradient_piece(delta, normed, own_factor[h], h, (place[h] + o) % 4, out)


def add_first_kernel(place, *refs):
    both = refs[16]
    for h in range(2):
        parts, outs = refs[4 * h : 4 * h + 4], refs[8 + 4 * h : 12 + 4 * h]
        total = parts[0][...].astype(f32)
        for part in parts[1:]:
            total = total + part[...].astype(f32)
        both[...] = total.astype(bf16)
        for o, out in enumerate(outs):
            columns = pl.ds(pl.multiple_of(((place[1 - h] + o) % 4) * 128, 128), 128)
            out[:384] = both[:384, columns]
            for i in range(4):
                out[384 + i * 16 : 400 + i * 16] = both[384:, i * 128 : i * 128 + 128]


def add_second_kernel(*refs):
    factor = refs[10]
    for h in range(2):
        parts, owned = refs[4 * h : 4 * h + 4], refs[8 + h]
        total = parts[0][...].astype(f32)
        for part in parts[1:]:
            total = total + part[...].astype(f32)
        for j in range(3):
            owned[j] = total[j * 128 : j * 128 + 128].T.astype(bf16)
        factor[h * 128 : h * 128 + 128] = total[384:].T.astype(bf16)


def line_kernel(*refs):
    lines, both = refs[8:10], refs[10]
    for h in range(2):
        for o in range(4):
            piece = refs[4 * h + o][...]
            lines[h][o] = piece
            both[h, o] = piece


def join_kernel(a, b, c, out):
    for k, ref in enumerate((a, b, c)):
        out[k] = ref[...]


def assemble_kernel(tags, aliased, with_out, place, *refs):
    arrays = 1 + max(tag[0] for tag in tags)
    count = len(tags)
    sources, refs = refs[:arrays], refs[arrays + aliased :]
    if with_out:
        factors, head_t, line, out, grad_out, line_out, held, ready, done, sems, whole, sent = refs
        line_out[...] = line[...]
    else:
        out, held, ready, done, sems = refs
    loads = []
    for k, tag in enumerate(tags):
        source = sources[tag[0]] if tag[1] is None else sources[tag[0]].at[tag[1]]
        loads.append(pltpu.make_async_copy(source, held.at[k], sems.at[k]))
        loads[-1].start()
    if with_out:
        whole[...] = dot(factors[...], head_t[...])
        leave = pltpu.make_async_copy(whole, grad_out, sent.at[0])
        leave.start()
    stores = [None, None]
    slot = 1
    for k, tag in enumerate(tags):
        o, theirs, h, inners = tag[2:]
        loads[k].wait()
        if k == 0 or tags[k - 1][2:5] != tag[2:5]:
            slot = 1 - slot
            if stores[slot] is not None:
                stores[slot].wait()
        first = (place[h] + 4 - o) % 4
        for i, inner in enumerate(inners):
            second = (place[1 - h] + 4 - inner) % 4
            ready[slot, :, pl.ds(pl.multiple_of(second * 128, 128), 128)] = held[k, i].astype(f32)
        if k + 1 < count and tags[k + 1][2:5] == tag[2:5]:
            continue
        core = place[2] if theirs == 0 else 1 - place[2]
        stores[slot] = pltpu.make_async_copy(
            ready.at[slot],
            out.at[
                :,
                pl.ds(pl.multiple_of(first * 512, 512), 512),
                pl.ds(pl.multiple_of(core * 256 + h * 128, 128), 128),
            ],
            done.at[slot],
        )
        stores[slot].start()
    for store in stores:
        store.wait()
    if with_out:
        leave.wait()


def assemble(place, arrays, tags, onto=None, product=()):
    tags = tuple(sorted(tags, key=lambda t: t[2:]))
    given = [] if onto is None else [onto]
    out_shape = [shape((3, 2048, 512), f32)]
    out_specs = [HBM]
    scratch = [
        pltpu.VMEM((len(tags), *arrays[0].shape[-4:]), bf16),
        pltpu.VMEM((2, 3, 512, 128), f32),
        pltpu.SemaphoreType.DMA((2,)),
        pltpu.SemaphoreType.DMA((len(tags),)),
    ]
    if product:
        out_shape += [shape((512, 2048), f32), shape((4, 3, 128, 128), bf16)]
        out_specs += [HBM, VMEM]
        scratch += [pltpu.VMEM((512, 2048), f32), pltpu.SemaphoreType.DMA((1,))]
    return pl.pallas_call(
        functools.partial(assemble_kernel, tags, len(given), bool(product)),
        in_specs=[SMEM] + [ANY] * len(arrays) + [HBM] * len(given) + [VMEM] * len(product),
        out_specs=out_specs,
        out_shape=out_shape,
        scratch_shapes=scratch,
        input_output_aliases={1 + len(arrays): 0} if given else {},
        compiler_params=params(12),
        cost_estimate=TINY,
    )(place, *arrays, *given, *product)


def call(kernel, out, *operands, scratch=(), mib=8):
    result = pl.pallas_call(
        kernel,
        in_specs=[spec for spec, _ in operands],
        out_specs=[spec for spec, _ in out],
        out_shape=[made for _, made in out],
        scratch_shapes=list(scratch),
        compiler_params=params(mib),
        cost_estimate=TINY,
    )(*(array for _, array in operands))
    return result


def near(*arrays):
    return [(VMEM, a) for a in arrays]


def far(*arrays):
    return [(HBM, a) for a in arrays]


def shards(act, cache_rows, row_dest, time_index, w_embed, norm_gain, w_qkv, w_out, w_head):
    x, y, core, frame = (lax.axis_index(a).astype(jnp.int32) for a in ("x", "y", "core", "frame"))
    here = (SMEM, jnp.stack([frame, core]))
    square = (SMEM, jnp.stack([x, y, core]))
    dma = pltpu.SemaphoreType.DMA

    before, after = shift(act, "frame", 1), shift(act, "frame", 3)
    act_theirs = shift(act, "core", 1)
    (sent,) = call(
        bucket_kernel, near(shape((16, 16, 128), bf16)), *near(cache_rows, row_dest.reshape(1, 128))
    )
    arrived = lax.all_to_all(sent, ("y", "x"), 0, 0, tiled=True).reshape(256, 128)
    half_act = shape((64, 2048), bf16)
    top, bottom, sides, spread = call(
        sides_kernel,
        near(half_act, half_act, shape((2, 128, 2048), bf16), shape((8, 256, 128), bf16)),
        *near(before, after, arrived),
    )
    top, bottom = shift(top, "frame", 1), shift(bottom, "frame", 3)
    sides_theirs = shift(sides, "core", 1)
    arrived = lax.all_to_all(spread, ("core", "frame"), 0, 0, tiled=True)
    moment = (time_index.astype(f32) + 0.5) / TIMESTEPS
    moments = jnp.concatenate([moment, shift(moment, "core", 1)])

    head_t = w_head.T
    w_t, mix, mix_t = call(
        prepare_kernel,
        far(shape((768, 2048), bf16)) + near(shape((256, 64), f32), shape((64, 256), f32)),
        here, *far(w_qkv, w_out), *near(head_t),
        scratch=[
            pltpu.VMEM((3, 2048, 256), bf16),
            pltpu.VMEM((256, 2048), bf16),
            pltpu.VMEM((6, 128, 2048), bf16),
            dma((4,)),
            dma((6,)),
        ],
        mib=12,
    )
    (pairs,) = call(fetch_kernel, near(shape((8, 128, 128), bf16)), here, *near(arrived))
    normed, proj, attended, probs, part_own, part_other = call(
        forward_kernel,
        far(shape((1024, 2048), bf16), shape((768, 1024), bf16), shape((256, 1024), bf16))
        + near(shape((4, 16, 128), f32), shape((64, 512), f32), shape((64, 512), f32)),
        (SMEM, moments),
        *near(act, act_theirs, sides, sides_theirs, top, shift(top, "core", 1), bottom, shift(bottom, "core", 1)),
        *near(pairs, w_embed, norm_gain.reshape(1, 2048)), *far(w_t), *near(head_t, mix_t),
        scratch=[
            pltpu.VMEM((768, 2048), bf16),
            pltpu.VMEM((1024, 2048), bf16),
            pltpu.VMEM((768, 1024), bf16),
            pltpu.VMEM((256, 1024), bf16),
            pltpu.VMEM((64, 128), f32),
            dma((4,)),
        ],
        mib=16,
    )

    clip_part = part_own + shift(part_other, "core", 1)
    heard = {0: clip_part, **{o: shift(clip_part, "frame", o) for o in (1, 3, 2)}}
    error_own = jnp.concatenate(
        [
            sum(
                heard[o][:, SPOT[(r - o) % 4] * 128 : SPOT[(r - o) % 4] * 128 + 128]
                for o in range(4)
            )
            for r in ORDER
        ],
        axis=1,
    )
    frame_loss = jnp.mean(error_own[:, :128] * error_own[:, :128]).reshape(1, 1)
    error_other = shift(error_own, "core", 1)

    piece = shape((400, 512), bf16)
    small = shape((448, 128), bf16)
    block = shape((3, 128, 128), bf16)
    line = shape((4, 3, 128, 128), bf16)
    axes = (("x", "y"), ("y", "x"))
    *first, delta, own_factor = call(
        backward_kernel,
        near(*[piece] * 5, shape((768, 1024), bf16), shape((2, 64, 128), bf16)),
        square, *near(error_own, error_other, probs, mix), *far(proj, attended, normed),
        scratch=[
            pltpu.VMEM((64, 1024), f32),
            pltpu.VMEM((256, 1024), f32),
            pltpu.VMEM((768, 1024), bf16),
            pltpu.VMEM((256, 1024), bf16),
            pltpu.VMEM((1024, 2048), bf16),
            dma((3,)),
        ],
        mib=16,
    )
    moved = [[], []]
    for (h, o), p in zip(FIRST, first):
        moved[h].append(shift(p, axes[h][0], o))
    own_x, own_y, last = call(
        late_kernel, near(*[piece] * 3), square, *near(delta, own_factor), *far(normed),
        scratch=[pltpu.VMEM((1024, 2048), bf16), dma((1,))],
    )
    moved[1].append(shift(last, axes[1][0], 1))
    second = call(
        add_first_kernel, near(*[small] * 8), square, *near(own_x, *moved[0], own_y, *moved[1]),
        scratch=[pltpu.VMEM((400, 512), bf16)],
    )
    moved = [[shift(second[h * 4 + o], axes[h][1], o) for o in (1, 3, 2)] for h in range(2)]
    *owned, factor = call(
        add_second_kernel, near(block, block, shape((256, 64), bf16)),
        *near(second[0], *moved[0], second[4], *moved[1]),
    )
    back = [
        {0: owned[h], **{o: shift(owned[h], axes[h][1], o) for o in (1, 3, 2)}} for h in range(2)
    ]
    factor_theirs = shift(factor, "core", 1)
    factors = jnp.concatenate(
        [jnp.where(core == 0, factor, factor_theirs), jnp.where(core == 0, factor_theirs, factor)]
    )
    line_x, line_y, lines = call(
        line_kernel, near(line, line, shape((2, 4, 3, 128, 128), bf16)),
        *near(*(back[h][o] for h in range(2) for o in range(4))),
    )
    every = (0, 1, 2, 3)
    wide = {(h, o): shift((line_x, line_y)[h], axes[h][0], o) for h, o in FIRST}
    grad_qkv, grad_out, line_last = assemble(
        square[1], (lines,), [(0, h, 0, 0, h, every) for h in range(2)], None, (factors, head_t, line_y)
    )
    wide[1, 1] = shift(line_last, axes[1][0], 1)
    lines_theirs = shift(lines, "core", 1)
    reach = (1, 3, 2)
    triple = near(shape((3, 4, 3, 128, 128), bf16))
    (wide_x,) = call(join_kernel, triple, *near(*(wide[0, o] for o in reach)))
    wide_x_theirs = shift(wide_x, "core", 1)
    (wide_y,) = call(join_kernel, triple, *near(*(wide[1, o] for o in reach)))
    wide_y_theirs = shift(wide_y, "core", 1)

    def placed(array, side, h):
        return [(array, k, reach[k], side, h, every) for k in range(3)]

    (grad_qkv,) = assemble(
        square[1], (lines_theirs,), [(0, h, 0, 1, h, every) for h in range(2)], grad_qkv
    )
    (grad_qkv,) = assemble(
        square[1], (wide_x, wide_x_theirs), placed(0, 0, 0) + placed(1, 1, 0), grad_qkv
    )
    (grad_qkv,) = assemble(square[1], (wide_y,), placed(0, 0, 1), grad_qkv)
    (grad_qkv,) = assemble(square[1], (wide_y_theirs,), placed(0, 1, 1), grad_qkv)
    return frame_loss, grad_qkv, grad_out


def solution(mesh):
    fine = Mesh(mesh.devices.reshape(4, 4, 2, 4), ("y", "x", "core", "frame"))
    store = ("y", "x", "core")
    in_specs = (
        P((*store, "frame"), None),
        P((*store, "frame"), None),
        P((*store, "frame")),
        P(store),
        P(),
        P(),
        P(None, None, "frame"),
        P("frame", None),
        P(),
    )
    out_specs = (P(store, "frame"), P(None, None, "frame"), P("frame", None))
    return jax.shard_map(shards, mesh=fine, in_specs=in_specs, out_specs=out_specs, check_vma=False)
```

profile of v0, /device:TPU:1, one launch (start us, length us, event | category | flops | bytes accessed | tf_op | source)
XLA Modules:
  0.0 201.5 jit_solution(10810465939871537745)
XLA Ops:
  0.6 2.5 %collective-permute-start.2 = (bf16[128,2048]{1,0:T(8,128)(2,1)}, bf16[128,2048]{1,0:T(8,128)(2,1)S(1)}, u32[]{:S(2)}, u32[]{:S(2)}) collective-permute-start(bf16[128,2048]{1,0:T(8,128)(2,1)} %refs_0_.1), channel_id=1, source_target_pairs={{0,1},{1,2},{2,3},{3,0},{4,5},{5,6},{6,7},{7,4},{8,9},{9,10},{10,1... | collective-permute-start | bytes 1572872 | tf_op jit(solution)/shard_map/ppermute | solution.py:47
  3.2 2.2 %collective-permute-start.3 = (bf16[128,2048]{1,0:T(8,128)(2,1)}, bf16[128,2048]{1,0:T(8,128)(2,1)S(1)}, u32[]{:S(2)}, u32[]{:S(2)}) collective-permute-start(bf16[128,2048]{1,0:T(8,128)(2,1)} %refs_0_.1), channel_id=1, source_target_pairs={{0,3},{1,0},{2,1},{3,2},{4,7},{5,4},{6,5},{7,6},{8,11},{9,8},{10,9... | collective-permute-start | bytes 1572872 | tf_op jit(solution)/shard_map/ppermute | solution.py:47
  7.1 13.1 %all_to_all.10 = bf16[16,16,128]{2,1,0:T(8,128)(2,1)S(1)} all-to-all(bf16[16,16,128]{2,1,0:T(8,128)(2,1)S(1)} %shard_map.112), channel_id=1, replica_groups=mesh['y'=4,'x'=4,'core'=2,'frame'=4] {'y','x'}, dimensions={0} | all-to-all | bytes 131072 | tf_op jit(solution)/shard_map/all_to_all | solution.py:408
  21.5 2.4 %collective-permute-start.4 = (bf16[2,128,2048]{2,1,0:T(8,128)(2,1)}, bf16[2,128,2048]{2,1,0:T(8,128)(2,1)}, u32[]{:S(2)}, u32[]{:S(2)}) collective-permute-start(bf16[2,128,2048]{2,1,0:T(8,128)(2,1)} %get-tuple-element.43.refs_2_), channel_id=1, source_target_pairs={{0,4},{4,0},{1,5},{5,1},{2,6},{6,2},{3,7},{7,3},{8,12},{12,8},{9,1... | collective-permute-start | bytes 3145736 | tf_op jit(solution)/shard_map/ppermute | solution.py:47
  23.8 2.7 %collective-permute-start.7 = (bf16[64,2048]{1,0:T(8,128)(2,1)S(1)}, bf16[64,2048]{1,0:T(8,128)(2,1)}, u32[]{:S(2)}, u32[]{:S(2)}) collective-permute-start(bf16[64,2048]{1,0:T(8,128)(2,1)S(1)} %get-tuple-element.45), channel_id=1, source_target_pairs={{0,3},{1,0},{2,1},{3,2},{4,7},{5,4},{6,5},{7,6},{8,11},{9,8},{10,9... | collective-permute-start | bytes 786440 | tf_op jit(solution)/shard_map/ppermute | solution.py:47
  26.5 5.1 %all-to-all-start.1 = ((bf16[8,256,128]{2,1,0:T(8,128)(2,1)}), bf16[8,256,128]{2,1,0:T(8,128)(2,1)}, u32[]{:S(2)}, u32[]{:S(2)}) async-start(bf16[8,256,128]{2,1,0:T(8,128)(2,1)} %get-tuple-element.46), calls=%async_computation.1 | async-start | bytes 1048576 | tf_op jit(solution)/shard_map/all_to_all | solution.py:417
  34.5 1.6 collective-permute-start
  36.2 2.8 %copy-done.2 = bf16[3,2048,512]{2,1,0:T(8,128)(2,1)S(1)} copy-done((bf16[3,2048,512]{2,1,0:T(8,128)(2,1)S(1)}, bf16[3,2048,512]{2,1,0:T(8,128)(2,1)}, u32[]{:S(2)}) %copy-start.2) | copy-done | bytes 6291480
  39.9 1.6 copy-done.5
  41.5 3.0 %shard_map.115 = (bf16[768,2048]{1,0:T(8,128)(2,1)S(1)}, f32[256,64]{1,0:T(8,128)S(1)}, f32[64,256]{1,0:T(8,128)S(1)}) custom-call(s32[2]{0:T(128)S(1)} %pad_add_fusion.place, bf16[3,2048,512]{2,1,0:T(8,128)(2,1)S(1)} %copy-done.2, bf16[512,2048]{1,0:T(8,128)(2,1)S(1)} %copy-done.5, bf16[64,2048]{1,0:T(8,128)(2,1)S(1)} %bitcast.9), custom_call_target="tpu_custom_call" | custom-call | bytes 1024 | tf_op jit(solution)/shard_map/pallas_call | solution.py:377
  45.9 4.9 %shard_map.114.refs_8_ = bf16[8,128,128]{2,1,0:T(8,128)(2,1)S(1)} custom-call(s32[2]{0:T(128)S(1)} %pad_add_fusion.place, bf16[8,256,128]{2,1,0:T(8,128)(2,1)} %all-to-all-done.1.arrived), custom_call_target="tpu_custom_call" | custom-call | bytes 1024 | tf_op jit(solution)/shard_map/pallas_call | solution.py:377
  53.6 10.9 %shard_map.116 = (bf16[1024,2048]{1,0:T(8,128)(2,1)S(1)}, bf16[768,1024]{1,0:T(8,128)(2,1)S(1)}, bf16[256,1024]{1,0:T(8,128)(2,1)S(1)}, f32[4,16,128]{2,1,0:T(8,...) custom-call(f32[2]{0:T(128)S(1)} %pad_maximum_fusion.2.moments, bf16[128,2048]{1,0:T(8,128)(2,1)S(1)} %copy-done.8, ...), custom_call_target="tpu_custom_call" | custom-call | bytes 1024 | tf_op jit(solution)/shard_map/pallas_call | solution.py:377
  64.6 2.0 copy-done
  69.2 3.7 %collective-permute-start.11 = (f32[64,512]{1,0:T(8,128)S(1)}, f32[64,512]{1,0:T(8,128)S(1)}, u32[]{:S(2)}, u32[]{:S(2)}) collective-permute-start(f32[64,512]{1,0:T(8,128)S(1)} %add.43), channel_id=1, source_target_pairs={{0,2},{1,3},{2,0},{3,1},{4,6},{5,7},{6,4},{7,5},{8,10},{9,11},{10,... | collective-permute-start | bytes 393224 | tf_op jit(solution)/shard_map/ppermute | solution.py:47
  72.9 2.4 %collective-permute-done.10 = f32[64,512]{1,0:T(8,128)S(1)} collective-permute-done((f32[64,512]{1,0:T(8,128)S(1)}, f32[64,512]{1,0:T(8,128)S(1)}, u32[]{:S(2)}, u32[]{:S(2)}) %collective-permute-start.10) | collective-permute-done | bytes 131104 | tf_op jit(solution)/shard_map/ppermute | solution.py:47
  75.3 3.6 %collective-permute-done.11 = f32[64,512]{1,0:T(8,128)S(1)} collective-permute-done((f32[64,512]{1,0:T(8,128)S(1)}, f32[64,512]{1,0:T(8,128)S(1)}, u32[]{:S(2)}, u32[]{:S(2)}) %collective-permute-start.11) | collective-permute-done | bytes 131104 | tf_op jit(solution)/shard_map/ppermute | solution.py:47
  81.9 2.2 %copy-done.1 = bf16[1024,2048]{1,0:T(8,128)(2,1)S(1)} copy-done((bf16[1024,2048]{1,0:T(8,128)(2,1)S(1)}, bf16[1024,2048]{1,0:T(8,128)(2,1)}, u32[]{:S(2)}) %copy-start.1) | copy-done | bytes 4194328
  84.1 1.4 copy-done.7
  87.3 6.9 %shard_map.117 = (bf16[400,512]{1,0:T(8,128)(2,1)S(1)}, bf16[400,512]{1,0:T(8,128)(2,1)S(1)}, bf16[400,512]{1,0:T(8,128)(2,1)S(1)}, bf16[400,512]{1,0:T(8,128)(2...) custom-call(s32[3]{0:T(128)S(1)} %pad_add_fusion.1.place, ...), custom_call_target="tpu_custom_call" | custom-call | bytes 1024 | tf_op jit(solution)/shard_map/pallas_call | solution.py:377
  94.3 2.2 %shard_map.118 = (bf16[400,512]{1,0:T(8,128)(2,1)S(1)}, bf16[400,512]{1,0:T(8,128)(2,1)S(1)}, bf16[400,512]{1,0:T(8,128)(2,1)S(1)}) custom-call(s32[3]{0:T(128)S(1)} %pad_add_fusion.1.place, bf16[768,1024]{1,0:T(8,128)(2,1)S(1)} %get-tuple-element.56.delta, bf16[2,64,128]{2,1,0:T(8,128)(2,1)S(1)} %get-tuple-element.57.own_factor, ...), custom_call_target="tpu_custom_call" | custom-call | bytes 1024 | tf_op jit(solution)/shard_map/pallas_call | solution.py:377
  97.1 2.4 %collective-permute-start.15 = (bf16[400,512]{1,0:T(8,128)(2,1)S(1)}, bf16[400,512]{1,0:T(8,128)(2,1)S(1)}, u32[]{:S(2)}, u32[]{:S(2)}) collective-permute-start(bf16[400,512]{1,0:T(8,128)(2,1)S(1)} %get-tuple-element.60), channel_id=1, source_target_pairs={{0,24},{8,0},{16,8},{24,16},{1,25},{9,1},{17,9},{25,17},{2,26},{10... | collective-permute-start | bytes 1228808 | tf_op jit(solution)/shard_map/ppermute | solution.py:47
  99.5 2.4 %collective-permute-start.17 = (bf16[400,512]{1,0:T(8,128)(2,1)S(1)}, bf16[400,512]{1,0:T(8,128)(2,1)S(1)}, u32[]{:S(2)}, u32[]{:S(2)}) collective-permute-start(bf16[400,512]{1,0:T(8,128)(2,1)S(1)} %get-tuple-element.63), channel_id=1, source_target_pairs={{0,96},{32,0},{64,32},{96,64},{1,97},{33,1},{65,33},{97,65},{2,98}... | collective-permute-start | bytes 1228808 | tf_op jit(solution)/shard_map/ppermute | solution.py:47
  101.9 6.5 %collective-permute-done.19.refs_7_ = bf16[400,512]{1,0:T(8,128)(2,1)S(1)} collective-permute-done((bf16[400,512]{1,0:T(8,128)(2,1)S(1)}, bf16[400,512]{1,0:T(8,128)(2,1)S(1)}, u32[]{:S(2)}, u32[]{:S(2)}) %collective-permute-start.19) | collective-permute-done | bytes 409632 | tf_op jit(solution)/shard_map/ppermute | solution.py:47
  109.0 7.7 %collective-permute-done.16.refs_3_ = bf16[400,512]{1,0:T(8,128)(2,1)S(1)} collective-permute-done((bf16[400,512]{1,0:T(8,128)(2,1)S(1)}, bf16[400,512]{1,0:T(8,128)(2,1)S(1)}, u32[]{:S(2)}, u32[]{:S(2)}) %collective-permute-start.16) | collective-permute-done | bytes 409632 | tf_op jit(solution)/shard_map/ppermute | solution.py:47
  116.7 3.1 %collective-permute-done.18.refs_6_ = bf16[400,512]{1,0:T(8,128)(2,1)S(1)} collective-permute-done((bf16[400,512]{1,0:T(8,128)(2,1)S(1)}, bf16[400,512]{1,0:T(8,128)(2,1)S(1)}, u32[]{:S(2)}, u32[]{:S(2)}) %collective-permute-start.18) | collective-permute-done | bytes 409632 | tf_op jit(solution)/shard_map/ppermute | solution.py:47
  119.8 1.5 shard_map.119
  121.9 2.0 %collective-permute-start.21 = (bf16[448,128]{1,0:T(8,128)(2,1)S(1)}, bf16[448,128]{1,0:T(8,128)(2,1)S(1)}, u32[]{:S(2)}, u32[]{:S(2)}) collective-permute-start(bf16[448,128]{1,0:T(8,128)(2,1)S(1)} %get-tuple-element.68), channel_id=1, source_target_pairs={{0,96},{32,0},{64,32},{96,64},{1,97},{33,1},{65,33},{97,65},{2,98}... | collective-permute-start | bytes 344072 | tf_op jit(solution)/shard_map/ppermute | solution.py:47
  124.3 2.4 %collective-permute-start.24 = (bf16[448,128]{1,0:T(8,128)(2,1)S(1)}, bf16[448,128]{1,0:T(8,128)(2,1)S(1)}, u32[]{:S(2)}, u32[]{:S(2)}) collective-permute-start(bf16[448,128]{1,0:T(8,128)(2,1)S(1)} %get-tuple-element.72), channel_id=1, source_target_pairs={{0,24},{8,0},{16,8},{24,16},{1,25},{9,1},{17,9},{25,17},{2,26},{10... | collective-permute-start | bytes 344072 | tf_op jit(solution)/shard_map/ppermute | solution.py:47
  127.4 2.8 %collective-permute-done.22.refs_3_ = bf16[448,128]{1,0:T(8,128)(2,1)S(1)} collective-permute-done((bf16[448,128]{1,0:T(8,128)(2,1)S(1)}, bf16[448,128]{1,0:T(8,128)(2,1)S(1)}, u32[]{:S(2)}, u32[]{:S(2)}) %collective-permute-start.22) | collective-permute-done | bytes 114720 | tf_op jit(solution)/shard_map/ppermute | solution.py:47
  130.3 2.2 %collective-permute-done.25.refs_7_ = bf16[448,128]{1,0:T(8,128)(2,1)S(1)} collective-permute-done((bf16[448,128]{1,0:T(8,128)(2,1)S(1)}, bf16[448,128]{1,0:T(8,128)(2,1)S(1)}, u32[]{:S(2)}, u32[]{:S(2)}) %collective-permute-start.25) | collective-permute-done | bytes 114720 | tf_op jit(solution)/shard_map/ppermute | solution.py:47
  133.2 3.1 %collective-permute-start.27 = (bf16[3,128,128]{2,1,0:T(8,128)(2,1)S(1)}, bf16[3,128,128]{2,1,0:T(8,128)(2,1)S(1)}, u32[]{:S(2)}, u32[]{:S(2)}) collective-permute-start(bf16[3,128,128]{2,1,0:T(8,128)(2,1)S(1)} %get-tuple-element.74.refs_0_), channel_id=1, source_target_pairs={{0,64},{32,96},{64,0},{96,32},{1,65},{33,97},{65,1},{97,33},{2,66}... | collective-permute-start | bytes 294920 | tf_op jit(solution)/shard_map/ppermute | solution.py:47
  136.3 2.0 collective-permute-start.28
  139.2 1.7 collective-permute-start.31
  141.0 3.1 %collective-permute-done.29.refs_5_ = bf16[3,128,128]{2,1,0:T(8,128)(2,1)S(1)} collective-permute-done((bf16[3,128,128]{2,1,0:T(8,128)(2,1)S(1)}, bf16[3,128,128]{2,1,0:T(8,128)(2,1)S(1)}, u32[]{:S(2)}, u32[]{:S(2)}) %collective-permute-start.29) | collective-permute-done | bytes 98336 | tf_op jit(solution)/shard_map/ppermute | solution.py:47
  146.2 6.3 %collective-permute-start.32 = (bf16[256,64]{1,0:T(8,128)(2,1)S(1)}, bf16[256,64]{1,0:T(8,128)(2,1)S(1)}, u32[]{:S(2)}, u32[]{:S(2)}) collective-permute-start(bf16[256,64]{1,0:T(8,128)(2,1)S(1)} %get-tuple-element.77), channel_id=1, source_target_pairs={{0,4},{4,0},{1,5},{5,1},{2,6},{6,2},{3,7},{7,3},{8,12},{12,8},{9,1... | collective-permute-start | bytes 98312 | tf_op jit(solution)/shard_map/ppermute | solution.py:47
  153.5 2.0 %collective-permute-start.38 = (bf16[4,3,128,128]{3,2,1,0:T(8,128)(2,1)S(1)}, bf16[4,3,128,128]{3,2,1,0:T(8,128)(2,1)S(1)}, u32[]{:S(2)}, u32[]{:S(2)}) collective-permute-start(bf16[4,3,128,128]{3,2,1,0:T(8,128)(2,1)S(1)} %get-tuple-element.80), channel_id=1, source_target_pairs={{0,24},{8,0},{16,8},{24,16},{1,25},{9,1},{17,9},{25,17},{2,26},{10... | collective-permute-start | bytes 1179656 | tf_op jit(solution)/shard_map/ppermute | solution.py:47
  156.6 4.3 %shard_map.122 = (f32[3,2048,512]{2,1,0:T(8,128)}, f32[512,2048]{1,0:T(8,128)}, bf16[4,3,128,128]{3,2,1,0:T(8,128)(2,1)S(1)}) custom-call(s32[3]{0:T(128)S(1)} %pad_add_fusion.1.place, bf16[2,4,3,128,128]{4,3,2,1,0:T(8,128)(2,1)} %get-tuple-element.76.refs_0_, bf16[512,64]{1,0:T(8,128)(2,1)S(1)} %pad_maximum_fusion.1.refs_1_, bf16[64,2048]{1,0:T(8,128)(2,1)S(1)} %bitcast.11, ...), custom_call_target="tpu_custom_call" | custom-call | bytes 1024 | tf_op jit(solution)/shard_map/pallas_call | solution.py:364
  160.8 1.5 collective-permute-start.33
  162.6 1.4 collective-permute-done.38.b
  164.0 4.3 %collective-permute-done.39.c = bf16[4,3,128,128]{3,2,1,0:T(8,128)(2,1)S(1)} collective-permute-done((bf16[4,3,128,128]{3,2,1,0:T(8,128)(2,1)S(1)}, bf16[4,3,128,128]{3,2,1,0:T(8,128)(2,1)S(1)}, u32[]{:S(2)}, u32[]{:S(2)}) %collective-permute-start.39) | collective-permute-done | bytes 393248 | tf_op jit(solution)/shard_map/ppermute | solution.py:47
  168.3 5.2 %collective-permute-start.40 = (bf16[3,4,3,128,128]{4,3,2,1,0:T(8,128)(2,1)S(1)}, bf16[3,4,3,128,128]{4,3,2,1,0:T(8,128)(2,1)S(1)}, u32[]{:S(2)}, u32[]{:S(2)}) collective-permute-start(bf16[3,4,3,128,128]{4,3,2,1,0:T(8,128)(2,1)S(1)} %shard_map.124.refs_0_), channel_id=1, source_target_pairs={{0,4},{4,0},{1,5},{5,1},{2,6},{6,2},{3,7},{7,3},{8,12},{12,8},{9,1... | collective-permute-start | bytes 3538952 | tf_op jit(solution)/shard_map/ppermute | solution.py:47
  173.5 5.8 %collective-permute-done.35.c = bf16[4,3,128,128]{3,2,1,0:T(8,128)(2,1)S(1)} collective-permute-done((bf16[4,3,128,128]{3,2,1,0:T(8,128)(2,1)}, bf16[4,3,128,128]{3,2,1,0:T(8,128)(2,1)S(1)}, u32[]{:S(2)}, u32[]{:S(2)}) %collective-permute-start.35) | collective-permute-done | bytes 393248 | tf_op jit(solution)/shard_map/ppermute | solution.py:47
  179.4 2.8 %collective-permute-start.36 = (bf16[3,4,3,128,128]{4,3,2,1,0:T(8,128)(2,1)S(1)}, bf16[3,4,3,128,128]{4,3,2,1,0:T(8,128)(2,1)}, u32[]{:S(2)}, u32[]{:S(2)}) collective-permute-start(bf16[3,4,3,128,128]{4,3,2,1,0:T(8,128)(2,1)S(1)} %shard_map.123.refs_0_), channel_id=1, source_target_pairs={{0,4},{4,0},{1,5},{5,1},{2,6},{6,2},{3,7},{7,3},{8,12},{12,8},{9,1... | collective-permute-start | bytes 3538952 | tf_op jit(solution)/shard_map/ppermute | solution.py:47
  183.0 3.2 %collective-permute-done.41.refs_0_ = bf16[2,4,3,128,128]{4,3,2,1,0:T(8,128)(2,1)} collective-permute-done((bf16[2,4,3,128,128]{4,3,2,1,0:T(8,128)(2,1)}, bf16[2,4,3,128,128]{4,3,2,1,0:T(8,128)(2,1)}, u32[]{:S(2)}, u32[]{:S(2)}) %collective-permute-start.41) | collective-permute-done | bytes 786464 | tf_op jit(solution)/shard_map/ppermute | solution.py:47
  186.2 2.8 %shard_map.125.refs_2_ = f32[3,2048,512]{2,1,0:T(8,128)} custom-call(s32[3]{0:T(128)S(1)} %pad_add_fusion.1.place, bf16[2,4,3,128,128]{4,3,2,1,0:T(8,128)(2,1)} %collective-permute-done.41.refs_0_, f32[3,2048,512]{2,1,0:T(8,128)} %get-tuple-element.81.refs_1_), custom_call_target="tpu_custom_call", output_to_operand_aliasing={{}: (2, {})} | custom-call | bytes 1024 | tf_op jit(solution)/shard_map/pallas_call | solution.py:364
  189.0 4.8 %shard_map.126.refs_1_ = f32[3,2048,512]{2,1,0:T(8,128)} custom-call(s32[3]{0:T(128)S(1)} %pad_add_fusion.1.place, bf16[3,4,3,128,128]{4,3,2,1,0:T(8,128)(2,1)S(1)} %shard_map.124.refs_0_, bf16[3,4,3,128,128]{4,3,2,1,0:T(8,128)(2,1)S(1)} %collective-permute-done.40.refs_1_, f32[3,2048,512]{2,1,0:T(8,128)} %shard_map.125.refs_2_), custom_call_target="tpu_custom_call", output_to_operand_aliasing={{}: (3, {})} | custom-call | bytes 1024 | tf_op jit(solution)/shard_map/pallas_call | solution.py:364
  193.8 3.0 %shard_map.127.refs_1_ = f32[3,2048,512]{2,1,0:T(8,128)} custom-call(s32[3]{0:T(128)S(1)} %pad_add_fusion.1.place, bf16[3,4,3,128,128]{4,3,2,1,0:T(8,128)(2,1)S(1)} %shard_map.123.refs_0_, f32[3,2048,512]{2,1,0:T(8,128)} %shard_map.126.refs_1_), custom_call_target="tpu_custom_call", output_to_operand_aliasing={{}: (2, {})} | custom-call | bytes 1024 | tf_op jit(solution)/shard_map/pallas_call | solution.py:364
  196.9 3.5 %shard_map.128 = f32[3,2048,512]{2,1,0:T(8,128)} custom-call(s32[3]{0:T(128)S(1)} %pad_add_fusion.1.place, bf16[3,4,3,128,128]{4,3,2,1,0:T(8,128)(2,1)} %collective-permute-done.36.refs_0_, f32[3,2048,512]{2,1,0:T(8,128)} %shard_map.127.refs_1_), custom_call_target="tpu_custom_call", output_to_operand_aliasing={{}: (2, {})} | custom-call | bytes 1024 | tf_op jit(solution)/shard_map/pallas_call | solution.py:364
  (102 shorter events, 27.0 us)
Async XLA Ops:
  0.6 19.5 %collective-permute-start.2 = (bf16[128,2048]{1,0:T(8,128)(2,1)}, bf16[128,2048]{1,0:T(8,128)(2,1)S(1)}, u32[]{:S(2)}, u32[]{:S(2)}) collective-permute-start(bf16[128,2048]{1,0:T(8,128)(2,1)} %refs_0_.1), channel_id=1, source_target_pairs={{0,1},{1,2},{2,3},{3,0},{4,5},{5,6},{6,7},{7,4},{8,9},{9,10},{10,1... | collective-permute-start | bytes 1572872 | tf_op jit(solution)/shard_map/ppermute | solution.py:47
  3.2 17.0 %collective-permute-start.3 = (bf16[128,2048]{1,0:T(8,128)(2,1)}, bf16[128,2048]{1,0:T(8,128)(2,1)S(1)}, u32[]{:S(2)}, u32[]{:S(2)}) collective-permute-start(bf16[128,2048]{1,0:T(8,128)(2,1)} %refs_0_.1), channel_id=1, source_target_pairs={{0,3},{1,0},{2,1},{3,2},{4,7},{5,4},{6,5},{7,6},{8,11},{9,8},{10,9... | collective-permute-start | bytes 1572872 | tf_op jit(solution)/shard_map/ppermute | solution.py:47
  21.5 29.3 %collective-permute-start.4 = (bf16[2,128,2048]{2,1,0:T(8,128)(2,1)}, bf16[2,128,2048]{2,1,0:T(8,128)(2,1)}, u32[]{:S(2)}, u32[]{:S(2)}) collective-permute-start(bf16[2,128,2048]{2,1,0:T(8,128)(2,1)} %get-tuple-element.43.refs_2_), channel_id=1, source_target_pairs={{0,4},{4,0},{1,5},{5,1},{2,6},{6,2},{3,7},{7,3},{8,12},{12,8},{9,1... | collective-permute-start | bytes 3145736 | tf_op jit(solution)/shard_map/ppermute | solution.py:47
  23.8 26.9 %collective-permute-start.1 = (bf16[128,2048]{1,0:T(8,128)(2,1)}, bf16[128,2048]{1,0:T(8,128)(2,1)}, u32[]{:S(2)}, u32[]{:S(2)}) collective-permute-start(bf16[128,2048]{1,0:T(8,128)(2,1)} %refs_0_.1), channel_id=1, source_target_pairs={{0,4},{4,0},{1,5},{5,1},{2,6},{6,2},{3,7},{7,3},{8,12},{12,8},{9,1... | collective-permute-start | bytes 1572872 | tf_op jit(solution)/shard_map/ppermute | solution.py:47
  23.8 8.7 %collective-permute-start.5 = (bf16[64,2048]{1,0:T(8,128)(2,1)S(1)}, bf16[64,2048]{1,0:T(8,128)(2,1)}, u32[]{:S(2)}, u32[]{:S(2)}) collective-permute-start(bf16[64,2048]{1,0:T(8,128)(2,1)S(1)} %get-tuple-element.44), channel_id=1, source_target_pairs={{0,1},{1,2},{2,3},{3,0},{4,5},{5,6},{6,7},{7,4},{8,9},{9,10},{10,1... | collective-permute-start | bytes 786440 | tf_op jit(solution)/shard_map/ppermute | solution.py:47
  23.8 10.0 %collective-permute-start.7 = (bf16[64,2048]{1,0:T(8,128)(2,1)S(1)}, bf16[64,2048]{1,0:T(8,128)(2,1)}, u32[]{:S(2)}, u32[]{:S(2)}) collective-permute-start(bf16[64,2048]{1,0:T(8,128)(2,1)S(1)} %get-tuple-element.45), channel_id=1, source_target_pairs={{0,3},{1,0},{2,1},{3,2},{4,7},{5,4},{6,5},{7,6},{8,11},{9,8},{10,9... | collective-permute-start | bytes 786440 | tf_op jit(solution)/shard_map/ppermute | solution.py:47
  26.5 19.4 %all-to-all-start.1 = ((bf16[8,256,128]{2,1,0:T(8,128)(2,1)}), bf16[8,256,128]{2,1,0:T(8,128)(2,1)}, u32[]{:S(2)}, u32[]{:S(2)}) async-start(bf16[8,256,128]{2,1,0:T(8,128)(2,1)} %get-tuple-element.46), calls=%async_computation.1 | async-start | bytes 1048576 | tf_op jit(solution)/shard_map/all_to_all | solution.py:417
  32.5 18.3 %collective-permute-start.6 = (bf16[64,2048]{1,0:T(8,128)(2,1)}, bf16[64,2048]{1,0:T(8,128)(2,1)}, u32[]{:S(2)}, u32[]{:S(2)}) collective-permute-start(bf16[64,2048]{1,0:T(8,128)(2,1)} %collective-permute-done.5.refs_4_), channel_id=1, source_target_pairs={{0,4},{4,0},{1,5},{5,1},{2,6},{6,2},{3,7},{7,3},{8,12},{12,8},{9,1... | collective-permute-start | bytes 786440 | tf_op jit(solution)/shard_map/ppermute | solution.py:47
  33.9 16.9 %collective-permute-start.8 = (bf16[64,2048]{1,0:T(8,128)(2,1)}, bf16[64,2048]{1,0:T(8,128)(2,1)}, u32[]{:S(2)}, u32[]{:S(2)}) collective-permute-start(bf16[64,2048]{1,0:T(8,128)(2,1)} %collective-permute-done.7.refs_6_), channel_id=1, source_target_pairs={{0,4},{4,0},{1,5},{5,1},{2,6},{6,2},{3,7},{7,3},{8,12},{12,8},{9,1... | collective-permute-start | bytes 786440 | tf_op jit(solution)/shard_map/ppermute | solution.py:47
  34.5 10.6 %collective-permute-start = (f32[1]{0:T(128)}, f32[1]{0:T(128)}, u32[]{:S(2)}, u32[]{:S(2)}) collective-permute-start(f32[1]{0:T(128)} %div.6), channel_id=1, source_target_pairs={{0,4},{4,0},{1,5},{5,1},{2,6},{6,2},{3,7},{7,3},{8,12},{12,8},{9,1... | collective-permute-start | bytes 20 | tf_op jit(solution)/shard_map/ppermute | solution.py:47
  36.2 2.8 %copy-start.2 = (bf16[3,2048,512]{2,1,0:T(8,128)(2,1)S(1)}, bf16[3,2048,512]{2,1,0:T(8,128)(2,1)}, u32[]{:S(2)}) copy-start(bf16[3,2048,512]{2,1,0:T(8,128)(2,1)} %w.1) | copy-start | bytes 18874372
  41.5 9.3 %copy-start.4 = (bf16[2048,64]{0,1:T(8,128)(2,1)S(1)}, bf16[2048,64]{0,1:T(8,128)(2,1)}, u32[]{:S(2)}) copy-start(bf16[2048,64]{0,1:T(8,128)(2,1)} %param.17) | copy-start | bytes 786436
  41.5 9.3 %copy-start.17 = (f32[2048]{0:T(1024)S(1)}, f32[2048]{0:T(1024)}, u32[]{:S(2)}) copy-start(f32[2048]{0:T(1024)} %param.14) | copy-start | bytes 24580
  67.7 11.9 %copy-start.9 = (bf16[256,1024]{1,0:T(8,128)(2,1)}, bf16[256,1024]{1,0:T(8,128)(2,1)S(1)}, u32[]{:S(2)}) copy-start(bf16[256,1024]{1,0:T(8,128)(2,1)S(1)} %get-tuple-element.54.attended_far) | copy-start | bytes 1572868
  67.7 11.9 %copy-start.14 = (f32[4,16,128]{2,1,0:T(8,128)}, f32[4,16,128]{2,1,0:T(8,128)S(1)}, u32[]{:S(2)}) copy-start(f32[4,16,128]{2,1,0:T(8,128)S(1)} %get-tuple-element.51.probs) | copy-start | bytes 98308
  67.7 1.3 collective-permute-start.9
  69.1 6.2 %collective-permute-start.10 = (f32[64,512]{1,0:T(8,128)S(1)}, f32[64,512]{1,0:T(8,128)S(1)}, u32[]{:S(2)}, u32[]{:S(2)}) collective-permute-start(f32[64,512]{1,0:T(8,128)S(1)} %add.43), channel_id=1, source_target_pairs={{0,1},{1,2},{2,3},{3,0},{4,5},{5,6},{6,7},{7,4},{8,9},{9,10},{10,1... | collective-permute-start | bytes 393224 | tf_op jit(solution)/shard_map/ppermute | solution.py:47
  69.2 9.8 %collective-permute-start.11 = (f32[64,512]{1,0:T(8,128)S(1)}, f32[64,512]{1,0:T(8,128)S(1)}, u32[]{:S(2)}, u32[]{:S(2)}) collective-permute-start(f32[64,512]{1,0:T(8,128)S(1)} %add.43), channel_id=1, source_target_pairs={{0,2},{1,3},{2,0},{3,1},{4,6},{5,7},{6,4},{7,5},{8,10},{9,11},{10,... | collective-permute-start | bytes 393224 | tf_op jit(solution)/shard_map/ppermute | solution.py:47
  72.9 6.1 %collective-permute-start.12 = (f32[64,512]{1,0:T(8,128)S(1)}, f32[64,512]{1,0:T(8,128)S(1)}, u32[]{:S(2)}, u32[]{:S(2)}) collective-permute-start(f32[64,512]{1,0:T(8,128)S(1)} %add.43), channel_id=1, source_target_pairs={{0,3},{1,0},{2,1},{3,2},{4,7},{5,4},{6,5},{7,6},{8,11},{9,8},{10,9... | collective-permute-start | bytes 393224 | tf_op jit(solution)/shard_map/ppermute | solution.py:47
  79.6 2.3 %collective-permute-start.13 = (f32[64,512]{1,0:T(8,128)S(1)}, f32[64,512]{1,0:T(8,128)S(1)}, u32[]{:S(2)}, u32[]{:S(2)}) collective-permute-start(f32[64,512]{1,0:T(8,128)S(1)} %pad_maximum_fusion.error_own), channel_id=1, source_target_pairs={{0,4},{4,0},{1,5},{5,1},{2,6},{6,2},{3,7},{7,3},{8,12},{12,8},{9,1... | collective-permute-start | bytes 393224 | tf_op jit(solution)/shard_map/ppermute | solution.py:47
  96.5 12.0 %collective-permute-start.19 = (bf16[400,512]{1,0:T(8,128)(2,1)S(1)}, bf16[400,512]{1,0:T(8,128)(2,1)S(1)}, u32[]{:S(2)}, u32[]{:S(2)}) collective-permute-start(bf16[400,512]{1,0:T(8,128)(2,1)S(1)} %get-tuple-element.65), channel_id=1, source_target_pairs={{0,32},{32,64},{64,96},{96,0},{1,33},{33,65},{65,97},{97,1},{2,34}... | collective-permute-start | bytes 1228808 | tf_op jit(solution)/shard_map/ppermute | solution.py:47
  96.8 12.1 %collective-permute-start.14 = (bf16[400,512]{1,0:T(8,128)(2,1)S(1)}, bf16[400,512]{1,0:T(8,128)(2,1)S(1)}, u32[]{:S(2)}, u32[]{:S(2)}) collective-permute-start(bf16[400,512]{1,0:T(8,128)(2,1)S(1)} %get-tuple-element.59), channel_id=1, source_target_pairs={{0,8},{8,16},{16,24},{24,0},{1,9},{9,17},{17,25},{25,1},{2,10},{10... | collective-permute-start | bytes 1228808 | tf_op jit(solution)/shard_map/ppermute | solution.py:47
  97.1 11.9 %collective-permute-start.15 = (bf16[400,512]{1,0:T(8,128)(2,1)S(1)}, bf16[400,512]{1,0:T(8,128)(2,1)S(1)}, u32[]{:S(2)}, u32[]{:S(2)}) collective-permute-start(bf16[400,512]{1,0:T(8,128)(2,1)S(1)} %get-tuple-element.60), channel_id=1, source_target_pairs={{0,24},{8,0},{16,8},{24,16},{1,25},{9,1},{17,9},{25,17},{2,26},{10... | collective-permute-start | bytes 1228808 | tf_op jit(solution)/shard_map/ppermute | solution.py:47
  99.5 17.2 %collective-permute-start.16 = (bf16[400,512]{1,0:T(8,128)(2,1)S(1)}, bf16[400,512]{1,0:T(8,128)(2,1)S(1)}, u32[]{:S(2)}, u32[]{:S(2)}) collective-permute-start(bf16[400,512]{1,0:T(8,128)(2,1)S(1)} %get-tuple-element.61), channel_id=1, source_target_pairs={{0,16},{8,24},{16,0},{24,8},{1,17},{9,25},{17,1},{25,9},{2,18},{10... | collective-permute-start | bytes 1228808 | tf_op jit(solution)/shard_map/ppermute | solution.py:47
  99.5 17.2 %collective-permute-start.17 = (bf16[400,512]{1,0:T(8,128)(2,1)S(1)}, bf16[400,512]{1,0:T(8,128)(2,1)S(1)}, u32[]{:S(2)}, u32[]{:S(2)}) collective-permute-start(bf16[400,512]{1,0:T(8,128)(2,1)S(1)} %get-tuple-element.63), channel_id=1, source_target_pairs={{0,96},{32,0},{64,32},{96,64},{1,97},{33,1},{65,33},{97,65},{2,98}... | collective-permute-start | bytes 1228808 | tf_op jit(solution)/shard_map/ppermute | solution.py:47
  108.5 11.3 %collective-permute-start.18 = (bf16[400,512]{1,0:T(8,128)(2,1)S(1)}, bf16[400,512]{1,0:T(8,128)(2,1)S(1)}, u32[]{:S(2)}, u32[]{:S(2)}) collective-permute-start(bf16[400,512]{1,0:T(8,128)(2,1)S(1)} %get-tuple-element.64), channel_id=1, source_target_pairs={{0,64},{32,96},{64,0},{96,32},{1,65},{33,97},{65,1},{97,33},{2,66}... | collective-permute-start | bytes 1228808 | tf_op jit(solution)/shard_map/ppermute | solution.py:47
  121.2 5.4 %collective-permute-start.20 = (bf16[448,128]{1,0:T(8,128)(2,1)S(1)}, bf16[448,128]{1,0:T(8,128)(2,1)S(1)}, u32[]{:S(2)}, u32[]{:S(2)}) collective-permute-start(bf16[448,128]{1,0:T(8,128)(2,1)S(1)} %get-tuple-element.67), channel_id=1, source_target_pairs={{0,32},{32,64},{64,96},{96,0},{1,33},{33,65},{65,97},{97,1},{2,34}... | collective-permute-start | bytes 344072 | tf_op jit(solution)/shard_map/ppermute | solution.py:47
  121.9 5.5 %collective-permute-start.21 = (bf16[448,128]{1,0:T(8,128)(2,1)S(1)}, bf16[448,128]{1,0:T(8,128)(2,1)S(1)}, u32[]{:S(2)}, u32[]{:S(2)}) collective-permute-start(bf16[448,128]{1,0:T(8,128)(2,1)S(1)} %get-tuple-element.68), channel_id=1, source_target_pairs={{0,96},{32,0},{64,32},{96,64},{1,97},{33,1},{65,33},{97,65},{2,98}... | collective-permute-start | bytes 344072 | tf_op jit(solution)/shard_map/ppermute | solution.py:47
  124.0 6.3 %collective-permute-start.22 = (bf16[448,128]{1,0:T(8,128)(2,1)S(1)}, bf16[448,128]{1,0:T(8,128)(2,1)S(1)}, u32[]{:S(2)}, u32[]{:S(2)}) collective-permute-start(bf16[448,128]{1,0:T(8,128)(2,1)S(1)} %get-tuple-element.69), channel_id=1, source_target_pairs={{0,64},{32,96},{64,0},{96,32},{1,65},{33,97},{65,1},{97,33},{2,66}... | collective-permute-start | bytes 344072 | tf_op jit(solution)/shard_map/ppermute | solution.py:47
  124.0 6.3 %collective-permute-start.23 = (bf16[448,128]{1,0:T(8,128)(2,1)S(1)}, bf16[448,128]{1,0:T(8,128)(2,1)S(1)}, u32[]{:S(2)}, u32[]{:S(2)}) collective-permute-start(bf16[448,128]{1,0:T(8,128)(2,1)S(1)} %get-tuple-element.71), channel_id=1, source_target_pairs={{0,8},{8,16},{16,24},{24,0},{1,9},{9,17},{17,25},{25,1},{2,10},{10... | collective-permute-start | bytes 344072 | tf_op jit(solution)/shard_map/ppermute | solution.py:47
  124.3 6.0 %collective-permute-start.24 = (bf16[448,128]{1,0:T(8,128)(2,1)S(1)}, bf16[448,128]{1,0:T(8,128)(2,1)S(1)}, u32[]{:S(2)}, u32[]{:S(2)}) collective-permute-start(bf16[448,128]{1,0:T(8,128)(2,1)S(1)} %get-tuple-element.72), channel_id=1, source_target_pairs={{0,24},{8,0},{16,8},{24,16},{1,25},{9,1},{17,9},{25,17},{2,26},{10... | collective-permute-start | bytes 344072 | tf_op jit(solution)/shard_map/ppermute | solution.py:47
  126.6 5.9 %collective-permute-start.25 = (bf16[448,128]{1,0:T(8,128)(2,1)S(1)}, bf16[448,128]{1,0:T(8,128)(2,1)S(1)}, u32[]{:S(2)}, u32[]{:S(2)}) collective-permute-start(bf16[448,128]{1,0:T(8,128)(2,1)S(1)} %get-tuple-element.73), channel_id=1, source_target_pairs={{0,16},{8,24},{16,0},{24,8},{1,17},{9,25},{17,1},{25,9},{2,18},{10... | collective-permute-start | bytes 344072 | tf_op jit(solution)/shard_map/ppermute | solution.py:47
  132.7 6.5 %collective-permute-start.26 = (bf16[3,128,128]{2,1,0:T(8,128)(2,1)S(1)}, bf16[3,128,128]{2,1,0:T(8,128)(2,1)S(1)}, u32[]{:S(2)}, u32[]{:S(2)}) collective-permute-start(bf16[3,128,128]{2,1,0:T(8,128)(2,1)S(1)} %get-tuple-element.74.refs_0_), channel_id=1, source_target_pairs={{0,32},{32,64},{64,96},{96,0},{1,33},{33,65},{65,97},{97,1},{2,34}... | collective-permute-start | bytes 294920 | tf_op jit(solution)/shard_map/ppermute | solution.py:47
  133.2 7.8 %collective-permute-start.27 = (bf16[3,128,128]{2,1,0:T(8,128)(2,1)S(1)}, bf16[3,128,128]{2,1,0:T(8,128)(2,1)S(1)}, u32[]{:S(2)}, u32[]{:S(2)}) collective-permute-start(bf16[3,128,128]{2,1,0:T(8,128)(2,1)S(1)} %get-tuple-element.74.refs_0_), channel_id=1, source_target_pairs={{0,64},{32,96},{64,0},{96,32},{1,65},{33,97},{65,1},{97,33},{2,66}... | collective-permute-start | bytes 294920 | tf_op jit(solution)/shard_map/ppermute | solution.py:47
  136.3 4.7 %collective-permute-start.28 = (bf16[3,128,128]{2,1,0:T(8,128)(2,1)S(1)}, bf16[3,128,128]{2,1,0:T(8,128)(2,1)S(1)}, u32[]{:S(2)}, u32[]{:S(2)}) collective-permute-start(bf16[3,128,128]{2,1,0:T(8,128)(2,1)S(1)} %get-tuple-element.74.refs_0_), channel_id=1, source_target_pairs={{0,96},{32,0},{64,32},{96,64},{1,97},{33,1},{65,33},{97,65},{2,98}... | collective-permute-start | bytes 294920 | tf_op jit(solution)/shard_map/ppermute | solution.py:47
  138.3 5.8 %collective-permute-start.29 = (bf16[3,128,128]{2,1,0:T(8,128)(2,1)S(1)}, bf16[3,128,128]{2,1,0:T(8,128)(2,1)S(1)}, u32[]{:S(2)}, u32[]{:S(2)}) collective-permute-start(bf16[3,128,128]{2,1,0:T(8,128)(2,1)S(1)} %get-tuple-element.75.refs_4_), channel_id=1, source_target_pairs={{0,8},{8,16},{16,24},{24,0},{1,9},{9,17},{17,25},{25,1},{2,10},{10... | collective-permute-start | bytes 294920 | tf_op jit(solution)/shard_map/ppermute | solution.py:47
  138.3 5.8 %collective-permute-start.30 = (bf16[3,128,128]{2,1,0:T(8,128)(2,1)S(1)}, bf16[3,128,128]{2,1,0:T(8,128)(2,1)S(1)}, u32[]{:S(2)}, u32[]{:S(2)}) collective-permute-start(bf16[3,128,128]{2,1,0:T(8,128)(2,1)S(1)} %get-tuple-element.75.refs_4_), channel_id=1, source_target_pairs={{0,16},{8,24},{16,0},{24,8},{1,17},{9,25},{17,1},{25,9},{2,18},{10... | collective-permute-start | bytes 294920 | tf_op jit(solution)/shard_map/ppermute | solution.py:47
  139.2 5.4 %collective-permute-start.31 = (bf16[3,128,128]{2,1,0:T(8,128)(2,1)S(1)}, bf16[3,128,128]{2,1,0:T(8,128)(2,1)S(1)}, u32[]{:S(2)}, u32[]{:S(2)}) collective-permute-start(bf16[3,128,128]{2,1,0:T(8,128)(2,1)S(1)} %get-tuple-element.75.refs_4_), channel_id=1, source_target_pairs={{0,24},{8,0},{16,8},{24,16},{1,25},{9,1},{17,9},{25,17},{2,26},{10... | collective-permute-start | bytes 294920 | tf_op jit(solution)/shard_map/ppermute | solution.py:47
  145.9 16.5 %collective-permute-start.37 = (bf16[4,3,128,128]{3,2,1,0:T(8,128)(2,1)S(1)}, bf16[4,3,128,128]{3,2,1,0:T(8,128)(2,1)S(1)}, u32[]{:S(2)}, u32[]{:S(2)}) collective-permute-start(bf16[4,3,128,128]{3,2,1,0:T(8,128)(2,1)S(1)} %get-tuple-element.80), channel_id=1, source_target_pairs={{0,8},{8,16},{16,24},{24,0},{1,9},{9,17},{17,25},{25,1},{2,10},{10... | collective-permute-start | bytes 1179656 | tf_op jit(solution)/shard_map/ppermute | solution.py:47
  146.2 7.2 %collective-permute-start.32 = (bf16[256,64]{1,0:T(8,128)(2,1)S(1)}, bf16[256,64]{1,0:T(8,128)(2,1)S(1)}, u32[]{:S(2)}, u32[]{:S(2)}) collective-permute-start(bf16[256,64]{1,0:T(8,128)(2,1)S(1)} %get-tuple-element.77), channel_id=1, source_target_pairs={{0,4},{4,0},{1,5},{5,1},{2,6},{6,2},{3,7},{7,3},{8,12},{12,8},{9,1... | collective-permute-start | bytes 98312 | tf_op jit(solution)/shard_map/ppermute | solution.py:47
  153.5 10.5 %collective-permute-start.38 = (bf16[4,3,128,128]{3,2,1,0:T(8,128)(2,1)S(1)}, bf16[4,3,128,128]{3,2,1,0:T(8,128)(2,1)S(1)}, u32[]{:S(2)}, u32[]{:S(2)}) collective-permute-start(bf16[4,3,128,128]{3,2,1,0:T(8,128)(2,1)S(1)} %get-tuple-element.80), channel_id=1, source_target_pairs={{0,24},{8,0},{16,8},{24,16},{1,25},{9,1},{17,9},{25,17},{2,26},{10... | collective-permute-start | bytes 1179656 | tf_op jit(solution)/shard_map/ppermute | solution.py:47
  155.6 12.7 %collective-permute-start.39 = (bf16[4,3,128,128]{3,2,1,0:T(8,128)(2,1)S(1)}, bf16[4,3,128,128]{3,2,1,0:T(8,128)(2,1)S(1)}, u32[]{:S(2)}, u32[]{:S(2)}) collective-permute-start(bf16[4,3,128,128]{3,2,1,0:T(8,128)(2,1)S(1)} %get-tuple-element.80), channel_id=1, source_target_pairs={{0,16},{8,24},{16,0},{24,8},{1,17},{9,25},{17,1},{25,9},{2,18},{10... | collective-permute-start | bytes 1179656 | tf_op jit(solution)/shard_map/ppermute | solution.py:47
  156.6 17.0 %collective-permute-start.34 = (bf16[4,3,128,128]{3,2,1,0:T(8,128)(2,1)}, bf16[4,3,128,128]{3,2,1,0:T(8,128)(2,1)S(1)}, u32[]{:S(2)}, u32[]{:S(2)}) collective-permute-start(bf16[4,3,128,128]{3,2,1,0:T(8,128)(2,1)} %get-tuple-element.78.refs_3_), channel_id=1, source_target_pairs={{0,96},{32,0},{64,32},{96,64},{1,97},{33,1},{65,33},{97,65},{2,98}... | collective-permute-start | bytes 1179656 | tf_op jit(solution)/shard_map/ppermute | solution.py:47
  160.8 12.7 %collective-permute-start.33 = (bf16[4,3,128,128]{3,2,1,0:T(8,128)(2,1)S(1)}, bf16[4,3,128,128]{3,2,1,0:T(8,128)(2,1)S(1)}, u32[]{:S(2)}, u32[]{:S(2)}) collective-permute-start(bf16[4,3,128,128]{3,2,1,0:T(8,128)(2,1)S(1)} %get-tuple-element.79), channel_id=1, source_target_pairs={{0,32},{32,64},{64,96},{96,0},{1,33},{33,65},{65,97},{97,1},{2,34}... | collective-permute-start | bytes 1179656 | tf_op jit(solution)/shard_map/ppermute | solution.py:47
  162.4 17.0 %collective-permute-start.35 = (bf16[4,3,128,128]{3,2,1,0:T(8,128)(2,1)}, bf16[4,3,128,128]{3,2,1,0:T(8,128)(2,1)S(1)}, u32[]{:S(2)}, u32[]{:S(2)}) collective-permute-start(bf16[4,3,128,128]{3,2,1,0:T(8,128)(2,1)} %get-tuple-element.78.refs_3_), channel_id=1, source_target_pairs={{0,64},{32,96},{64,0},{96,32},{1,65},{33,97},{65,1},{97,33},{2,66}... | collective-permute-start | bytes 1179656 | tf_op jit(solution)/shard_map/ppermute | solution.py:47
  168.3 20.6 %collective-permute-start.40 = (bf16[3,4,3,128,128]{4,3,2,1,0:T(8,128)(2,1)S(1)}, bf16[3,4,3,128,128]{4,3,2,1,0:T(8,128)(2,1)S(1)}, u32[]{:S(2)}, u32[]{:S(2)}) collective-permute-start(bf16[3,4,3,128,128]{4,3,2,1,0:T(8,128)(2,1)S(1)} %shard_map.124.refs_0_), channel_id=1, source_target_pairs={{0,4},{4,0},{1,5},{5,1},{2,6},{6,2},{3,7},{7,3},{8,12},{12,8},{9,1... | collective-permute-start | bytes 3538952 | tf_op jit(solution)/shard_map/ppermute | solution.py:47
  179.4 17.4 %collective-permute-start.36 = (bf16[3,4,3,128,128]{4,3,2,1,0:T(8,128)(2,1)S(1)}, bf16[3,4,3,128,128]{4,3,2,1,0:T(8,128)(2,1)}, u32[]{:S(2)}, u32[]{:S(2)}) collective-permute-start(bf16[3,4,3,128,128]{4,3,2,1,0:T(8,128)(2,1)S(1)} %shard_map.123.refs_0_), channel_id=1, source_target_pairs={{0,4},{4,0},{1,5},{5,1},{2,6},{6,2},{3,7},{7,3},{8,12},{12,8},{9,1... | collective-permute-start | bytes 3538952 | tf_op jit(solution)/shard_map/ppermute | solution.py:47
  182.2 3.9 %collective-permute-start.41 = (bf16[2,4,3,128,128]{4,3,2,1,0:T(8,128)(2,1)}, bf16[2,4,3,128,128]{4,3,2,1,0:T(8,128)(2,1)}, u32[]{:S(2)}, u32[]{:S(2)}) collective-permute-start(bf16[2,4,3,128,128]{4,3,2,1,0:T(8,128)(2,1)} %get-tuple-element.76.refs_0_), channel_id=1, source_target_pairs={{0,4},{4,0},{1,5},{5,1},{2,6},{6,2},{3,7},{7,3},{8,12},{12,8},{9,1... | collective-permute-start | bytes 2359304 | tf_op jit(solution)/shard_map/ppermute | solution.py:47
  (14 other events, 16.0 us)
where the time goes:
time: 202 us; the launch traced here: 201 us
  starting transfers between devices  62.4 us (31%)
  waiting for transfers between devices  51.4 us (25%)
  Pallas kernels  50.9 us (25%)
  local copies, waits for them, and re-layouts  18.7 us (9%)
  blocking collectives  13.1 us (6%)
  between operations  3.34 us (2%)
    ppermute x42, starting transfers between devices, shift(): lax.ppermute(value, axis, [(i, (i + offset) % size) for i in range(size)])  57.3 us
    ppermute x42, waiting for transfers between devices, shift(): lax.ppermute(value, axis, [(i, (i + offset) % size) for i in range(size)])  51.4 us
    pallas_call x12, Pallas kernels, call(): pl.pallas_call(kernel, in_specs=[spec for spec, _ in operands], out_specs...  32.6 us
    unnamed x38, local copies, waits for them, and re-layouts  18.7 us
    pallas_call x5, Pallas kernels, assemble(): pl.pallas_call(functools.partial(assemble_kernel, tags, len(given), bool(...  18.4 us
    all_to_all x1, blocking collectives, shards(): lax.all_to_all(sent, ('y', 'x'), 0, 0, tiled=True).reshape(256, 128)  13.1 us
    all_to_all x1, starting transfers between devices, shards(): arrived = lax.all_to_all(spread, ('core', 'frame'), 0, 0, tiled=True)  5.1 us
  transfers between devices with their start and end apart: 43, of which 18 were waited for; matrix products, arithmetic and copies ran while one was open for 0% of the time, Pallas kernels for 11%

commit v1 on v0

--- a/solution.py
+++ b/solution.py
@@ -11,7 +11,7 @@
 HEAD_DIM = 128
 TIMESTEPS = 1000
 UNUSED = 64.0
-FIRST = ((0, 1), (0, 3), (0, 2), (1, 3), (1, 2))
+FIRST = ((0, 1), (0, 3), (1, 1), (1, 3))
 f32 = jnp.float32
 bf16 = jnp.bfloat16
 HIGHEST = lax.Precision.HIGHEST
@@ -27,6 +27,9 @@
 ANY = pl.BlockSpec(memory_space=pl.ANY)
 
 
+LARGE = 52
+
+
 def params(mib):
     return pltpu.CompilerParams(vmem_limit_bytes=mib << 20)
 
@@ -61,7 +64,10 @@
     hot = jnp.where(lax.broadcasted_iota(jnp.int32, (256, 128), 0) == slot, 1.0, 0.0)
     used = jnp.max(hot, axis=1, keepdims=True)
     moved = dot(hot.astype(bf16), rows[...]) + (1.0 - used) * UNUSED
-    out[...] = moved.astype(bf16).reshape(16, 16, 128)
+    bucket = moved.astype(bf16).reshape(16, 16, 128)
+    for frame in range(4):
+        for core in range(2):
+            out[frame, :, core] = bucket
 
 
 def prepare_kernel(place, w, w_out, head_t, w_t, mix, mix_t, held, out_rows, turned, sems, leave):
@@ -87,33 +93,19 @@
         store.wait()
 
 
-def sides_kernel(before, after, arrived, top, bottom, both, spread):
-    top[...] = before[:64]
-    bottom[...] = after[64:]
-    both[0] = before[...]
-    both[1] = after[...]
-    for k in range(8):
-        spread[k] = arrived[...]
-
-
 def fetch_kernel(place, arrived, pairs):
     frame, core = place[0], place[1]
     slots = 512
-
-    def rank_of(i):
-        return ((i % 256) // 16) * 32 + (i // 256) * 16 + i % 16
-
     before = jnp.where(
-        rank_of(lax.broadcasted_iota(jnp.int32, (slots, slots), 1))
-        < rank_of(lax.broadcasted_iota(jnp.int32, (slots, slots), 0)),
+        lax.broadcasted_iota(jnp.int32, (slots, slots), 1)
+        < lax.broadcasted_iota(jnp.int32, (slots, slots), 0),
         1.0,
         0.0,
     ).astype(bf16)
     half = (lax.broadcasted_iota(jnp.int32, (slots, 128), 0) // 8) % 2
     lane = lax.broadcasted_iota(jnp.int32, (slots, 128), 1).astype(f32)
     for i, r in enumerate(ORDER):
-        from_frame = (frame + 4 - r) % 4
-        rows = jnp.concatenate([arrived[from_frame], arrived[4 + from_frame]], axis=0)
+        rows = arrived[(frame + 4 - r) % 4]
         valid = jnp.broadcast_to(rows[:, 0:1].astype(f32), (slots, 128)) < 32.0
         for other in range(2):
             clip = core + other - 2 * core * other
@@ -127,25 +119,30 @@
     return slice((2 * i + other) * 128, (2 * i + other) * 128 + 128)
 
 
-def forward_kernel(moments, *refs):
-    act, act_theirs, sides, sides_theirs, top, top_theirs, bottom, bottom_theirs = refs[:8]
-    pairs, w_embed, gain, w_t_far, head_t, mix_t = refs[8:14]
-    normed_far, proj_far, attended_far, probs, part_own, part_other = refs[14:20]
-    w_t, normed, proj, attended, rest, sems = refs[20:]
+def forward_kernel(place, moments, act_far, *refs):
+    pairs, w_embed, gain, w_t_far, head_t, mix_t = refs[:6]
+    normed_far, proj_far, attended_far, probs, part_own, part_other = refs[6:12]
+    act, w_t, normed, proj, attended, rest, sems, arrive = refs[12:]
+    frame, core = place[0], place[1]
+    loads = []
+    for i, r in enumerate(ORDER):
+        for other in range(2):
+            clip = core + other - 2 * core * other
+            start = pl.multiple_of((clip * 4 + (frame + 4 - r) % 4) * 128, 128)
+            b = 2 * i + other
+            loads.append(pltpu.make_async_copy(act_far.at[pl.ds(start, 128)], act.at[b], arrive.at[b]))
+            loads[b].start()
     weights = pltpu.make_async_copy(w_t_far, w_t, sems.at[0])
     weights.start()
-    work = [(0, 0, act[...]), (1, 0, act_theirs[...])]
-    for side in range(2):
-        work += [(2 + 2 * side, 0, sides[side]), (3 + 2 * side, 0, sides_theirs[side])]
-    work += [(6, 0, top[...]), (6, 64, bottom[...]), (7, 0, top_theirs[...]), (7, 64, bottom_theirs[...])]
-    for b, start, rows in work:
-        pair = pairs[b, start : start + rows.shape[0]].astype(f32)
+    for b in range(8):
+        pair = pairs[b].astype(f32)
         t = moments[b % 2]
         noised = ((1.0 - t) * pair[:, :64] + t * pair[:, 64:]).astype(bf16)
-        hidden = rows.astype(f32) + dot(noised, w_embed[...])
+        added = dot(noised, w_embed[...])
+        loads[b].wait()
+        hidden = act[b].astype(f32) + added
         scale = lax.rsqrt(jnp.mean(hidden * hidden, axis=1, keepdims=True) + 1e-06)
-        first = b * 128 + start
-        normed[first : first + rows.shape[0]] = (hidden * scale * gain[...]).astype(bf16)
+        normed[b * 128 : b * 128 + 128] = (hidden * scale * gain[...]).astype(bf16)
         if b == 0:
             turned = pair.T
             own = dot(head_t[...].astype(f32), hidden, NT, HIGHEST)
@@ -201,8 +198,8 @@
 
 
 def backward_kernel(place, error_own, error_other, probs, mix, proj_far, attended_far, normed_far, *refs):
-    pieces, delta, own_factor = refs[:5], refs[5], refs[6]
-    slope, grad, proj, attended, normed, sems = refs[7:]
+    pieces, delta, own_factor = refs[:4], refs[4], refs[5]
+    slope, grad, proj, attended, normed, sems = refs[6:]
     loads = [
         pltpu.make_async_copy(far, near, sems.at[k])
         for k, (far, near) in enumerate(((proj_far, proj), (attended_far, attended), (normed_far, normed)))
@@ -247,11 +244,11 @@
         gradient_piece(delta, normed, own_factor[h], h, (place[h] + o) % 4, out)
 
 
-def late_kernel(place, delta, own_factor, normed_far, own_x, own_y, last, normed, sems):
+def late_kernel(place, delta, own_factor, normed_far, far_x, far_y, own_x, own_y, normed, sems):
     load = pltpu.make_async_copy(normed_far, normed, sems.at[0])
     load.start()
     load.wait()
-    for (h, o), out in (((1, 1), last), ((0, 0), own_x), ((1, 0), own_y)):
+    for (h, o), out in (((0, 2), far_x), ((1, 2), far_y), ((0, 0), own_x), ((1, 0), own_y)):
         gradient_piece(delta, normed, own_factor[h], h, (place[h] + o) % 4, out)
 
 
@@ -282,18 +279,22 @@
         factor[h * 128 : h * 128 + 128] = total[384:].T.astype(bf16)
 
 
-def line_kernel(*refs):
-    lines, both = refs[8:10], refs[10]
+def line_kernel(place, *refs):
+    factor, factor_theirs, lines, both, factors = refs[8], refs[9], refs[10:12], refs[12], refs[13]
     for h in range(2):
         for o in range(4):
             piece = refs[4 * h + o][...]
             lines[h][o] = piece
             both[h, o] = piece
-
-
-def join_kernel(a, b, c, out):
-    for k, ref in enumerate((a, b, c)):
-        out[k] = ref[...]
+    start = pl.multiple_of(place[2] * 256, 256)
+    factors[pl.ds(start, 256)] = factor[...]
+    factors[pl.ds(256 - start, 256)] = factor_theirs[...]
+
+
+def join_kernel(*refs):
+    out = refs[-1]
+    for k in range(out.shape[0]):
+        out[k] = refs[k][...]
 
 
 def assemble_kernel(tags, aliased, with_out, place, *refs):
@@ -301,8 +302,10 @@
     count = len(tags)
     sources, refs = refs[:arrays], refs[arrays + aliased :]
     if with_out:
-        factors, head_t, line, out, grad_out, line_out, held, ready, done, sems, whole, sent = refs
-        line_out[...] = line[...]
+        factors, head_t, line_x, line_y, out, grad_out, copy_x, copy_y, *refs = refs
+        held, ready, done, sems, whole, sent = refs
+        copy_x[...] = line_x[...]
+        copy_y[...] = line_y[...]
     else:
         out, held, ready, done, sems = refs
     loads = []
@@ -358,8 +361,8 @@
         pltpu.SemaphoreType.DMA((len(tags),)),
     ]
     if product:
-        out_shape += [shape((512, 2048), f32), shape((4, 3, 128, 128), bf16)]
-        out_specs += [HBM, VMEM]
+        out_shape += [shape((512, 2048), f32)] + [shape((4, 3, 128, 128), bf16)] * 2
+        out_specs += [HBM, VMEM, VMEM]
         scratch += [pltpu.VMEM((512, 2048), f32), pltpu.SemaphoreType.DMA((1,))]
     return pl.pallas_call(
         functools.partial(assemble_kernel, tags, len(given), bool(product)),
@@ -368,7 +371,7 @@
         out_shape=out_shape,
         scratch_shapes=scratch,
         input_output_aliases={1 + len(arrays): 0} if given else {},
-        compiler_params=params(12),
+        compiler_params=params(LARGE),
         cost_estimate=TINY,
     )(place, *arrays, *given, *product)
 
@@ -400,21 +403,13 @@
     square = (SMEM, jnp.stack([x, y, core]))
     dma = pltpu.SemaphoreType.DMA
 
-    before, after = shift(act, "frame", 1), shift(act, "frame", 3)
-    act_theirs = shift(act, "core", 1)
+    act8 = lax.all_gather(act, ("core", "frame"), axis=0, tiled=True)
     (sent,) = call(
-        bucket_kernel, near(shape((16, 16, 128), bf16)), *near(cache_rows, row_dest.reshape(1, 128))
-    )
-    arrived = lax.all_to_all(sent, ("y", "x"), 0, 0, tiled=True).reshape(256, 128)
-    half_act = shape((64, 2048), bf16)
-    top, bottom, sides, spread = call(
-        sides_kernel,
-        near(half_act, half_act, shape((2, 128, 2048), bf16), shape((8, 256, 128), bf16)),
-        *near(before, after, arrived),
-    )
-    top, bottom = shift(top, "frame", 1), shift(bottom, "frame", 3)
-    sides_theirs = shift(sides, "core", 1)
-    arrived = lax.all_to_all(spread, ("core", "frame"), 0, 0, tiled=True)
+        bucket_kernel, near(shape((4, 16, 2, 16, 128), bf16)), *near(cache_rows, row_dest.reshape(1, 128))
+    )
+    arrived = lax.all_to_all(
+        sent.reshape(128, 16, 128), ("frame", "y", "x", "core"), 0, 0, tiled=True
+    ).reshape(4, 512, 128)
     moment = (time_index.astype(f32) + 0.5) / TIMESTEPS
     moments = jnp.concatenate([moment, shift(moment, "core", 1)])
 
@@ -430,25 +425,26 @@
             dma((4,)),
             dma((6,)),
         ],
-        mib=12,
+        mib=LARGE,
     )
     (pairs,) = call(fetch_kernel, near(shape((8, 128, 128), bf16)), here, *near(arrived))
     normed, proj, attended, probs, part_own, part_other = call(
         forward_kernel,
         far(shape((1024, 2048), bf16), shape((768, 1024), bf16), shape((256, 1024), bf16))
         + near(shape((4, 16, 128), f32), shape((64, 512), f32), shape((64, 512), f32)),
-        (SMEM, moments),
-        *near(act, act_theirs, sides, sides_theirs, top, shift(top, "core", 1), bottom, shift(bottom, "core", 1)),
+        here, (SMEM, moments), *far(act8),
         *near(pairs, w_embed, norm_gain.reshape(1, 2048)), *far(w_t), *near(head_t, mix_t),
         scratch=[
+            pltpu.VMEM((8, 128, 2048), bf16),
             pltpu.VMEM((768, 2048), bf16),
             pltpu.VMEM((1024, 2048), bf16),
             pltpu.VMEM((768, 1024), bf16),
             pltpu.VMEM((256, 1024), bf16),
             pltpu.VMEM((64, 128), f32),
             dma((4,)),
+            dma((8,)),
         ],
-        mib=16,
+        mib=LARGE,
     )
 
     clip_part = part_own + shift(part_other, "core", 1)
@@ -473,7 +469,7 @@
     axes = (("x", "y"), ("y", "x"))
     *first, delta, own_factor = call(
         backward_kernel,
-        near(*[piece] * 5, shape((768, 1024), bf16), shape((2, 64, 128), bf16)),
+        near(*[piece] * 4, shape((768, 1024), bf16), shape((2, 64, 128), bf16)),
         square, *near(error_own, error_other, probs, mix), *far(proj, attended, normed),
         scratch=[
             pltpu.VMEM((64, 1024), f32),
@@ -483,16 +479,18 @@
             pltpu.VMEM((1024, 2048), bf16),
             dma((3,)),
         ],
-        mib=16,
+        mib=LARGE,
     )
     moved = [[], []]
     for (h, o), p in zip(FIRST, first):
         moved[h].append(shift(p, axes[h][0], o))
-    own_x, own_y, last = call(
-        late_kernel, near(*[piece] * 3), square, *near(delta, own_factor), *far(normed),
+    far_x, far_y, own_x, own_y = call(
+        late_kernel, near(*[piece] * 4), square, *near(delta, own_factor), *far(normed),
         scratch=[pltpu.VMEM((1024, 2048), bf16), dma((1,))],
-    )
-    moved[1].append(shift(last, axes[1][0], 1))
+        mib=LARGE,
+    )
+    moved[0].append(shift(far_x, axes[0][0], 2))
+    moved[1].append(shift(far_y, axes[1][0], 2))
     second = call(
         add_first_kernel, near(*[small] * 8), square, *near(own_x, *moved[0], own_y, *moved[1]),
         scratch=[pltpu.VMEM((400, 512), bf16)],
@@ -506,38 +504,34 @@
         {0: owned[h], **{o: shift(owned[h], axes[h][1], o) for o in (1, 3, 2)}} for h in range(2)
     ]
     factor_theirs = shift(factor, "core", 1)
-    factors = jnp.concatenate(
-        [jnp.where(core == 0, factor, factor_theirs), jnp.where(core == 0, factor_theirs, factor)]
-    )
-    line_x, line_y, lines = call(
-        line_kernel, near(line, line, shape((2, 4, 3, 128, 128), bf16)),
-        *near(*(back[h][o] for h in range(2) for o in range(4))),
+    line_x, line_y, lines, factors = call(
+        line_kernel, near(line, line, shape((2, 4, 3, 128, 128), bf16), shape((512, 64), bf16)),
+        square, *near(*(back[h][o] for h in range(2) for o in range(4)), factor, factor_theirs),
     )
     every = (0, 1, 2, 3)
-    wide = {(h, o): shift((line_x, line_y)[h], axes[h][0], o) for h, o in FIRST}
-    grad_qkv, grad_out, line_last = assemble(
-        square[1], (lines,), [(0, h, 0, 0, h, every) for h in range(2)], None, (factors, head_t, line_y)
-    )
-    wide[1, 1] = shift(line_last, axes[1][0], 1)
-    lines_theirs = shift(lines, "core", 1)
-    reach = (1, 3, 2)
-    triple = near(shape((3, 4, 3, 128, 128), bf16))
-    (wide_x,) = call(join_kernel, triple, *near(*(wide[0, o] for o in reach)))
-    wide_x_theirs = shift(wide_x, "core", 1)
-    (wide_y,) = call(join_kernel, triple, *near(*(wide[1, o] for o in reach)))
-    wide_y_theirs = shift(wide_y, "core", 1)
-
-    def placed(array, side, h):
-        return [(array, k, reach[k], side, h, every) for k in range(3)]
-
-    (grad_qkv,) = assemble(
-        square[1], (lines_theirs,), [(0, h, 0, 1, h, every) for h in range(2)], grad_qkv
-    )
-    (grad_qkv,) = assemble(
-        square[1], (wide_x, wide_x_theirs), placed(0, 0, 0) + placed(1, 1, 0), grad_qkv
-    )
-    (grad_qkv,) = assemble(square[1], (wide_y,), placed(0, 0, 1), grad_qkv)
-    (grad_qkv,) = assemble(square[1], (wide_y_theirs,), placed(0, 1, 1), grad_qkv)
+    beside = [shift((line_x, line_y)[h], axes[h][0], o) for h, o in FIRST]
+    grad_qkv, grad_out, copy_x, copy_y = assemble(
+        square[1], (lines,), [(0, h, 0, 0, h, every) for h in range(2)], None,
+        (factors, head_t, line_x, line_y),
+    )
+    opposite = [shift((copy_x, copy_y)[h], axes[h][0], 2) for h in range(2)]
+    (sides,) = call(
+        join_kernel, near(shape((6, 4, 3, 128, 128), bf16)), *near(*beside, copy_x, copy_y)
+    )
+    sides_theirs = shift(sides, "core", 1)
+    side_tags = [(0, k, o, h) for k, (h, o) in enumerate((*FIRST, (0, 0), (1, 0)))]
+
+    def tagged(tags, side):
+        return [(array, k, o, side, h, every) for array, k, o, h in tags]
+
+    (grad_qkv,) = assemble(square[1], (sides,), tagged(side_tags[:4], 0), grad_qkv)
+    (grad_qkv,) = assemble(square[1], (sides_theirs,), tagged(side_tags, 1), grad_qkv)
+    (across,) = call(
+        join_kernel, near(shape((2, 4, 3, 128, 128), bf16)), *near(*opposite), *far(grad_qkv), mib=LARGE
+    )
+    across_theirs = shift(across, "core", 1)
+    for side, array in enumerate((across, across_theirs)):
+        (grad_qkv,) = assemble(square[1], (array,), tagged([(0, 0, 2, 0), (0, 1, 2, 1)], side), grad_qkv)
     return frame_loss, grad_qkv, grad_out
 
 

time: 202 us -> 189 us (0.936)
  local copies, waits for them, and re-layouts: 18.7 us -> 4.68 us
  between operations: 3.34 us -> 16.6 us
  blocking collectives: 13.1 us -> 0 us
  starting transfers between devices: 62.4 us -> 49.4 us
  waiting for transfers between devices: 51.4 us -> 62.1 us
  Pallas kernels: 50.9 us -> 54 us
    ppermute x42 -> x33, starting transfers between devices: 57.3 us -> 37.9 us  [shift(): lax.ppermute(value, axis, [(i, (i + offset) % size) for i in range(size)])]
    unnamed x38 -> x22, local copies, waits for them, and re-layouts: 18.7 us -> 4.68 us
    all_to_all x1 -> x0, blocking collectives: 13.1 us -> none  [shards(): lax.all_to_all(sent, ('y', 'x'), 0, 0, tiled=True).reshape(256, 128)]
    all_gather x0 -> x1, waiting for transfers between devices: none -> 10.9 us  [shards(): act8 = lax.all_gather(act, ('core', 'frame'), axis=0, tiled=True)]
    ppermute x42 -> x33, waiting for transfers between devices: 51.4 us -> 44.8 us  [shift(): lax.ppermute(value, axis, [(i, (i + offset) % size) for i in range(size)])]
    all_to_all x1, starting transfers between devices: 5.1 us -> 11.5 us  [shards(): lax.all_to_all(sent.reshape(128, 16, 128), ('frame', 'y', 'x', 'core'), 0...]
    all_to_all x1, waiting for transfers between devices: 0.01 us -> 5.65 us  [shards(): lax.all_to_all(sent.reshape(128, 16, 128), ('frame', 'y', 'x', 'core'), 0...]
    pallas_call x12 -> x11, Pallas kernels: 32.6 us -> 37.4 us  [call(): pl.pallas_call(kernel, in_specs=[spec for spec, _ in operands], out_specs...]
  transfers between devices with their start and end apart: 43 -> 35, of which waited for: 18 -> 24; matrix products, arithmetic and copies ran while one was open for 0% -> 0% of each run, Pallas kernels for 11% -> 12%
where the time goes in v1:
time: 189 us; the launch traced here: 188 us
  waiting for transfers between devices  62.1 us (33%)
  Pallas kernels  54 us (29%)
  starting transfers between devices  49.4 us (26%)
  between operations  16.6 us (9%)
  local copies, waits for them, and re-layouts  4.68 us (2%)
    ppermute x33, waiting for transfers between devices, shift(): lax.ppermute(value, axis, [(i, (i + offset) % size) for i in range(size)])  44.8 us
    ppermute x33, starting transfers between devices, shift(): lax.ppermute(value, axis, [(i, (i + offset) % size) for i in range(size)])  37.9 us
    pallas_call x11, Pallas kernels, call(): pl.pallas_call(kernel, in_specs=[spec for spec, _ in operands], out_specs...  37.4 us
    pallas_call x5, Pallas kernels, assemble(): pl.pallas_call(functools.partial(assemble_kernel, tags, len(given), bool(...  16.5 us
    all_to_all x1, starting transfers between devices, shards(): lax.all_to_all(sent.reshape(128, 16, 128), ('frame', 'y', 'x', 'core'), 0...  11.5 us
    all_gather x1, waiting for transfers between devices, shards(): act8 = lax.all_gather(act, ('core', 'frame'), axis=0, tiled=True)  10.9 us
    all_to_all x1, waiting for transfers between devices, shards(): lax.all_to_all(sent.reshape(128, 16, 128), ('frame', 'y', 'x', 'core'), 0...  5.65 us
    unnamed x22, local copies, waits for them, and re-layouts  4.68 us
  transfers between devices with their start and end apart: 35, of which 24 were waited for; matrix products, arithmetic and copies ran while one was open for 0% of the time, Pallas kernels for 12%

profile of v1, /device:TPU:1, one launch (start us, length us, event | category | flops | bytes accessed | tf_op | source)
XLA Modules:
  0.0 188.3 jit_solution(3214756003663121194)
XLA Ops:
  9.3 1.1 shard_map.112
  10.4 11.5 %all-to-all-start = ((bf16[128,16,128]{2,1,0:T(8,128)(2,1)}), bf16[128,16,128]{2,1,0:T(8,128)(2,1)S(1)}, u32[]{:S(2)}, u32[]{:S(2)}) async-start(bf16[128,16,128]{2,1,0:T(8,128)(2,1)} %bitcast.3), calls=%async_computation | async-start | bytes 1048576 | tf_op jit(solution)/shard_map/all_to_all | solution.py:410
  22.5 2.0 %collective-permute-start = (f32[1]{0:T(128)}, f32[1]{0:T(128)}, u32[]{:S(2)}, u32[]{:S(2)}) collective-permute-start(f32[1]{0:T(128)} %div.6), channel_id=1, source_target_pairs={{0,4},{4,0},{1,5},{5,1},{2,6},{6,2},{3,7},{7,3},{8,12},{12,8},{9,1... | collective-permute-start | bytes 20 | tf_op jit(solution)/shard_map/ppermute | solution.py:50
  25.5 3.7 %shard_map.114 = (bf16[768,2048]{1,0:T(8,128)(2,1)}, f32[256,64]{1,0:T(8,128)S(1)}, f32[64,256]{1,0:T(8,128)S(1)}) custom-call(s32[2]{0:T(128)S(1)} %pad_add_fusion.place, bf16[3,2048,512]{2,1,0:T(8,128)(2,1)} %w.1, bf16[512,2048]{1,0:T(8,128)(2,1)} %w_out.1, bf16[64,2048]{1,0:T(8,128)(2,1)S(1)} %bitcast.10), custom_call_target="tpu_custom_call" | custom-call | bytes 1024 | tf_op jit(solution)/shard_map/pallas_call | solution.py:380
  30.0 5.7 %all-to-all-done = bf16[128,16,128]{2,1,0:T(8,128)(2,1)S(1)} async-done(((bf16[128,16,128]{2,1,0:T(8,128)(2,1)}), bf16[128,16,128]{2,1,0:T(8,128)(2,1)S(1)}, u32[]{:S(2)}, u32[]{:S(2)}) %all-to-all-start) | async-done | bytes 524320 | tf_op jit(solution)/shard_map/all_to_all | solution.py:410
  35.6 4.3 %shard_map.113.refs_0_ = bf16[8,128,128]{2,1,0:T(8,128)(2,1)S(1)} custom-call(s32[2]{0:T(128)S(1)} %pad_add_fusion.place, bf16[4,512,128]{2,1,0:T(8,128)(2,1)S(1)} %bitcast.13), custom_call_target="tpu_custom_call" | custom-call | bytes 1024 | tf_op jit(solution)/shard_map/pallas_call | solution.py:380
  39.9 10.9 %all-gather.2.cloned.1.call-done.act_far = bf16[1024,2048]{1,0:T(8,128)(2,1)} async-done(((bf16[128,2048]{1,0:T(8,128)(2,1)}), bf16[1024,2048]{1,0:T(8,128)(2,1)}) %all-gather.2.cloned.1.call-update) | async-done | bytes 4194320 | tf_op jit(solution)/shard_map/all_gather | solution.py:406
  50.9 12.2 %shard_map.115 = (bf16[1024,2048]{1,0:T(8,128)(2,1)}, bf16[768,1024]{1,0:T(8,128)(2,1)}, bf16[256,1024]{1,0:T(8,128)(2,1)S(1)}, f32[4,16,128]{2,1,0:T(8,128)S(1)...) custom-call(s32[2]{0:T(128)S(1)} %pad_add_fusion.place, f32[2]{0:T(128)S(1)} %pad_maximum_fusion.1.moments, ...), custom_call_target="tpu_custom_call" | custom-call | bytes 1024 | tf_op jit(solution)/shard_map/pallas_call | solution.py:380
  63.4 1.1 collective-permute-done.1
  65.0 1.5 collective-permute-start.3
  66.7 2.7 %collective-permute-done.4 = f32[64,512]{1,0:T(8,128)S(1)} collective-permute-done((f32[64,512]{1,0:T(8,128)S(1)}, f32[64,512]{1,0:T(8,128)S(1)}, u32[]{:S(2)}, u32[]{:S(2)}) %collective-permute-start.4) | collective-permute-done | bytes 131104 | tf_op jit(solution)/shard_map/ppermute | solution.py:50
  69.4 1.6 collective-permute-done.3
  71.0 3.4 %collective-permute-done.2 = f32[64,512]{1,0:T(8,128)S(1)} collective-permute-done((f32[64,512]{1,0:T(8,128)S(1)}, f32[64,512]{1,0:T(8,128)S(1)}, u32[]{:S(2)}, u32[]{:S(2)}) %collective-permute-start.2) | collective-permute-done | bytes 131104 | tf_op jit(solution)/shard_map/ppermute | solution.py:50
  76.9 8.1 %shard_map.116 = (bf16[400,512]{1,0:T(8,128)(2,1)S(1)}, bf16[400,512]{1,0:T(8,128)(2,1)S(1)}, bf16[400,512]{1,0:T(8,128)(2,1)S(1)}, bf16[400,512]{1,0:T(8,128)(2...) custom-call(s32[3]{0:T(128)S(1)} %pad_add_fusion.1.place, f32[64,512]{1,0:T(8,128)S(1)} %pad_maximum_fusion.error_own, ...), custom_call_target="tpu_custom_call" | custom-call | bytes 1024 | tf_op jit(solution)/shard_map/pallas_call | solution.py:380
  85.0 5.5 %shard_map.117 = (bf16[400,512]{1,0:T(8,128)(2,1)S(1)}, bf16[400,512]{1,0:T(8,128)(2,1)S(1)}, bf16[400,512]{1,0:T(8,128)(2,1)S(1)}, bf16[400,512]{1,0:T(8,128)(2,1)S(1)}) custom-call(s32[3]{0:T(128)S(1)} %pad_add_fusion.1.place, bf16[768,1024]{1,0:T(8,128)(2,1)} %get-tuple-element.50.delta, bf16[2,64,128]{2,1,0:T(8,128)(2,1)S(1)} %get-tuple-element.51.own_factor, ...), custom_call_target="tpu_custom_call" | custom-call | bytes 1024 | tf_op jit(solution)/shard_map/pallas_call | solution.py:380
  90.5 2.5 %collective-permute-start.8 = (bf16[400,512]{1,0:T(8,128)(2,1)S(1)}, bf16[400,512]{1,0:T(8,128)(2,1)S(1)}, u32[]{:S(2)}, u32[]{:S(2)}) collective-permute-start(bf16[400,512]{1,0:T(8,128)(2,1)S(1)} %get-tuple-element.55), channel_id=1, source_target_pairs={{0,16},{8,24},{16,0},{24,8},{1,17},{9,25},{17,1},{25,9},{2,18},{10... | collective-permute-start | bytes 1228808 | tf_op jit(solution)/shard_map/ppermute | solution.py:50
  93.1 2.3 %collective-permute-start.11 = (bf16[400,512]{1,0:T(8,128)(2,1)S(1)}, bf16[400,512]{1,0:T(8,128)(2,1)S(1)}, u32[]{:S(2)}, u32[]{:S(2)}) collective-permute-start(bf16[400,512]{1,0:T(8,128)(2,1)S(1)} %get-tuple-element.59), channel_id=1, source_target_pairs={{0,64},{32,96},{64,0},{96,32},{1,65},{33,97},{65,1},{97,33},{2,66}... | collective-permute-start | bytes 1228808 | tf_op jit(solution)/shard_map/ppermute | solution.py:50
  95.6 2.4 %collective-permute-start.7 = (bf16[400,512]{1,0:T(8,128)(2,1)S(1)}, bf16[400,512]{1,0:T(8,128)(2,1)S(1)}, u32[]{:S(2)}, u32[]{:S(2)}) collective-permute-start(bf16[400,512]{1,0:T(8,128)(2,1)S(1)} %get-tuple-element.54), channel_id=1, source_target_pairs={{0,24},{8,0},{16,8},{24,16},{1,25},{9,1},{17,9},{25,17},{2,26},{10... | collective-permute-start | bytes 1228808 | tf_op jit(solution)/shard_map/ppermute | solution.py:50
  98.3 4.6 %collective-permute-done.8.refs_3_ = bf16[400,512]{1,0:T(8,128)(2,1)S(1)} collective-permute-done((bf16[400,512]{1,0:T(8,128)(2,1)S(1)}, bf16[400,512]{1,0:T(8,128)(2,1)S(1)}, u32[]{:S(2)}, u32[]{:S(2)}) %collective-permute-start.8) | collective-permute-done | bytes 409632 | tf_op jit(solution)/shard_map/ppermute | solution.py:50
  102.8 1.9 collective-permute-start.10
  105.0 7.3 %collective-permute-done.6.refs_1_ = bf16[400,512]{1,0:T(8,128)(2,1)S(1)} collective-permute-done((bf16[400,512]{1,0:T(8,128)(2,1)S(1)}, bf16[400,512]{1,0:T(8,128)(2,1)S(1)}, u32[]{:S(2)}, u32[]{:S(2)}) %collective-permute-start.6) | collective-permute-done | bytes 409632 | tf_op jit(solution)/shard_map/ppermute | solution.py:50
  112.3 2.5 %collective-permute-done.9.refs_5_ = bf16[400,512]{1,0:T(8,128)(2,1)S(1)} collective-permute-done((bf16[400,512]{1,0:T(8,128)(2,1)S(1)}, bf16[400,512]{1,0:T(8,128)(2,1)S(1)}, u32[]{:S(2)}, u32[]{:S(2)}) %collective-permute-start.9) | collective-permute-done | bytes 409632 | tf_op jit(solution)/shard_map/ppermute | solution.py:50
  114.7 1.5 shard_map.118
  116.3 2.7 %collective-permute-start.13 = (bf16[448,128]{1,0:T(8,128)(2,1)S(1)}, bf16[448,128]{1,0:T(8,128)(2,1)S(1)}, u32[]{:S(2)}, u32[]{:S(2)}) collective-permute-start(bf16[448,128]{1,0:T(8,128)(2,1)S(1)} %get-tuple-element.62), channel_id=1, source_target_pairs={{0,96},{32,0},{64,32},{96,64},{1,97},{33,1},{65,33},{97,65},{2,98}... | collective-permute-start | bytes 344072 | tf_op jit(solution)/shard_map/ppermute | solution.py:50
  118.9 1.1 collective-permute-start.14
  120.3 2.4 %collective-permute-start.16 = (bf16[448,128]{1,0:T(8,128)(2,1)S(1)}, bf16[448,128]{1,0:T(8,128)(2,1)S(1)}, u32[]{:S(2)}, u32[]{:S(2)}) collective-permute-start(bf16[448,128]{1,0:T(8,128)(2,1)S(1)} %get-tuple-element.66), channel_id=1, source_target_pairs={{0,24},{8,0},{16,8},{24,16},{1,25},{9,1},{17,9},{25,17},{2,26},{10... | collective-permute-start | bytes 344072 | tf_op jit(solution)/shard_map/ppermute | solution.py:50
  122.7 1.7 collective-permute-done.14.refs_3_
  125.8 2.4 %collective-permute-done.17.refs_7_ = bf16[448,128]{1,0:T(8,128)(2,1)S(1)} collective-permute-done((bf16[448,128]{1,0:T(8,128)(2,1)S(1)}, bf16[448,128]{1,0:T(8,128)(2,1)S(1)}, u32[]{:S(2)}, u32[]{:S(2)}) %collective-permute-start.17) | collective-permute-done | bytes 114720 | tf_op jit(solution)/shard_map/ppermute | solution.py:50
  128.5 1.0 collective-permute-start.20
  129.4 3.0 %collective-permute-start.24 = (bf16[256,64]{1,0:T(8,128)(2,1)S(1)}, bf16[256,64]{1,0:T(8,128)(2,1)S(1)}, u32[]{:S(2)}, u32[]{:S(2)}) collective-permute-start(bf16[256,64]{1,0:T(8,128)(2,1)S(1)} %get-tuple-element.70.refs_8_), channel_id=1, source_target_pairs={{0,4},{4,0},{1,5},{5,1},{2,6},{6,2},{3,7},{7,3},{8,12},{12,8},{9,1... | collective-permute-start | bytes 98312 | tf_op jit(solution)/shard_map/ppermute | solution.py:50
  132.4 1.7 collective-permute-start.19
  134.2 1.0 collective-permute-start.23
  136.3 2.0 %collective-permute-done.19.refs_2_ = bf16[3,128,128]{2,1,0:T(8,128)(2,1)S(1)} collective-permute-done((bf16[3,128,128]{2,1,0:T(8,128)(2,1)S(1)}, bf16[3,128,128]{2,1,0:T(8,128)(2,1)S(1)}, u32[]{:S(2)}, u32[]{:S(2)}) %collective-permute-start.19) | collective-permute-done | bytes 98336 | tf_op jit(solution)/shard_map/ppermute | solution.py:50
  138.3 2.3 %collective-permute-done.18.refs_1_ = bf16[3,128,128]{2,1,0:T(8,128)(2,1)S(1)} collective-permute-done((bf16[3,128,128]{2,1,0:T(8,128)(2,1)S(1)}, bf16[3,128,128]{2,1,0:T(8,128)(2,1)S(1)}, u32[]{:S(2)}, u32[]{:S(2)}) %collective-permute-start.18) | collective-permute-done | bytes 98336 | tf_op jit(solution)/shard_map/ppermute | solution.py:50
  140.6 2.5 %collective-permute-done.21.refs_5_ = bf16[3,128,128]{2,1,0:T(8,128)(2,1)S(1)} collective-permute-done((bf16[3,128,128]{2,1,0:T(8,128)(2,1)S(1)}, bf16[3,128,128]{2,1,0:T(8,128)(2,1)S(1)}, u32[]{:S(2)}, u32[]{:S(2)}) %collective-permute-start.21) | collective-permute-done | bytes 98336 | tf_op jit(solution)/shard_map/ppermute | solution.py:50
  144.8 1.5 collective-permute-start.27
  146.3 2.3 %collective-permute-start.30 = (bf16[4,3,128,128]{3,2,1,0:T(8,128)(2,1)S(1)}, bf16[4,3,128,128]{3,2,1,0:T(8,128)(2,1)S(1)}, u32[]{:S(2)}, u32[]{:S(2)}) collective-permute-start(bf16[4,3,128,128]{3,2,1,0:T(8,128)(2,1)S(1)} %get-tuple-element.74.refs_4_), channel_id=1, source_target_pairs={{0,96},{32,0},{64,32},{96,64},{1,97},{33,1},{65,33},{97,65},{2,98}... | collective-permute-start | bytes 1179656 | tf_op jit(solution)/shard_map/ppermute | solution.py:50
  148.6 3.8 %shard_map.121 = (f32[3,2048,512]{2,1,0:T(8,128)}, f32[512,2048]{1,0:T(8,128)}, bf16[4,3,128,128]{3,2,1,0:T(8,128)(2,1)S(1)}, bf16[4,3,128,128]{3,2,1,0:T(8,128)(2,1)S(1)}) custom-call(s32[3]{0:T(128)S(1)} %pad_add_fusion.1.place, bf16[2,4,3,128,128]{4,3,2,1,0:T(8,128)(2,1)} %copy-done.3, bf16[512,64]{1,0:T(8,128)(2,1)S(1)} %get-tuple-element.72.refs_1_, ...), custom_call_target="tpu_custom_call" | custom-call | bytes 1024 | tf_op jit(solution)/shard_map/pallas_call | solution.py:367
  152.3 2.2 %collective-permute-done.28.refs_1_ = bf16[4,3,128,128]{3,2,1,0:T(8,128)(2,1)S(1)} collective-permute-done((bf16[4,3,128,128]{3,2,1,0:T(8,128)(2,1)S(1)}, bf16[4,3,128,128]{3,2,1,0:T(8,128)(2,1)S(1)}, u32[]{:S(2)}, u32[]{:S(2)}) %collective-permute-start.28) | collective-permute-done | bytes 393248 | tf_op jit(solution)/shard_map/ppermute | solution.py:50
  155.5 3.0 %collective-permute-done.29.refs_2_ = bf16[4,3,128,128]{3,2,1,0:T(8,128)(2,1)S(1)} collective-permute-done((bf16[4,3,128,128]{3,2,1,0:T(8,128)(2,1)S(1)}, bf16[4,3,128,128]{3,2,1,0:T(8,128)(2,1)S(1)}, u32[]{:S(2)}, u32[]{:S(2)}) %collective-permute-start.29) | collective-permute-done | bytes 393248 | tf_op jit(solution)/shard_map/ppermute | solution.py:50
  158.6 2.9 %collective-permute-start.31 = (bf16[6,4,3,128,128]{4,3,2,1,0:T(8,128)(2,1)S(1)}, bf16[6,4,3,128,128]{4,3,2,1,0:T(8,128)(2,1)S(1)}, u32[]{:S(2)}, u32[]{:S(2)}) collective-permute-start(bf16[6,4,3,128,128]{4,3,2,1,0:T(8,128)(2,1)S(1)} %shard_map.122.refs_0_), channel_id=1, source_target_pairs={{0,4},{4,0},{1,5},{5,1},{2,6},{6,2},{3,7},{7,3},{8,12},{12,8},{9,1... | collective-permute-start | bytes 7077896 | tf_op jit(solution)/shard_map/ppermute | solution.py:50
  162.2 3.7 %shard_map.123.refs_1_ = f32[3,2048,512]{2,1,0:T(8,128)} custom-call(s32[3]{0:T(128)S(1)} %pad_add_fusion.1.place, bf16[6,4,3,128,128]{4,3,2,1,0:T(8,128)(2,1)} %copy-done, f32[3,2048,512]{2,1,0:T(8,128)} %get-tuple-element.77.refs_1_), custom_call_target="tpu_custom_call", output_to_operand_aliasing={{}: (2, {})} | custom-call | bytes 1024 | tf_op jit(solution)/shard_map/pallas_call | solution.py:367
  166.0 1.4 copy-done.9
  167.4 4.7 %shard_map.124.refs_2_.refs_1_ = f32[3,2048,512]{2,1,0:T(8,128)} custom-call(s32[3]{0:T(128)S(1)} %pad_add_fusion.1.place, bf16[6,4,3,128,128]{4,3,2,1,0:T(8,128)(2,1)} %copy-done.9, f32[3,2048,512]{2,1,0:T(8,128)} %shard_map.123.refs_1_), custom_call_target="tpu_custom_call", output_to_operand_aliasing={{}: (2, {})} | custom-call | bytes 1024 | tf_op jit(solution)/shard_map/pallas_call | solution.py:367
  172.1 1.6 collective-permute-done.25.refs_0_
  174.1 1.3 collective-permute-start.32
  176.0 2.2 %shard_map.126.refs_1_ = f32[3,2048,512]{2,1,0:T(8,128)} custom-call(s32[3]{0:T(128)S(1)} %pad_add_fusion.1.place, bf16[2,4,3,128,128]{4,3,2,1,0:T(8,128)(2,1)S(1)} %shard_map.125.refs_0_, f32[3,2048,512]{2,1,0:T(8,128)} %shard_map.124.refs_2_.refs_1_), custom_call_target="tpu_custom_call", output_to_operand_aliasing={{}: (2, {})} | custom-call | bytes 1024 | tf_op jit(solution)/shard_map/pallas_call | solution.py:367
  178.1 2.2 %shard_map.127 = f32[3,2048,512]{2,1,0:T(8,128)} custom-call(s32[3]{0:T(128)S(1)} %pad_add_fusion.1.place, bf16[2,4,3,128,128]{4,3,2,1,0:T(8,128)(2,1)S(1)} %collective-permute-done.32.refs_0_, f32[3,2048,512]{2,1,0:T(8,128)} %shard_map.126.refs_1_), custom_call_target="tpu_custom_call", output_to_operand_aliasing={{}: (2, {})} | custom-call | bytes 1024 | tf_op jit(solution)/shard_map/pallas_call | solution.py:367
  (67 shorter events, 15.2 us)
Async XLA Ops:
  7.2 43.7 %all-gather.2.cloned.1.call-start = ((), (), s32[]{:S(2)}) async-start(), calls=%async_computation.1 | async-start | bytes 4718592 | tf_op jit(solution)/shard_map/all_gather | solution.py:406
  7.9 0.8 copy-start.6
  8.7 0.7 copy-start.8
  10.4 25.2 %all-to-all-start = ((bf16[128,16,128]{2,1,0:T(8,128)(2,1)}), bf16[128,16,128]{2,1,0:T(8,128)(2,1)S(1)}, u32[]{:S(2)}, u32[]{:S(2)}) async-start(bf16[128,16,128]{2,1,0:T(8,128)(2,1)} %bitcast.3), calls=%async_computation | async-start | bytes 1048576 | tf_op jit(solution)/shard_map/all_to_all | solution.py:410
  22.5 6.7 %collective-permute-start = (f32[1]{0:T(128)}, f32[1]{0:T(128)}, u32[]{:S(2)}, u32[]{:S(2)}) collective-permute-start(f32[1]{0:T(128)} %div.6), channel_id=1, source_target_pairs={{0,4},{4,0},{1,5},{5,1},{2,6},{6,2},{3,7},{7,3},{8,12},{12,8},{9,1... | collective-permute-start | bytes 20 | tf_op jit(solution)/shard_map/ppermute | solution.py:50
  24.6 0.9 copy-start.1
  25.5 25.3 %copy-start.2 = (bf16[2048,64]{0,1:T(8,128)(2,1)S(1)}, bf16[2048,64]{0,1:T(8,128)(2,1)}, u32[]{:S(2)}) copy-start(bf16[2048,64]{0,1:T(8,128)(2,1)} %param.17) | copy-start | bytes 786436
  25.5 25.3 %copy-start.5 = (bf16[64,2048]{1,0:T(8,128)(2,1)S(1)}, bf16[64,2048]{1,0:T(8,128)(2,1)}, u32[]{:S(2)}) copy-start(bf16[64,2048]{1,0:T(8,128)(2,1)} %refs_1_.1) | copy-start | bytes 786436
  25.5 25.3 %copy-start.7 = (f32[2048]{0:T(1024)S(1)}, f32[2048]{0:T(1024)}, u32[]{:S(2)}) copy-start(f32[2048]{0:T(1024)} %param.14) | copy-start | bytes 24580
  63.0 12.0 %copy-start.4 = (bf16[256,1024]{1,0:T(8,128)(2,1)}, bf16[256,1024]{1,0:T(8,128)(2,1)S(1)}, u32[]{:S(2)}) copy-start(bf16[256,1024]{1,0:T(8,128)(2,1)S(1)} %get-tuple-element.48.attended_far) | copy-start | bytes 1572868
  63.0 1.4 collective-permute-start.1
  64.5 4.9 %collective-permute-start.4 = (f32[64,512]{1,0:T(8,128)S(1)}, f32[64,512]{1,0:T(8,128)S(1)}, u32[]{:S(2)}, u32[]{:S(2)}) collective-permute-start(f32[64,512]{1,0:T(8,128)S(1)} %add.43), channel_id=1, source_target_pairs={{0,3},{1,0},{2,1},{3,2},{4,7},{5,4},{6,5},{7,6},{8,11},{9,8},{10,9... | collective-permute-start | bytes 393224 | tf_op jit(solution)/shard_map/ppermute | solution.py:50
  65.0 6.0 %collective-permute-start.3 = (f32[64,512]{1,0:T(8,128)S(1)}, f32[64,512]{1,0:T(8,128)S(1)}, u32[]{:S(2)}, u32[]{:S(2)}) collective-permute-start(f32[64,512]{1,0:T(8,128)S(1)} %add.43), channel_id=1, source_target_pairs={{0,2},{1,3},{2,0},{3,1},{4,6},{5,7},{6,4},{7,5},{8,10},{9,11},{10,... | collective-permute-start | bytes 393224 | tf_op jit(solution)/shard_map/ppermute | solution.py:50
  66.5 7.9 %collective-permute-start.2 = (f32[64,512]{1,0:T(8,128)S(1)}, f32[64,512]{1,0:T(8,128)S(1)}, u32[]{:S(2)}, u32[]{:S(2)}) collective-permute-start(f32[64,512]{1,0:T(8,128)S(1)} %add.43), channel_id=1, source_target_pairs={{0,1},{1,2},{2,3},{3,0},{4,5},{5,6},{6,7},{7,4},{8,9},{9,10},{10,1... | collective-permute-start | bytes 393224 | tf_op jit(solution)/shard_map/ppermute | solution.py:50
  75.1 1.9 collective-permute-start.5
  85.0 17.8 %copy-start.10 = (bf16[400,512]{1,0:T(8,128)(2,1)S(1)}, bf16[400,512]{1,0:T(8,128)(2,1)}, u32[]{:S(2)}) copy-start(bf16[400,512]{1,0:T(8,128)(2,1)} %get-tuple-element.58) | copy-start | bytes 1228804
  90.5 12.3 %collective-permute-start.8 = (bf16[400,512]{1,0:T(8,128)(2,1)S(1)}, bf16[400,512]{1,0:T(8,128)(2,1)S(1)}, u32[]{:S(2)}, u32[]{:S(2)}) collective-permute-start(bf16[400,512]{1,0:T(8,128)(2,1)S(1)} %get-tuple-element.55), channel_id=1, source_target_pairs={{0,16},{8,24},{16,0},{24,8},{1,17},{9,25},{17,1},{25,9},{2,18},{10... | collective-permute-start | bytes 1228808 | tf_op jit(solution)/shard_map/ppermute | solution.py:50
  93.1 11.9 %collective-permute-start.11 = (bf16[400,512]{1,0:T(8,128)(2,1)S(1)}, bf16[400,512]{1,0:T(8,128)(2,1)S(1)}, u32[]{:S(2)}, u32[]{:S(2)}) collective-permute-start(bf16[400,512]{1,0:T(8,128)(2,1)S(1)} %get-tuple-element.59), channel_id=1, source_target_pairs={{0,64},{32,96},{64,0},{96,32},{1,65},{33,97},{65,1},{97,33},{2,66}... | collective-permute-start | bytes 1228808 | tf_op jit(solution)/shard_map/ppermute | solution.py:50
  95.3 16.9 %collective-permute-start.6 = (bf16[400,512]{1,0:T(8,128)(2,1)S(1)}, bf16[400,512]{1,0:T(8,128)(2,1)S(1)}, u32[]{:S(2)}, u32[]{:S(2)}) collective-permute-start(bf16[400,512]{1,0:T(8,128)(2,1)S(1)} %get-tuple-element.53), channel_id=1, source_target_pairs={{0,8},{8,16},{16,24},{24,0},{1,9},{9,17},{17,25},{25,1},{2,10},{10... | collective-permute-start | bytes 1228808 | tf_op jit(solution)/shard_map/ppermute | solution.py:50
  95.6 16.6 %collective-permute-start.7 = (bf16[400,512]{1,0:T(8,128)(2,1)S(1)}, bf16[400,512]{1,0:T(8,128)(2,1)S(1)}, u32[]{:S(2)}, u32[]{:S(2)}) collective-permute-start(bf16[400,512]{1,0:T(8,128)(2,1)S(1)} %get-tuple-element.54), channel_id=1, source_target_pairs={{0,24},{8,0},{16,8},{24,16},{1,25},{9,1},{17,9},{25,17},{2,26},{10... | collective-permute-start | bytes 1228808 | tf_op jit(solution)/shard_map/ppermute | solution.py:50
  98.0 16.7 %collective-permute-start.9 = (bf16[400,512]{1,0:T(8,128)(2,1)S(1)}, bf16[400,512]{1,0:T(8,128)(2,1)S(1)}, u32[]{:S(2)}, u32[]{:S(2)}) collective-permute-start(bf16[400,512]{1,0:T(8,128)(2,1)S(1)} %get-tuple-element.57), channel_id=1, source_target_pairs={{0,32},{32,64},{64,96},{96,0},{1,33},{33,65},{65,97},{97,1},{2,34}... | collective-permute-start | bytes 1228808 | tf_op jit(solution)/shard_map/ppermute | solution.py:50
  102.8 11.9 %collective-permute-start.10 = (bf16[400,512]{1,0:T(8,128)(2,1)S(1)}, bf16[400,512]{1,0:T(8,128)(2,1)S(1)}, u32[]{:S(2)}, u32[]{:S(2)}) collective-permute-start(bf16[400,512]{1,0:T(8,128)(2,1)S(1)} %copy-done.10), channel_id=1, source_target_pairs={{0,96},{32,0},{64,32},{96,64},{1,97},{33,1},{65,33},{97,65},{2,98}... | collective-permute-start | bytes 1228808 | tf_op jit(solution)/shard_map/ppermute | solution.py:50
  116.2 6.5 %collective-permute-start.12 = (bf16[448,128]{1,0:T(8,128)(2,1)S(1)}, bf16[448,128]{1,0:T(8,128)(2,1)S(1)}, u32[]{:S(2)}, u32[]{:S(2)}) collective-permute-start(bf16[448,128]{1,0:T(8,128)(2,1)S(1)} %get-tuple-element.61), channel_id=1, source_target_pairs={{0,32},{32,64},{64,96},{96,0},{1,33},{33,65},{65,97},{97,1},{2,34}... | collective-permute-start | bytes 344072 | tf_op jit(solution)/shard_map/ppermute | solution.py:50
  116.3 6.4 %collective-permute-start.13 = (bf16[448,128]{1,0:T(8,128)(2,1)S(1)}, bf16[448,128]{1,0:T(8,128)(2,1)S(1)}, u32[]{:S(2)}, u32[]{:S(2)}) collective-permute-start(bf16[448,128]{1,0:T(8,128)(2,1)S(1)} %get-tuple-element.62), channel_id=1, source_target_pairs={{0,96},{32,0},{64,32},{96,64},{1,97},{33,1},{65,33},{97,65},{2,98}... | collective-permute-start | bytes 344072 | tf_op jit(solution)/shard_map/ppermute | solution.py:50
  118.9 5.4 %collective-permute-start.14 = (bf16[448,128]{1,0:T(8,128)(2,1)S(1)}, bf16[448,128]{1,0:T(8,128)(2,1)S(1)}, u32[]{:S(2)}, u32[]{:S(2)}) collective-permute-start(bf16[448,128]{1,0:T(8,128)(2,1)S(1)} %get-tuple-element.63), channel_id=1, source_target_pairs={{0,64},{32,96},{64,0},{96,32},{1,65},{33,97},{65,1},{97,33},{2,66}... | collective-permute-start | bytes 344072 | tf_op jit(solution)/shard_map/ppermute | solution.py:50
  120.0 5.1 %collective-permute-start.15 = (bf16[448,128]{1,0:T(8,128)(2,1)S(1)}, bf16[448,128]{1,0:T(8,128)(2,1)S(1)}, u32[]{:S(2)}, u32[]{:S(2)}) collective-permute-start(bf16[448,128]{1,0:T(8,128)(2,1)S(1)} %get-tuple-element.65), channel_id=1, source_target_pairs={{0,8},{8,16},{16,24},{24,0},{1,9},{9,17},{17,25},{25,1},{2,10},{10... | collective-permute-start | bytes 344072 | tf_op jit(solution)/shard_map/ppermute | solution.py:50
  120.3 5.5 %collective-permute-start.16 = (bf16[448,128]{1,0:T(8,128)(2,1)S(1)}, bf16[448,128]{1,0:T(8,128)(2,1)S(1)}, u32[]{:S(2)}, u32[]{:S(2)}) collective-permute-start(bf16[448,128]{1,0:T(8,128)(2,1)S(1)} %get-tuple-element.66), channel_id=1, source_target_pairs={{0,24},{8,0},{16,8},{24,16},{1,25},{9,1},{17,9},{25,17},{2,26},{10... | collective-permute-start | bytes 344072 | tf_op jit(solution)/shard_map/ppermute | solution.py:50
  122.7 5.6 %collective-permute-start.17 = (bf16[448,128]{1,0:T(8,128)(2,1)S(1)}, bf16[448,128]{1,0:T(8,128)(2,1)S(1)}, u32[]{:S(2)}, u32[]{:S(2)}) collective-permute-start(bf16[448,128]{1,0:T(8,128)(2,1)S(1)} %get-tuple-element.67), channel_id=1, source_target_pairs={{0,16},{8,24},{16,0},{24,8},{1,17},{9,25},{17,1},{25,9},{2,18},{10... | collective-permute-start | bytes 344072 | tf_op jit(solution)/shard_map/ppermute | solution.py:50
  128.5 7.4 %collective-permute-start.20 = (bf16[3,128,128]{2,1,0:T(8,128)(2,1)S(1)}, bf16[3,128,128]{2,1,0:T(8,128)(2,1)S(1)}, u32[]{:S(2)}, u32[]{:S(2)}) collective-permute-start(bf16[3,128,128]{2,1,0:T(8,128)(2,1)S(1)} %get-tuple-element.68.refs_0_), channel_id=1, source_target_pairs={{0,96},{32,0},{64,32},{96,64},{1,97},{33,1},{65,33},{97,65},{2,98}... | collective-permute-start | bytes 294920 | tf_op jit(solution)/shard_map/ppermute | solution.py:50
  129.4 5.8 %collective-permute-start.24 = (bf16[256,64]{1,0:T(8,128)(2,1)S(1)}, bf16[256,64]{1,0:T(8,128)(2,1)S(1)}, u32[]{:S(2)}, u32[]{:S(2)}) collective-permute-start(bf16[256,64]{1,0:T(8,128)(2,1)S(1)} %get-tuple-element.70.refs_8_), channel_id=1, source_target_pairs={{0,4},{4,0},{1,5},{5,1},{2,6},{6,2},{3,7},{7,3},{8,12},{12,8},{9,1... | collective-permute-start | bytes 98312 | tf_op jit(solution)/shard_map/ppermute | solution.py:50
  132.4 5.9 %collective-permute-start.19 = (bf16[3,128,128]{2,1,0:T(8,128)(2,1)S(1)}, bf16[3,128,128]{2,1,0:T(8,128)(2,1)S(1)}, u32[]{:S(2)}, u32[]{:S(2)}) collective-permute-start(bf16[3,128,128]{2,1,0:T(8,128)(2,1)S(1)} %get-tuple-element.68.refs_0_), channel_id=1, source_target_pairs={{0,64},{32,96},{64,0},{96,32},{1,65},{33,97},{65,1},{97,33},{2,66}... | collective-permute-start | bytes 294920 | tf_op jit(solution)/shard_map/ppermute | solution.py:50
  134.1 6.5 %collective-permute-start.18 = (bf16[3,128,128]{2,1,0:T(8,128)(2,1)S(1)}, bf16[3,128,128]{2,1,0:T(8,128)(2,1)S(1)}, u32[]{:S(2)}, u32[]{:S(2)}) collective-permute-start(bf16[3,128,128]{2,1,0:T(8,128)(2,1)S(1)} %get-tuple-element.68.refs_0_), channel_id=1, source_target_pairs={{0,32},{32,64},{64,96},{96,0},{1,33},{33,65},{65,97},{97,1},{2,34}... | collective-permute-start | bytes 294920 | tf_op jit(solution)/shard_map/ppermute | solution.py:50
  134.2 6.4 %collective-permute-start.23 = (bf16[3,128,128]{2,1,0:T(8,128)(2,1)S(1)}, bf16[3,128,128]{2,1,0:T(8,128)(2,1)S(1)}, u32[]{:S(2)}, u32[]{:S(2)}) collective-permute-start(bf16[3,128,128]{2,1,0:T(8,128)(2,1)S(1)} %get-tuple-element.69.refs_4_), channel_id=1, source_target_pairs={{0,24},{8,0},{16,8},{24,16},{1,25},{9,1},{17,9},{25,17},{2,26},{10... | collective-permute-start | bytes 294920 | tf_op jit(solution)/shard_map/ppermute | solution.py:50
  135.2 5.4 %collective-permute-start.22 = (bf16[3,128,128]{2,1,0:T(8,128)(2,1)S(1)}, bf16[3,128,128]{2,1,0:T(8,128)(2,1)S(1)}, u32[]{:S(2)}, u32[]{:S(2)}) collective-permute-start(bf16[3,128,128]{2,1,0:T(8,128)(2,1)S(1)} %get-tuple-element.69.refs_4_), channel_id=1, source_target_pairs={{0,16},{8,24},{16,0},{24,8},{1,17},{9,25},{17,1},{25,9},{2,18},{10... | collective-permute-start | bytes 294920 | tf_op jit(solution)/shard_map/ppermute | solution.py:50
  135.8 7.4 %collective-permute-start.21 = (bf16[3,128,128]{2,1,0:T(8,128)(2,1)S(1)}, bf16[3,128,128]{2,1,0:T(8,128)(2,1)S(1)}, u32[]{:S(2)}, u32[]{:S(2)}) collective-permute-start(bf16[3,128,128]{2,1,0:T(8,128)(2,1)S(1)} %get-tuple-element.69.refs_4_), channel_id=1, source_target_pairs={{0,8},{8,16},{16,24},{24,0},{1,9},{9,17},{17,25},{25,1},{2,10},{10... | collective-permute-start | bytes 294920 | tf_op jit(solution)/shard_map/ppermute | solution.py:50
  143.9 0.9 copy-start.3
  144.8 9.7 %collective-permute-start.28 = (bf16[4,3,128,128]{3,2,1,0:T(8,128)(2,1)S(1)}, bf16[4,3,128,128]{3,2,1,0:T(8,128)(2,1)S(1)}, u32[]{:S(2)}, u32[]{:S(2)}) collective-permute-start(bf16[4,3,128,128]{3,2,1,0:T(8,128)(2,1)S(1)} %get-tuple-element.73.refs_3_), channel_id=1, source_target_pairs={{0,24},{8,0},{16,8},{24,16},{1,25},{9,1},{17,9},{25,17},{2,26},{10... | collective-permute-start | bytes 1179656 | tf_op jit(solution)/shard_map/ppermute | solution.py:50
  144.8 10.4 %collective-permute-start.27 = (bf16[4,3,128,128]{3,2,1,0:T(8,128)(2,1)S(1)}, bf16[4,3,128,128]{3,2,1,0:T(8,128)(2,1)S(1)}, u32[]{:S(2)}, u32[]{:S(2)}) collective-permute-start(bf16[4,3,128,128]{3,2,1,0:T(8,128)(2,1)S(1)} %get-tuple-element.73.refs_3_), channel_id=1, source_target_pairs={{0,8},{8,16},{16,24},{24,0},{1,9},{9,17},{17,25},{25,1},{2,10},{10... | collective-permute-start | bytes 1179656 | tf_op jit(solution)/shard_map/ppermute | solution.py:50
  146.3 9.2 %collective-permute-start.30 = (bf16[4,3,128,128]{3,2,1,0:T(8,128)(2,1)S(1)}, bf16[4,3,128,128]{3,2,1,0:T(8,128)(2,1)S(1)}, u32[]{:S(2)}, u32[]{:S(2)}) collective-permute-start(bf16[4,3,128,128]{3,2,1,0:T(8,128)(2,1)S(1)} %get-tuple-element.74.refs_4_), channel_id=1, source_target_pairs={{0,96},{32,0},{64,32},{96,64},{1,97},{33,1},{65,33},{97,65},{2,98}... | collective-permute-start | bytes 1179656 | tf_op jit(solution)/shard_map/ppermute | solution.py:50
  148.6 9.9 %collective-permute-start.29 = (bf16[4,3,128,128]{3,2,1,0:T(8,128)(2,1)S(1)}, bf16[4,3,128,128]{3,2,1,0:T(8,128)(2,1)S(1)}, u32[]{:S(2)}, u32[]{:S(2)}) collective-permute-start(bf16[4,3,128,128]{3,2,1,0:T(8,128)(2,1)S(1)} %get-tuple-element.74.refs_4_), channel_id=1, source_target_pairs={{0,32},{32,64},{64,96},{96,0},{1,33},{33,65},{65,97},{97,1},{2,34}... | collective-permute-start | bytes 1179656 | tf_op jit(solution)/shard_map/ppermute | solution.py:50
  158.6 3.7 %copy-start = (bf16[6,4,3,128,128]{4,3,2,1,0:T(8,128)(2,1)}, bf16[6,4,3,128,128]{4,3,2,1,0:T(8,128)(2,1)S(1)}, u32[]{:S(2)}) copy-start(bf16[6,4,3,128,128]{4,3,2,1,0:T(8,128)(2,1)S(1)} %shard_map.122.refs_0_) | copy-start | bytes 7077892
  158.6 7.4 %collective-permute-start.31 = (bf16[6,4,3,128,128]{4,3,2,1,0:T(8,128)(2,1)S(1)}, bf16[6,4,3,128,128]{4,3,2,1,0:T(8,128)(2,1)S(1)}, u32[]{:S(2)}, u32[]{:S(2)}) collective-permute-start(bf16[6,4,3,128,128]{4,3,2,1,0:T(8,128)(2,1)S(1)} %shard_map.122.refs_0_), channel_id=1, source_target_pairs={{0,4},{4,0},{1,5},{5,1},{2,6},{6,2},{3,7},{7,3},{8,12},{12,8},{9,1... | collective-permute-start | bytes 7077896 | tf_op jit(solution)/shard_map/ppermute | solution.py:50
  161.5 12.2 %collective-permute-start.25 = (bf16[4,3,128,128]{3,2,1,0:T(8,128)(2,1)S(1)}, bf16[4,3,128,128]{3,2,1,0:T(8,128)(2,1)S(1)}, u32[]{:S(2)}, u32[]{:S(2)}) collective-permute-start(bf16[4,3,128,128]{3,2,1,0:T(8,128)(2,1)S(1)} %get-tuple-element.75.refs_4_), channel_id=1, source_target_pairs={{0,16},{8,24},{16,0},{24,8},{1,17},{9,25},{17,1},{25,9},{2,18},{10... | collective-permute-start | bytes 1179656 | tf_op jit(solution)/shard_map/ppermute | solution.py:50
  162.2 11.8 %collective-permute-start.26 = (bf16[4,3,128,128]{3,2,1,0:T(8,128)(2,1)S(1)}, bf16[4,3,128,128]{3,2,1,0:T(8,128)(2,1)S(1)}, u32[]{:S(2)}, u32[]{:S(2)}) collective-permute-start(bf16[4,3,128,128]{3,2,1,0:T(8,128)(2,1)S(1)} %get-tuple-element.76.refs_5_), channel_id=1, source_target_pairs={{0,64},{32,96},{64,0},{96,32},{1,65},{33,97},{65,1},{97,33},{2,66}... | collective-permute-start | bytes 1179656 | tf_op jit(solution)/shard_map/ppermute | solution.py:50
  166.0 1.4 copy-start.9
  174.1 4.0 %collective-permute-start.32 = (bf16[2,4,3,128,128]{4,3,2,1,0:T(8,128)(2,1)S(1)}, bf16[2,4,3,128,128]{4,3,2,1,0:T(8,128)(2,1)S(1)}, u32[]{:S(2)}, u32[]{:S(2)}) collective-permute-start(bf16[2,4,3,128,128]{4,3,2,1,0:T(8,128)(2,1)S(1)} %shard_map.125.refs_0_), channel_id=1, source_target_pairs={{0,4},{4,0},{1,5},{5,1},{2,6},{6,2},{3,7},{7,3},{8,12},{12,8},{9,1... | collective-permute-start | bytes 2359304 | tf_op jit(solution)/shard_map/ppermute | solution.py:50
Sparse Core Ops, SparseCore 0:
  9.7 41.0 all-gather.1

commit v2 on v0

--- a/solution.py
+++ b/solution.py
@@ -11,7 +11,8 @@
 HEAD_DIM = 128
 TIMESTEPS = 1000
 UNUSED = 64.0
-FIRST = ((0, 1), (0, 3), (0, 2), (1, 3), (1, 2))
+NEAR = ((0, 1), (0, 3), (1, 1), (1, 3))
+PIECES = (*NEAR, (0, 2), (1, 2), (0, 0), (1, 0))
 f32 = jnp.float32
 bf16 = jnp.bfloat16
 HIGHEST = lax.Precision.HIGHEST
@@ -25,6 +26,9 @@
 SMEM = pl.BlockSpec(memory_space=pltpu.SMEM)
 HBM = pl.BlockSpec(memory_space=pltpu.HBM)
 ANY = pl.BlockSpec(memory_space=pl.ANY)
+
+
+LARGE = 52
 
 
 def params(mib):
@@ -100,27 +104,31 @@
     frame, core = place[0], place[1]
     slots = 512
 
-    def rank_of(i):
+    def order_of(i):
         return ((i % 256) // 16) * 32 + (i // 256) * 16 + i % 16
 
     before = jnp.where(
-        rank_of(lax.broadcasted_iota(jnp.int32, (slots, slots), 1))
-        < rank_of(lax.broadcasted_iota(jnp.int32, (slots, slots), 0)),
+        order_of(lax.broadcasted_iota(jnp.int32, (slots, slots), 0))
+        < order_of(lax.broadcasted_iota(jnp.int32, (slots, slots), 1)),
         1.0,
         0.0,
     ).astype(bf16)
-    half = (lax.broadcasted_iota(jnp.int32, (slots, 128), 0) // 8) % 2
-    lane = lax.broadcasted_iota(jnp.int32, (slots, 128), 1).astype(f32)
+    half = (lax.broadcasted_iota(jnp.int32, (8, slots), 1) // 8) % 2
+    which = lax.broadcasted_iota(jnp.int32, (8, slots), 0)
+    clip = core + (which % 2) - 2 * core * (which % 2)
+    first = jnp.where(lax.broadcasted_iota(jnp.int32, (16, 128), 1) == 0, 1.0, 0.0).astype(bf16)
+    rows, values = [], jnp.zeros((8, slots), f32)
     for i, r in enumerate(ORDER):
         from_frame = (frame + 4 - r) % 4
-        rows = jnp.concatenate([arrived[from_frame], arrived[4 + from_frame]], axis=0)
-        valid = jnp.broadcast_to(rows[:, 0:1].astype(f32), (slots, 128)) < 32.0
-        for other in range(2):
-            clip = core + other - 2 * core * other
-            mine = jnp.where(valid & (half == clip), 1.0, 0.0)
-            rank = dot(before, mine.astype(bf16))
-            pick = jnp.where(rank == lane, mine, 0.0)
-            pairs[2 * i + other] = dot(pick.astype(bf16), rows, TN).astype(bf16)
+        rows.append(jnp.concatenate([arrived[from_frame], arrived[4 + from_frame]], axis=0))
+        values = jnp.where(which // 2 == i, dot(first, rows[i], NT)[:8], values)
+    mine = jnp.where((values < 32.0) & (half == clip), 1.0, 0.0)
+    doubled = jnp.concatenate([mine, mine], axis=0).astype(bf16)
+    rank = jnp.where(mine > 0.5, dot(doubled, before)[:8], -1.0)
+    line = lax.broadcasted_iota(jnp.int32, (128, slots), 0).astype(f32)
+    for b in range(8):
+        pick = jnp.where(rank[b : b + 1] == line, 1.0, 0.0).astype(bf16)
+        pairs[b] = dot(pick, rows[b // 2]).astype(bf16)
 
 
 def lanes(i, other):
@@ -128,24 +136,31 @@
 
 
 def forward_kernel(moments, *refs):
-    act, act_theirs, sides, sides_theirs, top, top_theirs, bottom, bottom_theirs = refs[:8]
+    act_own, act_theirs, sides, sides_theirs, top, top_theirs, bottom, bottom_theirs = refs[:8]
     pairs, w_embed, gain, w_t_far, head_t, mix_t = refs[8:14]
     normed_far, proj_far, attended_far, probs, part_own, part_other = refs[14:20]
-    w_t, normed, proj, attended, rest, sems = refs[20:]
+    act, w_t, normed, proj, attended, rest, sems, arrive = refs[20:]
+    whole, low, high = pl.ds(0, 128), pl.ds(0, 64), pl.ds(64, 64)
+    moves = [(act_own, 0, whole), (act_theirs, 1, whole)]
+    for side in range(2):
+        moves += [(sides.at[side], 2 + 2 * side, whole), (sides_theirs.at[side], 3 + 2 * side, whole)]
+    moves += [(top, 6, low), (bottom, 6, high), (top_theirs, 7, low), (bottom_theirs, 7, high)]
+    loads = [[] for _ in range(8)]
+    for k, (source, b, rows) in enumerate(moves):
+        loads[b].append(pltpu.make_async_copy(source, act.at[b, rows], arrive.at[k]))
+        loads[b][-1].start()
     weights = pltpu.make_async_copy(w_t_far, w_t, sems.at[0])
     weights.start()
-    work = [(0, 0, act[...]), (1, 0, act_theirs[...])]
-    for side in range(2):
-        work += [(2 + 2 * side, 0, sides[side]), (3 + 2 * side, 0, sides_theirs[side])]
-    work += [(6, 0, top[...]), (6, 64, bottom[...]), (7, 0, top_theirs[...]), (7, 64, bottom_theirs[...])]
-    for b, start, rows in work:
-        pair = pairs[b, start : start + rows.shape[0]].astype(f32)
+    for b in range(8):
+        pair = pairs[b].astype(f32)
         t = moments[b % 2]
         noised = ((1.0 - t) * pair[:, :64] + t * pair[:, 64:]).astype(bf16)
-        hidden = rows.astype(f32) + dot(noised, w_embed[...])
+        added = dot(noised, w_embed[...])
+        for load in loads[b]:
+            load.wait()
+        hidden = act[b].astype(f32) + added
         scale = lax.rsqrt(jnp.mean(hidden * hidden, axis=1, keepdims=True) + 1e-06)
-        first = b * 128 + start
-        normed[first : first + rows.shape[0]] = (hidden * scale * gain[...]).astype(bf16)
+        normed[b * 128 : b * 128 + 128] = (hidden * scale * gain[...]).astype(bf16)
         if b == 0:
             turned = pair.T
             own = dot(head_t[...].astype(f32), hidden, NT, HIGHEST)
@@ -201,8 +216,8 @@
 
 
 def backward_kernel(place, error_own, error_other, probs, mix, proj_far, attended_far, normed_far, *refs):
-    pieces, delta, own_factor = refs[:5], refs[5], refs[6]
-    slope, grad, proj, attended, normed, sems = refs[7:]
+    pieces = refs[:8]
+    delta, own_factor, slope, grad, proj, attended, normed, sems = refs[8:]
     loads = [
         pltpu.make_async_copy(far, near, sems.at[k])
         for k, (far, near) in enumerate(((proj_far, proj), (attended_far, attended), (normed_far, normed)))
@@ -243,15 +258,7 @@
         factor = dot(slope[...], attended[h * 128 : h * 128 + 128].astype(f32), NT, HIGHEST)
         own_factor[h] = factor.astype(bf16)
     loads[2].wait()
-    for (h, o), out in zip(FIRST, pieces):
-        gradient_piece(delta, normed, own_factor[h], h, (place[h] + o) % 4, out)
-
-
-def late_kernel(place, delta, own_factor, normed_far, own_x, own_y, last, normed, sems):
-    load = pltpu.make_async_copy(normed_far, normed, sems.at[0])
-    load.start()
-    load.wait()
-    for (h, o), out in (((1, 1), last), ((0, 0), own_x), ((1, 0), own_y)):
+    for (h, o), out in zip(PIECES, pieces):
         gradient_piece(delta, normed, own_factor[h], h, (place[h] + o) % 4, out)
 
 
@@ -283,17 +290,17 @@
 
 
 def line_kernel(*refs):
-    lines, both = refs[8:10], refs[10]
+    factor, lines, factor_out = refs[8], refs[9:11], refs[11]
     for h in range(2):
         for o in range(4):
-            piece = refs[4 * h + o][...]
-            lines[h][o] = piece
-            both[h, o] = piece
-
-
-def join_kernel(a, b, c, out):
-    for k, ref in enumerate((a, b, c)):
-        out[k] = ref[...]
+            lines[h][o] = refs[4 * h + o][...]
+    factor_out[...] = factor[...]
+
+
+def join_kernel(*refs):
+    out = refs[-1]
+    for k in range(out.shape[0]):
+        out[k] = refs[k][...]
 
 
 def assemble_kernel(tags, aliased, with_out, place, *refs):
@@ -301,8 +308,10 @@
     count = len(tags)
     sources, refs = refs[:arrays], refs[arrays + aliased :]
     if with_out:
-        factors, head_t, line, out, grad_out, line_out, held, ready, done, sems, whole, sent = refs
-        line_out[...] = line[...]
+        factor, factor_theirs, head_t, out, grad_out, held, ready, done, sems, whole, sent, factors = refs
+        start = pl.multiple_of(place[2] * 256, 256)
+        factors[pl.ds(start, 256)] = factor[...]
+        factors[pl.ds(pl.multiple_of(256 - start, 256), 256)] = factor_theirs[...]
     else:
         out, held, ready, done, sems = refs
     loads = []
@@ -314,32 +323,27 @@
         whole[...] = dot(factors[...], head_t[...])
         leave = pltpu.make_async_copy(whole, grad_out, sent.at[0])
         leave.start()
-    stores = [None, None]
-    slot = 1
+    stores = []
     for k, tag in enumerate(tags):
         o, theirs, h, inners = tag[2:]
         loads[k].wait()
-        if k == 0 or tags[k - 1][2:5] != tag[2:5]:
-            slot = 1 - slot
-            if stores[slot] is not None:
-                stores[slot].wait()
         first = (place[h] + 4 - o) % 4
         for i, inner in enumerate(inners):
             second = (place[1 - h] + 4 - inner) % 4
-            ready[slot, :, pl.ds(pl.multiple_of(second * 128, 128), 128)] = held[k, i].astype(f32)
-        if k + 1 < count and tags[k + 1][2:5] == tag[2:5]:
-            continue
+            ready[k, :, pl.ds(pl.multiple_of(second * 128, 128), 128)] = held[k, i].astype(f32)
         core = place[2] if theirs == 0 else 1 - place[2]
-        stores[slot] = pltpu.make_async_copy(
-            ready.at[slot],
-            out.at[
-                :,
-                pl.ds(pl.multiple_of(first * 512, 512), 512),
-                pl.ds(pl.multiple_of(core * 256 + h * 128, 128), 128),
-            ],
-            done.at[slot],
+        stores.append(
+            pltpu.make_async_copy(
+                ready.at[k],
+                out.at[
+                    :,
+                    pl.ds(pl.multiple_of(first * 512, 512), 512),
+                    pl.ds(pl.multiple_of(core * 256 + h * 128, 128), 128),
+                ],
+                done.at[k],
+            )
         )
-        stores[slot].start()
+        stores[k].start()
     for store in stores:
         store.wait()
     if with_out:
@@ -353,14 +357,18 @@
     out_specs = [HBM]
     scratch = [
         pltpu.VMEM((len(tags), *arrays[0].shape[-4:]), bf16),
-        pltpu.VMEM((2, 3, 512, 128), f32),
-        pltpu.SemaphoreType.DMA((2,)),
+        pltpu.VMEM((len(tags), 3, 512, 128), f32),
+        pltpu.SemaphoreType.DMA((len(tags),)),
         pltpu.SemaphoreType.DMA((len(tags),)),
     ]
     if product:
-        out_shape += [shape((512, 2048), f32), shape((4, 3, 128, 128), bf16)]
-        out_specs += [HBM, VMEM]
-        scratch += [pltpu.VMEM((512, 2048), f32), pltpu.SemaphoreType.DMA((1,))]
+        out_shape.append(shape((512, 2048), f32))
+        out_specs.append(HBM)
+        scratch += [
+            pltpu.VMEM((512, 2048), f32),
+            pltpu.SemaphoreType.DMA((1,)),
+            pltpu.VMEM((512, 64), bf16),
+        ]
     return pl.pallas_call(
         functools.partial(assemble_kernel, tags, len(given), bool(product)),
         in_specs=[SMEM] + [ANY] * len(arrays) + [HBM] * len(given) + [VMEM] * len(product),
@@ -368,7 +376,7 @@
         out_shape=out_shape,
         scratch_shapes=scratch,
         input_output_aliases={1 + len(arrays): 0} if given else {},
-        compiler_params=params(12),
+        compiler_params=params(LARGE),
         cost_estimate=TINY,
     )(place, *arrays, *given, *product)
 
@@ -411,6 +419,7 @@
         sides_kernel,
         near(half_act, half_act, shape((2, 128, 2048), bf16), shape((8, 256, 128), bf16)),
         *near(before, after, arrived),
+        mib=LARGE,
     )
     top, bottom = shift(top, "frame", 1), shift(bottom, "frame", 3)
     sides_theirs = shift(sides, "core", 1)
@@ -430,7 +439,7 @@
             dma((4,)),
             dma((6,)),
         ],
-        mib=12,
+        mib=LARGE,
     )
     (pairs,) = call(fetch_kernel, near(shape((8, 128, 128), bf16)), here, *near(arrived))
     normed, proj, attended, probs, part_own, part_other = call(
@@ -438,17 +447,19 @@
         far(shape((1024, 2048), bf16), shape((768, 1024), bf16), shape((256, 1024), bf16))
         + near(shape((4, 16, 128), f32), shape((64, 512), f32), shape((64, 512), f32)),
         (SMEM, moments),
-        *near(act, act_theirs, sides, sides_theirs, top, shift(top, "core", 1), bottom, shift(bottom, "core", 1)),
+        *far(act, act_theirs, sides, sides_theirs, top, shift(top, "core", 1), bottom, shift(bottom, "core", 1)),
         *near(pairs, w_embed, norm_gain.reshape(1, 2048)), *far(w_t), *near(head_t, mix_t),
         scratch=[
+            pltpu.VMEM((8, 128, 2048), bf16),
             pltpu.VMEM((768, 2048), bf16),
             pltpu.VMEM((1024, 2048), bf16),
             pltpu.VMEM((768, 1024), bf16),
             pltpu.VMEM((256, 1024), bf16),
             pltpu.VMEM((64, 128), f32),
             dma((4,)),
+            dma((10,)),
         ],
-        mib=16,
+        mib=LARGE,
     )
 
     clip_part = part_own + shift(part_other, "core", 1)
@@ -471,11 +482,13 @@
     block = shape((3, 128, 128), bf16)
     line = shape((4, 3, 128, 128), bf16)
     axes = (("x", "y"), ("y", "x"))
-    *first, delta, own_factor = call(
+    pieces = call(
         backward_kernel,
-        near(*[piece] * 5, shape((768, 1024), bf16), shape((2, 64, 128), bf16)),
+        near(*[piece] * 8),
         square, *near(error_own, error_other, probs, mix), *far(proj, attended, normed),
         scratch=[
+            pltpu.VMEM((768, 1024), bf16),
+            pltpu.VMEM((2, 64, 128), bf16),
             pltpu.VMEM((64, 1024), f32),
             pltpu.VMEM((256, 1024), f32),
             pltpu.VMEM((768, 1024), bf16),
@@ -483,16 +496,12 @@
             pltpu.VMEM((1024, 2048), bf16),
             dma((3,)),
         ],
-        mib=16,
+        mib=LARGE,
     )
     moved = [[], []]
-    for (h, o), p in zip(FIRST, first):
+    for (h, o), p in zip(PIECES, pieces[:6]):
         moved[h].append(shift(p, axes[h][0], o))
-    own_x, own_y, last = call(
-        late_kernel, near(*[piece] * 3), square, *near(delta, own_factor), *far(normed),
-        scratch=[pltpu.VMEM((1024, 2048), bf16), dma((1,))],
-    )
-    moved[1].append(shift(last, axes[1][0], 1))
+    own_x, own_y = pieces[6:]
     second = call(
         add_first_kernel, near(*[small] * 8), square, *near(own_x, *moved[0], own_y, *moved[1]),
         scratch=[pltpu.VMEM((400, 512), bf16)],
@@ -505,39 +514,36 @@
     back = [
         {0: owned[h], **{o: shift(owned[h], axes[h][1], o) for o in (1, 3, 2)}} for h in range(2)
     ]
+    line_x, line_y, factor = call(
+        line_kernel, near(line, line, shape((256, 64), bf16)),
+        *near(*(back[h][o] for h in range(2) for o in range(4)), factor),
+    )
     factor_theirs = shift(factor, "core", 1)
-    factors = jnp.concatenate(
-        [jnp.where(core == 0, factor, factor_theirs), jnp.where(core == 0, factor_theirs, factor)]
-    )
-    line_x, line_y, lines = call(
-        line_kernel, near(line, line, shape((2, 4, 3, 128, 128), bf16)),
-        *near(*(back[h][o] for h in range(2) for o in range(4))),
-    )
     every = (0, 1, 2, 3)
-    wide = {(h, o): shift((line_x, line_y)[h], axes[h][0], o) for h, o in FIRST}
-    grad_qkv, grad_out, line_last = assemble(
-        square[1], (lines,), [(0, h, 0, 0, h, every) for h in range(2)], None, (factors, head_t, line_y)
-    )
-    wide[1, 1] = shift(line_last, axes[1][0], 1)
-    lines_theirs = shift(lines, "core", 1)
-    reach = (1, 3, 2)
-    triple = near(shape((3, 4, 3, 128, 128), bf16))
-    (wide_x,) = call(join_kernel, triple, *near(*(wide[0, o] for o in reach)))
-    wide_x_theirs = shift(wide_x, "core", 1)
-    (wide_y,) = call(join_kernel, triple, *near(*(wide[1, o] for o in reach)))
-    wide_y_theirs = shift(wide_y, "core", 1)
-
-    def placed(array, side, h):
-        return [(array, k, reach[k], side, h, every) for k in range(3)]
-
-    (grad_qkv,) = assemble(
-        square[1], (lines_theirs,), [(0, h, 0, 1, h, every) for h in range(2)], grad_qkv
-    )
-    (grad_qkv,) = assemble(
-        square[1], (wide_x, wide_x_theirs), placed(0, 0, 0) + placed(1, 1, 0), grad_qkv
-    )
-    (grad_qkv,) = assemble(square[1], (wide_y,), placed(0, 0, 1), grad_qkv)
-    (grad_qkv,) = assemble(square[1], (wide_y_theirs,), placed(0, 1, 1), grad_qkv)
+    lines = (line_x, line_y)
+    beside = [shift(lines[h], axes[h][0], o) for h, o in NEAR]
+    opposite = [shift(lines[h], axes[h][0], 2) for h in range(2)]
+    (grad_qkv,) = assemble(square[1], lines, [(h, None, 0, 0, h, every) for h in range(2)])
+    (sides,) = call(
+        join_kernel, near(shape((6, 4, 3, 128, 128), bf16)), *near(*beside, *lines), *far(grad_qkv),
+        mib=LARGE,
+    )
+    sides_theirs = shift(sides, "core", 1)
+    side_tags = [(0, k, o, h) for k, (h, o) in enumerate((*NEAR, (0, 0), (1, 0)))]
+
+    def tagged(tags, side):
+        return [(array, k, o, side, h, every) for array, k, o, h in tags]
+
+    grad_qkv, grad_out = assemble(
+        square[1], (sides,), tagged(side_tags[:4], 0), grad_qkv, (factor, factor_theirs, head_t)
+    )
+    (grad_qkv,) = assemble(square[1], (sides_theirs,), tagged(side_tags, 1), grad_qkv)
+    (across,) = call(
+        join_kernel, near(shape((2, 4, 3, 128, 128), bf16)), *near(*opposite), *far(grad_qkv), mib=LARGE
+    )
+    across_theirs = shift(across, "core", 1)
+    for side, array in enumerate((across, across_theirs)):
+        (grad_qkv,) = assemble(square[1], (array,), tagged([(0, 0, 2, 0), (0, 1, 2, 1)], side), grad_qkv)
     return frame_loss, grad_qkv, grad_out
 
 

time: 202 us -> 184 us (0.911)
  local copies, waits for them, and re-layouts: 18.7 us -> 7.52 us
  waiting for transfers between devices: 51.4 us -> 45.4 us
  Pallas kernels: 50.9 us -> 48.8 us
    unnamed x38 -> x24, local copies, waits for them, and re-layouts: 18.7 us -> 7.52 us
    ppermute x42 -> x41, waiting for transfers between devices: 51.4 us -> 45.4 us  [shift(): lax.ppermute(value, axis, [(i, (i + offset) % size) for i in range(size)])]
    pallas_call x5, Pallas kernels: 18.4 us -> 14.7 us  [assemble(): pl.pallas_call(functools.partial(assemble_kernel, tags, len(given), bool(...]
    ppermute x42 -> x41, starting transfers between devices: 57.3 us -> 59.5 us  [shift(): lax.ppermute(value, axis, [(i, (i + offset) % size) for i in range(size)])]
    pallas_call x12 -> x11, Pallas kernels: 32.6 us -> 34.2 us  [call(): pl.pallas_call(kernel, in_specs=[spec for spec, _ in operands], out_specs...]
  transfers between devices with their start and end apart: 43 -> 42, of which waited for: 18 -> 18; matrix products, arithmetic and copies ran while one was open for 0% -> 0% of each run, Pallas kernels for 11% -> 10%
where the time goes in v2:
time: 184 us
  starting transfers between devices  64 us (35%)
  Pallas kernels  48.8 us (27%)
  waiting for transfers between devices  45.4 us (25%)
  blocking collectives  13.1 us (7%)
  local copies, waits for them, and re-layouts  7.52 us (4%)
  between operations  3.36 us (2%)
    ppermute x41, starting transfers between devices, shift(): lax.ppermute(value, axis, [(i, (i + offset) % size) for i in range(size)])  59.5 us
    ppermute x41, waiting for transfers between devices, shift(): lax.ppermute(value, axis, [(i, (i + offset) % size) for i in range(size)])  45.4 us
    pallas_call x11, Pallas kernels, call(): pl.pallas_call(kernel, in_specs=[spec for spec, _ in operands], out_specs...  34.2 us
    pallas_call x5, Pallas kernels, assemble(): pl.pallas_call(functools.partial(assemble_kernel, tags, len(given), bool(...  14.7 us
    all_to_all x1, blocking collectives, shards(): lax.all_to_all(sent, ('y', 'x'), 0, 0, tiled=True).reshape(256, 128)  13.1 us
    unnamed x24, local copies, waits for them, and re-layouts  7.52 us
    all_to_all x1, starting transfers between devices, shards(): arrived = lax.all_to_all(spread, ('core', 'frame'), 0, 0, tiled=True)  4.48 us
  transfers between devices with their start and end apart: 42, of which 18 were waited for; matrix products, arithmetic and copies ran while one was open for 0% of the time, Pallas kernels for 10%

profile of v2, /device:TPU:1, one launch (start us, length us, event | category | flops | bytes accessed | tf_op | source)
XLA Modules:
  0.0 183.7 jit_solution(5322031350510964142)
XLA Ops:
  0.6 2.5 %collective-permute-start.2 = (bf16[128,2048]{1,0:T(8,128)(2,1)}, bf16[128,2048]{1,0:T(8,128)(2,1)S(1)}, u32[]{:S(2)}, u32[]{:S(2)}) collective-permute-start(bf16[128,2048]{1,0:T(8,128)(2,1)} %refs_0_.1), channel_id=1, source_target_pairs={{0,1},{1,2},{2,3},{3,0},{4,5},{5,6},{6,7},{7,4},{8,9},{9,10},{10,1... | collective-permute-start | bytes 1572872 | tf_op jit(solution)/shard_map/ppermute | solution.py:51
  3.2 2.2 %collective-permute-start.3 = (bf16[128,2048]{1,0:T(8,128)(2,1)}, bf16[128,2048]{1,0:T(8,128)(2,1)S(1)}, u32[]{:S(2)}, u32[]{:S(2)}) collective-permute-start(bf16[128,2048]{1,0:T(8,128)(2,1)} %refs_0_.1), channel_id=1, source_target_pairs={{0,3},{1,0},{2,1},{3,2},{4,7},{5,4},{6,5},{7,6},{8,11},{9,8},{10,9... | collective-permute-start | bytes 1572872 | tf_op jit(solution)/shard_map/ppermute | solution.py:51
  7.1 13.1 %all_to_all.10 = bf16[16,16,128]{2,1,0:T(8,128)(2,1)S(1)} all-to-all(bf16[16,16,128]{2,1,0:T(8,128)(2,1)S(1)} %shard_map.112), channel_id=1, replica_groups=mesh['y'=4,'x'=4,'core'=2,'frame'=4] {'y','x'}, dimensions={0} | all-to-all | bytes 131072 | tf_op jit(solution)/shard_map/all_to_all | solution.py:416
  21.0 2.3 %shard_map.113 = (bf16[64,2048]{1,0:T(8,128)(2,1)S(1)}, bf16[64,2048]{1,0:T(8,128)(2,1)S(1)}, bf16[2,128,2048]{2,1,0:T(8,128)(2,1)}, bf16[8,256,128]{2,1,0:T(8,128)(2,1)}) custom-call(bf16[128,2048]{1,0:T(8,128)(2,1)S(1)} %collective-permute-done.2.before, bf16[128,2048]{1,0:T(8,128)(2,1)} %copy-done.11, bf16[256,128]{1,0:T(8,128)(2,1)S(1)} %bitcast.12), custom_call_target="tpu_custom_call" | custom-call | bytes 1024 | tf_op jit(solution)/shard_map/pallas_call | solution.py:385
  23.2 2.4 %collective-permute-start.4 = (bf16[2,128,2048]{2,1,0:T(8,128)(2,1)}, bf16[2,128,2048]{2,1,0:T(8,128)(2,1)S(1)}, u32[]{:S(2)}, u32[]{:S(2)}) collective-permute-start(bf16[2,128,2048]{2,1,0:T(8,128)(2,1)} %get-tuple-element.40.refs_2_), channel_id=1, source_target_pairs={{0,4},{4,0},{1,5},{5,1},{2,6},{6,2},{3,7},{7,3},{8,12},{12,8},{9,1... | collective-permute-start | bytes 3145736 | tf_op jit(solution)/shard_map/ppermute | solution.py:51
  25.6 2.7 %collective-permute-start.7 = (bf16[64,2048]{1,0:T(8,128)(2,1)S(1)}, bf16[64,2048]{1,0:T(8,128)(2,1)S(1)}, u32[]{:S(2)}, u32[]{:S(2)}) collective-permute-start(bf16[64,2048]{1,0:T(8,128)(2,1)S(1)} %get-tuple-element.42), channel_id=1, source_target_pairs={{0,3},{1,0},{2,1},{3,2},{4,7},{5,4},{6,5},{7,6},{8,11},{9,8},{10,9... | collective-permute-start | bytes 786440 | tf_op jit(solution)/shard_map/ppermute | solution.py:51
  28.3 4.5 %all-to-all-start.1 = ((bf16[8,256,128]{2,1,0:T(8,128)(2,1)}), bf16[8,256,128]{2,1,0:T(8,128)(2,1)S(1)}, u32[]{:S(2)}, u32[]{:S(2)}) async-start(bf16[8,256,128]{2,1,0:T(8,128)(2,1)} %get-tuple-element.43), calls=%async_computation.1 | async-start | bytes 1048576 | tf_op jit(solution)/shard_map/all_to_all | solution.py:426
  32.8 1.4 collective-permute-done.5.refs_4_
  34.2 1.4 collective-permute-start.6
  36.3 1.6 collective-permute-start
  38.9 3.7 %shard_map.115 = (bf16[768,2048]{1,0:T(8,128)(2,1)}, f32[256,64]{1,0:T(8,128)S(1)}, f32[64,256]{1,0:T(8,128)S(1)}) custom-call(s32[2]{0:T(128)S(1)} %pad_add_fusion.place, bf16[3,2048,512]{2,1,0:T(8,128)(2,1)} %w.1, bf16[512,2048]{1,0:T(8,128)(2,1)} %w_out.1, bf16[64,2048]{1,0:T(8,128)(2,1)S(1)} %bitcast.10), custom_call_target="tpu_custom_call" | custom-call | bytes 1024 | tf_op jit(solution)/shard_map/pallas_call | solution.py:385
  43.3 1.4 shard_map.114.refs_8_
  45.7 12.5 %shard_map.116 = (bf16[1024,2048]{1,0:T(8,128)(2,1)}, bf16[768,1024]{1,0:T(8,128)(2,1)}, bf16[256,1024]{1,0:T(8,128)(2,1)}, f32[4,16,128]{2,1,0:T(8,128)S(1)}, f...) custom-call(f32[2]{0:T(128)S(1)} %pad_maximum_fusion.1.moments, bf16[128,2048]{1,0:T(8,128)(2,1)} %refs_0_.1, ...), custom_call_target="tpu_custom_call" | custom-call | bytes 1024 | tf_op jit(solution)/shard_map/pallas_call | solution.py:385
  58.4 1.2 collective-permute-done.9
  59.7 4.3 %collective-permute-start.11 = (f32[64,512]{1,0:T(8,128)S(1)}, f32[64,512]{1,0:T(8,128)S(1)}, u32[]{:S(2)}, u32[]{:S(2)}) collective-permute-start(f32[64,512]{1,0:T(8,128)S(1)} %add.43), channel_id=1, source_target_pairs={{0,2},{1,3},{2,0},{3,1},{4,6},{5,7},{6,4},{7,5},{8,10},{9,11},{10,... | collective-permute-start | bytes 393224 | tf_op jit(solution)/shard_map/ppermute | solution.py:51
  64.1 2.4 %collective-permute-done.10 = f32[64,512]{1,0:T(8,128)S(1)} collective-permute-done((f32[64,512]{1,0:T(8,128)S(1)}, f32[64,512]{1,0:T(8,128)S(1)}, u32[]{:S(2)}, u32[]{:S(2)}) %collective-permute-start.10) | collective-permute-done | bytes 131104 | tf_op jit(solution)/shard_map/ppermute | solution.py:51
  66.5 3.7 %collective-permute-done.11 = f32[64,512]{1,0:T(8,128)S(1)} collective-permute-done((f32[64,512]{1,0:T(8,128)S(1)}, f32[64,512]{1,0:T(8,128)S(1)}, u32[]{:S(2)}, u32[]{:S(2)}) %collective-permute-start.11) | collective-permute-done | bytes 131104 | tf_op jit(solution)/shard_map/ppermute | solution.py:51
  70.8 1.5 collective-permute-start.13
  73.3 9.8 %shard_map.117 = (bf16[400,512]{1,0:T(8,128)(2,1)S(1)}, bf16[400,512]{1,0:T(8,128)(2,1)S(1)}, bf16[400,512]{1,0:T(8,128)(2,1)S(1)}, bf16[400,512]{1,0:T(8,128)(2...) custom-call(s32[3]{0:T(128)S(1)} %pad_add_fusion.1.place, ...), custom_call_target="tpu_custom_call" | custom-call | bytes 1024 | tf_op jit(solution)/shard_map/pallas_call | solution.py:385
  83.4 2.4 %collective-permute-start.15 = (bf16[400,512]{1,0:T(8,128)(2,1)S(1)}, bf16[400,512]{1,0:T(8,128)(2,1)S(1)}, u32[]{:S(2)}, u32[]{:S(2)}) collective-permute-start(bf16[400,512]{1,0:T(8,128)(2,1)S(1)} %get-tuple-element.55), channel_id=1, source_target_pairs={{0,24},{8,0},{16,8},{24,16},{1,25},{9,1},{17,9},{25,17},{2,26},{10... | collective-permute-start | bytes 1228808 | tf_op jit(solution)/shard_map/ppermute | solution.py:51
  86.0 2.4 %collective-permute-start.18 = (bf16[400,512]{1,0:T(8,128)(2,1)}, bf16[400,512]{1,0:T(8,128)(2,1)S(1)}, u32[]{:S(2)}, u32[]{:S(2)}) collective-permute-start(bf16[400,512]{1,0:T(8,128)(2,1)} %get-tuple-element.59), channel_id=1, source_target_pairs={{0,96},{32,0},{64,32},{96,64},{1,97},{33,1},{65,33},{97,65},{2,98}... | collective-permute-start | bytes 1228808 | tf_op jit(solution)/shard_map/ppermute | solution.py:51
  88.5 7.1 %collective-permute-done.14.refs_1_ = bf16[400,512]{1,0:T(8,128)(2,1)S(1)} collective-permute-done((bf16[400,512]{1,0:T(8,128)(2,1)S(1)}, bf16[400,512]{1,0:T(8,128)(2,1)S(1)}, u32[]{:S(2)}, u32[]{:S(2)}) %collective-permute-start.14) | collective-permute-done | bytes 409632 | tf_op jit(solution)/shard_map/ppermute | solution.py:51
  96.4 6.8 %collective-permute-done.16.refs_3_ = bf16[400,512]{1,0:T(8,128)(2,1)S(1)} collective-permute-done((bf16[400,512]{1,0:T(8,128)(2,1)}, bf16[400,512]{1,0:T(8,128)(2,1)S(1)}, u32[]{:S(2)}, u32[]{:S(2)}) %collective-permute-start.16) | collective-permute-done | bytes 409632 | tf_op jit(solution)/shard_map/ppermute | solution.py:51
  104.1 1.0 copy-done.3
  105.1 1.0 copy-done.4
  106.1 1.4 shard_map.118
  108.1 2.2 %collective-permute-start.21 = (bf16[448,128]{1,0:T(8,128)(2,1)S(1)}, bf16[448,128]{1,0:T(8,128)(2,1)S(1)}, u32[]{:S(2)}, u32[]{:S(2)}) collective-permute-start(bf16[448,128]{1,0:T(8,128)(2,1)S(1)} %get-tuple-element.63), channel_id=1, source_target_pairs={{0,96},{32,0},{64,32},{96,64},{1,97},{33,1},{65,33},{97,65},{2,98}... | collective-permute-start | bytes 344072 | tf_op jit(solution)/shard_map/ppermute | solution.py:51
  110.3 2.6 %collective-permute-start.23 = (bf16[448,128]{1,0:T(8,128)(2,1)S(1)}, bf16[448,128]{1,0:T(8,128)(2,1)S(1)}, u32[]{:S(2)}, u32[]{:S(2)}) collective-permute-start(bf16[448,128]{1,0:T(8,128)(2,1)S(1)} %get-tuple-element.66), channel_id=1, source_target_pairs={{0,8},{8,16},{16,24},{24,0},{1,9},{9,17},{17,25},{25,1},{2,10},{10... | collective-permute-start | bytes 344072 | tf_op jit(solution)/shard_map/ppermute | solution.py:51
  113.0 3.7 %collective-permute-done.20.refs_1_ = bf16[448,128]{1,0:T(8,128)(2,1)S(1)} collective-permute-done((bf16[448,128]{1,0:T(8,128)(2,1)S(1)}, bf16[448,128]{1,0:T(8,128)(2,1)S(1)}, u32[]{:S(2)}, u32[]{:S(2)}) %collective-permute-start.20) | collective-permute-done | bytes 114720 | tf_op jit(solution)/shard_map/ppermute | solution.py:51
  116.7 5.1 %collective-permute-done.25.refs_7_ = bf16[448,128]{1,0:T(8,128)(2,1)S(1)} collective-permute-done((bf16[448,128]{1,0:T(8,128)(2,1)S(1)}, bf16[448,128]{1,0:T(8,128)(2,1)S(1)}, u32[]{:S(2)}, u32[]{:S(2)}) %collective-permute-start.25) | collective-permute-done | bytes 114720 | tf_op jit(solution)/shard_map/ppermute | solution.py:51
  122.2 2.6 %collective-permute-start.28 = (bf16[3,128,128]{2,1,0:T(8,128)(2,1)S(1)}, bf16[3,128,128]{2,1,0:T(8,128)(2,1)S(1)}, u32[]{:S(2)}, u32[]{:S(2)}) collective-permute-start(bf16[3,128,128]{2,1,0:T(8,128)(2,1)S(1)} %get-tuple-element.69.refs_0_), channel_id=1, source_target_pairs={{0,96},{32,0},{64,32},{96,64},{1,97},{33,1},{65,33},{97,65},{2,98}... | collective-permute-start | bytes 294920 | tf_op jit(solution)/shard_map/ppermute | solution.py:51
  124.8 1.8 collective-permute-start.30
  126.5 1.3 collective-permute-done.26.refs_1_
  129.0 2.2 %collective-permute-done.29.refs_5_ = bf16[3,128,128]{2,1,0:T(8,128)(2,1)S(1)} collective-permute-done((bf16[3,128,128]{2,1,0:T(8,128)(2,1)S(1)}, bf16[3,128,128]{2,1,0:T(8,128)(2,1)S(1)}, u32[]{:S(2)}, u32[]{:S(2)}) %collective-permute-start.29) | collective-permute-done | bytes 98336 | tf_op jit(solution)/shard_map/ppermute | solution.py:51
  131.3 1.2 collective-permute-done.31.refs_7_
  133.4 2.2 %collective-permute-start.35 = (bf16[4,3,128,128]{3,2,1,0:T(8,128)(2,1)S(1)}, bf16[4,3,128,128]{3,2,1,0:T(8,128)(2,1)S(1)}, u32[]{:S(2)}, u32[]{:S(2)}) collective-permute-start(bf16[4,3,128,128]{3,2,1,0:T(8,128)(2,1)S(1)} %get-tuple-element.72.refs_0_.refs_4_), channel_id=1, source_target_pairs={{0,24},{8,0},{16,8},{24,16},{1,25},{9,1},{17,9},{25,17},{2,26},{10... | collective-permute-start | bytes 1179656 | tf_op jit(solution)/shard_map/ppermute | solution.py:51
  136.2 2.2 %collective-permute-start.37 = (bf16[4,3,128,128]{3,2,1,0:T(8,128)(2,1)S(1)}, bf16[4,3,128,128]{3,2,1,0:T(8,128)(2,1)S(1)}, u32[]{:S(2)}, u32[]{:S(2)}) collective-permute-start(bf16[4,3,128,128]{3,2,1,0:T(8,128)(2,1)S(1)} %get-tuple-element.73.refs_1_.refs_5_), channel_id=1, source_target_pairs={{0,96},{32,0},{64,32},{96,64},{1,97},{33,1},{65,33},{97,65},{2,98}... | collective-permute-start | bytes 1179656 | tf_op jit(solution)/shard_map/ppermute | solution.py:51
  138.4 2.2 %shard_map.121.refs_6_.refs_1_ = f32[3,2048,512]{2,1,0:T(8,128)} custom-call(s32[3]{0:T(128)S(1)} %pad_add_fusion.1.place, bf16[4,3,128,128]{3,2,1,0:T(8,128)(2,1)S(1)} %get-tuple-element.72.refs_0_.refs_4_, bf16[4,3,128,128]{3,2,1,0:T(8,128)(2,1)S(1)} %get-tuple-element.73.refs_1_.refs_5_), custom_call_target="tpu_custom_call" | custom-call | bytes 1024 | tf_op jit(solution)/shard_map/pallas_call | solution.py:372
  141.1 3.5 %collective-permute-done.36.refs_2_ = bf16[4,3,128,128]{3,2,1,0:T(8,128)(2,1)S(1)} collective-permute-done((bf16[4,3,128,128]{3,2,1,0:T(8,128)(2,1)S(1)}, bf16[4,3,128,128]{3,2,1,0:T(8,128)(2,1)S(1)}, u32[]{:S(2)}, u32[]{:S(2)}) %collective-permute-start.36) | collective-permute-done | bytes 393248 | tf_op jit(solution)/shard_map/ppermute | solution.py:51
  145.0 2.5 %shard_map.122.refs_0_ = bf16[6,4,3,128,128]{4,3,2,1,0:T(8,128)(2,1)} custom-call(bf16[4,3,128,128]{3,2,1,0:T(8,128)(2,1)S(1)} %collective-permute-done.34.refs_0_, bf16[4,3,128,128]{3,2,1,0:T(8,128)(2,1)S(1)} %collective-permute-done.35.refs_1_, bf16[4,3,128,128]{3,2,1,0:T(8,128)(2,1)S(1)} %collective-permute-done.36.refs_2_, ...), custom_call_target="tpu_custom_call" | custom-call | bytes 1024 | tf_op jit(solution)/shard_map/pallas_call | solution.py:385
  147.6 15.6 %collective-permute-start.38 = (bf16[6,4,3,128,128]{4,3,2,1,0:T(8,128)(2,1)}, bf16[6,4,3,128,128]{4,3,2,1,0:T(8,128)(2,1)S(1)}, u32[]{:S(2)}, u32[]{:S(2)}) collective-permute-start(bf16[6,4,3,128,128]{4,3,2,1,0:T(8,128)(2,1)} %shard_map.122.refs_0_), channel_id=1, source_target_pairs={{0,4},{4,0},{1,5},{5,1},{2,6},{6,2},{3,7},{7,3},{8,12},{12,8},{9,1... | collective-permute-start | bytes 7077896 | tf_op jit(solution)/shard_map/ppermute | solution.py:51
  163.2 1.2 collective-permute-start.33
  164.9 2.5 %collective-permute-done.39.refs_3_ = bf16[256,64]{1,0:T(8,128)(2,1)S(1)} collective-permute-done((bf16[256,64]{1,0:T(8,128)(2,1)S(1)}, bf16[256,64]{1,0:T(8,128)(2,1)S(1)}, u32[]{:S(2)}, u32[]{:S(2)}) %collective-permute-start.39) | collective-permute-done | bytes 32800 | tf_op jit(solution)/shard_map/ppermute | solution.py:51
  167.4 4.3 %shard_map.123 = (f32[3,2048,512]{2,1,0:T(8,128)}, f32[512,2048]{1,0:T(8,128)}) custom-call(s32[3]{0:T(128)S(1)} %pad_add_fusion.1.place, bf16[6,4,3,128,128]{4,3,2,1,0:T(8,128)(2,1)} %shard_map.122.refs_0_, f32[3,2048,512]{2,1,0:T(8,128)} %shard_map.121.refs_6_.refs_1_, ...), custom_call_target="tpu_custom_call", output_to_operand_aliasing={{0}: (2, {})} | custom-call | bytes 1024 | tf_op jit(solution)/shard_map/pallas_call | solution.py:372
  171.8 1.4 copy-done.9
  173.1 3.9 %shard_map.124.refs_2_.refs_1_ = f32[3,2048,512]{2,1,0:T(8,128)} custom-call(s32[3]{0:T(128)S(1)} %pad_add_fusion.1.place, bf16[6,4,3,128,128]{4,3,2,1,0:T(8,128)(2,1)} %copy-done.9, f32[3,2048,512]{2,1,0:T(8,128)} %get-tuple-element.75.refs_1_), custom_call_target="tpu_custom_call", output_to_operand_aliasing={{}: (2, {})} | custom-call | bytes 1024 | tf_op jit(solution)/shard_map/pallas_call | solution.py:372
  178.2 2.2 %shard_map.126.refs_1_ = f32[3,2048,512]{2,1,0:T(8,128)} custom-call(s32[3]{0:T(128)S(1)} %pad_add_fusion.1.place, bf16[2,4,3,128,128]{4,3,2,1,0:T(8,128)(2,1)S(1)} %shard_map.125.refs_0_, f32[3,2048,512]{2,1,0:T(8,128)} %shard_map.124.refs_2_.refs_1_), custom_call_target="tpu_custom_call", output_to_operand_aliasing={{}: (2, {})} | custom-call | bytes 1024 | tf_op jit(solution)/shard_map/pallas_call | solution.py:372
  180.4 2.2 %shard_map.127 = f32[3,2048,512]{2,1,0:T(8,128)} custom-call(s32[3]{0:T(128)S(1)} %pad_add_fusion.1.place, bf16[2,4,3,128,128]{4,3,2,1,0:T(8,128)(2,1)S(1)} %collective-permute-done.40.refs_0_, f32[3,2048,512]{2,1,0:T(8,128)} %shard_map.126.refs_1_), custom_call_target="tpu_custom_call", output_to_operand_aliasing={{}: (2, {})} | custom-call | bytes 1024 | tf_op jit(solution)/shard_map/pallas_call | solution.py:372
  (83 shorter events, 15.3 us)
Async XLA Ops:
  0.6 19.5 %collective-permute-start.2 = (bf16[128,2048]{1,0:T(8,128)(2,1)}, bf16[128,2048]{1,0:T(8,128)(2,1)S(1)}, u32[]{:S(2)}, u32[]{:S(2)}) collective-permute-start(bf16[128,2048]{1,0:T(8,128)(2,1)} %refs_0_.1), channel_id=1, source_target_pairs={{0,1},{1,2},{2,3},{3,0},{4,5},{5,6},{6,7},{7,4},{8,9},{9,10},{10,1... | collective-permute-start | bytes 1572872 | tf_op jit(solution)/shard_map/ppermute | solution.py:51
  3.2 17.0 %collective-permute-start.3 = (bf16[128,2048]{1,0:T(8,128)(2,1)}, bf16[128,2048]{1,0:T(8,128)(2,1)S(1)}, u32[]{:S(2)}, u32[]{:S(2)}) collective-permute-start(bf16[128,2048]{1,0:T(8,128)(2,1)} %refs_0_.1), channel_id=1, source_target_pairs={{0,3},{1,0},{2,1},{3,2},{4,7},{5,4},{6,5},{7,6},{8,11},{9,8},{10,9... | collective-permute-start | bytes 1572872 | tf_op jit(solution)/shard_map/ppermute | solution.py:51
  23.2 21.5 %collective-permute-start.4 = (bf16[2,128,2048]{2,1,0:T(8,128)(2,1)}, bf16[2,128,2048]{2,1,0:T(8,128)(2,1)S(1)}, u32[]{:S(2)}, u32[]{:S(2)}) collective-permute-start(bf16[2,128,2048]{2,1,0:T(8,128)(2,1)} %get-tuple-element.40.refs_2_), channel_id=1, source_target_pairs={{0,4},{4,0},{1,5},{5,1},{2,6},{6,2},{3,7},{7,3},{8,12},{12,8},{9,1... | collective-permute-start | bytes 3145736 | tf_op jit(solution)/shard_map/ppermute | solution.py:51
  25.6 19.1 %collective-permute-start.1 = (bf16[128,2048]{1,0:T(8,128)(2,1)}, bf16[128,2048]{1,0:T(8,128)(2,1)}, u32[]{:S(2)}, u32[]{:S(2)}) collective-permute-start(bf16[128,2048]{1,0:T(8,128)(2,1)} %refs_0_.1), channel_id=1, source_target_pairs={{0,4},{4,0},{1,5},{5,1},{2,6},{6,2},{3,7},{7,3},{8,12},{12,8},{9,1... | collective-permute-start | bytes 1572872 | tf_op jit(solution)/shard_map/ppermute | solution.py:51
  25.6 8.6 %collective-permute-start.5 = (bf16[64,2048]{1,0:T(8,128)(2,1)S(1)}, bf16[64,2048]{1,0:T(8,128)(2,1)S(1)}, u32[]{:S(2)}, u32[]{:S(2)}) collective-permute-start(bf16[64,2048]{1,0:T(8,128)(2,1)S(1)} %get-tuple-element.41), channel_id=1, source_target_pairs={{0,1},{1,2},{2,3},{3,0},{4,5},{5,6},{6,7},{7,4},{8,9},{9,10},{10,1... | collective-permute-start | bytes 786440 | tf_op jit(solution)/shard_map/ppermute | solution.py:51
  25.6 9.9 %collective-permute-start.7 = (bf16[64,2048]{1,0:T(8,128)(2,1)S(1)}, bf16[64,2048]{1,0:T(8,128)(2,1)S(1)}, u32[]{:S(2)}, u32[]{:S(2)}) collective-permute-start(bf16[64,2048]{1,0:T(8,128)(2,1)S(1)} %get-tuple-element.42), channel_id=1, source_target_pairs={{0,3},{1,0},{2,1},{3,2},{4,7},{5,4},{6,5},{7,6},{8,11},{9,8},{10,9... | collective-permute-start | bytes 786440 | tf_op jit(solution)/shard_map/ppermute | solution.py:51
  28.3 15.0 %all-to-all-start.1 = ((bf16[8,256,128]{2,1,0:T(8,128)(2,1)}), bf16[8,256,128]{2,1,0:T(8,128)(2,1)S(1)}, u32[]{:S(2)}, u32[]{:S(2)}) async-start(bf16[8,256,128]{2,1,0:T(8,128)(2,1)} %get-tuple-element.43), calls=%async_computation.1 | async-start | bytes 1048576 | tf_op jit(solution)/shard_map/all_to_all | solution.py:426
  34.2 10.5 %collective-permute-start.6 = (bf16[64,2048]{1,0:T(8,128)(2,1)S(1)}, bf16[64,2048]{1,0:T(8,128)(2,1)S(1)}, u32[]{:S(2)}, u32[]{:S(2)}) collective-permute-start(bf16[64,2048]{1,0:T(8,128)(2,1)S(1)} %collective-permute-done.5.refs_4_), channel_id=1, source_target_pairs={{0,4},{4,0},{1,5},{5,1},{2,6},{6,2},{3,7},{7,3},{8,12},{12,8},{9,1... | collective-permute-start | bytes 786440 | tf_op jit(solution)/shard_map/ppermute | solution.py:51
  35.5 9.1 %collective-permute-start.8 = (bf16[64,2048]{1,0:T(8,128)(2,1)S(1)}, bf16[64,2048]{1,0:T(8,128)(2,1)S(1)}, u32[]{:S(2)}, u32[]{:S(2)}) collective-permute-start(bf16[64,2048]{1,0:T(8,128)(2,1)S(1)} %collective-permute-done.7.refs_6_), channel_id=1, source_target_pairs={{0,4},{4,0},{1,5},{5,1},{2,6},{6,2},{3,7},{7,3},{8,12},{12,8},{9,1... | collective-permute-start | bytes 786440 | tf_op jit(solution)/shard_map/ppermute | solution.py:51
  36.3 6.3 %collective-permute-start = (f32[1]{0:T(128)}, f32[1]{0:T(128)}, u32[]{:S(2)}, u32[]{:S(2)}) collective-permute-start(f32[1]{0:T(128)} %div.6), channel_id=1, source_target_pairs={{0,4},{4,0},{1,5},{5,1},{2,6},{6,2},{3,7},{7,3},{8,12},{12,8},{9,1... | collective-permute-start | bytes 20 | tf_op jit(solution)/shard_map/ppermute | solution.py:51
  38.9 6.7 %copy-start.5 = (bf16[64,2048]{1,0:T(8,128)(2,1)S(1)}, bf16[64,2048]{1,0:T(8,128)(2,1)}, u32[]{:S(2)}) copy-start(bf16[64,2048]{1,0:T(8,128)(2,1)} %refs_9_.1) | copy-start | bytes 786436
  38.9 6.7 %copy-start.7 = (f32[2048]{0:T(1024)S(1)}, f32[2048]{0:T(1024)}, u32[]{:S(2)}) copy-start(f32[2048]{0:T(1024)} %param.14) | copy-start | bytes 24580
  58.2 1.4 collective-permute-start.9
  59.6 6.8 %collective-permute-start.10 = (f32[64,512]{1,0:T(8,128)S(1)}, f32[64,512]{1,0:T(8,128)S(1)}, u32[]{:S(2)}, u32[]{:S(2)}) collective-permute-start(f32[64,512]{1,0:T(8,128)S(1)} %add.43), channel_id=1, source_target_pairs={{0,1},{1,2},{2,3},{3,0},{4,5},{5,6},{6,7},{7,4},{8,9},{9,10},{10,1... | collective-permute-start | bytes 393224 | tf_op jit(solution)/shard_map/ppermute | solution.py:51
  59.7 10.4 %collective-permute-start.11 = (f32[64,512]{1,0:T(8,128)S(1)}, f32[64,512]{1,0:T(8,128)S(1)}, u32[]{:S(2)}, u32[]{:S(2)}) collective-permute-start(f32[64,512]{1,0:T(8,128)S(1)} %add.43), channel_id=1, source_target_pairs={{0,2},{1,3},{2,0},{3,1},{4,6},{5,7},{6,4},{7,5},{8,10},{9,11},{10,... | collective-permute-start | bytes 393224 | tf_op jit(solution)/shard_map/ppermute | solution.py:51
  64.1 6.1 %collective-permute-start.12 = (f32[64,512]{1,0:T(8,128)S(1)}, f32[64,512]{1,0:T(8,128)S(1)}, u32[]{:S(2)}, u32[]{:S(2)}) collective-permute-start(f32[64,512]{1,0:T(8,128)S(1)} %add.43), channel_id=1, source_target_pairs={{0,3},{1,0},{2,1},{3,2},{4,7},{5,4},{6,5},{7,6},{8,11},{9,8},{10,9... | collective-permute-start | bytes 393224 | tf_op jit(solution)/shard_map/ppermute | solution.py:51
  70.8 2.5 %collective-permute-start.13 = (f32[64,512]{1,0:T(8,128)S(1)}, f32[64,512]{1,0:T(8,128)S(1)}, u32[]{:S(2)}, u32[]{:S(2)}) collective-permute-start(f32[64,512]{1,0:T(8,128)S(1)} %pad_maximum_fusion.error_own), channel_id=1, source_target_pairs={{0,4},{4,0},{1,5},{5,1},{2,6},{6,2},{3,7},{7,3},{8,12},{12,8},{9,1... | collective-permute-start | bytes 393224 | tf_op jit(solution)/shard_map/ppermute | solution.py:51
  83.0 12.6 %collective-permute-start.14 = (bf16[400,512]{1,0:T(8,128)(2,1)S(1)}, bf16[400,512]{1,0:T(8,128)(2,1)S(1)}, u32[]{:S(2)}, u32[]{:S(2)}) collective-permute-start(bf16[400,512]{1,0:T(8,128)(2,1)S(1)} %get-tuple-element.54), channel_id=1, source_target_pairs={{0,8},{8,16},{16,24},{24,0},{1,9},{9,17},{17,25},{25,1},{2,10},{10... | collective-permute-start | bytes 1228808 | tf_op jit(solution)/shard_map/ppermute | solution.py:51
  83.4 13.0 %collective-permute-start.15 = (bf16[400,512]{1,0:T(8,128)(2,1)S(1)}, bf16[400,512]{1,0:T(8,128)(2,1)S(1)}, u32[]{:S(2)}, u32[]{:S(2)}) collective-permute-start(bf16[400,512]{1,0:T(8,128)(2,1)S(1)} %get-tuple-element.55), channel_id=1, source_target_pairs={{0,24},{8,0},{16,8},{24,16},{1,25},{9,1},{17,9},{25,17},{2,26},{10... | collective-permute-start | bytes 1228808 | tf_op jit(solution)/shard_map/ppermute | solution.py:51
  85.8 17.4 %collective-permute-start.16 = (bf16[400,512]{1,0:T(8,128)(2,1)}, bf16[400,512]{1,0:T(8,128)(2,1)S(1)}, u32[]{:S(2)}, u32[]{:S(2)}) collective-permute-start(bf16[400,512]{1,0:T(8,128)(2,1)} %get-tuple-element.56), channel_id=1, source_target_pairs={{0,16},{8,24},{16,0},{24,8},{1,17},{9,25},{17,1},{25,9},{2,18},{10... | collective-permute-start | bytes 1228808 | tf_op jit(solution)/shard_map/ppermute | solution.py:51
  85.8 17.4 %collective-permute-start.17 = (bf16[400,512]{1,0:T(8,128)(2,1)S(1)}, bf16[400,512]{1,0:T(8,128)(2,1)S(1)}, u32[]{:S(2)}, u32[]{:S(2)}) collective-permute-start(bf16[400,512]{1,0:T(8,128)(2,1)S(1)} %get-tuple-element.58), channel_id=1, source_target_pairs={{0,32},{32,64},{64,96},{96,0},{1,33},{33,65},{65,97},{97,1},{2,34}... | collective-permute-start | bytes 1228808 | tf_op jit(solution)/shard_map/ppermute | solution.py:51
  86.0 17.2 %collective-permute-start.18 = (bf16[400,512]{1,0:T(8,128)(2,1)}, bf16[400,512]{1,0:T(8,128)(2,1)S(1)}, u32[]{:S(2)}, u32[]{:S(2)}) collective-permute-start(bf16[400,512]{1,0:T(8,128)(2,1)} %get-tuple-element.59), channel_id=1, source_target_pairs={{0,96},{32,0},{64,32},{96,64},{1,97},{33,1},{65,33},{97,65},{2,98}... | collective-permute-start | bytes 1228808 | tf_op jit(solution)/shard_map/ppermute | solution.py:51
  95.6 8.5 %collective-permute-start.19 = (bf16[400,512]{1,0:T(8,128)(2,1)}, bf16[400,512]{1,0:T(8,128)(2,1)S(1)}, u32[]{:S(2)}, u32[]{:S(2)}) collective-permute-start(bf16[400,512]{1,0:T(8,128)(2,1)} %get-tuple-element.60), channel_id=1, source_target_pairs={{0,64},{32,96},{64,0},{96,32},{1,65},{33,97},{65,1},{97,33},{2,66}... | collective-permute-start | bytes 1228808 | tf_op jit(solution)/shard_map/ppermute | solution.py:51
  104.1 1.0 copy-start.3
  107.6 9.1 %collective-permute-start.20 = (bf16[448,128]{1,0:T(8,128)(2,1)S(1)}, bf16[448,128]{1,0:T(8,128)(2,1)S(1)}, u32[]{:S(2)}, u32[]{:S(2)}) collective-permute-start(bf16[448,128]{1,0:T(8,128)(2,1)S(1)} %get-tuple-element.62), channel_id=1, source_target_pairs={{0,32},{32,64},{64,96},{96,0},{1,33},{33,65},{65,97},{97,1},{2,34}... | collective-permute-start | bytes 344072 | tf_op jit(solution)/shard_map/ppermute | solution.py:51
  108.1 8.6 %collective-permute-start.21 = (bf16[448,128]{1,0:T(8,128)(2,1)S(1)}, bf16[448,128]{1,0:T(8,128)(2,1)S(1)}, u32[]{:S(2)}, u32[]{:S(2)}) collective-permute-start(bf16[448,128]{1,0:T(8,128)(2,1)S(1)} %get-tuple-element.63), channel_id=1, source_target_pairs={{0,96},{32,0},{64,32},{96,64},{1,97},{33,1},{65,33},{97,65},{2,98}... | collective-permute-start | bytes 344072 | tf_op jit(solution)/shard_map/ppermute | solution.py:51
  110.3 6.4 %collective-permute-start.22 = (bf16[448,128]{1,0:T(8,128)(2,1)S(1)}, bf16[448,128]{1,0:T(8,128)(2,1)S(1)}, u32[]{:S(2)}, u32[]{:S(2)}) collective-permute-start(bf16[448,128]{1,0:T(8,128)(2,1)S(1)} %get-tuple-element.64), channel_id=1, source_target_pairs={{0,64},{32,96},{64,0},{96,32},{1,65},{33,97},{65,1},{97,33},{2,66}... | collective-permute-start | bytes 344072 | tf_op jit(solution)/shard_map/ppermute | solution.py:51
  110.3 6.4 %collective-permute-start.23 = (bf16[448,128]{1,0:T(8,128)(2,1)S(1)}, bf16[448,128]{1,0:T(8,128)(2,1)S(1)}, u32[]{:S(2)}, u32[]{:S(2)}) collective-permute-start(bf16[448,128]{1,0:T(8,128)(2,1)S(1)} %get-tuple-element.66), channel_id=1, source_target_pairs={{0,8},{8,16},{16,24},{24,0},{1,9},{9,17},{17,25},{25,1},{2,10},{10... | collective-permute-start | bytes 344072 | tf_op jit(solution)/shard_map/ppermute | solution.py:51
  112.9 3.8 %collective-permute-start.24 = (bf16[448,128]{1,0:T(8,128)(2,1)S(1)}, bf16[448,128]{1,0:T(8,128)(2,1)S(1)}, u32[]{:S(2)}, u32[]{:S(2)}) collective-permute-start(bf16[448,128]{1,0:T(8,128)(2,1)S(1)} %get-tuple-element.67), channel_id=1, source_target_pairs={{0,24},{8,0},{16,8},{24,16},{1,25},{9,1},{17,9},{25,17},{2,26},{10... | collective-permute-start | bytes 344072 | tf_op jit(solution)/shard_map/ppermute | solution.py:51
  116.7 5.1 %collective-permute-start.25 = (bf16[448,128]{1,0:T(8,128)(2,1)S(1)}, bf16[448,128]{1,0:T(8,128)(2,1)S(1)}, u32[]{:S(2)}, u32[]{:S(2)}) collective-permute-start(bf16[448,128]{1,0:T(8,128)(2,1)S(1)} %get-tuple-element.68), channel_id=1, source_target_pairs={{0,16},{8,24},{16,0},{24,8},{1,17},{9,25},{17,1},{25,9},{2,18},{10... | collective-permute-start | bytes 344072 | tf_op jit(solution)/shard_map/ppermute | solution.py:51
  122.0 5.8 %collective-permute-start.26 = (bf16[3,128,128]{2,1,0:T(8,128)(2,1)S(1)}, bf16[3,128,128]{2,1,0:T(8,128)(2,1)S(1)}, u32[]{:S(2)}, u32[]{:S(2)}) collective-permute-start(bf16[3,128,128]{2,1,0:T(8,128)(2,1)S(1)} %get-tuple-element.69.refs_0_), channel_id=1, source_target_pairs={{0,32},{32,64},{64,96},{96,0},{1,33},{33,65},{65,97},{97,1},{2,34}... | collective-permute-start | bytes 294920 | tf_op jit(solution)/shard_map/ppermute | solution.py:51
  122.1 6.5 %collective-permute-start.27 = (bf16[3,128,128]{2,1,0:T(8,128)(2,1)S(1)}, bf16[3,128,128]{2,1,0:T(8,128)(2,1)S(1)}, u32[]{:S(2)}, u32[]{:S(2)}) collective-permute-start(bf16[3,128,128]{2,1,0:T(8,128)(2,1)S(1)} %get-tuple-element.69.refs_0_), channel_id=1, source_target_pairs={{0,64},{32,96},{64,0},{96,32},{1,65},{33,97},{65,1},{97,33},{2,66}... | collective-permute-start | bytes 294920 | tf_op jit(solution)/shard_map/ppermute | solution.py:51
  122.2 6.8 %collective-permute-start.28 = (bf16[3,128,128]{2,1,0:T(8,128)(2,1)S(1)}, bf16[3,128,128]{2,1,0:T(8,128)(2,1)S(1)}, u32[]{:S(2)}, u32[]{:S(2)}) collective-permute-start(bf16[3,128,128]{2,1,0:T(8,128)(2,1)S(1)} %get-tuple-element.69.refs_0_), channel_id=1, source_target_pairs={{0,96},{32,0},{64,32},{96,64},{1,97},{33,1},{65,33},{97,65},{2,98}... | collective-permute-start | bytes 294920 | tf_op jit(solution)/shard_map/ppermute | solution.py:51
  124.8 6.5 %collective-permute-start.29 = (bf16[3,128,128]{2,1,0:T(8,128)(2,1)S(1)}, bf16[3,128,128]{2,1,0:T(8,128)(2,1)S(1)}, u32[]{:S(2)}, u32[]{:S(2)}) collective-permute-start(bf16[3,128,128]{2,1,0:T(8,128)(2,1)S(1)} %get-tuple-element.70.refs_4_), channel_id=1, source_target_pairs={{0,8},{8,16},{16,24},{24,0},{1,9},{9,17},{17,25},{25,1},{2,10},{10... | collective-permute-start | bytes 294920 | tf_op jit(solution)/shard_map/ppermute | solution.py:51
  124.8 6.5 %collective-permute-start.30 = (bf16[3,128,128]{2,1,0:T(8,128)(2,1)S(1)}, bf16[3,128,128]{2,1,0:T(8,128)(2,1)S(1)}, u32[]{:S(2)}, u32[]{:S(2)}) collective-permute-start(bf16[3,128,128]{2,1,0:T(8,128)(2,1)S(1)} %get-tuple-element.70.refs_4_), channel_id=1, source_target_pairs={{0,16},{8,24},{16,0},{24,8},{1,17},{9,25},{17,1},{25,9},{2,18},{10... | collective-permute-start | bytes 294920 | tf_op jit(solution)/shard_map/ppermute | solution.py:51
  127.8 4.6 %collective-permute-start.31 = (bf16[3,128,128]{2,1,0:T(8,128)(2,1)S(1)}, bf16[3,128,128]{2,1,0:T(8,128)(2,1)S(1)}, u32[]{:S(2)}, u32[]{:S(2)}) collective-permute-start(bf16[3,128,128]{2,1,0:T(8,128)(2,1)S(1)} %get-tuple-element.70.refs_4_), channel_id=1, source_target_pairs={{0,24},{8,0},{16,8},{24,16},{1,25},{9,1},{17,9},{25,17},{2,26},{10... | collective-permute-start | bytes 294920 | tf_op jit(solution)/shard_map/ppermute | solution.py:51
  132.5 12.5 %copy-start.2 = (bf16[4,3,128,128]{3,2,1,0:T(8,128)(2,1)}, bf16[4,3,128,128]{3,2,1,0:T(8,128)(2,1)S(1)}, u32[]{:S(2)}) copy-start(bf16[4,3,128,128]{3,2,1,0:T(8,128)(2,1)S(1)} %get-tuple-element.73.refs_1_.refs_5_) | copy-start | bytes 1179652
  132.5 8.5 %collective-permute-start.34 = (bf16[4,3,128,128]{3,2,1,0:T(8,128)(2,1)S(1)}, bf16[4,3,128,128]{3,2,1,0:T(8,128)(2,1)S(1)}, u32[]{:S(2)}, u32[]{:S(2)}) collective-permute-start(bf16[4,3,128,128]{3,2,1,0:T(8,128)(2,1)S(1)} %get-tuple-element.72.refs_0_.refs_4_), channel_id=1, source_target_pairs={{0,8},{8,16},{16,24},{24,0},{1,9},{9,17},{17,25},{25,1},{2,10},{10... | collective-permute-start | bytes 1179656 | tf_op jit(solution)/shard_map/ppermute | solution.py:51
  133.4 7.6 %collective-permute-start.35 = (bf16[4,3,128,128]{3,2,1,0:T(8,128)(2,1)S(1)}, bf16[4,3,128,128]{3,2,1,0:T(8,128)(2,1)S(1)}, u32[]{:S(2)}, u32[]{:S(2)}) collective-permute-start(bf16[4,3,128,128]{3,2,1,0:T(8,128)(2,1)S(1)} %get-tuple-element.72.refs_0_.refs_4_), channel_id=1, source_target_pairs={{0,24},{8,0},{16,8},{24,16},{1,25},{9,1},{17,9},{25,17},{2,26},{10... | collective-permute-start | bytes 1179656 | tf_op jit(solution)/shard_map/ppermute | solution.py:51
  135.7 8.9 %collective-permute-start.36 = (bf16[4,3,128,128]{3,2,1,0:T(8,128)(2,1)S(1)}, bf16[4,3,128,128]{3,2,1,0:T(8,128)(2,1)S(1)}, u32[]{:S(2)}, u32[]{:S(2)}) collective-permute-start(bf16[4,3,128,128]{3,2,1,0:T(8,128)(2,1)S(1)} %get-tuple-element.73.refs_1_.refs_5_), channel_id=1, source_target_pairs={{0,32},{32,64},{64,96},{96,0},{1,33},{33,65},{65,97},{97,1},{2,34}... | collective-permute-start | bytes 1179656 | tf_op jit(solution)/shard_map/ppermute | solution.py:51
  136.2 8.9 %collective-permute-start.37 = (bf16[4,3,128,128]{3,2,1,0:T(8,128)(2,1)S(1)}, bf16[4,3,128,128]{3,2,1,0:T(8,128)(2,1)S(1)}, u32[]{:S(2)}, u32[]{:S(2)}) collective-permute-start(bf16[4,3,128,128]{3,2,1,0:T(8,128)(2,1)S(1)} %get-tuple-element.73.refs_1_.refs_5_), channel_id=1, source_target_pairs={{0,96},{32,0},{64,32},{96,64},{1,97},{33,1},{65,33},{97,65},{2,98}... | collective-permute-start | bytes 1179656 | tf_op jit(solution)/shard_map/ppermute | solution.py:51
  140.5 26.9 %copy-start.1 = (bf16[2048,64]{0,1:T(8,128)(2,1)S(1)}, bf16[2048,64]{0,1:T(8,128)(2,1)}, u32[]{:S(2)}) copy-start(bf16[2048,64]{0,1:T(8,128)(2,1)} %param.17) | copy-start | bytes 786436
  147.6 24.1 %collective-permute-start.38 = (bf16[6,4,3,128,128]{4,3,2,1,0:T(8,128)(2,1)}, bf16[6,4,3,128,128]{4,3,2,1,0:T(8,128)(2,1)S(1)}, u32[]{:S(2)}, u32[]{:S(2)}) collective-permute-start(bf16[6,4,3,128,128]{4,3,2,1,0:T(8,128)(2,1)} %shard_map.122.refs_0_), channel_id=1, source_target_pairs={{0,4},{4,0},{1,5},{5,1},{2,6},{6,2},{3,7},{7,3},{8,12},{12,8},{9,1... | collective-permute-start | bytes 7077896 | tf_op jit(solution)/shard_map/ppermute | solution.py:51
  163.2 13.9 %collective-permute-start.32 = (bf16[4,3,128,128]{3,2,1,0:T(8,128)(2,1)S(1)}, bf16[4,3,128,128]{3,2,1,0:T(8,128)(2,1)S(1)}, u32[]{:S(2)}, u32[]{:S(2)}) collective-permute-start(bf16[4,3,128,128]{3,2,1,0:T(8,128)(2,1)S(1)} %get-tuple-element.72.refs_0_.refs_4_), channel_id=1, source_target_pairs={{0,16},{8,24},{16,0},{24,8},{1,17},{9,25},{17,1},{25,9},{2,18},{10... | collective-permute-start | bytes 1179656 | tf_op jit(solution)/shard_map/ppermute | solution.py:51
  163.2 13.9 %collective-permute-start.33 = (bf16[4,3,128,128]{3,2,1,0:T(8,128)(2,1)}, bf16[4,3,128,128]{3,2,1,0:T(8,128)(2,1)S(1)}, u32[]{:S(2)}, u32[]{:S(2)}) collective-permute-start(bf16[4,3,128,128]{3,2,1,0:T(8,128)(2,1)} %copy-done.2), channel_id=1, source_target_pairs={{0,64},{32,96},{64,0},{96,32},{1,65},{33,97},{65,1},{97,33},{2,66}... | collective-permute-start | bytes 1179656 | tf_op jit(solution)/shard_map/ppermute | solution.py:51
  164.4 3.1 %collective-permute-start.39 = (bf16[256,64]{1,0:T(8,128)(2,1)S(1)}, bf16[256,64]{1,0:T(8,128)(2,1)S(1)}, u32[]{:S(2)}, u32[]{:S(2)}) collective-permute-start(bf16[256,64]{1,0:T(8,128)(2,1)S(1)} %get-tuple-element.74.refs_2_), channel_id=1, source_target_pairs={{0,4},{4,0},{1,5},{5,1},{2,6},{6,2},{3,7},{7,3},{8,12},{12,8},{9,1... | collective-permute-start | bytes 98312 | tf_op jit(solution)/shard_map/ppermute | solution.py:51
  171.7 1.4 copy-start.9
  177.1 3.3 %collective-permute-start.40 = (bf16[2,4,3,128,128]{4,3,2,1,0:T(8,128)(2,1)S(1)}, bf16[2,4,3,128,128]{4,3,2,1,0:T(8,128)(2,1)S(1)}, u32[]{:S(2)}, u32[]{:S(2)}) collective-permute-start(bf16[2,4,3,128,128]{4,3,2,1,0:T(8,128)(2,1)S(1)} %shard_map.125.refs_0_), channel_id=1, source_target_pairs={{0,4},{4,0},{1,5},{5,1},{2,6},{6,2},{3,7},{7,3},{8,12},{12,8},{9,1... | collective-permute-start | bytes 2359304 | tf_op jit(solution)/shard_map/ppermute | solution.py:51
  (6 other events, 5.1 us)

commit v3 on v2

--- a/solution.py
+++ b/solution.py
@@ -12,7 +12,7 @@
 TIMESTEPS = 1000
 UNUSED = 64.0
 NEAR = ((0, 1), (0, 3), (1, 1), (1, 3))
-PIECES = (*NEAR, (0, 2), (1, 2), (0, 0), (1, 0))
+PIECES = ((0, 2), (1, 2), (0, 1), (1, 1), (0, 3), (1, 3), (0, 0), (1, 0))
 f32 = jnp.float32
 bf16 = jnp.bfloat16
 HIGHEST = lax.Precision.HIGHEST
@@ -91,16 +91,19 @@
         store.wait()
 
 
-def sides_kernel(before, after, arrived, top, bottom, both, spread):
+def sides_kernel(time, before, after, arrived, top, bottom, both, spread):
+    column = lax.broadcasted_iota(jnp.int32, (16, 128), 1)
+    digits = jnp.where(column == 0, time[0] // 32, jnp.where(column == 1, time[0] % 32, 0))
     top[...] = before[:64]
     bottom[...] = after[64:]
     both[0] = before[...]
     both[1] = after[...]
     for k in range(8):
-        spread[k] = arrived[...]
-
-
-def fetch_kernel(place, arrived, pairs):
+        spread[k, :256] = arrived[...]
+        spread[k, 256:] = digits.astype(f32).astype(bf16)
+
+
+def fetch_kernel(place, arrived, pairs, moments):
     frame, core = place[0], place[1]
     slots = 512
 
@@ -120,7 +123,7 @@
     rows, values = [], jnp.zeros((8, slots), f32)
     for i, r in enumerate(ORDER):
         from_frame = (frame + 4 - r) % 4
-        rows.append(jnp.concatenate([arrived[from_frame], arrived[4 + from_frame]], axis=0))
+        rows.append(jnp.concatenate([arrived[from_frame, :256], arrived[4 + from_frame, :256]], axis=0))
         values = jnp.where(which // 2 == i, dot(first, rows[i], NT)[:8], values)
     mine = jnp.where((values < 32.0) & (half == clip), 1.0, 0.0)
     doubled = jnp.concatenate([mine, mine], axis=0).astype(bf16)
@@ -129,6 +132,10 @@
     for b in range(8):
         pick = jnp.where(rank[b : b + 1] == line, 1.0, 0.0).astype(bf16)
         pairs[b] = dot(pick, rows[b // 2]).astype(bf16)
+    for other in range(2):
+        digits = arrived[(core + other - 2 * core * other) * 4 + frame, 256:].astype(f32)
+        time = digits[:, 0:1] * 32.0 + digits[:, 1:2]
+        moments[other] = jnp.broadcast_to((time + 0.5) / TIMESTEPS, (16, 128))
 
 
 def lanes(i, other):
@@ -153,7 +160,7 @@
     weights.start()
     for b in range(8):
         pair = pairs[b].astype(f32)
-        t = moments[b % 2]
+        t = moments[b % 2, 0:1, :64]
         noised = ((1.0 - t) * pair[:, :64] + t * pair[:, 64:]).astype(bf16)
         added = dot(noised, w_embed[...])
         for load in loads[b]:
@@ -265,7 +272,7 @@
 def add_first_kernel(place, *refs):
     both = refs[16]
     for h in range(2):
-        parts, outs = refs[4 * h : 4 * h + 4], refs[8 + 4 * h : 12 + 4 * h]
+        parts, outs = refs[h:8:2], refs[8 + 4 * h : 12 + 4 * h]
         total = parts[0][...].astype(f32)
         for part in parts[1:]:
             total = total + part[...].astype(f32)
@@ -280,7 +287,7 @@
 def add_second_kernel(*refs):
     factor = refs[10]
     for h in range(2):
-        parts, owned = refs[4 * h : 4 * h + 4], refs[8 + h]
+        parts, owned = refs[h:8:2], refs[8 + h]
         total = parts[0][...].astype(f32)
         for part in parts[1:]:
             total = total + part[...].astype(f32)
@@ -290,11 +297,19 @@
 
 
 def line_kernel(*refs):
-    factor, lines, factor_out = refs[8], refs[9:11], refs[11]
     for h in range(2):
-        for o in range(4):
-            lines[h][o] = refs[4 * h + o][...]
-    factor_out[...] = factor[...]
+        for k, o in enumerate((2, 1, 3, 0)):
+            refs[8 + h][o] = refs[2 * k + h][...]
+
+
+def sides_join_kernel(a, b, c, d, line_x, line_y, factor, token, out):
+    for k, ref in enumerate((a, b, c, d, line_x, line_y)):
+        out[k] = ref[...]
+    out[6, 0] = jnp.zeros((3, 128, 128), bf16)
+    for k in range(2):
+        out[6, 0, k, :, :64] = factor[k * 128 : k * 128 + 128]
+    for k in range(1, 4):
+        out[6, k] = jnp.zeros((3, 128, 128), bf16)
 
 
 def join_kernel(*refs):
@@ -303,24 +318,29 @@
         out[k] = refs[k][...]
 
 
-def assemble_kernel(tags, aliased, with_out, place, *refs):
-    arrays = 1 + max(tag[0] for tag in tags)
+def assemble_kernel(tags, arrays, aliased, with_out, place, *refs):
     count = len(tags)
     sources, refs = refs[:arrays], refs[arrays + aliased :]
     if with_out:
-        factor, factor_theirs, head_t, out, grad_out, held, ready, done, sems, whole, sent, factors = refs
-        start = pl.multiple_of(place[2] * 256, 256)
-        factors[pl.ds(start, 256)] = factor[...]
-        factors[pl.ds(pl.multiple_of(256 - start, 256), 256)] = factor_theirs[...]
+        head_t, out, token, grad_out, held, ready, done, sems, whole, sent, factors = refs
+        fetched = []
+        for k, core in ((0, 1 - place[2]), (1, place[2])):
+            target = factors.at[pl.ds(core * 2, 2)]
+            fetched.append(pltpu.make_async_copy(sources[k].at[6, 0, 0:2], target, sent.at[1 + k]))
+            fetched[k].start()
     else:
-        out, held, ready, done, sems = refs
+        out, token, held, ready, done, sems = refs
+    token[...] = jnp.zeros((8, 128), f32)
     loads = []
     for k, tag in enumerate(tags):
         source = sources[tag[0]] if tag[1] is None else sources[tag[0]].at[tag[1]]
         loads.append(pltpu.make_async_copy(source, held.at[k], sems.at[k]))
         loads[-1].start()
     if with_out:
-        whole[...] = dot(factors[...], head_t[...])
+        for copy in fetched:
+            copy.wait()
+        for k in range(4):
+            whole[k * 128 : k * 128 + 128] = dot(factors[k, :, :64], head_t[...])
         leave = pltpu.make_async_copy(whole, grad_out, sent.at[0])
         leave.start()
     stores = []
@@ -353,30 +373,27 @@
 def assemble(place, arrays, tags, onto=None, product=()):
     tags = tuple(sorted(tags, key=lambda t: t[2:]))
     given = [] if onto is None else [onto]
-    out_shape = [shape((3, 2048, 512), f32)]
-    out_specs = [HBM]
+    out_shape = [shape((3, 2048, 512), f32), shape((8, 128), f32)]
+    out_specs = [HBM, VMEM]
+    dma = pltpu.SemaphoreType.DMA
     scratch = [
         pltpu.VMEM((len(tags), *arrays[0].shape[-4:]), bf16),
         pltpu.VMEM((len(tags), 3, 512, 128), f32),
-        pltpu.SemaphoreType.DMA((len(tags),)),
-        pltpu.SemaphoreType.DMA((len(tags),)),
+        dma((len(tags),)),
+        dma((len(tags),)),
     ]
     if product:
         out_shape.append(shape((512, 2048), f32))
         out_specs.append(HBM)
-        scratch += [
-            pltpu.VMEM((512, 2048), f32),
-            pltpu.SemaphoreType.DMA((1,)),
-            pltpu.VMEM((512, 64), bf16),
-        ]
+        scratch += [pltpu.VMEM((512, 2048), f32), dma((3,)), pltpu.VMEM((4, 128, 128), bf16)]
     return pl.pallas_call(
-        functools.partial(assemble_kernel, tags, len(given), bool(product)),
+        functools.partial(assemble_kernel, tags, len(arrays), len(given), bool(product)),
         in_specs=[SMEM] + [ANY] * len(arrays) + [HBM] * len(given) + [VMEM] * len(product),
         out_specs=out_specs,
         out_shape=out_shape,
         scratch_shapes=scratch,
         input_output_aliases={1 + len(arrays): 0} if given else {},
-        compiler_params=params(LARGE),
+        compiler_params=params(20),
         cost_estimate=TINY,
     )(place, *arrays, *given, *product)
 
@@ -417,16 +434,12 @@
     half_act = shape((64, 2048), bf16)
     top, bottom, sides, spread = call(
         sides_kernel,
-        near(half_act, half_act, shape((2, 128, 2048), bf16), shape((8, 256, 128), bf16)),
-        *near(before, after, arrived),
-        mib=LARGE,
+        near(half_act, half_act, shape((2, 128, 2048), bf16), shape((8, 272, 128), bf16)),
+        (SMEM, time_index), *near(before, after, arrived),
     )
     top, bottom = shift(top, "frame", 1), shift(bottom, "frame", 3)
     sides_theirs = shift(sides, "core", 1)
     arrived = lax.all_to_all(spread, ("core", "frame"), 0, 0, tiled=True)
-    moment = (time_index.astype(f32) + 0.5) / TIMESTEPS
-    moments = jnp.concatenate([moment, shift(moment, "core", 1)])
-
     head_t = w_head.T
     w_t, mix, mix_t = call(
         prepare_kernel,
@@ -441,12 +454,14 @@
         ],
         mib=LARGE,
     )
-    (pairs,) = call(fetch_kernel, near(shape((8, 128, 128), bf16)), here, *near(arrived))
+    pairs, moments = call(
+        fetch_kernel, near(shape((8, 128, 128), bf16), shape((2, 16, 128), f32)), here, *near(arrived)
+    )
     normed, proj, attended, probs, part_own, part_other = call(
         forward_kernel,
         far(shape((1024, 2048), bf16), shape((768, 1024), bf16), shape((256, 1024), bf16))
         + near(shape((4, 16, 128), f32), shape((64, 512), f32), shape((64, 512), f32)),
-        (SMEM, moments),
+        *near(moments),
         *far(act, act_theirs, sides, sides_theirs, top, shift(top, "core", 1), bottom, shift(bottom, "core", 1)),
         *near(pairs, w_embed, norm_gain.reshape(1, 2048)), *far(w_t), *near(head_t, mix_t),
         scratch=[
@@ -463,7 +478,7 @@
     )
 
     clip_part = part_own + shift(part_other, "core", 1)
-    heard = {0: clip_part, **{o: shift(clip_part, "frame", o) for o in (1, 3, 2)}}
+    heard = {0: clip_part, **{o: shift(clip_part, "frame", o) for o in (2, 1, 3)}}
     error_own = jnp.concatenate(
         [
             sum(
@@ -496,37 +511,28 @@
             pltpu.VMEM((1024, 2048), bf16),
             dma((3,)),
         ],
-        mib=LARGE,
-    )
-    moved = [[], []]
-    for (h, o), p in zip(PIECES, pieces[:6]):
-        moved[h].append(shift(p, axes[h][0], o))
-    own_x, own_y = pieces[6:]
+        mib=49,
+    )
+    moved = [shift(p, axes[h][0], o) for (h, o), p in zip(PIECES[:6], pieces)]
     second = call(
-        add_first_kernel, near(*[small] * 8), square, *near(own_x, *moved[0], own_y, *moved[1]),
+        add_first_kernel, near(*[small] * 8), square, *near(*moved, *pieces[6:]),
         scratch=[pltpu.VMEM((400, 512), bf16)],
     )
-    moved = [[shift(second[h * 4 + o], axes[h][1], o) for o in (1, 3, 2)] for h in range(2)]
+    moved = [shift(second[h * 4 + o], axes[h][1], o) for h, o in PIECES[:6]]
     *owned, factor = call(
         add_second_kernel, near(block, block, shape((256, 64), bf16)),
-        *near(second[0], *moved[0], second[4], *moved[1]),
-    )
-    back = [
-        {0: owned[h], **{o: shift(owned[h], axes[h][1], o) for o in (1, 3, 2)}} for h in range(2)
-    ]
-    line_x, line_y, factor = call(
-        line_kernel, near(line, line, shape((256, 64), bf16)),
-        *near(*(back[h][o] for h in range(2) for o in range(4)), factor),
-    )
-    factor_theirs = shift(factor, "core", 1)
+        *near(*moved, second[0], second[4]),
+    )
+    back = [shift(owned[h], axes[h][1], o) for h, o in PIECES[:6]]
+    lines = call(
+        line_kernel, near(line, line), *near(*back, *owned),
+    )
     every = (0, 1, 2, 3)
-    lines = (line_x, line_y)
+    opposite = [shift(lines[h], axes[h][0], 2) for h in range(2)]
     beside = [shift(lines[h], axes[h][0], o) for h, o in NEAR]
-    opposite = [shift(lines[h], axes[h][0], 2) for h in range(2)]
-    (grad_qkv,) = assemble(square[1], lines, [(h, None, 0, 0, h, every) for h in range(2)])
+    grad_qkv, token = assemble(square[1], lines, [(h, None, 0, 0, h, every) for h in range(2)])
     (sides,) = call(
-        join_kernel, near(shape((6, 4, 3, 128, 128), bf16)), *near(*beside, *lines), *far(grad_qkv),
-        mib=LARGE,
+        sides_join_kernel, near(shape((7, 4, 3, 128, 128), bf16)), *near(*beside, *lines, factor, token)
     )
     sides_theirs = shift(sides, "core", 1)
     side_tags = [(0, k, o, h) for k, (h, o) in enumerate((*NEAR, (0, 0), (1, 0)))]
@@ -534,16 +540,18 @@
     def tagged(tags, side):
         return [(array, k, o, side, h, every) for array, k, o, h in tags]
 
-    grad_qkv, grad_out = assemble(
-        square[1], (sides,), tagged(side_tags[:4], 0), grad_qkv, (factor, factor_theirs, head_t)
-    )
-    (grad_qkv,) = assemble(square[1], (sides_theirs,), tagged(side_tags, 1), grad_qkv)
+    grad_qkv, token = assemble(square[1], (sides,), tagged(side_tags[:4], 0), grad_qkv)
+    grad_qkv, token, grad_out = assemble(
+        square[1], (sides_theirs, sides), tagged(side_tags, 1), grad_qkv, (head_t,)
+    )
     (across,) = call(
-        join_kernel, near(shape((2, 4, 3, 128, 128), bf16)), *near(*opposite), *far(grad_qkv), mib=LARGE
+        join_kernel, near(shape((2, 4, 3, 128, 128), bf16)), *near(*opposite, token)
     )
     across_theirs = shift(across, "core", 1)
     for side, array in enumerate((across, across_theirs)):
-        (grad_qkv,) = assemble(square[1], (array,), tagged([(0, 0, 2, 0), (0, 1, 2, 1)], side), grad_qkv)
+        grad_qkv, token = assemble(
+            square[1], (array,), tagged([(0, 0, 2, 0), (0, 1, 2, 1)], side), grad_qkv
+        )
     return frame_loss, grad_qkv, grad_out
 
 

time: 184 us -> 170 us (0.924)
  blocking collectives: 13.1 us -> 0 us
  waiting for transfers between devices: 45.4 us -> 50.7 us
  local copies, waits for them, and re-layouts: 7.52 us -> 3.42 us
    all_to_all x1 -> x0, blocking collectives: 13.1 us -> none  [shards(): lax.all_to_all(sent, ('y', 'x'), 0, 0, tiled=True).reshape(256, 128)]
    all_to_all x0 -> x1, starting transfers between devices: none -> 6.75 us  [shards(): lax.all_to_all(sent, ('y', 'x'), 0, 0, tiled=True).reshape(256, 128)]
    ppermute x41 -> x39, starting transfers between devices: 59.5 us -> 52.8 us  [shift(): lax.ppermute(value, axis, [(i, (i + offset) % size) for i in range(size)])]
    all_to_all x0 -> x1, waiting for transfers between devices: none -> 5.9 us  [shards(): lax.all_to_all(sent, ('y', 'x'), 0, 0, tiled=True).reshape(256, 128)]
    pallas_call x11, Pallas kernels: 34.2 us -> 29.6 us  [call(): pl.pallas_call(kernel, in_specs=[spec for spec, _ in operands], out_specs...]
    unnamed x24 -> x16, local copies, waits for them, and re-layouts: 7.52 us -> 3.42 us
    pallas_call x5, Pallas kernels: 14.7 us -> 17.4 us  [assemble(): pl.pallas_call(functools.partial(assemble_kernel, tags, len(arrays), len(...]
    ppermute x41 -> x39, waiting for transfers between devices: 45.4 us -> 43 us  [shift(): lax.ppermute(value, axis, [(i, (i + offset) % size) for i in range(size)])]
  transfers between devices with their start and end apart: 42 -> 41, of which waited for: 18 -> 22; matrix products, arithmetic and copies ran while one was open for 0% -> 0% of each run, Pallas kernels for 10% -> 12%
where the time goes in v3:
time: 170 us; the launch traced here: 169 us
  starting transfers between devices  63.8 us (38%)
  waiting for transfers between devices  50.7 us (30%)
  Pallas kernels  47 us (28%)
  local copies, waits for them, and re-layouts  3.42 us (2%)
  between operations  3.33 us (2%)
    ppermute x39, starting transfers between devices, shift(): lax.ppermute(value, axis, [(i, (i + offset) % size) for i in range(size)])  52.8 us
    ppermute x39, waiting for transfers between devices, shift(): lax.ppermute(value, axis, [(i, (i + offset) % size) for i in range(size)])  43 us
    pallas_call x11, Pallas kernels, call(): pl.pallas_call(kernel, in_specs=[spec for spec, _ in operands], out_specs...  29.6 us
    pallas_call x5, Pallas kernels, assemble(): pl.pallas_call(functools.partial(assemble_kernel, tags, len(arrays), len(...  17.4 us
    all_to_all x1, starting transfers between devices, shards(): lax.all_to_all(sent, ('y', 'x'), 0, 0, tiled=True).reshape(256, 128)  6.75 us
    all_to_all x1, waiting for transfers between devices, shards(): lax.all_to_all(sent, ('y', 'x'), 0, 0, tiled=True).reshape(256, 128)  5.9 us
    all_to_all x1, starting transfers between devices, shards(): arrived = lax.all_to_all(spread, ('core', 'frame'), 0, 0, tiled=True)  4.25 us
    unnamed x16, local copies, waits for them, and re-layouts  3.42 us
  transfers between devices with their start and end apart: 41, of which 22 were waited for; matrix products, arithmetic and copies ran while one was open for 0% of the time, Pallas kernels for 12%

profile of v3, /device:TPU:1, one launch (start us, length us, event | category | flops | bytes accessed | tf_op | source)
XLA Modules:
  0.0 169.1 jit_solution(6346602863914357141)
XLA Ops:
  0.6 4.7 %collective-permute-start.1 = (bf16[128,2048]{1,0:T(8,128)(2,1)}, bf16[128,2048]{1,0:T(8,128)(2,1)S(1)}, u32[]{:S(2)}, u32[]{:S(2)}) collective-permute-start(bf16[128,2048]{1,0:T(8,128)(2,1)} %refs_0_.1), channel_id=1, source_target_pairs={{0,3},{1,0},{2,1},{3,2},{4,7},{5,4},{6,5},{7,6},{8,11},{9,8},{10,9... | collective-permute-start | bytes 1572872 | tf_op jit(solution)/shard_map/ppermute | solution.py:51
  7.6 6.8 %all-to-all-start = ((bf16[16,16,128]{2,1,0:T(8,128)(2,1)}), bf16[16,16,128]{2,1,0:T(8,128)(2,1)S(1)}, u32[]{:S(2)}, u32[]{:S(2)}) async-start(bf16[16,16,128]{2,1,0:T(8,128)(2,1)} %shard_map.112), calls=%async_computation | async-start | bytes 131072 | tf_op jit(solution)/shard_map/all_to_all | solution.py:433
  15.0 5.9 %all-to-all-done = bf16[16,16,128]{2,1,0:T(8,128)(2,1)S(1)} async-done(((bf16[16,16,128]{2,1,0:T(8,128)(2,1)}), bf16[16,16,128]{2,1,0:T(8,128)(2,1)S(1)}, u32[]{:S(2)}, u32[]{:S(2)}) %all-to-all-start) | async-done | bytes 65568 | tf_op jit(solution)/shard_map/all_to_all | solution.py:433
  21.9 2.4 %collective-permute-start.3 = (bf16[2,128,2048]{2,1,0:T(8,128)(2,1)S(1)}, bf16[2,128,2048]{2,1,0:T(8,128)(2,1)}, u32[]{:S(2)}, u32[]{:S(2)}) collective-permute-start(bf16[2,128,2048]{2,1,0:T(8,128)(2,1)S(1)} %get-tuple-element.49.refs_2_), channel_id=1, source_target_pairs={{0,4},{4,0},{1,5},{5,1},{2,6},{6,2},{3,7},{7,3},{8,12},{12,8},{9,1... | collective-permute-start | bytes 3145736 | tf_op jit(solution)/shard_map/ppermute | solution.py:51
  24.3 3.0 %collective-permute-start.6 = (bf16[64,2048]{1,0:T(8,128)(2,1)S(1)}, bf16[64,2048]{1,0:T(8,128)(2,1)S(1)}, u32[]{:S(2)}, u32[]{:S(2)}) collective-permute-start(bf16[64,2048]{1,0:T(8,128)(2,1)S(1)} %get-tuple-element.51), channel_id=1, source_target_pairs={{0,3},{1,0},{2,1},{3,2},{4,7},{5,4},{6,5},{7,6},{8,11},{9,8},{10,9... | collective-permute-start | bytes 786440 | tf_op jit(solution)/shard_map/ppermute | solution.py:51
  27.2 4.2 %all-to-all-start.1 = ((bf16[8,272,128]{2,1,0:T(8,128)(2,1)}), bf16[8,272,128]{2,1,0:T(8,128)(2,1)S(1)}, u32[]{:S(2)}, u32[]{:S(2)}) async-start(bf16[8,272,128]{2,1,0:T(8,128)(2,1)} %get-tuple-element.47), calls=%async_computation.1 | async-start | bytes 1114112 | tf_op jit(solution)/shard_map/all_to_all | solution.py:442
  31.5 2.0 %collective-permute-done.4.refs_4_ = bf16[64,2048]{1,0:T(8,128)(2,1)S(1)} collective-permute-done((bf16[64,2048]{1,0:T(8,128)(2,1)S(1)}, bf16[64,2048]{1,0:T(8,128)(2,1)S(1)}, u32[]{:S(2)}, u32[]{:S(2)}) %collective-permute-start.4) | collective-permute-done | bytes 262176 | tf_op jit(solution)/shard_map/ppermute | solution.py:51
  33.4 1.0 collective-permute-start.5
  35.7 3.7 %shard_map.115 = (bf16[768,2048]{1,0:T(8,128)(2,1)}, f32[256,64]{1,0:T(8,128)S(1)}, f32[64,256]{1,0:T(8,128)S(1)}) custom-call(s32[2]{0:T(128)S(1)} %pad_add_fusion.place, bf16[3,2048,512]{2,1,0:T(8,128)(2,1)} %w.1, bf16[512,2048]{1,0:T(8,128)(2,1)} %w_out.1, bf16[64,2048]{1,0:T(8,128)(2,1)S(1)} %bitcast.10), custom_call_target="tpu_custom_call" | custom-call | bytes 1024 | tf_op jit(solution)/shard_map/pallas_call | solution.py:402
  39.4 1.7 %all-to-all-done.1.arrived = bf16[8,272,128]{2,1,0:T(8,128)(2,1)S(1)} async-done(((bf16[8,272,128]{2,1,0:T(8,128)(2,1)}), bf16[8,272,128]{2,1,0:T(8,128)(2,1)S(1)}, u32[]{:S(2)}, u32[]{:S(2)}) %all-to-all-start.1) | async-done | bytes 557088 | tf_op jit(solution)/shard_map/all_to_all | solution.py:442
  41.2 1.4 shard_map.114
  42.6 12.5 %shard_map.116 = (bf16[1024,2048]{1,0:T(8,128)(2,1)}, bf16[768,1024]{1,0:T(8,128)(2,1)}, bf16[256,1024]{1,0:T(8,128)(2,1)}, f32[4,16,128]{2,1,0:T(8,128)S(1)}, f...) custom-call(f32[2,16,128]{2,1,0:T(8,128)S(1)} %get-tuple-element.48.moments, bf16[128,2048]{1,0:T(8,128)(2,1)} %refs_0_.1, ...), custom_call_target="tpu_custom_call" | custom-call | bytes 1024 | tf_op jit(solution)/shard_map/pallas_call | solution.py:402
  55.5 1.0 collective-permute-done.8
  56.6 1.7 %collective-permute-start.11 = (f32[64,512]{1,0:T(8,128)S(1)}, f32[64,512]{1,0:T(8,128)S(1)}, u32[]{:S(2)}, u32[]{:S(2)}) collective-permute-start(f32[64,512]{1,0:T(8,128)S(1)} %add.39), channel_id=1, source_target_pairs={{0,3},{1,0},{2,1},{3,2},{4,7},{5,4},{6,5},{7,6},{8,11},{9,8},{10,9... | collective-permute-start | bytes 393224 | tf_op jit(solution)/shard_map/ppermute | solution.py:51
  59.0 2.3 %collective-permute-done.11 = f32[64,512]{1,0:T(8,128)S(1)} collective-permute-done((f32[64,512]{1,0:T(8,128)S(1)}, f32[64,512]{1,0:T(8,128)S(1)}, u32[]{:S(2)}, u32[]{:S(2)}) %collective-permute-start.11) | collective-permute-done | bytes 131104 | tf_op jit(solution)/shard_map/ppermute | solution.py:51
  61.4 3.0 %collective-permute-done.10 = f32[64,512]{1,0:T(8,128)S(1)} collective-permute-done((f32[64,512]{1,0:T(8,128)S(1)}, f32[64,512]{1,0:T(8,128)S(1)}, u32[]{:S(2)}, u32[]{:S(2)}) %collective-permute-start.10) | collective-permute-done | bytes 131104 | tf_op jit(solution)/shard_map/ppermute | solution.py:51
  64.3 3.7 %collective-permute-done.9 = f32[64,512]{1,0:T(8,128)S(1)} collective-permute-done((f32[64,512]{1,0:T(8,128)S(1)}, f32[64,512]{1,0:T(8,128)S(1)}, u32[]{:S(2)}, u32[]{:S(2)}) %collective-permute-start.9) | collective-permute-done | bytes 131104 | tf_op jit(solution)/shard_map/ppermute | solution.py:51
  70.5 1.0 copy-done.3
  71.6 8.2 %shard_map.117 = (bf16[400,512]{1,0:T(8,128)(2,1)S(1)}, bf16[400,512]{1,0:T(8,128)(2,1)S(1)}, bf16[400,512]{1,0:T(8,128)(2,1)S(1)}, bf16[400,512]{1,0:T(8,128)(2...) custom-call(s32[3]{0:T(128)S(1)} %pad_add_fusion.1.place, ...), custom_call_target="tpu_custom_call" | custom-call | bytes 1024 | tf_op jit(solution)/shard_map/pallas_call | solution.py:402
  79.8 1.1 collective-permute-start.13
  80.9 2.2 %collective-permute-start.14 = (bf16[400,512]{1,0:T(8,128)(2,1)S(1)}, bf16[400,512]{1,0:T(8,128)(2,1)S(1)}, u32[]{:S(2)}, u32[]{:S(2)}) collective-permute-start(bf16[400,512]{1,0:T(8,128)(2,1)S(1)} %get-tuple-element.63), channel_id=1, source_target_pairs={{0,64},{32,96},{64,0},{96,32},{1,65},{33,97},{65,1},{97,33},{2,66}... | collective-permute-start | bytes 1228808 | tf_op jit(solution)/shard_map/ppermute | solution.py:51
  83.8 2.4 %collective-permute-start.17 = (bf16[400,512]{1,0:T(8,128)(2,1)S(1)}, bf16[400,512]{1,0:T(8,128)(2,1)S(1)}, u32[]{:S(2)}, u32[]{:S(2)}) collective-permute-start(bf16[400,512]{1,0:T(8,128)(2,1)S(1)} %get-tuple-element.66), channel_id=1, source_target_pairs={{0,24},{8,0},{16,8},{24,16},{1,25},{9,1},{17,9},{25,17},{2,26},{10... | collective-permute-start | bytes 1228808 | tf_op jit(solution)/shard_map/ppermute | solution.py:51
  86.2 5.9 %collective-permute-done.13.refs_0_ = bf16[400,512]{1,0:T(8,128)(2,1)S(1)} collective-permute-done((bf16[400,512]{1,0:T(8,128)(2,1)S(1)}, bf16[400,512]{1,0:T(8,128)(2,1)S(1)}, u32[]{:S(2)}, u32[]{:S(2)}) %collective-permute-start.13) | collective-permute-done | bytes 409632 | tf_op jit(solution)/shard_map/ppermute | solution.py:51
  92.9 8.6 %collective-permute-done.15.refs_2_ = bf16[400,512]{1,0:T(8,128)(2,1)S(1)} collective-permute-done((bf16[400,512]{1,0:T(8,128)(2,1)S(1)}, bf16[400,512]{1,0:T(8,128)(2,1)S(1)}, u32[]{:S(2)}, u32[]{:S(2)}) %collective-permute-start.15) | collective-permute-done | bytes 409632 | tf_op jit(solution)/shard_map/ppermute | solution.py:51
  101.5 1.0 collective-permute-done.16.refs_3_
  102.5 1.5 shard_map.118
  104.0 1.6 collective-permute-start.19
  105.6 1.3 collective-permute-start.20
  107.8 2.7 %collective-permute-start.23 = (bf16[448,128]{1,0:T(8,128)(2,1)S(1)}, bf16[448,128]{1,0:T(8,128)(2,1)S(1)}, u32[]{:S(2)}, u32[]{:S(2)}) collective-permute-start(bf16[448,128]{1,0:T(8,128)(2,1)S(1)} %get-tuple-element.74), channel_id=1, source_target_pairs={{0,96},{32,0},{64,32},{96,64},{1,97},{33,1},{65,33},{97,65},{2,98}... | collective-permute-start | bytes 344072 | tf_op jit(solution)/shard_map/ppermute | solution.py:51
  110.4 1.9 %collective-permute-start.24 = (bf16[448,128]{1,0:T(8,128)(2,1)S(1)}, bf16[448,128]{1,0:T(8,128)(2,1)S(1)}, u32[]{:S(2)}, u32[]{:S(2)}) collective-permute-start(bf16[448,128]{1,0:T(8,128)(2,1)S(1)} %get-tuple-element.75), channel_id=1, source_target_pairs={{0,24},{8,0},{16,8},{24,16},{1,25},{9,1},{17,9},{25,17},{2,26},{10... | collective-permute-start | bytes 344072 | tf_op jit(solution)/shard_map/ppermute | solution.py:51
  114.6 1.0 collective-permute-start.29
  116.8 2.9 %collective-permute-start.30 = (bf16[3,128,128]{2,1,0:T(8,128)(2,1)S(1)}, bf16[3,128,128]{2,1,0:T(8,128)(2,1)S(1)}, u32[]{:S(2)}, u32[]{:S(2)}) collective-permute-start(bf16[3,128,128]{2,1,0:T(8,128)(2,1)S(1)} %get-tuple-element.79.refs_7_), channel_id=1, source_target_pairs={{0,24},{8,0},{16,8},{24,16},{1,25},{9,1},{17,9},{25,17},{2,26},{10... | collective-permute-start | bytes 294920 | tf_op jit(solution)/shard_map/ppermute | solution.py:51
  119.7 1.2 collective-permute-start.26
  121.4 4.4 %collective-permute-done.28.refs_3_ = bf16[3,128,128]{2,1,0:T(8,128)(2,1)S(1)} collective-permute-done((bf16[3,128,128]{2,1,0:T(8,128)(2,1)S(1)}, bf16[3,128,128]{2,1,0:T(8,128)(2,1)S(1)}, u32[]{:S(2)}, u32[]{:S(2)}) %collective-permute-start.28) | collective-permute-done | bytes 98336 | tf_op jit(solution)/shard_map/ppermute | solution.py:51
  125.8 2.4 %collective-permute-start.34 = (bf16[4,3,128,128]{3,2,1,0:T(8,128)(2,1)S(1)}, bf16[4,3,128,128]{3,2,1,0:T(8,128)(2,1)S(1)}, u32[]{:S(2)}, u32[]{:S(2)}) collective-permute-start(bf16[4,3,128,128]{3,2,1,0:T(8,128)(2,1)S(1)} %get-tuple-element.80.refs_0_.line_x), channel_id=1, source_target_pairs={{0,24},{8,0},{16,8},{24,16},{1,25},{9,1},{17,9},{25,17},{2,26},{10... | collective-permute-start | bytes 1179656 | tf_op jit(solution)/shard_map/ppermute | solution.py:51
  128.3 1.5 collective-permute-start.36
  129.8 2.2 %shard_map.121 = (f32[3,2048,512]{2,1,0:T(8,128)}, f32[8,128]{1,0:T(8,128)S(1)}) custom-call(s32[3]{0:T(128)S(1)} %pad_add_fusion.1.place, bf16[4,3,128,128]{3,2,1,0:T(8,128)(2,1)S(1)} %get-tuple-element.80.refs_0_.line_x, bf16[4,3,128,128]{3,2,1,0:T(8,128)(2,1)S(1)} %get-tuple-element.81.refs_1_.line_y), custom_call_target="tpu_custom_call" | custom-call | bytes 1024 | tf_op jit(solution)/shard_map/pallas_call | solution.py:389
  132.0 2.1 %collective-permute-done.34.b = bf16[4,3,128,128]{3,2,1,0:T(8,128)(2,1)S(1)} collective-permute-done((bf16[4,3,128,128]{3,2,1,0:T(8,128)(2,1)S(1)}, bf16[4,3,128,128]{3,2,1,0:T(8,128)(2,1)S(1)}, u32[]{:S(2)}, u32[]{:S(2)}) %collective-permute-start.34) | collective-permute-done | bytes 393248 | tf_op jit(solution)/shard_map/ppermute | solution.py:51
  134.0 2.1 %collective-permute-done.33.a = bf16[4,3,128,128]{3,2,1,0:T(8,128)(2,1)S(1)} collective-permute-done((bf16[4,3,128,128]{3,2,1,0:T(8,128)(2,1)S(1)}, bf16[4,3,128,128]{3,2,1,0:T(8,128)(2,1)S(1)}, u32[]{:S(2)}, u32[]{:S(2)}) %collective-permute-start.33) | collective-permute-done | bytes 393248 | tf_op jit(solution)/shard_map/ppermute | solution.py:51
  136.1 1.5 collective-permute-done.35.c
  137.9 9.5 %collective-permute-start.37 = (bf16[7,4,3,128,128]{4,3,2,1,0:T(8,128)(2,1)S(1)}, bf16[7,4,3,128,128]{4,3,2,1,0:T(8,128)(2,1)S(1)}, u32[]{:S(2)}, u32[]{:S(2)}) collective-permute-start(bf16[7,4,3,128,128]{4,3,2,1,0:T(8,128)(2,1)S(1)} %shard_map.122.refs_0_.refs_1_), channel_id=1, source_target_pairs={{0,4},{4,0},{1,5},{5,1},{2,6},{6,2},{3,7},{7,3},{8,12},{12,8},{9,1... | collective-permute-start | bytes 8257544 | tf_op jit(solution)/shard_map/ppermute | solution.py:51
  147.3 1.3 collective-permute-start.31
  148.6 3.7 %shard_map.123 = (f32[3,2048,512]{2,1,0:T(8,128)}, f32[8,128]{1,0:T(8,128)}) custom-call(s32[3]{0:T(128)S(1)} %pad_add_fusion.1.place, bf16[7,4,3,128,128]{4,3,2,1,0:T(8,128)(2,1)S(1)} %shard_map.122.refs_0_.refs_1_, f32[3,2048,512]{2,1,0:T(8,128)} %get-tuple-element.84.refs_1_), custom_call_target="tpu_custom_call", output_to_operand_aliasing={{0}: (2, {})} | custom-call | bytes 1024 | tf_op jit(solution)/shard_map/pallas_call | solution.py:389
  152.3 6.1 %shard_map.124 = (f32[3,2048,512]{2,1,0:T(8,128)}, f32[8,128]{1,0:T(8,128)S(1)}, f32[512,2048]{1,0:T(8,128)}) custom-call(s32[3]{0:T(128)S(1)} %pad_add_fusion.1.place, bf16[7,4,3,128,128]{4,3,2,1,0:T(8,128)(2,1)S(1)} %collective-permute-done.37.refs_0_, ...), custom_call_target="tpu_custom_call", output_to_operand_aliasing={{0}: (3, {})} | custom-call | bytes 1024 | tf_op jit(solution)/shard_map/pallas_call | solution.py:389
  158.5 1.1 collective-permute-done.31.refs_0_
  160.5 1.3 collective-permute-start.38
  162.5 2.7 %shard_map.126 = (f32[3,2048,512]{2,1,0:T(8,128)}, f32[8,128]{1,0:T(8,128)}) custom-call(s32[3]{0:T(128)S(1)} %pad_add_fusion.1.place, bf16[2,4,3,128,128]{4,3,2,1,0:T(8,128)(2,1)S(1)} %shard_map.125.refs_0_, f32[3,2048,512]{2,1,0:T(8,128)} %get-tuple-element.87.refs_1_), custom_call_target="tpu_custom_call", output_to_operand_aliasing={{0}: (2, {})} | custom-call | bytes 1024 | tf_op jit(solution)/shard_map/pallas_call | solution.py:389
  165.2 2.7 %shard_map.127 = (f32[3,2048,512]{2,1,0:T(8,128)}, f32[8,128]{1,0:T(8,128)}) custom-call(s32[3]{0:T(128)S(1)} %pad_add_fusion.1.place, bf16[2,4,3,128,128]{4,3,2,1,0:T(8,128)(2,1)S(1)} %collective-permute-done.38.refs_0_, f32[3,2048,512]{2,1,0:T(8,128)} %get-tuple-element.88.refs_1_), custom_call_target="tpu_custom_call", output_to_operand_aliasing={{0}: (2, {})} | custom-call | bytes 1024 | tf_op jit(solution)/shard_map/pallas_call | solution.py:389
  (71 shorter events, 15.9 us)
Async XLA Ops:
  0.6 20.3 %collective-permute-start.1 = (bf16[128,2048]{1,0:T(8,128)(2,1)}, bf16[128,2048]{1,0:T(8,128)(2,1)S(1)}, u32[]{:S(2)}, u32[]{:S(2)}) collective-permute-start(bf16[128,2048]{1,0:T(8,128)(2,1)} %refs_0_.1), channel_id=1, source_target_pairs={{0,3},{1,0},{2,1},{3,2},{4,7},{5,4},{6,5},{7,6},{8,11},{9,8},{10,9... | collective-permute-start | bytes 1572872 | tf_op jit(solution)/shard_map/ppermute | solution.py:51
  5.3 15.6 %collective-permute-start = (bf16[128,2048]{1,0:T(8,128)(2,1)}, bf16[128,2048]{1,0:T(8,128)(2,1)S(1)}, u32[]{:S(2)}, u32[]{:S(2)}) collective-permute-start(bf16[128,2048]{1,0:T(8,128)(2,1)} %refs_0_.1), channel_id=1, source_target_pairs={{0,1},{1,2},{2,3},{3,0},{4,5},{5,6},{6,7},{7,4},{8,9},{9,10},{10,1... | collective-permute-start | bytes 1572872 | tf_op jit(solution)/shard_map/ppermute | solution.py:51
  5.3 0.8 copy-start.5
  7.6 13.3 %all-to-all-start = ((bf16[16,16,128]{2,1,0:T(8,128)(2,1)}), bf16[16,16,128]{2,1,0:T(8,128)(2,1)S(1)}, u32[]{:S(2)}, u32[]{:S(2)}) async-start(bf16[16,16,128]{2,1,0:T(8,128)(2,1)} %shard_map.112), calls=%async_computation | async-start | bytes 131072 | tf_op jit(solution)/shard_map/all_to_all | solution.py:433
  21.9 17.5 %copy-start.2 = (bf16[2,128,2048]{2,1,0:T(8,128)(2,1)}, bf16[2,128,2048]{2,1,0:T(8,128)(2,1)S(1)}, u32[]{:S(2)}) copy-start(bf16[2,128,2048]{2,1,0:T(8,128)(2,1)S(1)} %get-tuple-element.49.refs_2_) | copy-start | bytes 3145732
  21.9 20.7 %collective-permute-start.3 = (bf16[2,128,2048]{2,1,0:T(8,128)(2,1)S(1)}, bf16[2,128,2048]{2,1,0:T(8,128)(2,1)}, u32[]{:S(2)}, u32[]{:S(2)}) collective-permute-start(bf16[2,128,2048]{2,1,0:T(8,128)(2,1)S(1)} %get-tuple-element.49.refs_2_), channel_id=1, source_target_pairs={{0,4},{4,0},{1,5},{5,1},{2,6},{6,2},{3,7},{7,3},{8,12},{12,8},{9,1... | collective-permute-start | bytes 3145736 | tf_op jit(solution)/shard_map/ppermute | solution.py:51
  24.3 18.3 %collective-permute-start.2 = (bf16[128,2048]{1,0:T(8,128)(2,1)}, bf16[128,2048]{1,0:T(8,128)(2,1)}, u32[]{:S(2)}, u32[]{:S(2)}) collective-permute-start(bf16[128,2048]{1,0:T(8,128)(2,1)} %refs_0_.1), channel_id=1, source_target_pairs={{0,4},{4,0},{1,5},{5,1},{2,6},{6,2},{3,7},{7,3},{8,12},{12,8},{9,1... | collective-permute-start | bytes 1572872 | tf_op jit(solution)/shard_map/ppermute | solution.py:51
  24.3 9.2 %collective-permute-start.4 = (bf16[64,2048]{1,0:T(8,128)(2,1)S(1)}, bf16[64,2048]{1,0:T(8,128)(2,1)S(1)}, u32[]{:S(2)}, u32[]{:S(2)}) collective-permute-start(bf16[64,2048]{1,0:T(8,128)(2,1)S(1)} %get-tuple-element.50), channel_id=1, source_target_pairs={{0,1},{1,2},{2,3},{3,0},{4,5},{5,6},{6,7},{7,4},{8,9},{9,10},{10,1... | collective-permute-start | bytes 786440 | tf_op jit(solution)/shard_map/ppermute | solution.py:51
  24.3 10.2 %collective-permute-start.6 = (bf16[64,2048]{1,0:T(8,128)(2,1)S(1)}, bf16[64,2048]{1,0:T(8,128)(2,1)S(1)}, u32[]{:S(2)}, u32[]{:S(2)}) collective-permute-start(bf16[64,2048]{1,0:T(8,128)(2,1)S(1)} %get-tuple-element.51), channel_id=1, source_target_pairs={{0,3},{1,0},{2,1},{3,2},{4,7},{5,4},{6,5},{7,6},{8,11},{9,8},{10,9... | collective-permute-start | bytes 786440 | tf_op jit(solution)/shard_map/ppermute | solution.py:51
  27.2 14.0 %all-to-all-start.1 = ((bf16[8,272,128]{2,1,0:T(8,128)(2,1)}), bf16[8,272,128]{2,1,0:T(8,128)(2,1)S(1)}, u32[]{:S(2)}, u32[]{:S(2)}) async-start(bf16[8,272,128]{2,1,0:T(8,128)(2,1)} %get-tuple-element.47), calls=%async_computation.1 | async-start | bytes 1114112 | tf_op jit(solution)/shard_map/all_to_all | solution.py:442
  33.4 9.1 %collective-permute-start.5 = (bf16[64,2048]{1,0:T(8,128)(2,1)S(1)}, bf16[64,2048]{1,0:T(8,128)(2,1)S(1)}, u32[]{:S(2)}, u32[]{:S(2)}) collective-permute-start(bf16[64,2048]{1,0:T(8,128)(2,1)S(1)} %collective-permute-done.4.refs_4_), channel_id=1, source_target_pairs={{0,4},{4,0},{1,5},{5,1},{2,6},{6,2},{3,7},{7,3},{8,12},{12,8},{9,1... | collective-permute-start | bytes 786440 | tf_op jit(solution)/shard_map/ppermute | solution.py:51
  34.5 8.1 %collective-permute-start.7 = (bf16[64,2048]{1,0:T(8,128)(2,1)S(1)}, bf16[64,2048]{1,0:T(8,128)(2,1)S(1)}, u32[]{:S(2)}, u32[]{:S(2)}) collective-permute-start(bf16[64,2048]{1,0:T(8,128)(2,1)S(1)} %collective-permute-done.6.refs_6_), channel_id=1, source_target_pairs={{0,4},{4,0},{1,5},{5,1},{2,6},{6,2},{3,7},{7,3},{8,12},{12,8},{9,1... | collective-permute-start | bytes 786440 | tf_op jit(solution)/shard_map/ppermute | solution.py:51
  34.8 0.9 copy-start
  35.7 6.9 %copy-start.4 = (bf16[64,2048]{1,0:T(8,128)(2,1)S(1)}, bf16[64,2048]{1,0:T(8,128)(2,1)}, u32[]{:S(2)}) copy-start(bf16[64,2048]{1,0:T(8,128)(2,1)} %refs_9_.1) | copy-start | bytes 786436
  35.7 6.9 %copy-start.6 = (f32[2048]{0:T(1024)S(1)}, f32[2048]{0:T(1024)}, u32[]{:S(2)}) copy-start(f32[2048]{0:T(1024)} %param.14) | copy-start | bytes 24580
  55.1 1.4 collective-permute-start.8
  56.6 4.8 %collective-permute-start.11 = (f32[64,512]{1,0:T(8,128)S(1)}, f32[64,512]{1,0:T(8,128)S(1)}, u32[]{:S(2)}, u32[]{:S(2)}) collective-permute-start(f32[64,512]{1,0:T(8,128)S(1)} %add.39), channel_id=1, source_target_pairs={{0,3},{1,0},{2,1},{3,2},{4,7},{5,4},{6,5},{7,6},{8,11},{9,8},{10,9... | collective-permute-start | bytes 393224 | tf_op jit(solution)/shard_map/ppermute | solution.py:51
  58.3 6.0 %collective-permute-start.10 = (f32[64,512]{1,0:T(8,128)S(1)}, f32[64,512]{1,0:T(8,128)S(1)}, u32[]{:S(2)}, u32[]{:S(2)}) collective-permute-start(f32[64,512]{1,0:T(8,128)S(1)} %add.39), channel_id=1, source_target_pairs={{0,2},{1,3},{2,0},{3,1},{4,6},{5,7},{6,4},{7,5},{8,10},{9,11},{10,... | collective-permute-start | bytes 393224 | tf_op jit(solution)/shard_map/ppermute | solution.py:51
  59.0 9.0 %collective-permute-start.9 = (f32[64,512]{1,0:T(8,128)S(1)}, f32[64,512]{1,0:T(8,128)S(1)}, u32[]{:S(2)}, u32[]{:S(2)}) collective-permute-start(f32[64,512]{1,0:T(8,128)S(1)} %add.39), channel_id=1, source_target_pairs={{0,1},{1,2},{2,3},{3,0},{4,5},{5,6},{6,7},{7,4},{8,9},{9,10},{10,1... | collective-permute-start | bytes 393224 | tf_op jit(solution)/shard_map/ppermute | solution.py:51
  68.7 1.8 %collective-permute-start.12 = (f32[64,512]{1,0:T(8,128)S(1)}, f32[64,512]{1,0:T(8,128)S(1)}, u32[]{:S(2)}, u32[]{:S(2)}) collective-permute-start(f32[64,512]{1,0:T(8,128)S(1)} %pad_maximum_fusion.error_own), channel_id=1, source_target_pairs={{0,4},{4,0},{1,5},{5,1},{2,6},{6,2},{3,7},{7,3},{8,12},{12,8},{9,1... | collective-permute-start | bytes 393224 | tf_op jit(solution)/shard_map/ppermute | solution.py:51
  70.5 1.0 copy-start.3
  79.8 12.3 %collective-permute-start.13 = (bf16[400,512]{1,0:T(8,128)(2,1)S(1)}, bf16[400,512]{1,0:T(8,128)(2,1)S(1)}, u32[]{:S(2)}, u32[]{:S(2)}) collective-permute-start(bf16[400,512]{1,0:T(8,128)(2,1)S(1)} %get-tuple-element.62), channel_id=1, source_target_pairs={{0,16},{8,24},{16,0},{24,8},{1,17},{9,25},{17,1},{25,9},{2,18},{10... | collective-permute-start | bytes 1228808 | tf_op jit(solution)/shard_map/ppermute | solution.py:51
  80.9 12.1 %collective-permute-start.14 = (bf16[400,512]{1,0:T(8,128)(2,1)S(1)}, bf16[400,512]{1,0:T(8,128)(2,1)S(1)}, u32[]{:S(2)}, u32[]{:S(2)}) collective-permute-start(bf16[400,512]{1,0:T(8,128)(2,1)S(1)} %get-tuple-element.63), channel_id=1, source_target_pairs={{0,64},{32,96},{64,0},{96,32},{1,65},{33,97},{65,1},{97,33},{2,66}... | collective-permute-start | bytes 1228808 | tf_op jit(solution)/shard_map/ppermute | solution.py:51
  83.1 18.4 %collective-permute-start.15 = (bf16[400,512]{1,0:T(8,128)(2,1)S(1)}, bf16[400,512]{1,0:T(8,128)(2,1)S(1)}, u32[]{:S(2)}, u32[]{:S(2)}) collective-permute-start(bf16[400,512]{1,0:T(8,128)(2,1)S(1)} %get-tuple-element.64), channel_id=1, source_target_pairs={{0,8},{8,16},{16,24},{24,0},{1,9},{9,17},{17,25},{25,1},{2,10},{10... | collective-permute-start | bytes 1228808 | tf_op jit(solution)/shard_map/ppermute | solution.py:51
  83.4 19.1 %collective-permute-start.16 = (bf16[400,512]{1,0:T(8,128)(2,1)S(1)}, bf16[400,512]{1,0:T(8,128)(2,1)S(1)}, u32[]{:S(2)}, u32[]{:S(2)}) collective-permute-start(bf16[400,512]{1,0:T(8,128)(2,1)S(1)} %get-tuple-element.65), channel_id=1, source_target_pairs={{0,32},{32,64},{64,96},{96,0},{1,33},{33,65},{65,97},{97,1},{2,34}... | collective-permute-start | bytes 1228808 | tf_op jit(solution)/shard_map/ppermute | solution.py:51
  83.8 18.7 %collective-permute-start.17 = (bf16[400,512]{1,0:T(8,128)(2,1)S(1)}, bf16[400,512]{1,0:T(8,128)(2,1)S(1)}, u32[]{:S(2)}, u32[]{:S(2)}) collective-permute-start(bf16[400,512]{1,0:T(8,128)(2,1)S(1)} %get-tuple-element.66), channel_id=1, source_target_pairs={{0,24},{8,0},{16,8},{24,16},{1,25},{9,1},{17,9},{25,17},{2,26},{10... | collective-permute-start | bytes 1228808 | tf_op jit(solution)/shard_map/ppermute | solution.py:51
  92.1 10.5 %collective-permute-start.18 = (bf16[400,512]{1,0:T(8,128)(2,1)S(1)}, bf16[400,512]{1,0:T(8,128)(2,1)S(1)}, u32[]{:S(2)}, u32[]{:S(2)}) collective-permute-start(bf16[400,512]{1,0:T(8,128)(2,1)S(1)} %get-tuple-element.67), channel_id=1, source_target_pairs={{0,96},{32,0},{64,32},{96,64},{1,97},{33,1},{65,33},{97,65},{2,98}... | collective-permute-start | bytes 1228808 | tf_op jit(solution)/shard_map/ppermute | solution.py:51
  104.0 6.4 %collective-permute-start.19 = (bf16[448,128]{1,0:T(8,128)(2,1)S(1)}, bf16[448,128]{1,0:T(8,128)(2,1)S(1)}, u32[]{:S(2)}, u32[]{:S(2)}) collective-permute-start(bf16[448,128]{1,0:T(8,128)(2,1)S(1)} %get-tuple-element.70), channel_id=1, source_target_pairs={{0,64},{32,96},{64,0},{96,32},{1,65},{33,97},{65,1},{97,33},{2,66}... | collective-permute-start | bytes 344072 | tf_op jit(solution)/shard_map/ppermute | solution.py:51
  105.6 6.7 %collective-permute-start.20 = (bf16[448,128]{1,0:T(8,128)(2,1)S(1)}, bf16[448,128]{1,0:T(8,128)(2,1)S(1)}, u32[]{:S(2)}, u32[]{:S(2)}) collective-permute-start(bf16[448,128]{1,0:T(8,128)(2,1)S(1)} %get-tuple-element.71), channel_id=1, source_target_pairs={{0,16},{8,24},{16,0},{24,8},{1,17},{9,25},{17,1},{25,9},{2,18},{10... | collective-permute-start | bytes 344072 | tf_op jit(solution)/shard_map/ppermute | solution.py:51
  106.9 6.0 %collective-permute-start.21 = (bf16[448,128]{1,0:T(8,128)(2,1)S(1)}, bf16[448,128]{1,0:T(8,128)(2,1)S(1)}, u32[]{:S(2)}, u32[]{:S(2)}) collective-permute-start(bf16[448,128]{1,0:T(8,128)(2,1)S(1)} %get-tuple-element.72), channel_id=1, source_target_pairs={{0,32},{32,64},{64,96},{96,0},{1,33},{33,65},{65,97},{97,1},{2,34}... | collective-permute-start | bytes 344072 | tf_op jit(solution)/shard_map/ppermute | solution.py:51
  107.5 6.3 %collective-permute-start.22 = (bf16[448,128]{1,0:T(8,128)(2,1)S(1)}, bf16[448,128]{1,0:T(8,128)(2,1)S(1)}, u32[]{:S(2)}, u32[]{:S(2)}) collective-permute-start(bf16[448,128]{1,0:T(8,128)(2,1)S(1)} %get-tuple-element.73), channel_id=1, source_target_pairs={{0,8},{8,16},{16,24},{24,0},{1,9},{9,17},{17,25},{25,1},{2,10},{10... | collective-permute-start | bytes 344072 | tf_op jit(solution)/shard_map/ppermute | solution.py:51
  107.8 6.0 %collective-permute-start.23 = (bf16[448,128]{1,0:T(8,128)(2,1)S(1)}, bf16[448,128]{1,0:T(8,128)(2,1)S(1)}, u32[]{:S(2)}, u32[]{:S(2)}) collective-permute-start(bf16[448,128]{1,0:T(8,128)(2,1)S(1)} %get-tuple-element.74), channel_id=1, source_target_pairs={{0,96},{32,0},{64,32},{96,64},{1,97},{33,1},{65,33},{97,65},{2,98}... | collective-permute-start | bytes 344072 | tf_op jit(solution)/shard_map/ppermute | solution.py:51
  110.4 3.9 %collective-permute-start.24 = (bf16[448,128]{1,0:T(8,128)(2,1)S(1)}, bf16[448,128]{1,0:T(8,128)(2,1)S(1)}, u32[]{:S(2)}, u32[]{:S(2)}) collective-permute-start(bf16[448,128]{1,0:T(8,128)(2,1)S(1)} %get-tuple-element.75), channel_id=1, source_target_pairs={{0,24},{8,0},{16,8},{24,16},{1,25},{9,1},{17,9},{25,17},{2,26},{10... | collective-permute-start | bytes 344072 | tf_op jit(solution)/shard_map/ppermute | solution.py:51
  114.6 5.2 %collective-permute-start.29 = (bf16[3,128,128]{2,1,0:T(8,128)(2,1)S(1)}, bf16[3,128,128]{2,1,0:T(8,128)(2,1)S(1)}, u32[]{:S(2)}, u32[]{:S(2)}) collective-permute-start(bf16[3,128,128]{2,1,0:T(8,128)(2,1)S(1)} %get-tuple-element.78.refs_6_), channel_id=1, source_target_pairs={{0,96},{32,0},{64,32},{96,64},{1,97},{33,1},{65,33},{97,65},{2,98}... | collective-permute-start | bytes 294920 | tf_op jit(solution)/shard_map/ppermute | solution.py:51
  115.6 5.7 %collective-permute-start.27 = (bf16[3,128,128]{2,1,0:T(8,128)(2,1)S(1)}, bf16[3,128,128]{2,1,0:T(8,128)(2,1)S(1)}, u32[]{:S(2)}, u32[]{:S(2)}) collective-permute-start(bf16[3,128,128]{2,1,0:T(8,128)(2,1)S(1)} %get-tuple-element.78.refs_6_), channel_id=1, source_target_pairs={{0,32},{32,64},{64,96},{96,0},{1,33},{33,65},{65,97},{97,1},{2,34}... | collective-permute-start | bytes 294920 | tf_op jit(solution)/shard_map/ppermute | solution.py:51
  116.1 5.2 %collective-permute-start.25 = (bf16[3,128,128]{2,1,0:T(8,128)(2,1)S(1)}, bf16[3,128,128]{2,1,0:T(8,128)(2,1)S(1)}, u32[]{:S(2)}, u32[]{:S(2)}) collective-permute-start(bf16[3,128,128]{2,1,0:T(8,128)(2,1)S(1)} %get-tuple-element.78.refs_6_), channel_id=1, source_target_pairs={{0,64},{32,96},{64,0},{96,32},{1,65},{33,97},{65,1},{97,33},{2,66}... | collective-permute-start | bytes 294920 | tf_op jit(solution)/shard_map/ppermute | solution.py:51
  116.8 4.5 %collective-permute-start.30 = (bf16[3,128,128]{2,1,0:T(8,128)(2,1)S(1)}, bf16[3,128,128]{2,1,0:T(8,128)(2,1)S(1)}, u32[]{:S(2)}, u32[]{:S(2)}) collective-permute-start(bf16[3,128,128]{2,1,0:T(8,128)(2,1)S(1)} %get-tuple-element.79.refs_7_), channel_id=1, source_target_pairs={{0,24},{8,0},{16,8},{24,16},{1,25},{9,1},{17,9},{25,17},{2,26},{10... | collective-permute-start | bytes 294920 | tf_op jit(solution)/shard_map/ppermute | solution.py:51
  119.7 6.0 %collective-permute-start.28 = (bf16[3,128,128]{2,1,0:T(8,128)(2,1)S(1)}, bf16[3,128,128]{2,1,0:T(8,128)(2,1)S(1)}, u32[]{:S(2)}, u32[]{:S(2)}) collective-permute-start(bf16[3,128,128]{2,1,0:T(8,128)(2,1)S(1)} %get-tuple-element.79.refs_7_), channel_id=1, source_target_pairs={{0,8},{8,16},{16,24},{24,0},{1,9},{9,17},{17,25},{25,1},{2,10},{10... | collective-permute-start | bytes 294920 | tf_op jit(solution)/shard_map/ppermute | solution.py:51
  119.7 6.0 %collective-permute-start.26 = (bf16[3,128,128]{2,1,0:T(8,128)(2,1)S(1)}, bf16[3,128,128]{2,1,0:T(8,128)(2,1)S(1)}, u32[]{:S(2)}, u32[]{:S(2)}) collective-permute-start(bf16[3,128,128]{2,1,0:T(8,128)(2,1)S(1)} %get-tuple-element.79.refs_7_), channel_id=1, source_target_pairs={{0,16},{8,24},{16,0},{24,8},{1,17},{9,25},{17,1},{25,9},{2,18},{10... | collective-permute-start | bytes 294920 | tf_op jit(solution)/shard_map/ppermute | solution.py:51
  125.8 8.2 %collective-permute-start.34 = (bf16[4,3,128,128]{3,2,1,0:T(8,128)(2,1)S(1)}, bf16[4,3,128,128]{3,2,1,0:T(8,128)(2,1)S(1)}, u32[]{:S(2)}, u32[]{:S(2)}) collective-permute-start(bf16[4,3,128,128]{3,2,1,0:T(8,128)(2,1)S(1)} %get-tuple-element.80.refs_0_.line_x), channel_id=1, source_target_pairs={{0,24},{8,0},{16,8},{24,16},{1,25},{9,1},{17,9},{25,17},{2,26},{10... | collective-permute-start | bytes 1179656 | tf_op jit(solution)/shard_map/ppermute | solution.py:51
  128.3 7.8 %collective-permute-start.33 = (bf16[4,3,128,128]{3,2,1,0:T(8,128)(2,1)S(1)}, bf16[4,3,128,128]{3,2,1,0:T(8,128)(2,1)S(1)}, u32[]{:S(2)}, u32[]{:S(2)}) collective-permute-start(bf16[4,3,128,128]{3,2,1,0:T(8,128)(2,1)S(1)} %get-tuple-element.80.refs_0_.line_x), channel_id=1, source_target_pairs={{0,8},{8,16},{16,24},{24,0},{1,9},{9,17},{17,25},{25,1},{2,10},{10... | collective-permute-start | bytes 1179656 | tf_op jit(solution)/shard_map/ppermute | solution.py:51
  128.3 7.8 %collective-permute-start.36 = (bf16[4,3,128,128]{3,2,1,0:T(8,128)(2,1)S(1)}, bf16[4,3,128,128]{3,2,1,0:T(8,128)(2,1)S(1)}, u32[]{:S(2)}, u32[]{:S(2)}) collective-permute-start(bf16[4,3,128,128]{3,2,1,0:T(8,128)(2,1)S(1)} %get-tuple-element.81.refs_1_.line_y), channel_id=1, source_target_pairs={{0,96},{32,0},{64,32},{96,64},{1,97},{33,1},{65,33},{97,65},{2,98}... | collective-permute-start | bytes 1179656 | tf_op jit(solution)/shard_map/ppermute | solution.py:51
  129.8 7.8 %collective-permute-start.35 = (bf16[4,3,128,128]{3,2,1,0:T(8,128)(2,1)S(1)}, bf16[4,3,128,128]{3,2,1,0:T(8,128)(2,1)S(1)}, u32[]{:S(2)}, u32[]{:S(2)}) collective-permute-start(bf16[4,3,128,128]{3,2,1,0:T(8,128)(2,1)S(1)} %get-tuple-element.81.refs_1_.line_y), channel_id=1, source_target_pairs={{0,32},{32,64},{64,96},{96,0},{1,33},{33,65},{65,97},{97,1},{2,34}... | collective-permute-start | bytes 1179656 | tf_op jit(solution)/shard_map/ppermute | solution.py:51
  137.9 14.5 %collective-permute-start.37 = (bf16[7,4,3,128,128]{4,3,2,1,0:T(8,128)(2,1)S(1)}, bf16[7,4,3,128,128]{4,3,2,1,0:T(8,128)(2,1)S(1)}, u32[]{:S(2)}, u32[]{:S(2)}) collective-permute-start(bf16[7,4,3,128,128]{4,3,2,1,0:T(8,128)(2,1)S(1)} %shard_map.122.refs_0_.refs_1_), channel_id=1, source_target_pairs={{0,4},{4,0},{1,5},{5,1},{2,6},{6,2},{3,7},{7,3},{8,12},{12,8},{9,1... | collective-permute-start | bytes 8257544 | tf_op jit(solution)/shard_map/ppermute | solution.py:51
  147.3 12.2 %collective-permute-start.31 = (bf16[4,3,128,128]{3,2,1,0:T(8,128)(2,1)S(1)}, bf16[4,3,128,128]{3,2,1,0:T(8,128)(2,1)S(1)}, u32[]{:S(2)}, u32[]{:S(2)}) collective-permute-start(bf16[4,3,128,128]{3,2,1,0:T(8,128)(2,1)S(1)} %get-tuple-element.80.refs_0_.line_x), channel_id=1, source_target_pairs={{0,16},{8,24},{16,0},{24,8},{1,17},{9,25},{17,1},{25,9},{2,18},{10... | collective-permute-start | bytes 1179656 | tf_op jit(solution)/shard_map/ppermute | solution.py:51
  148.6 11.8 %collective-permute-start.32 = (bf16[4,3,128,128]{3,2,1,0:T(8,128)(2,1)S(1)}, bf16[4,3,128,128]{3,2,1,0:T(8,128)(2,1)S(1)}, u32[]{:S(2)}, u32[]{:S(2)}) collective-permute-start(bf16[4,3,128,128]{3,2,1,0:T(8,128)(2,1)S(1)} %get-tuple-element.81.refs_1_.line_y), channel_id=1, source_target_pairs={{0,64},{32,96},{64,0},{96,32},{1,65},{33,97},{65,1},{97,33},{2,66}... | collective-permute-start | bytes 1179656 | tf_op jit(solution)/shard_map/ppermute | solution.py:51
  148.6 3.7 %copy-start.1 = (bf16[2048,64]{0,1:T(8,128)(2,1)S(1)}, bf16[2048,64]{0,1:T(8,128)(2,1)}, u32[]{:S(2)}) copy-start(bf16[2048,64]{0,1:T(8,128)(2,1)} %param.17) | copy-start | bytes 786436
  160.5 4.7 %collective-permute-start.38 = (bf16[2,4,3,128,128]{4,3,2,1,0:T(8,128)(2,1)S(1)}, bf16[2,4,3,128,128]{4,3,2,1,0:T(8,128)(2,1)S(1)}, u32[]{:S(2)}, u32[]{:S(2)}) collective-permute-start(bf16[2,4,3,128,128]{4,3,2,1,0:T(8,128)(2,1)S(1)} %shard_map.125.refs_0_), channel_id=1, source_target_pairs={{0,4},{4,0},{1,5},{5,1},{2,6},{6,2},{3,7},{7,3},{8,12},{12,8},{9,1... | collective-permute-start | bytes 2359304 | tf_op jit(solution)/shard_map/ppermute | solution.py:51
  (1 other events, 0.7 us)

commit v4 on v3

--- a/solution.py
+++ b/solution.py
@@ -44,6 +44,19 @@
 
 def dot(a, b, dims=NN, precision=None):
     return lax.dot_general(a, b, dims, preferred_element_type=f32, precision=precision)
+
+
+def thirds(value):
+    high = value.astype(bf16)
+    left = value - high.astype(f32)
+    middle = left.astype(bf16)
+    return high, middle, (left - middle.astype(f32)).astype(bf16)
+
+
+def split_dot(value, exact, dims=NN):
+    rows = value.shape[0]
+    out = dot(jnp.concatenate(thirds(value), axis=0), exact, dims)
+    return out[:rows] + out[rows : 2 * rows] + out[2 * rows :]
 
 
 def shift(value, axis, offset):
@@ -170,7 +183,7 @@
         normed[b * 128 : b * 128 + 128] = (hidden * scale * gain[...]).astype(bf16)
         if b == 0:
             turned = pair.T
-            own = dot(head_t[...].astype(f32), hidden, NT, HIGHEST)
+            own = sum(dot(head_t[...], term, NT) for term in thirds(hidden))
             rest[...] = own - (turned[64:] - turned[:64])
     leave = [pltpu.make_async_copy(normed, normed_far, sems.at[1])]
     leave[0].start()
@@ -205,12 +218,11 @@
                     probs[h * 2 + other, f * 4 + g : f * 4 + g + 1] = prob[g]
     leave.append(pltpu.make_async_copy(attended, attended_far, sems.at[3]))
     leave[2].start()
+    value = split_dot(mix_t[...], attended[...])
     for other, part in ((0, part_own), (1, part_other)):
         for f in range(4):
-            value = dot(mix_t[...], attended[:, lanes(f, other)].astype(f32), NN, HIGHEST)
-            if other == 0 and f == 0:
-                value = value + rest[...]
-            part[:, f * 128 : f * 128 + 128] = value
+            added = rest[...] if other == 0 and f == 0 else 0.0
+            part[:, f * 128 : f * 128 + 128] = value[:, lanes(f, other)] + added
     for copy in leave:
         copy.wait()
 
@@ -261,9 +273,9 @@
                     row = h * 384 + j * 128
                     delta[row : row + 128, lanes(g, other)] = out.astype(bf16)
     loads[1].wait()
+    factor = split_dot(slope[...], attended[...], NT)
     for h in range(2):
-        factor = dot(slope[...], attended[h * 128 : h * 128 + 128].astype(f32), NT, HIGHEST)
-        own_factor[h] = factor.astype(bf16)
+        own_factor[h] = factor[:, h * 128 : h * 128 + 128].astype(bf16)
     loads[2].wait()
     for (h, o), out in zip(PIECES, pieces):
         gradient_piece(delta, normed, own_factor[h], h, (place[h] + o) % 4, out)
@@ -302,14 +314,14 @@
             refs[8 + h][o] = refs[2 * k + h][...]
 
 
-def sides_join_kernel(a, b, c, d, line_x, line_y, factor, token, out):
-    for k, ref in enumerate((a, b, c, d, line_x, line_y)):
+def first_join_kernel(a, b, c, line, factor, out):
+    for k, ref in enumerate((a, b, c, line)):
         out[k] = ref[...]
-    out[6, 0] = jnp.zeros((3, 128, 128), bf16)
+    out[4, 0] = jnp.zeros((3, 128, 128), bf16)
     for k in range(2):
-        out[6, 0, k, :, :64] = factor[k * 128 : k * 128 + 128]
+        out[4, 0, k, :, :64] = factor[k * 128 : k * 128 + 128]
     for k in range(1, 4):
-        out[6, k] = jnp.zeros((3, 128, 128), bf16)
+        out[4, k] = jnp.zeros((3, 128, 128), bf16)
 
 
 def join_kernel(*refs):
@@ -326,7 +338,7 @@
         fetched = []
         for k, core in ((0, 1 - place[2]), (1, place[2])):
             target = factors.at[pl.ds(core * 2, 2)]
-            fetched.append(pltpu.make_async_copy(sources[k].at[6, 0, 0:2], target, sent.at[1 + k]))
+            fetched.append(pltpu.make_async_copy(sources[k].at[4, 0, 0:2], target, sent.at[1 + k]))
             fetched[k].start()
     else:
         out, token, held, ready, done, sems = refs
@@ -528,30 +540,29 @@
         line_kernel, near(line, line), *near(*back, *owned),
     )
     every = (0, 1, 2, 3)
-    opposite = [shift(lines[h], axes[h][0], 2) for h in range(2)]
-    beside = [shift(lines[h], axes[h][0], o) for h, o in NEAR]
-    grad_qkv, token = assemble(square[1], lines, [(h, None, 0, 0, h, every) for h in range(2)])
-    (sides,) = call(
-        sides_join_kernel, near(shape((7, 4, 3, 128, 128), bf16)), *near(*beside, *lines, factor, token)
-    )
-    sides_theirs = shift(sides, "core", 1)
-    side_tags = [(0, k, o, h) for k, (h, o) in enumerate((*NEAR, (0, 0), (1, 0)))]
-
-    def tagged(tags, side):
-        return [(array, k, o, side, h, every) for array, k, o, h in tags]
-
-    grad_qkv, token = assemble(square[1], (sides,), tagged(side_tags[:4], 0), grad_qkv)
+    reach = (2, 1, 3)
+    wide = [[shift(lines[h], axes[h][0], o) for o in reach] for h in range(2)]
+    (half_x,) = call(
+        first_join_kernel, near(shape((5, 4, 3, 128, 128), bf16)),
+        *near(*wide[0], lines[0], factor),
+    )
+    half_x_theirs = shift(half_x, "core", 1)
+
+    def tagged(array, side, h, distances):
+        return [(array, k, o, side, h, every) for k, o in enumerate(distances)]
+
+    grad_qkv, token = assemble(
+        square[1], (half_x, lines[1]), tagged(0, 0, 0, (*reach, 0)) + [(1, None, 0, 0, 1, every)]
+    )
+    (half_y,) = call(
+        join_kernel, near(shape((4, 4, 3, 128, 128), bf16)), *near(*wide[1], lines[1], token)
+    )
+    half_y_theirs = shift(half_y, "core", 1)
     grad_qkv, token, grad_out = assemble(
-        square[1], (sides_theirs, sides), tagged(side_tags, 1), grad_qkv, (head_t,)
-    )
-    (across,) = call(
-        join_kernel, near(shape((2, 4, 3, 128, 128), bf16)), *near(*opposite, token)
-    )
-    across_theirs = shift(across, "core", 1)
-    for side, array in enumerate((across, across_theirs)):
-        grad_qkv, token = assemble(
-            square[1], (array,), tagged([(0, 0, 2, 0), (0, 1, 2, 1)], side), grad_qkv
-        )
+        square[1], (half_x_theirs, half_x, half_y),
+        tagged(0, 1, 0, (*reach, 0)) + tagged(2, 0, 1, reach), grad_qkv, (head_t,),
+    )
+    grad_qkv, token = assemble(square[1], (half_y_theirs,), tagged(0, 1, 1, (*reach, 0)), grad_qkv)
     return frame_loss, grad_qkv, grad_out
 
 

time: 170 us -> 169 us (level)
  Pallas kernels: 47 us -> 41.9 us
  starting transfers between devices: 63.8 us -> 67.5 us
    ppermute x39, starting transfers between devices: 52.8 us -> 56.5 us  [shift(): lax.ppermute(value, axis, [(i, (i + offset) % size) for i in range(size)])]
    pallas_call x5 -> x3, Pallas kernels: 17.4 us -> 14 us  [assemble(): pl.pallas_call(functools.partial(assemble_kernel, tags, len(arrays), len(...]
  transfers between devices with their start and end apart: 41 -> 41, of which waited for: 22 -> 19; matrix products, arithmetic and copies ran while one was open for 0% -> 0% of each run, Pallas kernels for 12% -> 10%
where the time goes in v4:
time: 169 us; the launch traced here: 168 us
  starting transfers between devices  67.5 us (40%)
  waiting for transfers between devices  50.2 us (30%)
  Pallas kernels  41.9 us (25%)
  local copies, waits for them, and re-layouts  4.36 us (3%)
  between operations  3.29 us (2%)
    ppermute x39, starting transfers between devices, shift(): lax.ppermute(value, axis, [(i, (i + offset) % size) for i in range(size)])  56.5 us
    ppermute x39, waiting for transfers between devices, shift(): lax.ppermute(value, axis, [(i, (i + offset) % size) for i in range(size)])  42.5 us
    pallas_call x11, Pallas kernels, call(): pl.pallas_call(kernel, in_specs=[spec for spec, _ in operands], out_specs...  28 us
    pallas_call x3, Pallas kernels, assemble(): pl.pallas_call(functools.partial(assemble_kernel, tags, len(arrays), len(...  14 us
    all_to_all x1, starting transfers between devices, shards(): lax.all_to_all(sent, ('y', 'x'), 0, 0, tiled=True).reshape(256, 128)  6.75 us
    all_to_all x1, waiting for transfers between devices, shards(): lax.all_to_all(sent, ('y', 'x'), 0, 0, tiled=True).reshape(256, 128)  5.9 us
    unnamed x16, local copies, waits for them, and re-layouts  4.36 us
    all_to_all x1, starting transfers between devices, shards(): arrived = lax.all_to_all(spread, ('core', 'frame'), 0, 0, tiled=True)  4.25 us
  transfers between devices with their start and end apart: 41, of which 19 were waited for; matrix products, arithmetic and copies ran while one was open for 0% of the time, Pallas kernels for 10%

profile of v4, /device:TPU:1, one launch (start us, length us, event | category | flops | bytes accessed | tf_op | source)
XLA Modules:
  0.0 168.1 jit_solution(18445017994858654496)
XLA Ops:
  0.6 4.7 %collective-permute-start.1 = (bf16[128,2048]{1,0:T(8,128)(2,1)}, bf16[128,2048]{1,0:T(8,128)(2,1)S(1)}, u32[]{:S(2)}, u32[]{:S(2)}) collective-permute-start(bf16[128,2048]{1,0:T(8,128)(2,1)} %refs_0_.1), channel_id=1, source_target_pairs={{0,3},{1,0},{2,1},{3,2},{4,7},{5,4},{6,5},{7,6},{8,11},{9,8},{10,9... | collective-permute-start | bytes 1572872 | tf_op jit(solution)/shard_map/ppermute | solution.py:64
  7.6 6.8 %all-to-all-start = ((bf16[16,16,128]{2,1,0:T(8,128)(2,1)}), bf16[16,16,128]{2,1,0:T(8,128)(2,1)S(1)}, u32[]{:S(2)}, u32[]{:S(2)}) async-start(bf16[16,16,128]{2,1,0:T(8,128)(2,1)} %shard_map.112), calls=%async_computation | async-start | bytes 131072 | tf_op jit(solution)/shard_map/all_to_all | solution.py:445
  15.0 5.9 %all-to-all-done = bf16[16,16,128]{2,1,0:T(8,128)(2,1)S(1)} async-done(((bf16[16,16,128]{2,1,0:T(8,128)(2,1)}), bf16[16,16,128]{2,1,0:T(8,128)(2,1)S(1)}, u32[]{:S(2)}, u32[]{:S(2)}) %all-to-all-start) | async-done | bytes 65568 | tf_op jit(solution)/shard_map/all_to_all | solution.py:445
  20.9 1.0 shard_map.113
  21.9 2.4 %collective-permute-start.3 = (bf16[2,128,2048]{2,1,0:T(8,128)(2,1)S(1)}, bf16[2,128,2048]{2,1,0:T(8,128)(2,1)}, u32[]{:S(2)}, u32[]{:S(2)}) collective-permute-start(bf16[2,128,2048]{2,1,0:T(8,128)(2,1)S(1)} %get-tuple-element.46.refs_2_), channel_id=1, source_target_pairs={{0,4},{4,0},{1,5},{5,1},{2,6},{6,2},{3,7},{7,3},{8,12},{12,8},{9,1... | collective-permute-start | bytes 3145736 | tf_op jit(solution)/shard_map/ppermute | solution.py:64
  24.3 3.0 %collective-permute-start.6 = (bf16[64,2048]{1,0:T(8,128)(2,1)S(1)}, bf16[64,2048]{1,0:T(8,128)(2,1)S(1)}, u32[]{:S(2)}, u32[]{:S(2)}) collective-permute-start(bf16[64,2048]{1,0:T(8,128)(2,1)S(1)} %get-tuple-element.48), channel_id=1, source_target_pairs={{0,3},{1,0},{2,1},{3,2},{4,7},{5,4},{6,5},{7,6},{8,11},{9,8},{10,9... | collective-permute-start | bytes 786440 | tf_op jit(solution)/shard_map/ppermute | solution.py:64
  27.2 4.2 %all-to-all-start.1 = ((bf16[8,272,128]{2,1,0:T(8,128)(2,1)}), bf16[8,272,128]{2,1,0:T(8,128)(2,1)S(1)}, u32[]{:S(2)}, u32[]{:S(2)}) async-start(bf16[8,272,128]{2,1,0:T(8,128)(2,1)} %get-tuple-element.44), calls=%async_computation.1 | async-start | bytes 1114112 | tf_op jit(solution)/shard_map/all_to_all | solution.py:454
  31.5 2.0 %collective-permute-done.4.refs_4_ = bf16[64,2048]{1,0:T(8,128)(2,1)S(1)} collective-permute-done((bf16[64,2048]{1,0:T(8,128)(2,1)S(1)}, bf16[64,2048]{1,0:T(8,128)(2,1)S(1)}, u32[]{:S(2)}, u32[]{:S(2)}) %collective-permute-start.4) | collective-permute-done | bytes 262176 | tf_op jit(solution)/shard_map/ppermute | solution.py:64
  33.4 1.0 collective-permute-start.5
  34.8 0.9 copy-done
  35.7 3.7 %shard_map.115 = (bf16[768,2048]{1,0:T(8,128)(2,1)}, f32[256,64]{1,0:T(8,128)S(1)}, f32[64,256]{1,0:T(8,128)S(1)}) custom-call(s32[2]{0:T(128)S(1)} %pad_add_fusion.place, bf16[3,2048,512]{2,1,0:T(8,128)(2,1)} %w.1, bf16[512,2048]{1,0:T(8,128)(2,1)} %w_out.1, bf16[64,2048]{1,0:T(8,128)(2,1)S(1)} %bitcast.10), custom_call_target="tpu_custom_call" | custom-call | bytes 1024 | tf_op jit(solution)/shard_map/pallas_call | solution.py:414
  39.4 1.7 %all-to-all-done.1.arrived = bf16[8,272,128]{2,1,0:T(8,128)(2,1)S(1)} async-done(((bf16[8,272,128]{2,1,0:T(8,128)(2,1)}), bf16[8,272,128]{2,1,0:T(8,128)(2,1)S(1)}, u32[]{:S(2)}, u32[]{:S(2)}) %all-to-all-start.1) | async-done | bytes 557088 | tf_op jit(solution)/shard_map/all_to_all | solution.py:454
  41.2 1.4 shard_map.114
  42.6 11.5 %shard_map.116 = (bf16[1024,2048]{1,0:T(8,128)(2,1)}, bf16[768,1024]{1,0:T(8,128)(2,1)}, bf16[256,1024]{1,0:T(8,128)(2,1)}, f32[4,16,128]{2,1,0:T(8,128)S(1)}, f...) custom-call(f32[2,16,128]{2,1,0:T(8,128)S(1)} %get-tuple-element.45.moments, bf16[128,2048]{1,0:T(8,128)(2,1)} %refs_0_.1, ...), custom_call_target="tpu_custom_call" | custom-call | bytes 1024 | tf_op jit(solution)/shard_map/pallas_call | solution.py:414
  54.6 1.0 collective-permute-done.8
  55.6 1.7 %collective-permute-start.11 = (f32[64,512]{1,0:T(8,128)S(1)}, f32[64,512]{1,0:T(8,128)S(1)}, u32[]{:S(2)}, u32[]{:S(2)}) collective-permute-start(f32[64,512]{1,0:T(8,128)S(1)} %add.39), channel_id=1, source_target_pairs={{0,3},{1,0},{2,1},{3,2},{4,7},{5,4},{6,5},{7,6},{8,11},{9,8},{10,9... | collective-permute-start | bytes 393224 | tf_op jit(solution)/shard_map/ppermute | solution.py:64
  58.0 2.3 %collective-permute-done.11 = f32[64,512]{1,0:T(8,128)S(1)} collective-permute-done((f32[64,512]{1,0:T(8,128)S(1)}, f32[64,512]{1,0:T(8,128)S(1)}, u32[]{:S(2)}, u32[]{:S(2)}) %collective-permute-start.11) | collective-permute-done | bytes 131104 | tf_op jit(solution)/shard_map/ppermute | solution.py:64
  60.4 3.0 %collective-permute-done.10 = f32[64,512]{1,0:T(8,128)S(1)} collective-permute-done((f32[64,512]{1,0:T(8,128)S(1)}, f32[64,512]{1,0:T(8,128)S(1)}, u32[]{:S(2)}, u32[]{:S(2)}) %collective-permute-start.10) | collective-permute-done | bytes 131104 | tf_op jit(solution)/shard_map/ppermute | solution.py:64
  63.4 3.7 %collective-permute-done.9 = f32[64,512]{1,0:T(8,128)S(1)} collective-permute-done((f32[64,512]{1,0:T(8,128)S(1)}, f32[64,512]{1,0:T(8,128)S(1)}, u32[]{:S(2)}, u32[]{:S(2)}) %collective-permute-start.9) | collective-permute-done | bytes 131104 | tf_op jit(solution)/shard_map/ppermute | solution.py:64
  69.6 1.0 copy-done.3
  70.6 7.5 %shard_map.117 = (bf16[400,512]{1,0:T(8,128)(2,1)S(1)}, bf16[400,512]{1,0:T(8,128)(2,1)S(1)}, bf16[400,512]{1,0:T(8,128)(2,1)S(1)}, bf16[400,512]{1,0:T(8,128)(2...) custom-call(s32[3]{0:T(128)S(1)} %pad_add_fusion.1.place, ...), custom_call_target="tpu_custom_call" | custom-call | bytes 1024 | tf_op jit(solution)/shard_map/pallas_call | solution.py:414
  78.1 1.1 collective-permute-start.13
  79.3 2.2 %collective-permute-start.14 = (bf16[400,512]{1,0:T(8,128)(2,1)S(1)}, bf16[400,512]{1,0:T(8,128)(2,1)S(1)}, u32[]{:S(2)}, u32[]{:S(2)}) collective-permute-start(bf16[400,512]{1,0:T(8,128)(2,1)S(1)} %get-tuple-element.60), channel_id=1, source_target_pairs={{0,64},{32,96},{64,0},{96,32},{1,65},{33,97},{65,1},{97,33},{2,66}... | collective-permute-start | bytes 1228808 | tf_op jit(solution)/shard_map/ppermute | solution.py:64
  82.2 2.4 %collective-permute-start.17 = (bf16[400,512]{1,0:T(8,128)(2,1)S(1)}, bf16[400,512]{1,0:T(8,128)(2,1)S(1)}, u32[]{:S(2)}, u32[]{:S(2)}) collective-permute-start(bf16[400,512]{1,0:T(8,128)(2,1)S(1)} %get-tuple-element.63), channel_id=1, source_target_pairs={{0,24},{8,0},{16,8},{24,16},{1,25},{9,1},{17,9},{25,17},{2,26},{10... | collective-permute-start | bytes 1228808 | tf_op jit(solution)/shard_map/ppermute | solution.py:64
  84.6 5.9 %collective-permute-done.13.refs_0_ = bf16[400,512]{1,0:T(8,128)(2,1)S(1)} collective-permute-done((bf16[400,512]{1,0:T(8,128)(2,1)S(1)}, bf16[400,512]{1,0:T(8,128)(2,1)S(1)}, u32[]{:S(2)}, u32[]{:S(2)}) %collective-permute-start.13) | collective-permute-done | bytes 409632 | tf_op jit(solution)/shard_map/ppermute | solution.py:64
  91.3 8.6 %collective-permute-done.15.refs_2_ = bf16[400,512]{1,0:T(8,128)(2,1)S(1)} collective-permute-done((bf16[400,512]{1,0:T(8,128)(2,1)S(1)}, bf16[400,512]{1,0:T(8,128)(2,1)S(1)}, u32[]{:S(2)}, u32[]{:S(2)}) %collective-permute-start.15) | collective-permute-done | bytes 409632 | tf_op jit(solution)/shard_map/ppermute | solution.py:64
  99.9 1.0 collective-permute-done.16.refs_3_
  100.9 1.5 shard_map.118
  102.4 1.6 collective-permute-start.19
  104.0 1.3 collective-permute-start.20
  106.2 2.6 %collective-permute-start.23 = (bf16[448,128]{1,0:T(8,128)(2,1)S(1)}, bf16[448,128]{1,0:T(8,128)(2,1)S(1)}, u32[]{:S(2)}, u32[]{:S(2)}) collective-permute-start(bf16[448,128]{1,0:T(8,128)(2,1)S(1)} %get-tuple-element.71), channel_id=1, source_target_pairs={{0,96},{32,0},{64,32},{96,64},{1,97},{33,1},{65,33},{97,65},{2,98}... | collective-permute-start | bytes 344072 | tf_op jit(solution)/shard_map/ppermute | solution.py:64
  108.8 1.9 %collective-permute-start.24 = (bf16[448,128]{1,0:T(8,128)(2,1)S(1)}, bf16[448,128]{1,0:T(8,128)(2,1)S(1)}, u32[]{:S(2)}, u32[]{:S(2)}) collective-permute-start(bf16[448,128]{1,0:T(8,128)(2,1)S(1)} %get-tuple-element.72), channel_id=1, source_target_pairs={{0,24},{8,0},{16,8},{24,16},{1,25},{9,1},{17,9},{25,17},{2,26},{10... | collective-permute-start | bytes 344072 | tf_op jit(solution)/shard_map/ppermute | solution.py:64
  112.9 1.0 collective-permute-start.29
  115.2 2.9 %collective-permute-start.30 = (bf16[3,128,128]{2,1,0:T(8,128)(2,1)S(1)}, bf16[3,128,128]{2,1,0:T(8,128)(2,1)S(1)}, u32[]{:S(2)}, u32[]{:S(2)}) collective-permute-start(bf16[3,128,128]{2,1,0:T(8,128)(2,1)S(1)} %get-tuple-element.76.refs_7_), channel_id=1, source_target_pairs={{0,24},{8,0},{16,8},{24,16},{1,25},{9,1},{17,9},{25,17},{2,26},{10... | collective-permute-start | bytes 294920 | tf_op jit(solution)/shard_map/ppermute | solution.py:64
  118.1 1.2 collective-permute-start.26
  119.8 4.4 %collective-permute-done.28.refs_3_ = bf16[3,128,128]{2,1,0:T(8,128)(2,1)S(1)} collective-permute-done((bf16[3,128,128]{2,1,0:T(8,128)(2,1)S(1)}, bf16[3,128,128]{2,1,0:T(8,128)(2,1)S(1)}, u32[]{:S(2)}, u32[]{:S(2)}) %collective-permute-start.28) | collective-permute-done | bytes 98336 | tf_op jit(solution)/shard_map/ppermute | solution.py:64
  124.2 2.4 %collective-permute-start.36 = (bf16[4,3,128,128]{3,2,1,0:T(8,128)(2,1)S(1)}, bf16[4,3,128,128]{3,2,1,0:T(8,128)(2,1)S(1)}, u32[]{:S(2)}, u32[]{:S(2)}) collective-permute-start(bf16[4,3,128,128]{3,2,1,0:T(8,128)(2,1)S(1)} %get-tuple-element.78.line), channel_id=1, source_target_pairs={{0,24},{8,0},{16,8},{24,16},{1,25},{9,1},{17,9},{25,17},{2,26},{10... | collective-permute-start | bytes 1179656 | tf_op jit(solution)/shard_map/ppermute | solution.py:64
  126.6 1.3 collective-permute-start.34
  127.9 1.6 collective-permute-start.33
  129.4 5.1 %collective-permute-done.36.c = bf16[4,3,128,128]{3,2,1,0:T(8,128)(2,1)S(1)} collective-permute-done((bf16[4,3,128,128]{3,2,1,0:T(8,128)(2,1)S(1)}, bf16[4,3,128,128]{3,2,1,0:T(8,128)(2,1)S(1)}, u32[]{:S(2)}, u32[]{:S(2)}) %collective-permute-start.36) | collective-permute-done | bytes 393248 | tf_op jit(solution)/shard_map/ppermute | solution.py:64
  134.5 2.8 %collective-permute-start.31 = (bf16[4,3,128,128]{3,2,1,0:T(8,128)(2,1)S(1)}, bf16[4,3,128,128]{3,2,1,0:T(8,128)(2,1)S(1)}, u32[]{:S(2)}, u32[]{:S(2)}) collective-permute-start(bf16[4,3,128,128]{3,2,1,0:T(8,128)(2,1)S(1)} %get-tuple-element.77.refs_1_.refs_3_), channel_id=1, source_target_pairs={{0,64},{32,96},{64,0},{96,32},{1,65},{33,97},{65,1},{97,33},{2,66}... | collective-permute-start | bytes 1179656 | tf_op jit(solution)/shard_map/ppermute | solution.py:64
  137.3 2.1 %collective-permute-done.35.b = bf16[4,3,128,128]{3,2,1,0:T(8,128)(2,1)S(1)} collective-permute-done((bf16[4,3,128,128]{3,2,1,0:T(8,128)(2,1)S(1)}, bf16[4,3,128,128]{3,2,1,0:T(8,128)(2,1)S(1)}, u32[]{:S(2)}, u32[]{:S(2)}) %collective-permute-start.35) | collective-permute-done | bytes 393248 | tf_op jit(solution)/shard_map/ppermute | solution.py:64
  139.6 8.4 %collective-permute-start.38 = (bf16[5,4,3,128,128]{4,3,2,1,0:T(8,128)(2,1)S(1)}, bf16[5,4,3,128,128]{4,3,2,1,0:T(8,128)(2,1)}, u32[]{:S(2)}, u32[]{:S(2)}) collective-permute-start(bf16[5,4,3,128,128]{4,3,2,1,0:T(8,128)(2,1)S(1)} %shard_map.121.refs_0_.refs_1_), channel_id=1, source_target_pairs={{0,4},{4,0},{1,5},{5,1},{2,6},{6,2},{3,7},{7,3},{8,12},{12,8},{9,1... | collective-permute-start | bytes 5898248 | tf_op jit(solution)/shard_map/ppermute | solution.py:64
  148.0 3.5 %shard_map.122 = (f32[3,2048,512]{2,1,0:T(8,128)}, f32[8,128]{1,0:T(8,128)S(1)}) custom-call(s32[3]{0:T(128)S(1)} %pad_add_fusion.1.place, bf16[5,4,3,128,128]{4,3,2,1,0:T(8,128)(2,1)S(1)} %shard_map.121.refs_0_.refs_1_, bf16[4,3,128,128]{3,2,1,0:T(8,128)(2,1)S(1)} %get-tuple-element.77.refs_1_.refs_3_), custom_call_target="tpu_custom_call" | custom-call | bytes 1024 | tf_op jit(solution)/shard_map/pallas_call | solution.py:401
  151.7 3.2 %collective-permute-start.37 = (bf16[4,4,3,128,128]{4,3,2,1,0:T(8,128)(2,1)S(1)}, bf16[4,4,3,128,128]{4,3,2,1,0:T(8,128)(2,1)}, u32[]{:S(2)}, u32[]{:S(2)}) collective-permute-start(bf16[4,4,3,128,128]{4,3,2,1,0:T(8,128)(2,1)S(1)} %shard_map.123.refs_2_), channel_id=1, source_target_pairs={{0,4},{4,0},{1,5},{5,1},{2,6},{6,2},{3,7},{7,3},{8,12},{12,8},{9,1... | collective-permute-start | bytes 4718600 | tf_op jit(solution)/shard_map/ppermute | solution.py:64
  155.6 0.9 copy-done.1
  156.5 6.5 %shard_map.124 = (f32[3,2048,512]{2,1,0:T(8,128)}, f32[8,128]{1,0:T(8,128)}, f32[512,2048]{1,0:T(8,128)}) custom-call(s32[3]{0:T(128)S(1)} %pad_add_fusion.1.place, bf16[5,4,3,128,128]{4,3,2,1,0:T(8,128)(2,1)} %collective-permute-done.38.refs_0_, bf16[5,4,3,128,128]{4,3,2,1,0:T(8,128)(2,1)S(1)} %shard_map.121.refs_0_.refs_1_, ...), custom_call_target="tpu_custom_call", output_to_operand_aliasing={{0}: (4, {})} | custom-call | bytes 1024 | tf_op jit(solution)/shard_map/pallas_call | solution.py:401
  163.0 3.9 %shard_map.125 = (f32[3,2048,512]{2,1,0:T(8,128)}, f32[8,128]{1,0:T(8,128)}) custom-call(s32[3]{0:T(128)S(1)} %pad_add_fusion.1.place, bf16[4,4,3,128,128]{4,3,2,1,0:T(8,128)(2,1)} %collective-permute-done.37.refs_0_, f32[3,2048,512]{2,1,0:T(8,128)} %get-tuple-element.82.refs_1_), custom_call_target="tpu_custom_call", output_to_operand_aliasing={{0}: (2, {})} | custom-call | bytes 1024 | tf_op jit(solution)/shard_map/pallas_call | solution.py:401
  (69 shorter events, 13.1 us)
Async XLA Ops:
  0.6 20.3 %collective-permute-start.1 = (bf16[128,2048]{1,0:T(8,128)(2,1)}, bf16[128,2048]{1,0:T(8,128)(2,1)S(1)}, u32[]{:S(2)}, u32[]{:S(2)}) collective-permute-start(bf16[128,2048]{1,0:T(8,128)(2,1)} %refs_0_.1), channel_id=1, source_target_pairs={{0,3},{1,0},{2,1},{3,2},{4,7},{5,4},{6,5},{7,6},{8,11},{9,8},{10,9... | collective-permute-start | bytes 1572872 | tf_op jit(solution)/shard_map/ppermute | solution.py:64
  5.3 15.6 %collective-permute-start = (bf16[128,2048]{1,0:T(8,128)(2,1)}, bf16[128,2048]{1,0:T(8,128)(2,1)S(1)}, u32[]{:S(2)}, u32[]{:S(2)}) collective-permute-start(bf16[128,2048]{1,0:T(8,128)(2,1)} %refs_0_.1), channel_id=1, source_target_pairs={{0,1},{1,2},{2,3},{3,0},{4,5},{5,6},{6,7},{7,4},{8,9},{9,10},{10,1... | collective-permute-start | bytes 1572872 | tf_op jit(solution)/shard_map/ppermute | solution.py:64
  5.3 0.8 copy-start.5
  7.6 13.3 %all-to-all-start = ((bf16[16,16,128]{2,1,0:T(8,128)(2,1)}), bf16[16,16,128]{2,1,0:T(8,128)(2,1)S(1)}, u32[]{:S(2)}, u32[]{:S(2)}) async-start(bf16[16,16,128]{2,1,0:T(8,128)(2,1)} %shard_map.112), calls=%async_computation | async-start | bytes 131072 | tf_op jit(solution)/shard_map/all_to_all | solution.py:445
  21.9 17.5 %copy-start.2 = (bf16[2,128,2048]{2,1,0:T(8,128)(2,1)}, bf16[2,128,2048]{2,1,0:T(8,128)(2,1)S(1)}, u32[]{:S(2)}) copy-start(bf16[2,128,2048]{2,1,0:T(8,128)(2,1)S(1)} %get-tuple-element.46.refs_2_) | copy-start | bytes 3145732
  21.9 20.7 %collective-permute-start.3 = (bf16[2,128,2048]{2,1,0:T(8,128)(2,1)S(1)}, bf16[2,128,2048]{2,1,0:T(8,128)(2,1)}, u32[]{:S(2)}, u32[]{:S(2)}) collective-permute-start(bf16[2,128,2048]{2,1,0:T(8,128)(2,1)S(1)} %get-tuple-element.46.refs_2_), channel_id=1, source_target_pairs={{0,4},{4,0},{1,5},{5,1},{2,6},{6,2},{3,7},{7,3},{8,12},{12,8},{9,1... | collective-permute-start | bytes 3145736 | tf_op jit(solution)/shard_map/ppermute | solution.py:64
  24.3 18.3 %collective-permute-start.2 = (bf16[128,2048]{1,0:T(8,128)(2,1)}, bf16[128,2048]{1,0:T(8,128)(2,1)}, u32[]{:S(2)}, u32[]{:S(2)}) collective-permute-start(bf16[128,2048]{1,0:T(8,128)(2,1)} %refs_0_.1), channel_id=1, source_target_pairs={{0,4},{4,0},{1,5},{5,1},{2,6},{6,2},{3,7},{7,3},{8,12},{12,8},{9,1... | collective-permute-start | bytes 1572872 | tf_op jit(solution)/shard_map/ppermute | solution.py:64
  24.3 9.2 %collective-permute-start.4 = (bf16[64,2048]{1,0:T(8,128)(2,1)S(1)}, bf16[64,2048]{1,0:T(8,128)(2,1)S(1)}, u32[]{:S(2)}, u32[]{:S(2)}) collective-permute-start(bf16[64,2048]{1,0:T(8,128)(2,1)S(1)} %get-tuple-element.47), channel_id=1, source_target_pairs={{0,1},{1,2},{2,3},{3,0},{4,5},{5,6},{6,7},{7,4},{8,9},{9,10},{10,1... | collective-permute-start | bytes 786440 | tf_op jit(solution)/shard_map/ppermute | solution.py:64
  24.3 10.2 %collective-permute-start.6 = (bf16[64,2048]{1,0:T(8,128)(2,1)S(1)}, bf16[64,2048]{1,0:T(8,128)(2,1)S(1)}, u32[]{:S(2)}, u32[]{:S(2)}) collective-permute-start(bf16[64,2048]{1,0:T(8,128)(2,1)S(1)} %get-tuple-element.48), channel_id=1, source_target_pairs={{0,3},{1,0},{2,1},{3,2},{4,7},{5,4},{6,5},{7,6},{8,11},{9,8},{10,9... | collective-permute-start | bytes 786440 | tf_op jit(solution)/shard_map/ppermute | solution.py:64
  27.2 14.0 %all-to-all-start.1 = ((bf16[8,272,128]{2,1,0:T(8,128)(2,1)}), bf16[8,272,128]{2,1,0:T(8,128)(2,1)S(1)}, u32[]{:S(2)}, u32[]{:S(2)}) async-start(bf16[8,272,128]{2,1,0:T(8,128)(2,1)} %get-tuple-element.44), calls=%async_computation.1 | async-start | bytes 1114112 | tf_op jit(solution)/shard_map/all_to_all | solution.py:454
  33.4 9.1 %collective-permute-start.5 = (bf16[64,2048]{1,0:T(8,128)(2,1)S(1)}, bf16[64,2048]{1,0:T(8,128)(2,1)S(1)}, u32[]{:S(2)}, u32[]{:S(2)}) collective-permute-start(bf16[64,2048]{1,0:T(8,128)(2,1)S(1)} %collective-permute-done.4.refs_4_), channel_id=1, source_target_pairs={{0,4},{4,0},{1,5},{5,1},{2,6},{6,2},{3,7},{7,3},{8,12},{12,8},{9,1... | collective-permute-start | bytes 786440 | tf_op jit(solution)/shard_map/ppermute | solution.py:64
  34.5 8.1 %collective-permute-start.7 = (bf16[64,2048]{1,0:T(8,128)(2,1)S(1)}, bf16[64,2048]{1,0:T(8,128)(2,1)S(1)}, u32[]{:S(2)}, u32[]{:S(2)}) collective-permute-start(bf16[64,2048]{1,0:T(8,128)(2,1)S(1)} %collective-permute-done.6.refs_6_), channel_id=1, source_target_pairs={{0,4},{4,0},{1,5},{5,1},{2,6},{6,2},{3,7},{7,3},{8,12},{12,8},{9,1... | collective-permute-start | bytes 786440 | tf_op jit(solution)/shard_map/ppermute | solution.py:64
  34.8 0.9 copy-start
  35.7 6.9 %copy-start.4 = (bf16[64,2048]{1,0:T(8,128)(2,1)S(1)}, bf16[64,2048]{1,0:T(8,128)(2,1)}, u32[]{:S(2)}) copy-start(bf16[64,2048]{1,0:T(8,128)(2,1)} %refs_9_.1) | copy-start | bytes 786436
  35.7 6.9 %copy-start.6 = (f32[2048]{0:T(1024)S(1)}, f32[2048]{0:T(1024)}, u32[]{:S(2)}) copy-start(f32[2048]{0:T(1024)} %param.14) | copy-start | bytes 24580
  54.1 1.4 collective-permute-start.8
  55.6 4.8 %collective-permute-start.11 = (f32[64,512]{1,0:T(8,128)S(1)}, f32[64,512]{1,0:T(8,128)S(1)}, u32[]{:S(2)}, u32[]{:S(2)}) collective-permute-start(f32[64,512]{1,0:T(8,128)S(1)} %add.39), channel_id=1, source_target_pairs={{0,3},{1,0},{2,1},{3,2},{4,7},{5,4},{6,5},{7,6},{8,11},{9,8},{10,9... | collective-permute-start | bytes 393224 | tf_op jit(solution)/shard_map/ppermute | solution.py:64
  57.3 6.0 %collective-permute-start.10 = (f32[64,512]{1,0:T(8,128)S(1)}, f32[64,512]{1,0:T(8,128)S(1)}, u32[]{:S(2)}, u32[]{:S(2)}) collective-permute-start(f32[64,512]{1,0:T(8,128)S(1)} %add.39), channel_id=1, source_target_pairs={{0,2},{1,3},{2,0},{3,1},{4,6},{5,7},{6,4},{7,5},{8,10},{9,11},{10,... | collective-permute-start | bytes 393224 | tf_op jit(solution)/shard_map/ppermute | solution.py:64
  58.0 9.0 %collective-permute-start.9 = (f32[64,512]{1,0:T(8,128)S(1)}, f32[64,512]{1,0:T(8,128)S(1)}, u32[]{:S(2)}, u32[]{:S(2)}) collective-permute-start(f32[64,512]{1,0:T(8,128)S(1)} %add.39), channel_id=1, source_target_pairs={{0,1},{1,2},{2,3},{3,0},{4,5},{5,6},{6,7},{7,4},{8,9},{9,10},{10,1... | collective-permute-start | bytes 393224 | tf_op jit(solution)/shard_map/ppermute | solution.py:64
  67.8 1.8 %collective-permute-start.12 = (f32[64,512]{1,0:T(8,128)S(1)}, f32[64,512]{1,0:T(8,128)S(1)}, u32[]{:S(2)}, u32[]{:S(2)}) collective-permute-start(f32[64,512]{1,0:T(8,128)S(1)} %pad_maximum_fusion.error_own), channel_id=1, source_target_pairs={{0,4},{4,0},{1,5},{5,1},{2,6},{6,2},{3,7},{7,3},{8,12},{12,8},{9,1... | collective-permute-start | bytes 393224 | tf_op jit(solution)/shard_map/ppermute | solution.py:64
  69.5 1.0 copy-start.3
  78.1 12.3 %collective-permute-start.13 = (bf16[400,512]{1,0:T(8,128)(2,1)S(1)}, bf16[400,512]{1,0:T(8,128)(2,1)S(1)}, u32[]{:S(2)}, u32[]{:S(2)}) collective-permute-start(bf16[400,512]{1,0:T(8,128)(2,1)S(1)} %get-tuple-element.59), channel_id=1, source_target_pairs={{0,16},{8,24},{16,0},{24,8},{1,17},{9,25},{17,1},{25,9},{2,18},{10... | collective-permute-start | bytes 1228808 | tf_op jit(solution)/shard_map/ppermute | solution.py:64
  79.3 12.1 %collective-permute-start.14 = (bf16[400,512]{1,0:T(8,128)(2,1)S(1)}, bf16[400,512]{1,0:T(8,128)(2,1)S(1)}, u32[]{:S(2)}, u32[]{:S(2)}) collective-permute-start(bf16[400,512]{1,0:T(8,128)(2,1)S(1)} %get-tuple-element.60), channel_id=1, source_target_pairs={{0,64},{32,96},{64,0},{96,32},{1,65},{33,97},{65,1},{97,33},{2,66}... | collective-permute-start | bytes 1228808 | tf_op jit(solution)/shard_map/ppermute | solution.py:64
  81.5 18.4 %collective-permute-start.15 = (bf16[400,512]{1,0:T(8,128)(2,1)S(1)}, bf16[400,512]{1,0:T(8,128)(2,1)S(1)}, u32[]{:S(2)}, u32[]{:S(2)}) collective-permute-start(bf16[400,512]{1,0:T(8,128)(2,1)S(1)} %get-tuple-element.61), channel_id=1, source_target_pairs={{0,8},{8,16},{16,24},{24,0},{1,9},{9,17},{17,25},{25,1},{2,10},{10... | collective-permute-start | bytes 1228808 | tf_op jit(solution)/shard_map/ppermute | solution.py:64
  81.8 19.2 %collective-permute-start.16 = (bf16[400,512]{1,0:T(8,128)(2,1)S(1)}, bf16[400,512]{1,0:T(8,128)(2,1)S(1)}, u32[]{:S(2)}, u32[]{:S(2)}) collective-permute-start(bf16[400,512]{1,0:T(8,128)(2,1)S(1)} %get-tuple-element.62), channel_id=1, source_target_pairs={{0,32},{32,64},{64,96},{96,0},{1,33},{33,65},{65,97},{97,1},{2,34}... | collective-permute-start | bytes 1228808 | tf_op jit(solution)/shard_map/ppermute | solution.py:64
  82.2 18.8 %collective-permute-start.17 = (bf16[400,512]{1,0:T(8,128)(2,1)S(1)}, bf16[400,512]{1,0:T(8,128)(2,1)S(1)}, u32[]{:S(2)}, u32[]{:S(2)}) collective-permute-start(bf16[400,512]{1,0:T(8,128)(2,1)S(1)} %get-tuple-element.63), channel_id=1, source_target_pairs={{0,24},{8,0},{16,8},{24,16},{1,25},{9,1},{17,9},{25,17},{2,26},{10... | collective-permute-start | bytes 1228808 | tf_op jit(solution)/shard_map/ppermute | solution.py:64
  90.5 10.5 %collective-permute-start.18 = (bf16[400,512]{1,0:T(8,128)(2,1)S(1)}, bf16[400,512]{1,0:T(8,128)(2,1)S(1)}, u32[]{:S(2)}, u32[]{:S(2)}) collective-permute-start(bf16[400,512]{1,0:T(8,128)(2,1)S(1)} %get-tuple-element.64), channel_id=1, source_target_pairs={{0,96},{32,0},{64,32},{96,64},{1,97},{33,1},{65,33},{97,65},{2,98}... | collective-permute-start | bytes 1228808 | tf_op jit(solution)/shard_map/ppermute | solution.py:64
  102.4 6.4 %collective-permute-start.19 = (bf16[448,128]{1,0:T(8,128)(2,1)S(1)}, bf16[448,128]{1,0:T(8,128)(2,1)S(1)}, u32[]{:S(2)}, u32[]{:S(2)}) collective-permute-start(bf16[448,128]{1,0:T(8,128)(2,1)S(1)} %get-tuple-element.67), channel_id=1, source_target_pairs={{0,64},{32,96},{64,0},{96,32},{1,65},{33,97},{65,1},{97,33},{2,66}... | collective-permute-start | bytes 344072 | tf_op jit(solution)/shard_map/ppermute | solution.py:64
  104.0 6.7 %collective-permute-start.20 = (bf16[448,128]{1,0:T(8,128)(2,1)S(1)}, bf16[448,128]{1,0:T(8,128)(2,1)S(1)}, u32[]{:S(2)}, u32[]{:S(2)}) collective-permute-start(bf16[448,128]{1,0:T(8,128)(2,1)S(1)} %get-tuple-element.68), channel_id=1, source_target_pairs={{0,16},{8,24},{16,0},{24,8},{1,17},{9,25},{17,1},{25,9},{2,18},{10... | collective-permute-start | bytes 344072 | tf_op jit(solution)/shard_map/ppermute | solution.py:64
  105.3 6.0 %collective-permute-start.21 = (bf16[448,128]{1,0:T(8,128)(2,1)S(1)}, bf16[448,128]{1,0:T(8,128)(2,1)S(1)}, u32[]{:S(2)}, u32[]{:S(2)}) collective-permute-start(bf16[448,128]{1,0:T(8,128)(2,1)S(1)} %get-tuple-element.69), channel_id=1, source_target_pairs={{0,32},{32,64},{64,96},{96,0},{1,33},{33,65},{65,97},{97,1},{2,34}... | collective-permute-start | bytes 344072 | tf_op jit(solution)/shard_map/ppermute | solution.py:64
  105.9 6.3 %collective-permute-start.22 = (bf16[448,128]{1,0:T(8,128)(2,1)S(1)}, bf16[448,128]{1,0:T(8,128)(2,1)S(1)}, u32[]{:S(2)}, u32[]{:S(2)}) collective-permute-start(bf16[448,128]{1,0:T(8,128)(2,1)S(1)} %get-tuple-element.70), channel_id=1, source_target_pairs={{0,8},{8,16},{16,24},{24,0},{1,9},{9,17},{17,25},{25,1},{2,10},{10... | collective-permute-start | bytes 344072 | tf_op jit(solution)/shard_map/ppermute | solution.py:64
  106.2 6.0 %collective-permute-start.23 = (bf16[448,128]{1,0:T(8,128)(2,1)S(1)}, bf16[448,128]{1,0:T(8,128)(2,1)S(1)}, u32[]{:S(2)}, u32[]{:S(2)}) collective-permute-start(bf16[448,128]{1,0:T(8,128)(2,1)S(1)} %get-tuple-element.71), channel_id=1, source_target_pairs={{0,96},{32,0},{64,32},{96,64},{1,97},{33,1},{65,33},{97,65},{2,98}... | collective-permute-start | bytes 344072 | tf_op jit(solution)/shard_map/ppermute | solution.py:64
  108.8 3.9 %collective-permute-start.24 = (bf16[448,128]{1,0:T(8,128)(2,1)S(1)}, bf16[448,128]{1,0:T(8,128)(2,1)S(1)}, u32[]{:S(2)}, u32[]{:S(2)}) collective-permute-start(bf16[448,128]{1,0:T(8,128)(2,1)S(1)} %get-tuple-element.72), channel_id=1, source_target_pairs={{0,24},{8,0},{16,8},{24,16},{1,25},{9,1},{17,9},{25,17},{2,26},{10... | collective-permute-start | bytes 344072 | tf_op jit(solution)/shard_map/ppermute | solution.py:64
  112.9 5.2 %collective-permute-start.29 = (bf16[3,128,128]{2,1,0:T(8,128)(2,1)S(1)}, bf16[3,128,128]{2,1,0:T(8,128)(2,1)S(1)}, u32[]{:S(2)}, u32[]{:S(2)}) collective-permute-start(bf16[3,128,128]{2,1,0:T(8,128)(2,1)S(1)} %get-tuple-element.75.refs_6_), channel_id=1, source_target_pairs={{0,96},{32,0},{64,32},{96,64},{1,97},{33,1},{65,33},{97,65},{2,98}... | collective-permute-start | bytes 294920 | tf_op jit(solution)/shard_map/ppermute | solution.py:64
  113.9 5.7 %collective-permute-start.27 = (bf16[3,128,128]{2,1,0:T(8,128)(2,1)S(1)}, bf16[3,128,128]{2,1,0:T(8,128)(2,1)S(1)}, u32[]{:S(2)}, u32[]{:S(2)}) collective-permute-start(bf16[3,128,128]{2,1,0:T(8,128)(2,1)S(1)} %get-tuple-element.75.refs_6_), channel_id=1, source_target_pairs={{0,32},{32,64},{64,96},{96,0},{1,33},{33,65},{65,97},{97,1},{2,34}... | collective-permute-start | bytes 294920 | tf_op jit(solution)/shard_map/ppermute | solution.py:64
  114.5 5.2 %collective-permute-start.25 = (bf16[3,128,128]{2,1,0:T(8,128)(2,1)S(1)}, bf16[3,128,128]{2,1,0:T(8,128)(2,1)S(1)}, u32[]{:S(2)}, u32[]{:S(2)}) collective-permute-start(bf16[3,128,128]{2,1,0:T(8,128)(2,1)S(1)} %get-tuple-element.75.refs_6_), channel_id=1, source_target_pairs={{0,64},{32,96},{64,0},{96,32},{1,65},{33,97},{65,1},{97,33},{2,66}... | collective-permute-start | bytes 294920 | tf_op jit(solution)/shard_map/ppermute | solution.py:64
  115.2 4.5 %collective-permute-start.30 = (bf16[3,128,128]{2,1,0:T(8,128)(2,1)S(1)}, bf16[3,128,128]{2,1,0:T(8,128)(2,1)S(1)}, u32[]{:S(2)}, u32[]{:S(2)}) collective-permute-start(bf16[3,128,128]{2,1,0:T(8,128)(2,1)S(1)} %get-tuple-element.76.refs_7_), channel_id=1, source_target_pairs={{0,24},{8,0},{16,8},{24,16},{1,25},{9,1},{17,9},{25,17},{2,26},{10... | collective-permute-start | bytes 294920 | tf_op jit(solution)/shard_map/ppermute | solution.py:64
  118.1 6.0 %collective-permute-start.28 = (bf16[3,128,128]{2,1,0:T(8,128)(2,1)S(1)}, bf16[3,128,128]{2,1,0:T(8,128)(2,1)S(1)}, u32[]{:S(2)}, u32[]{:S(2)}) collective-permute-start(bf16[3,128,128]{2,1,0:T(8,128)(2,1)S(1)} %get-tuple-element.76.refs_7_), channel_id=1, source_target_pairs={{0,8},{8,16},{16,24},{24,0},{1,9},{9,17},{17,25},{25,1},{2,10},{10... | collective-permute-start | bytes 294920 | tf_op jit(solution)/shard_map/ppermute | solution.py:64
  118.1 6.0 %collective-permute-start.26 = (bf16[3,128,128]{2,1,0:T(8,128)(2,1)S(1)}, bf16[3,128,128]{2,1,0:T(8,128)(2,1)S(1)}, u32[]{:S(2)}, u32[]{:S(2)}) collective-permute-start(bf16[3,128,128]{2,1,0:T(8,128)(2,1)S(1)} %get-tuple-element.76.refs_7_), channel_id=1, source_target_pairs={{0,16},{8,24},{16,0},{24,8},{1,17},{9,25},{17,1},{25,9},{2,18},{10... | collective-permute-start | bytes 294920 | tf_op jit(solution)/shard_map/ppermute | solution.py:64
  124.2 10.3 %collective-permute-start.36 = (bf16[4,3,128,128]{3,2,1,0:T(8,128)(2,1)S(1)}, bf16[4,3,128,128]{3,2,1,0:T(8,128)(2,1)S(1)}, u32[]{:S(2)}, u32[]{:S(2)}) collective-permute-start(bf16[4,3,128,128]{3,2,1,0:T(8,128)(2,1)S(1)} %get-tuple-element.78.line), channel_id=1, source_target_pairs={{0,24},{8,0},{16,8},{24,16},{1,25},{9,1},{17,9},{25,17},{2,26},{10... | collective-permute-start | bytes 1179656 | tf_op jit(solution)/shard_map/ppermute | solution.py:64
  126.6 12.8 %collective-permute-start.35 = (bf16[4,3,128,128]{3,2,1,0:T(8,128)(2,1)S(1)}, bf16[4,3,128,128]{3,2,1,0:T(8,128)(2,1)S(1)}, u32[]{:S(2)}, u32[]{:S(2)}) collective-permute-start(bf16[4,3,128,128]{3,2,1,0:T(8,128)(2,1)S(1)} %get-tuple-element.78.line), channel_id=1, source_target_pairs={{0,8},{8,16},{16,24},{24,0},{1,9},{9,17},{17,25},{25,1},{2,10},{10... | collective-permute-start | bytes 1179656 | tf_op jit(solution)/shard_map/ppermute | solution.py:64
  126.6 12.8 %collective-permute-start.34 = (bf16[4,3,128,128]{3,2,1,0:T(8,128)(2,1)S(1)}, bf16[4,3,128,128]{3,2,1,0:T(8,128)(2,1)S(1)}, u32[]{:S(2)}, u32[]{:S(2)}) collective-permute-start(bf16[4,3,128,128]{3,2,1,0:T(8,128)(2,1)S(1)} %get-tuple-element.78.line), channel_id=1, source_target_pairs={{0,16},{8,24},{16,0},{24,8},{1,17},{9,25},{17,1},{25,9},{2,18},{10... | collective-permute-start | bytes 1179656 | tf_op jit(solution)/shard_map/ppermute | solution.py:64
  127.9 23.7 %collective-permute-start.33 = (bf16[4,3,128,128]{3,2,1,0:T(8,128)(2,1)S(1)}, bf16[4,3,128,128]{3,2,1,0:T(8,128)(2,1)S(1)}, u32[]{:S(2)}, u32[]{:S(2)}) collective-permute-start(bf16[4,3,128,128]{3,2,1,0:T(8,128)(2,1)S(1)} %get-tuple-element.77.refs_1_.refs_3_), channel_id=1, source_target_pairs={{0,96},{32,0},{64,32},{96,64},{1,97},{33,1},{65,33},{97,65},{2,98}... | collective-permute-start | bytes 1179656 | tf_op jit(solution)/shard_map/ppermute | solution.py:64
  129.4 22.2 %collective-permute-start.32 = (bf16[4,3,128,128]{3,2,1,0:T(8,128)(2,1)S(1)}, bf16[4,3,128,128]{3,2,1,0:T(8,128)(2,1)S(1)}, u32[]{:S(2)}, u32[]{:S(2)}) collective-permute-start(bf16[4,3,128,128]{3,2,1,0:T(8,128)(2,1)S(1)} %get-tuple-element.77.refs_1_.refs_3_), channel_id=1, source_target_pairs={{0,32},{32,64},{64,96},{96,0},{1,33},{33,65},{65,97},{97,1},{2,34}... | collective-permute-start | bytes 1179656 | tf_op jit(solution)/shard_map/ppermute | solution.py:64
  134.5 17.1 %collective-permute-start.31 = (bf16[4,3,128,128]{3,2,1,0:T(8,128)(2,1)S(1)}, bf16[4,3,128,128]{3,2,1,0:T(8,128)(2,1)S(1)}, u32[]{:S(2)}, u32[]{:S(2)}) collective-permute-start(bf16[4,3,128,128]{3,2,1,0:T(8,128)(2,1)S(1)} %get-tuple-element.77.refs_1_.refs_3_), channel_id=1, source_target_pairs={{0,64},{32,96},{64,0},{96,32},{1,65},{33,97},{65,1},{97,33},{2,66}... | collective-permute-start | bytes 1179656 | tf_op jit(solution)/shard_map/ppermute | solution.py:64
  139.6 15.9 %collective-permute-start.38 = (bf16[5,4,3,128,128]{4,3,2,1,0:T(8,128)(2,1)S(1)}, bf16[5,4,3,128,128]{4,3,2,1,0:T(8,128)(2,1)}, u32[]{:S(2)}, u32[]{:S(2)}) collective-permute-start(bf16[5,4,3,128,128]{4,3,2,1,0:T(8,128)(2,1)S(1)} %shard_map.121.refs_0_.refs_1_), channel_id=1, source_target_pairs={{0,4},{4,0},{1,5},{5,1},{2,6},{6,2},{3,7},{7,3},{8,12},{12,8},{9,1... | collective-permute-start | bytes 5898248 | tf_op jit(solution)/shard_map/ppermute | solution.py:64
  151.7 11.3 %collective-permute-start.37 = (bf16[4,4,3,128,128]{4,3,2,1,0:T(8,128)(2,1)S(1)}, bf16[4,4,3,128,128]{4,3,2,1,0:T(8,128)(2,1)}, u32[]{:S(2)}, u32[]{:S(2)}) collective-permute-start(bf16[4,4,3,128,128]{4,3,2,1,0:T(8,128)(2,1)S(1)} %shard_map.123.refs_2_), channel_id=1, source_target_pairs={{0,4},{4,0},{1,5},{5,1},{2,6},{6,2},{3,7},{7,3},{8,12},{12,8},{9,1... | collective-permute-start | bytes 4718600 | tf_op jit(solution)/shard_map/ppermute | solution.py:64
  155.6 1.0 copy-start.1
  (1 other events, 0.7 us)

commit v5 on v4

--- a/solution.py
+++ b/solution.py
@@ -68,7 +68,15 @@
     return jax.ShapeDtypeStruct(dims, kind)
 
 
-def bucket_kernel(rows, dest_row, out):
+def bucket_kernel(rows_far, dest_far, out, rows, dest_row, sems):
+    loads = [
+        pltpu.make_async_copy(rows_far, rows, sems.at[0]),
+        pltpu.make_async_copy(dest_far, dest_row, sems.at[1]),
+    ]
+    for load in loads:
+        load.start()
+    for load in loads:
+        load.wait()
     dest_col = jnp.broadcast_to(dest_row[...].astype(f32), (128, 128)).T
     earlier = lax.broadcasted_iota(jnp.int32, (128, 128), 0) < lax.broadcasted_iota(
         jnp.int32, (128, 128), 1
@@ -158,8 +166,9 @@
 def forward_kernel(moments, *refs):
     act_own, act_theirs, sides, sides_theirs, top, top_theirs, bottom, bottom_theirs = refs[:8]
     pairs, w_embed, gain, w_t_far, head_t, mix_t = refs[8:14]
-    normed_far, proj_far, attended_far, probs, part_own, part_other = refs[14:20]
-    act, w_t, normed, proj, attended, rest, sems, arrive = refs[20:]
+    normed_far, proj_far, probs, part_own, part_other = refs[14:19]
+    act, w_t, normed, proj, rest, sems, arrive = refs[19:]
+    attended = proj.at[768:1024]
     whole, low, high = pl.ds(0, 128), pl.ds(0, 64), pl.ds(64, 64)
     moves = [(act_own, 0, whole), (act_theirs, 1, whole)]
     for side in range(2):
@@ -191,7 +200,7 @@
     for i in range(3):
         rows = slice(i * 256, i * 256 + 256)
         proj[rows] = dot(w_t[rows], normed[...], NT).astype(bf16)
-    leave.append(pltpu.make_async_copy(proj, proj_far, sems.at[2]))
+    leave.append(pltpu.make_async_copy(proj.at[:768], proj_far.at[:768], sems.at[2]))
     leave[1].start()
     for h in range(2):
         for other in range(2):
@@ -216,7 +225,7 @@
                 attended[h * 128 : h * 128 + 128, lanes(f, other)] = out.astype(bf16)
                 for g in range(4):
                     probs[h * 2 + other, f * 4 + g : f * 4 + g + 1] = prob[g]
-    leave.append(pltpu.make_async_copy(attended, attended_far, sems.at[3]))
+    leave.append(pltpu.make_async_copy(attended, proj_far.at[768:1024], sems.at[3]))
     leave[2].start()
     value = split_dot(mix_t[...], attended[...])
     for other, part in ((0, part_own), (1, part_other)):
@@ -234,12 +243,13 @@
         out[384:, i * 128 : i * 128 + 128] = factor[i * 16 : i * 16 + 16]
 
 
-def backward_kernel(place, error_own, error_other, probs, mix, proj_far, attended_far, normed_far, *refs):
+def backward_kernel(place, error_own, error_other, probs, mix, proj_far, normed_far, *refs):
     pieces = refs[:8]
-    delta, own_factor, slope, grad, proj, attended, normed, sems = refs[8:]
+    delta, own_factor, slope, grad, proj, normed, sems = refs[8:]
+    attended = proj.at[768:1024]
     loads = [
         pltpu.make_async_copy(far, near, sems.at[k])
-        for k, (far, near) in enumerate(((proj_far, proj), (attended_far, attended), (normed_far, normed)))
+        for k, (far, near) in enumerate(((proj_far, proj), (normed_far, normed)))
     ]
     for load in loads:
         load.start()
@@ -272,11 +282,10 @@
                 for j, out in enumerate((query, key, value)):
                     row = h * 384 + j * 128
                     delta[row : row + 128, lanes(g, other)] = out.astype(bf16)
-    loads[1].wait()
     factor = split_dot(slope[...], attended[...], NT)
     for h in range(2):
         own_factor[h] = factor[:, h * 128 : h * 128 + 128].astype(bf16)
-    loads[2].wait()
+    loads[1].wait()
     for (h, o), out in zip(PIECES, pieces):
         gradient_piece(delta, normed, own_factor[h], h, (place[h] + o) % 4, out)
 
@@ -310,7 +319,7 @@
 
 def line_kernel(*refs):
     for h in range(2):
-        for k, o in enumerate((2, 1, 3, 0)):
+        for k, o in enumerate((3, 1, 2, 0)):
             refs[8 + h][o] = refs[2 * k + h][...]
 
 
@@ -440,7 +449,9 @@
     before, after = shift(act, "frame", 1), shift(act, "frame", 3)
     act_theirs = shift(act, "core", 1)
     (sent,) = call(
-        bucket_kernel, near(shape((16, 16, 128), bf16)), *near(cache_rows, row_dest.reshape(1, 128))
+        bucket_kernel, near(shape((16, 16, 128), bf16)), *far(cache_rows, row_dest.reshape(1, 128)),
+        scratch=[pltpu.VMEM((128, 128), bf16), pltpu.VMEM((1, 128), jnp.int32), dma((2,))],
+        mib=LARGE,
     )
     arrived = lax.all_to_all(sent, ("y", "x"), 0, 0, tiled=True).reshape(256, 128)
     half_act = shape((64, 2048), bf16)
@@ -469,9 +480,9 @@
     pairs, moments = call(
         fetch_kernel, near(shape((8, 128, 128), bf16), shape((2, 16, 128), f32)), here, *near(arrived)
     )
-    normed, proj, attended, probs, part_own, part_other = call(
+    normed, proj, probs, part_own, part_other = call(
         forward_kernel,
-        far(shape((1024, 2048), bf16), shape((768, 1024), bf16), shape((256, 1024), bf16))
+        far(shape((1024, 2048), bf16), shape((1024, 1024), bf16))
         + near(shape((4, 16, 128), f32), shape((64, 512), f32), shape((64, 512), f32)),
         *near(moments),
         *far(act, act_theirs, sides, sides_theirs, top, shift(top, "core", 1), bottom, shift(bottom, "core", 1)),
@@ -480,8 +491,7 @@
             pltpu.VMEM((8, 128, 2048), bf16),
             pltpu.VMEM((768, 2048), bf16),
             pltpu.VMEM((1024, 2048), bf16),
-            pltpu.VMEM((768, 1024), bf16),
-            pltpu.VMEM((256, 1024), bf16),
+            pltpu.VMEM((1024, 1024), bf16),
             pltpu.VMEM((64, 128), f32),
             dma((4,)),
             dma((10,)),
@@ -509,19 +519,19 @@
     block = shape((3, 128, 128), bf16)
     line = shape((4, 3, 128, 128), bf16)
     axes = (("x", "y"), ("y", "x"))
+    reach = (3, 1, 2)
     pieces = call(
         backward_kernel,
         near(*[piece] * 8),
-        square, *near(error_own, error_other, probs, mix), *far(proj, attended, normed),
+        square, *near(error_own, error_other, probs, mix), *far(proj, normed),
         scratch=[
             pltpu.VMEM((768, 1024), bf16),
             pltpu.VMEM((2, 64, 128), bf16),
             pltpu.VMEM((64, 1024), f32),
             pltpu.VMEM((256, 1024), f32),
-            pltpu.VMEM((768, 1024), bf16),
-            pltpu.VMEM((256, 1024), bf16),
+            pltpu.VMEM((1024, 1024), bf16),
             pltpu.VMEM((1024, 2048), bf16),
-            dma((3,)),
+            dma((2,)),
         ],
         mib=49,
     )
@@ -535,12 +545,11 @@
         add_second_kernel, near(block, block, shape((256, 64), bf16)),
         *near(*moved, second[0], second[4]),
     )
-    back = [shift(owned[h], axes[h][1], o) for h, o in PIECES[:6]]
+    back = [shift(owned[h], axes[h][1], o) for o in reach for h in range(2)]
     lines = call(
         line_kernel, near(line, line), *near(*back, *owned),
     )
     every = (0, 1, 2, 3)
-    reach = (2, 1, 3)
     wide = [[shift(lines[h], axes[h][0], o) for o in reach] for h in range(2)]
     (half_x,) = call(
         first_join_kernel, near(shape((5, 4, 3, 128, 128), bf16)),

time: 169 us -> 165 us (0.976)
  waiting for transfers between devices: 50.2 us -> 47.8 us
    ppermute x39, waiting for transfers between devices: 42.5 us -> 40.2 us  [shift(): lax.ppermute(value, axis, [(i, (i + offset) % size) for i in range(size)])]
    unnamed x16 -> x14, local copies, waits for them, and re-layouts: 4.36 us -> 3.32 us
  transfers between devices with their start and end apart: 41 -> 41, of which waited for: 19 -> 20; matrix products, arithmetic and copies ran while one was open for 0% -> 0% of each run, Pallas kernels for 10% -> 10%
where the time goes in v5:
time: 165 us
  starting transfers between devices  66.7 us (40%)
  waiting for transfers between devices  47.8 us (29%)
  Pallas kernels  42.6 us (26%)
  local copies, waits for them, and re-layouts  3.32 us (2%)
  between operations  3.29 us (2%)
    ppermute x39, starting transfers between devices, shift(): lax.ppermute(value, axis, [(i, (i + offset) % size) for i in range(size)])  55.7 us
    ppermute x39, waiting for transfers between devices, shift(): lax.ppermute(value, axis, [(i, (i + offset) % size) for i in range(size)])  40.2 us
    pallas_call x11, Pallas kernels, call(): pl.pallas_call(kernel, in_specs=[spec for spec, _ in operands], out_specs...  28.6 us
    pallas_call x3, Pallas kernels, assemble(): pl.pallas_call(functools.partial(assemble_kernel, tags, len(arrays), len(...  13.9 us
    all_to_all x1, starting transfers between devices, shards(): lax.all_to_all(sent, ('y', 'x'), 0, 0, tiled=True).reshape(256, 128)  6.77 us
    all_to_all x1, waiting for transfers between devices, shards(): lax.all_to_all(sent, ('y', 'x'), 0, 0, tiled=True).reshape(256, 128)  5.9 us
    all_to_all x1, starting transfers between devices, shards(): arrived = lax.all_to_all(spread, ('core', 'frame'), 0, 0, tiled=True)  4.25 us
    unnamed x14, local copies, waits for them, and re-layouts  3.32 us
  transfers between devices with their start and end apart: 41, of which 20 were waited for; matrix products, arithmetic and copies ran while one was open for 0% of the time, Pallas kernels for 10%

profile of v5, /device:TPU:1, one launch (start us, length us, event | category | flops | bytes accessed | tf_op | source)
XLA Modules:
  0.0 164.6 jit_solution(5543994084753765914)
XLA Ops:
  0.6 4.7 %collective-permute-start.1 = (bf16[128,2048]{1,0:T(8,128)(2,1)}, bf16[128,2048]{1,0:T(8,128)(2,1)S(1)}, u32[]{:S(2)}, u32[]{:S(2)}) collective-permute-start(bf16[128,2048]{1,0:T(8,128)(2,1)} %refs_0_.1), channel_id=1, source_target_pairs={{0,3},{1,0},{2,1},{3,2},{4,7},{5,4},{6,5},{7,6},{8,11},{9,8},{10,9... | collective-permute-start | bytes 1572872 | tf_op jit(solution)/shard_map/ppermute | solution.py:64
  7.6 6.8 %all-to-all-start = ((bf16[16,16,128]{2,1,0:T(8,128)(2,1)}), bf16[16,16,128]{2,1,0:T(8,128)(2,1)S(1)}, u32[]{:S(2)}, u32[]{:S(2)}) async-start(bf16[16,16,128]{2,1,0:T(8,128)(2,1)} %shard_map.112), calls=%async_computation | async-start | bytes 131072 | tf_op jit(solution)/shard_map/all_to_all | solution.py:456
  15.1 5.9 %all-to-all-done = bf16[16,16,128]{2,1,0:T(8,128)(2,1)S(1)} async-done(((bf16[16,16,128]{2,1,0:T(8,128)(2,1)}), bf16[16,16,128]{2,1,0:T(8,128)(2,1)S(1)}, u32[]{:S(2)}, u32[]{:S(2)}) %all-to-all-start) | async-done | bytes 65568 | tf_op jit(solution)/shard_map/all_to_all | solution.py:456
  21.0 1.0 shard_map.113
  21.9 2.4 %collective-permute-start.3 = (bf16[2,128,2048]{2,1,0:T(8,128)(2,1)S(1)}, bf16[2,128,2048]{2,1,0:T(8,128)(2,1)}, u32[]{:S(2)}, u32[]{:S(2)}) collective-permute-start(bf16[2,128,2048]{2,1,0:T(8,128)(2,1)S(1)} %get-tuple-element.45.refs_2_), channel_id=1, source_target_pairs={{0,4},{4,0},{1,5},{5,1},{2,6},{6,2},{3,7},{7,3},{8,12},{12,8},{9,1... | collective-permute-start | bytes 3145736 | tf_op jit(solution)/shard_map/ppermute | solution.py:64
  24.3 3.0 %collective-permute-start.6 = (bf16[64,2048]{1,0:T(8,128)(2,1)S(1)}, bf16[64,2048]{1,0:T(8,128)(2,1)S(1)}, u32[]{:S(2)}, u32[]{:S(2)}) collective-permute-start(bf16[64,2048]{1,0:T(8,128)(2,1)S(1)} %get-tuple-element.47), channel_id=1, source_target_pairs={{0,3},{1,0},{2,1},{3,2},{4,7},{5,4},{6,5},{7,6},{8,11},{9,8},{10,9... | collective-permute-start | bytes 786440 | tf_op jit(solution)/shard_map/ppermute | solution.py:64
  27.3 4.2 %all-to-all-start.1 = ((bf16[8,272,128]{2,1,0:T(8,128)(2,1)}), bf16[8,272,128]{2,1,0:T(8,128)(2,1)S(1)}, u32[]{:S(2)}, u32[]{:S(2)}) async-start(bf16[8,272,128]{2,1,0:T(8,128)(2,1)} %get-tuple-element.43), calls=%async_computation.1 | async-start | bytes 1114112 | tf_op jit(solution)/shard_map/all_to_all | solution.py:465
  31.5 2.0 %collective-permute-done.4.refs_4_ = bf16[64,2048]{1,0:T(8,128)(2,1)S(1)} collective-permute-done((bf16[64,2048]{1,0:T(8,128)(2,1)S(1)}, bf16[64,2048]{1,0:T(8,128)(2,1)S(1)}, u32[]{:S(2)}, u32[]{:S(2)}) %collective-permute-start.4) | collective-permute-done | bytes 262176 | tf_op jit(solution)/shard_map/ppermute | solution.py:64
  33.5 1.0 collective-permute-start.5
  34.8 0.9 copy-done
  35.8 3.7 %shard_map.115 = (bf16[768,2048]{1,0:T(8,128)(2,1)}, f32[256,64]{1,0:T(8,128)S(1)}, f32[64,256]{1,0:T(8,128)S(1)}) custom-call(s32[2]{0:T(128)S(1)} %pad_add_fusion.place, bf16[3,2048,512]{2,1,0:T(8,128)(2,1)} %w.1, bf16[512,2048]{1,0:T(8,128)(2,1)} %w_out.1, bf16[64,2048]{1,0:T(8,128)(2,1)S(1)} %bitcast.10), custom_call_target="tpu_custom_call" | custom-call | bytes 1024 | tf_op jit(solution)/shard_map/pallas_call | solution.py:423
  39.5 1.7 %all-to-all-done.1.arrived = bf16[8,272,128]{2,1,0:T(8,128)(2,1)S(1)} async-done(((bf16[8,272,128]{2,1,0:T(8,128)(2,1)}), bf16[8,272,128]{2,1,0:T(8,128)(2,1)S(1)}, u32[]{:S(2)}, u32[]{:S(2)}) %all-to-all-start.1) | async-done | bytes 557088 | tf_op jit(solution)/shard_map/all_to_all | solution.py:465
  41.2 1.4 shard_map.114
  42.7 11.3 %shard_map.116 = (bf16[1024,2048]{1,0:T(8,128)(2,1)}, bf16[1024,1024]{1,0:T(8,128)(2,1)}, f32[4,16,128]{2,1,0:T(8,128)S(1)}, f32[64,512]{1,0:T(8,128)S(1)}, f32[64,512]{1,0:T(8,128)S(1)}) custom-call(f32[2,16,128]{2,1,0:T(8,128)S(1)} %get-tuple-element.44.moments, bf16[128,2048]{1,0:T(8,128)(2,1)} %refs_0_.1, ...), custom_call_target="tpu_custom_call" | custom-call | bytes 1024 | tf_op jit(solution)/shard_map/pallas_call | solution.py:423
  54.4 1.0 collective-permute-done.8
  55.4 1.7 %collective-permute-start.11 = (f32[64,512]{1,0:T(8,128)S(1)}, f32[64,512]{1,0:T(8,128)S(1)}, u32[]{:S(2)}, u32[]{:S(2)}) collective-permute-start(f32[64,512]{1,0:T(8,128)S(1)} %add.39), channel_id=1, source_target_pairs={{0,3},{1,0},{2,1},{3,2},{4,7},{5,4},{6,5},{7,6},{8,11},{9,8},{10,9... | collective-permute-start | bytes 393224 | tf_op jit(solution)/shard_map/ppermute | solution.py:64
  57.9 2.3 %collective-permute-done.11 = f32[64,512]{1,0:T(8,128)S(1)} collective-permute-done((f32[64,512]{1,0:T(8,128)S(1)}, f32[64,512]{1,0:T(8,128)S(1)}, u32[]{:S(2)}, u32[]{:S(2)}) %collective-permute-start.11) | collective-permute-done | bytes 131104 | tf_op jit(solution)/shard_map/ppermute | solution.py:64
  60.2 3.0 %collective-permute-done.10 = f32[64,512]{1,0:T(8,128)S(1)} collective-permute-done((f32[64,512]{1,0:T(8,128)S(1)}, f32[64,512]{1,0:T(8,128)S(1)}, u32[]{:S(2)}, u32[]{:S(2)}) %collective-permute-start.10) | collective-permute-done | bytes 131104 | tf_op jit(solution)/shard_map/ppermute | solution.py:64
  63.2 3.7 %collective-permute-done.9 = f32[64,512]{1,0:T(8,128)S(1)} collective-permute-done((f32[64,512]{1,0:T(8,128)S(1)}, f32[64,512]{1,0:T(8,128)S(1)}, u32[]{:S(2)}, u32[]{:S(2)}) %collective-permute-start.9) | collective-permute-done | bytes 131104 | tf_op jit(solution)/shard_map/ppermute | solution.py:64
  69.3 8.4 %shard_map.117 = (bf16[400,512]{1,0:T(8,128)(2,1)S(1)}, bf16[400,512]{1,0:T(8,128)(2,1)S(1)}, bf16[400,512]{1,0:T(8,128)(2,1)S(1)}, bf16[400,512]{1,0:T(8,128)(2...) custom-call(s32[3]{0:T(128)S(1)} %pad_add_fusion.1.place, ...), custom_call_target="tpu_custom_call" | custom-call | bytes 1024 | tf_op jit(solution)/shard_map/pallas_call | solution.py:423
  77.7 1.1 collective-permute-start.13
  78.8 2.2 %collective-permute-start.14 = (bf16[400,512]{1,0:T(8,128)(2,1)S(1)}, bf16[400,512]{1,0:T(8,128)(2,1)S(1)}, u32[]{:S(2)}, u32[]{:S(2)}) collective-permute-start(bf16[400,512]{1,0:T(8,128)(2,1)S(1)} %get-tuple-element.58), channel_id=1, source_target_pairs={{0,64},{32,96},{64,0},{96,32},{1,65},{33,97},{65,1},{97,33},{2,66}... | collective-permute-start | bytes 1228808 | tf_op jit(solution)/shard_map/ppermute | solution.py:64
  81.7 2.4 %collective-permute-start.17 = (bf16[400,512]{1,0:T(8,128)(2,1)S(1)}, bf16[400,512]{1,0:T(8,128)(2,1)S(1)}, u32[]{:S(2)}, u32[]{:S(2)}) collective-permute-start(bf16[400,512]{1,0:T(8,128)(2,1)S(1)} %get-tuple-element.61), channel_id=1, source_target_pairs={{0,24},{8,0},{16,8},{24,16},{1,25},{9,1},{17,9},{25,17},{2,26},{10... | collective-permute-start | bytes 1228808 | tf_op jit(solution)/shard_map/ppermute | solution.py:64
  84.1 6.0 %collective-permute-done.13.refs_0_ = bf16[400,512]{1,0:T(8,128)(2,1)S(1)} collective-permute-done((bf16[400,512]{1,0:T(8,128)(2,1)S(1)}, bf16[400,512]{1,0:T(8,128)(2,1)S(1)}, u32[]{:S(2)}, u32[]{:S(2)}) %collective-permute-start.13) | collective-permute-done | bytes 409632 | tf_op jit(solution)/shard_map/ppermute | solution.py:64
  90.9 8.6 %collective-permute-done.15.refs_2_ = bf16[400,512]{1,0:T(8,128)(2,1)S(1)} collective-permute-done((bf16[400,512]{1,0:T(8,128)(2,1)S(1)}, bf16[400,512]{1,0:T(8,128)(2,1)S(1)}, u32[]{:S(2)}, u32[]{:S(2)}) %collective-permute-start.15) | collective-permute-done | bytes 409632 | tf_op jit(solution)/shard_map/ppermute | solution.py:64
  99.5 1.0 collective-permute-done.16.refs_3_
  100.5 1.5 shard_map.118
  102.0 1.6 collective-permute-start.19
  103.6 1.3 collective-permute-start.20
  105.7 2.7 %collective-permute-start.23 = (bf16[448,128]{1,0:T(8,128)(2,1)S(1)}, bf16[448,128]{1,0:T(8,128)(2,1)S(1)}, u32[]{:S(2)}, u32[]{:S(2)}) collective-permute-start(bf16[448,128]{1,0:T(8,128)(2,1)S(1)} %get-tuple-element.69), channel_id=1, source_target_pairs={{0,96},{32,0},{64,32},{96,64},{1,97},{33,1},{65,33},{97,65},{2,98}... | collective-permute-start | bytes 344072 | tf_op jit(solution)/shard_map/ppermute | solution.py:64
  108.4 1.9 %collective-permute-start.24 = (bf16[448,128]{1,0:T(8,128)(2,1)S(1)}, bf16[448,128]{1,0:T(8,128)(2,1)S(1)}, u32[]{:S(2)}, u32[]{:S(2)}) collective-permute-start(bf16[448,128]{1,0:T(8,128)(2,1)S(1)} %get-tuple-element.70), channel_id=1, source_target_pairs={{0,24},{8,0},{16,8},{24,16},{1,25},{9,1},{17,9},{25,17},{2,26},{10... | collective-permute-start | bytes 344072 | tf_op jit(solution)/shard_map/ppermute | solution.py:64
  114.1 1.9 %collective-permute-start.25 = (bf16[3,128,128]{2,1,0:T(8,128)(2,1)S(1)}, bf16[3,128,128]{2,1,0:T(8,128)(2,1)S(1)}, u32[]{:S(2)}, u32[]{:S(2)}) collective-permute-start(bf16[3,128,128]{2,1,0:T(8,128)(2,1)S(1)} %get-tuple-element.73.refs_6_), channel_id=1, source_target_pairs={{0,96},{32,0},{64,32},{96,64},{1,97},{33,1},{65,33},{97,65},{2,98}... | collective-permute-start | bytes 294920 | tf_op jit(solution)/shard_map/ppermute | solution.py:64
  116.0 1.7 %collective-permute-start.30 = (bf16[3,128,128]{2,1,0:T(8,128)(2,1)S(1)}, bf16[3,128,128]{2,1,0:T(8,128)(2,1)S(1)}, u32[]{:S(2)}, u32[]{:S(2)}) collective-permute-start(bf16[3,128,128]{2,1,0:T(8,128)(2,1)S(1)} %get-tuple-element.74.refs_7_), channel_id=1, source_target_pairs={{0,16},{8,24},{16,0},{24,8},{1,17},{9,25},{17,1},{25,9},{2,18},{10... | collective-permute-start | bytes 294920 | tf_op jit(solution)/shard_map/ppermute | solution.py:64
  117.8 1.7 %collective-permute-start.28 = (bf16[3,128,128]{2,1,0:T(8,128)(2,1)S(1)}, bf16[3,128,128]{2,1,0:T(8,128)(2,1)S(1)}, u32[]{:S(2)}, u32[]{:S(2)}) collective-permute-start(bf16[3,128,128]{2,1,0:T(8,128)(2,1)S(1)} %get-tuple-element.74.refs_7_), channel_id=1, source_target_pairs={{0,8},{8,16},{16,24},{24,0},{1,9},{9,17},{17,25},{25,1},{2,10},{10... | collective-permute-start | bytes 294920 | tf_op jit(solution)/shard_map/ppermute | solution.py:64
  119.5 0.9 collective-permute-start.26
  121.3 1.4 collective-permute-done.28.refs_3_
  123.2 1.4 collective-permute-start.36
  124.6 1.6 collective-permute-start.35
  126.1 1.1 collective-permute-start.34
  127.3 1.1 collective-permute-start.33
  128.6 3.2 %collective-permute-done.36.c = bf16[4,3,128,128]{3,2,1,0:T(8,128)(2,1)S(1)} collective-permute-done((bf16[4,3,128,128]{3,2,1,0:T(8,128)(2,1)S(1)}, bf16[4,3,128,128]{3,2,1,0:T(8,128)(2,1)S(1)}, u32[]{:S(2)}, u32[]{:S(2)}) %collective-permute-start.36) | collective-permute-done | bytes 393248 | tf_op jit(solution)/shard_map/ppermute | solution.py:64
  131.9 0.9 collective-permute-start.31
  132.8 3.3 %collective-permute-done.35.b = bf16[4,3,128,128]{3,2,1,0:T(8,128)(2,1)S(1)} collective-permute-done((bf16[4,3,128,128]{3,2,1,0:T(8,128)(2,1)S(1)}, bf16[4,3,128,128]{3,2,1,0:T(8,128)(2,1)S(1)}, u32[]{:S(2)}, u32[]{:S(2)}) %collective-permute-start.35) | collective-permute-done | bytes 393248 | tf_op jit(solution)/shard_map/ppermute | solution.py:64
  136.7 10.9 %collective-permute-start.38 = (bf16[5,4,3,128,128]{4,3,2,1,0:T(8,128)(2,1)S(1)}, bf16[5,4,3,128,128]{4,3,2,1,0:T(8,128)(2,1)}, u32[]{:S(2)}, u32[]{:S(2)}) collective-permute-start(bf16[5,4,3,128,128]{4,3,2,1,0:T(8,128)(2,1)S(1)} %shard_map.121.refs_0_.refs_1_), channel_id=1, source_target_pairs={{0,4},{4,0},{1,5},{5,1},{2,6},{6,2},{3,7},{7,3},{8,12},{12,8},{9,1... | collective-permute-start | bytes 5898248 | tf_op jit(solution)/shard_map/ppermute | solution.py:64
  147.6 3.5 %shard_map.122 = (f32[3,2048,512]{2,1,0:T(8,128)}, f32[8,128]{1,0:T(8,128)S(1)}) custom-call(s32[3]{0:T(128)S(1)} %pad_add_fusion.1.place, bf16[5,4,3,128,128]{4,3,2,1,0:T(8,128)(2,1)S(1)} %shard_map.121.refs_0_.refs_1_, bf16[4,3,128,128]{3,2,1,0:T(8,128)(2,1)S(1)} %get-tuple-element.75.refs_1_.refs_3_), custom_call_target="tpu_custom_call" | custom-call | bytes 1024 | tf_op jit(solution)/shard_map/pallas_call | solution.py:410
  152.1 0.9 copy-done.1
  153.0 6.5 %shard_map.124 = (f32[3,2048,512]{2,1,0:T(8,128)}, f32[8,128]{1,0:T(8,128)}, f32[512,2048]{1,0:T(8,128)}) custom-call(s32[3]{0:T(128)S(1)} %pad_add_fusion.1.place, bf16[5,4,3,128,128]{4,3,2,1,0:T(8,128)(2,1)} %collective-permute-done.38.refs_0_, bf16[5,4,3,128,128]{4,3,2,1,0:T(8,128)(2,1)S(1)} %shard_map.121.refs_0_.refs_1_, ...), custom_call_target="tpu_custom_call", output_to_operand_aliasing={{0}: (4, {})} | custom-call | bytes 1024 | tf_op jit(solution)/shard_map/pallas_call | solution.py:410
  159.5 3.9 %shard_map.125 = (f32[3,2048,512]{2,1,0:T(8,128)}, f32[8,128]{1,0:T(8,128)}) custom-call(s32[3]{0:T(128)S(1)} %pad_add_fusion.1.place, bf16[4,4,3,128,128]{4,3,2,1,0:T(8,128)(2,1)} %collective-permute-done.37.refs_0_, f32[3,2048,512]{2,1,0:T(8,128)} %get-tuple-element.80.refs_1_), custom_call_target="tpu_custom_call", output_to_operand_aliasing={{0}: (2, {})} | custom-call | bytes 1024 | tf_op jit(solution)/shard_map/pallas_call | solution.py:410
  (67 shorter events, 14.9 us)
Async XLA Ops:
  0.6 20.3 %collective-permute-start.1 = (bf16[128,2048]{1,0:T(8,128)(2,1)}, bf16[128,2048]{1,0:T(8,128)(2,1)S(1)}, u32[]{:S(2)}, u32[]{:S(2)}) collective-permute-start(bf16[128,2048]{1,0:T(8,128)(2,1)} %refs_0_.1), channel_id=1, source_target_pairs={{0,3},{1,0},{2,1},{3,2},{4,7},{5,4},{6,5},{7,6},{8,11},{9,8},{10,9... | collective-permute-start | bytes 1572872 | tf_op jit(solution)/shard_map/ppermute | solution.py:64
  5.3 15.7 %collective-permute-start = (bf16[128,2048]{1,0:T(8,128)(2,1)}, bf16[128,2048]{1,0:T(8,128)(2,1)S(1)}, u32[]{:S(2)}, u32[]{:S(2)}) collective-permute-start(bf16[128,2048]{1,0:T(8,128)(2,1)} %refs_0_.1), channel_id=1, source_target_pairs={{0,1},{1,2},{2,3},{3,0},{4,5},{5,6},{6,7},{7,4},{8,9},{9,10},{10,1... | collective-permute-start | bytes 1572872 | tf_op jit(solution)/shard_map/ppermute | solution.py:64
  5.3 0.8 copy-start.4
  6.0 0.7 copy-start.6
  7.6 13.3 %all-to-all-start = ((bf16[16,16,128]{2,1,0:T(8,128)(2,1)}), bf16[16,16,128]{2,1,0:T(8,128)(2,1)S(1)}, u32[]{:S(2)}, u32[]{:S(2)}) async-start(bf16[16,16,128]{2,1,0:T(8,128)(2,1)} %shard_map.112), calls=%async_computation | async-start | bytes 131072 | tf_op jit(solution)/shard_map/all_to_all | solution.py:456
  21.9 17.5 %copy-start.2 = (bf16[2,128,2048]{2,1,0:T(8,128)(2,1)}, bf16[2,128,2048]{2,1,0:T(8,128)(2,1)S(1)}, u32[]{:S(2)}) copy-start(bf16[2,128,2048]{2,1,0:T(8,128)(2,1)S(1)} %get-tuple-element.45.refs_2_) | copy-start | bytes 3145732
  21.9 20.7 %collective-permute-start.3 = (bf16[2,128,2048]{2,1,0:T(8,128)(2,1)S(1)}, bf16[2,128,2048]{2,1,0:T(8,128)(2,1)}, u32[]{:S(2)}, u32[]{:S(2)}) collective-permute-start(bf16[2,128,2048]{2,1,0:T(8,128)(2,1)S(1)} %get-tuple-element.45.refs_2_), channel_id=1, source_target_pairs={{0,4},{4,0},{1,5},{5,1},{2,6},{6,2},{3,7},{7,3},{8,12},{12,8},{9,1... | collective-permute-start | bytes 3145736 | tf_op jit(solution)/shard_map/ppermute | solution.py:64
  24.3 18.3 %collective-permute-start.2 = (bf16[128,2048]{1,0:T(8,128)(2,1)}, bf16[128,2048]{1,0:T(8,128)(2,1)}, u32[]{:S(2)}, u32[]{:S(2)}) collective-permute-start(bf16[128,2048]{1,0:T(8,128)(2,1)} %refs_0_.1), channel_id=1, source_target_pairs={{0,4},{4,0},{1,5},{5,1},{2,6},{6,2},{3,7},{7,3},{8,12},{12,8},{9,1... | collective-permute-start | bytes 1572872 | tf_op jit(solution)/shard_map/ppermute | solution.py:64
  24.3 9.2 %collective-permute-start.4 = (bf16[64,2048]{1,0:T(8,128)(2,1)S(1)}, bf16[64,2048]{1,0:T(8,128)(2,1)S(1)}, u32[]{:S(2)}, u32[]{:S(2)}) collective-permute-start(bf16[64,2048]{1,0:T(8,128)(2,1)S(1)} %get-tuple-element.46), channel_id=1, source_target_pairs={{0,1},{1,2},{2,3},{3,0},{4,5},{5,6},{6,7},{7,4},{8,9},{9,10},{10,1... | collective-permute-start | bytes 786440 | tf_op jit(solution)/shard_map/ppermute | solution.py:64
  24.3 10.2 %collective-permute-start.6 = (bf16[64,2048]{1,0:T(8,128)(2,1)S(1)}, bf16[64,2048]{1,0:T(8,128)(2,1)S(1)}, u32[]{:S(2)}, u32[]{:S(2)}) collective-permute-start(bf16[64,2048]{1,0:T(8,128)(2,1)S(1)} %get-tuple-element.47), channel_id=1, source_target_pairs={{0,3},{1,0},{2,1},{3,2},{4,7},{5,4},{6,5},{7,6},{8,11},{9,8},{10,9... | collective-permute-start | bytes 786440 | tf_op jit(solution)/shard_map/ppermute | solution.py:64
  27.3 14.0 %all-to-all-start.1 = ((bf16[8,272,128]{2,1,0:T(8,128)(2,1)}), bf16[8,272,128]{2,1,0:T(8,128)(2,1)S(1)}, u32[]{:S(2)}, u32[]{:S(2)}) async-start(bf16[8,272,128]{2,1,0:T(8,128)(2,1)} %get-tuple-element.43), calls=%async_computation.1 | async-start | bytes 1114112 | tf_op jit(solution)/shard_map/all_to_all | solution.py:465
  33.5 9.1 %collective-permute-start.5 = (bf16[64,2048]{1,0:T(8,128)(2,1)S(1)}, bf16[64,2048]{1,0:T(8,128)(2,1)S(1)}, u32[]{:S(2)}, u32[]{:S(2)}) collective-permute-start(bf16[64,2048]{1,0:T(8,128)(2,1)S(1)} %collective-permute-done.4.refs_4_), channel_id=1, source_target_pairs={{0,4},{4,0},{1,5},{5,1},{2,6},{6,2},{3,7},{7,3},{8,12},{12,8},{9,1... | collective-permute-start | bytes 786440 | tf_op jit(solution)/shard_map/ppermute | solution.py:64
  34.5 8.1 %collective-permute-start.7 = (bf16[64,2048]{1,0:T(8,128)(2,1)S(1)}, bf16[64,2048]{1,0:T(8,128)(2,1)S(1)}, u32[]{:S(2)}, u32[]{:S(2)}) collective-permute-start(bf16[64,2048]{1,0:T(8,128)(2,1)S(1)} %collective-permute-done.6.refs_6_), channel_id=1, source_target_pairs={{0,4},{4,0},{1,5},{5,1},{2,6},{6,2},{3,7},{7,3},{8,12},{12,8},{9,1... | collective-permute-start | bytes 786440 | tf_op jit(solution)/shard_map/ppermute | solution.py:64
  34.8 0.9 copy-start
  35.8 6.9 %copy-start.3 = (bf16[64,2048]{1,0:T(8,128)(2,1)S(1)}, bf16[64,2048]{1,0:T(8,128)(2,1)}, u32[]{:S(2)}) copy-start(bf16[64,2048]{1,0:T(8,128)(2,1)} %refs_9_.1) | copy-start | bytes 786436
  35.8 6.9 %copy-start.5 = (f32[2048]{0:T(1024)S(1)}, f32[2048]{0:T(1024)}, u32[]{:S(2)}) copy-start(f32[2048]{0:T(1024)} %param.14) | copy-start | bytes 24580
  53.9 1.4 collective-permute-start.8
  55.4 4.8 %collective-permute-start.11 = (f32[64,512]{1,0:T(8,128)S(1)}, f32[64,512]{1,0:T(8,128)S(1)}, u32[]{:S(2)}, u32[]{:S(2)}) collective-permute-start(f32[64,512]{1,0:T(8,128)S(1)} %add.39), channel_id=1, source_target_pairs={{0,3},{1,0},{2,1},{3,2},{4,7},{5,4},{6,5},{7,6},{8,11},{9,8},{10,9... | collective-permute-start | bytes 393224 | tf_op jit(solution)/shard_map/ppermute | solution.py:64
  57.1 6.0 %collective-permute-start.10 = (f32[64,512]{1,0:T(8,128)S(1)}, f32[64,512]{1,0:T(8,128)S(1)}, u32[]{:S(2)}, u32[]{:S(2)}) collective-permute-start(f32[64,512]{1,0:T(8,128)S(1)} %add.39), channel_id=1, source_target_pairs={{0,2},{1,3},{2,0},{3,1},{4,6},{5,7},{6,4},{7,5},{8,10},{9,11},{10,... | collective-permute-start | bytes 393224 | tf_op jit(solution)/shard_map/ppermute | solution.py:64
  57.9 9.0 %collective-permute-start.9 = (f32[64,512]{1,0:T(8,128)S(1)}, f32[64,512]{1,0:T(8,128)S(1)}, u32[]{:S(2)}, u32[]{:S(2)}) collective-permute-start(f32[64,512]{1,0:T(8,128)S(1)} %add.39), channel_id=1, source_target_pairs={{0,1},{1,2},{2,3},{3,0},{4,5},{5,6},{6,7},{7,4},{8,9},{9,10},{10,1... | collective-permute-start | bytes 393224 | tf_op jit(solution)/shard_map/ppermute | solution.py:64
  67.5 1.8 %collective-permute-start.12 = (f32[64,512]{1,0:T(8,128)S(1)}, f32[64,512]{1,0:T(8,128)S(1)}, u32[]{:S(2)}, u32[]{:S(2)}) collective-permute-start(f32[64,512]{1,0:T(8,128)S(1)} %pad_maximum_fusion.error_own), channel_id=1, source_target_pairs={{0,4},{4,0},{1,5},{5,1},{2,6},{6,2},{3,7},{7,3},{8,12},{12,8},{9,1... | collective-permute-start | bytes 393224 | tf_op jit(solution)/shard_map/ppermute | solution.py:64
  77.7 12.3 %collective-permute-start.13 = (bf16[400,512]{1,0:T(8,128)(2,1)S(1)}, bf16[400,512]{1,0:T(8,128)(2,1)S(1)}, u32[]{:S(2)}, u32[]{:S(2)}) collective-permute-start(bf16[400,512]{1,0:T(8,128)(2,1)S(1)} %get-tuple-element.57), channel_id=1, source_target_pairs={{0,16},{8,24},{16,0},{24,8},{1,17},{9,25},{17,1},{25,9},{2,18},{10... | collective-permute-start | bytes 1228808 | tf_op jit(solution)/shard_map/ppermute | solution.py:64
  78.8 12.1 %collective-permute-start.14 = (bf16[400,512]{1,0:T(8,128)(2,1)S(1)}, bf16[400,512]{1,0:T(8,128)(2,1)S(1)}, u32[]{:S(2)}, u32[]{:S(2)}) collective-permute-start(bf16[400,512]{1,0:T(8,128)(2,1)S(1)} %get-tuple-element.58), channel_id=1, source_target_pairs={{0,64},{32,96},{64,0},{96,32},{1,65},{33,97},{65,1},{97,33},{2,66}... | collective-permute-start | bytes 1228808 | tf_op jit(solution)/shard_map/ppermute | solution.py:64
  81.0 18.5 %collective-permute-start.15 = (bf16[400,512]{1,0:T(8,128)(2,1)S(1)}, bf16[400,512]{1,0:T(8,128)(2,1)S(1)}, u32[]{:S(2)}, u32[]{:S(2)}) collective-permute-start(bf16[400,512]{1,0:T(8,128)(2,1)S(1)} %get-tuple-element.59), channel_id=1, source_target_pairs={{0,8},{8,16},{16,24},{24,0},{1,9},{9,17},{17,25},{25,1},{2,10},{10... | collective-permute-start | bytes 1228808 | tf_op jit(solution)/shard_map/ppermute | solution.py:64
  81.3 19.2 %collective-permute-start.16 = (bf16[400,512]{1,0:T(8,128)(2,1)S(1)}, bf16[400,512]{1,0:T(8,128)(2,1)S(1)}, u32[]{:S(2)}, u32[]{:S(2)}) collective-permute-start(bf16[400,512]{1,0:T(8,128)(2,1)S(1)} %get-tuple-element.60), channel_id=1, source_target_pairs={{0,32},{32,64},{64,96},{96,0},{1,33},{33,65},{65,97},{97,1},{2,34}... | collective-permute-start | bytes 1228808 | tf_op jit(solution)/shard_map/ppermute | solution.py:64
  81.7 18.8 %collective-permute-start.17 = (bf16[400,512]{1,0:T(8,128)(2,1)S(1)}, bf16[400,512]{1,0:T(8,128)(2,1)S(1)}, u32[]{:S(2)}, u32[]{:S(2)}) collective-permute-start(bf16[400,512]{1,0:T(8,128)(2,1)S(1)} %get-tuple-element.61), channel_id=1, source_target_pairs={{0,24},{8,0},{16,8},{24,16},{1,25},{9,1},{17,9},{25,17},{2,26},{10... | collective-permute-start | bytes 1228808 | tf_op jit(solution)/shard_map/ppermute | solution.py:64
  90.1 10.5 %collective-permute-start.18 = (bf16[400,512]{1,0:T(8,128)(2,1)S(1)}, bf16[400,512]{1,0:T(8,128)(2,1)S(1)}, u32[]{:S(2)}, u32[]{:S(2)}) collective-permute-start(bf16[400,512]{1,0:T(8,128)(2,1)S(1)} %get-tuple-element.62), channel_id=1, source_target_pairs={{0,96},{32,0},{64,32},{96,64},{1,97},{33,1},{65,33},{97,65},{2,98}... | collective-permute-start | bytes 1228808 | tf_op jit(solution)/shard_map/ppermute | solution.py:64
  102.0 6.4 %collective-permute-start.19 = (bf16[448,128]{1,0:T(8,128)(2,1)S(1)}, bf16[448,128]{1,0:T(8,128)(2,1)S(1)}, u32[]{:S(2)}, u32[]{:S(2)}) collective-permute-start(bf16[448,128]{1,0:T(8,128)(2,1)S(1)} %get-tuple-element.65), channel_id=1, source_target_pairs={{0,64},{32,96},{64,0},{96,32},{1,65},{33,97},{65,1},{97,33},{2,66}... | collective-permute-start | bytes 344072 | tf_op jit(solution)/shard_map/ppermute | solution.py:64
  103.6 6.7 %collective-permute-start.20 = (bf16[448,128]{1,0:T(8,128)(2,1)S(1)}, bf16[448,128]{1,0:T(8,128)(2,1)S(1)}, u32[]{:S(2)}, u32[]{:S(2)}) collective-permute-start(bf16[448,128]{1,0:T(8,128)(2,1)S(1)} %get-tuple-element.66), channel_id=1, source_target_pairs={{0,16},{8,24},{16,0},{24,8},{1,17},{9,25},{17,1},{25,9},{2,18},{10... | collective-permute-start | bytes 344072 | tf_op jit(solution)/shard_map/ppermute | solution.py:64
  104.9 6.0 %collective-permute-start.21 = (bf16[448,128]{1,0:T(8,128)(2,1)S(1)}, bf16[448,128]{1,0:T(8,128)(2,1)S(1)}, u32[]{:S(2)}, u32[]{:S(2)}) collective-permute-start(bf16[448,128]{1,0:T(8,128)(2,1)S(1)} %get-tuple-element.67), channel_id=1, source_target_pairs={{0,32},{32,64},{64,96},{96,0},{1,33},{33,65},{65,97},{97,1},{2,34}... | collective-permute-start | bytes 344072 | tf_op jit(solution)/shard_map/ppermute | solution.py:64
  105.4 6.3 %collective-permute-start.22 = (bf16[448,128]{1,0:T(8,128)(2,1)S(1)}, bf16[448,128]{1,0:T(8,128)(2,1)S(1)}, u32[]{:S(2)}, u32[]{:S(2)}) collective-permute-start(bf16[448,128]{1,0:T(8,128)(2,1)S(1)} %get-tuple-element.68), channel_id=1, source_target_pairs={{0,8},{8,16},{16,24},{24,0},{1,9},{9,17},{17,25},{25,1},{2,10},{10... | collective-permute-start | bytes 344072 | tf_op jit(solution)/shard_map/ppermute | solution.py:64
  105.7 6.0 %collective-permute-start.23 = (bf16[448,128]{1,0:T(8,128)(2,1)S(1)}, bf16[448,128]{1,0:T(8,128)(2,1)S(1)}, u32[]{:S(2)}, u32[]{:S(2)}) collective-permute-start(bf16[448,128]{1,0:T(8,128)(2,1)S(1)} %get-tuple-element.69), channel_id=1, source_target_pairs={{0,96},{32,0},{64,32},{96,64},{1,97},{33,1},{65,33},{97,65},{2,98}... | collective-permute-start | bytes 344072 | tf_op jit(solution)/shard_map/ppermute | solution.py:64
  108.4 3.9 %collective-permute-start.24 = (bf16[448,128]{1,0:T(8,128)(2,1)S(1)}, bf16[448,128]{1,0:T(8,128)(2,1)S(1)}, u32[]{:S(2)}, u32[]{:S(2)}) collective-permute-start(bf16[448,128]{1,0:T(8,128)(2,1)S(1)} %get-tuple-element.70), channel_id=1, source_target_pairs={{0,24},{8,0},{16,8},{24,16},{1,25},{9,1},{17,9},{25,17},{2,26},{10... | collective-permute-start | bytes 344072 | tf_op jit(solution)/shard_map/ppermute | solution.py:64
  112.5 7.0 %collective-permute-start.29 = (bf16[3,128,128]{2,1,0:T(8,128)(2,1)S(1)}, bf16[3,128,128]{2,1,0:T(8,128)(2,1)S(1)}, u32[]{:S(2)}, u32[]{:S(2)}) collective-permute-start(bf16[3,128,128]{2,1,0:T(8,128)(2,1)S(1)} %get-tuple-element.73.refs_6_), channel_id=1, source_target_pairs={{0,64},{32,96},{64,0},{96,32},{1,65},{33,97},{65,1},{97,33},{2,66}... | collective-permute-start | bytes 294920 | tf_op jit(solution)/shard_map/ppermute | solution.py:64
  113.4 7.1 %collective-permute-start.27 = (bf16[3,128,128]{2,1,0:T(8,128)(2,1)S(1)}, bf16[3,128,128]{2,1,0:T(8,128)(2,1)S(1)}, u32[]{:S(2)}, u32[]{:S(2)}) collective-permute-start(bf16[3,128,128]{2,1,0:T(8,128)(2,1)S(1)} %get-tuple-element.73.refs_6_), channel_id=1, source_target_pairs={{0,32},{32,64},{64,96},{96,0},{1,33},{33,65},{65,97},{97,1},{2,34}... | collective-permute-start | bytes 294920 | tf_op jit(solution)/shard_map/ppermute | solution.py:64
  114.1 6.4 %collective-permute-start.25 = (bf16[3,128,128]{2,1,0:T(8,128)(2,1)S(1)}, bf16[3,128,128]{2,1,0:T(8,128)(2,1)S(1)}, u32[]{:S(2)}, u32[]{:S(2)}) collective-permute-start(bf16[3,128,128]{2,1,0:T(8,128)(2,1)S(1)} %get-tuple-element.73.refs_6_), channel_id=1, source_target_pairs={{0,96},{32,0},{64,32},{96,64},{1,97},{33,1},{65,33},{97,65},{2,98}... | collective-permute-start | bytes 294920 | tf_op jit(solution)/shard_map/ppermute | solution.py:64
  116.0 5.3 %collective-permute-start.30 = (bf16[3,128,128]{2,1,0:T(8,128)(2,1)S(1)}, bf16[3,128,128]{2,1,0:T(8,128)(2,1)S(1)}, u32[]{:S(2)}, u32[]{:S(2)}) collective-permute-start(bf16[3,128,128]{2,1,0:T(8,128)(2,1)S(1)} %get-tuple-element.74.refs_7_), channel_id=1, source_target_pairs={{0,16},{8,24},{16,0},{24,8},{1,17},{9,25},{17,1},{25,9},{2,18},{10... | collective-permute-start | bytes 294920 | tf_op jit(solution)/shard_map/ppermute | solution.py:64
  117.8 5.0 %collective-permute-start.28 = (bf16[3,128,128]{2,1,0:T(8,128)(2,1)S(1)}, bf16[3,128,128]{2,1,0:T(8,128)(2,1)S(1)}, u32[]{:S(2)}, u32[]{:S(2)}) collective-permute-start(bf16[3,128,128]{2,1,0:T(8,128)(2,1)S(1)} %get-tuple-element.74.refs_7_), channel_id=1, source_target_pairs={{0,8},{8,16},{16,24},{24,0},{1,9},{9,17},{17,25},{25,1},{2,10},{10... | collective-permute-start | bytes 294920 | tf_op jit(solution)/shard_map/ppermute | solution.py:64
  119.5 3.6 %collective-permute-start.26 = (bf16[3,128,128]{2,1,0:T(8,128)(2,1)S(1)}, bf16[3,128,128]{2,1,0:T(8,128)(2,1)S(1)}, u32[]{:S(2)}, u32[]{:S(2)}) collective-permute-start(bf16[3,128,128]{2,1,0:T(8,128)(2,1)S(1)} %get-tuple-element.74.refs_7_), channel_id=1, source_target_pairs={{0,24},{8,0},{16,8},{24,16},{1,25},{9,1},{17,9},{25,17},{2,26},{10... | collective-permute-start | bytes 294920 | tf_op jit(solution)/shard_map/ppermute | solution.py:64
  123.2 8.6 %collective-permute-start.36 = (bf16[4,3,128,128]{3,2,1,0:T(8,128)(2,1)S(1)}, bf16[4,3,128,128]{3,2,1,0:T(8,128)(2,1)S(1)}, u32[]{:S(2)}, u32[]{:S(2)}) collective-permute-start(bf16[4,3,128,128]{3,2,1,0:T(8,128)(2,1)S(1)} %get-tuple-element.76.line), channel_id=1, source_target_pairs={{0,16},{8,24},{16,0},{24,8},{1,17},{9,25},{17,1},{25,9},{2,18},{10... | collective-permute-start | bytes 1179656 | tf_op jit(solution)/shard_map/ppermute | solution.py:64
  124.6 11.5 %collective-permute-start.35 = (bf16[4,3,128,128]{3,2,1,0:T(8,128)(2,1)S(1)}, bf16[4,3,128,128]{3,2,1,0:T(8,128)(2,1)S(1)}, u32[]{:S(2)}, u32[]{:S(2)}) collective-permute-start(bf16[4,3,128,128]{3,2,1,0:T(8,128)(2,1)S(1)} %get-tuple-element.76.line), channel_id=1, source_target_pairs={{0,8},{8,16},{16,24},{24,0},{1,9},{9,17},{17,25},{25,1},{2,10},{10... | collective-permute-start | bytes 1179656 | tf_op jit(solution)/shard_map/ppermute | solution.py:64
  126.1 10.4 %collective-permute-start.34 = (bf16[4,3,128,128]{3,2,1,0:T(8,128)(2,1)S(1)}, bf16[4,3,128,128]{3,2,1,0:T(8,128)(2,1)S(1)}, u32[]{:S(2)}, u32[]{:S(2)}) collective-permute-start(bf16[4,3,128,128]{3,2,1,0:T(8,128)(2,1)S(1)} %get-tuple-element.76.line), channel_id=1, source_target_pairs={{0,24},{8,0},{16,8},{24,16},{1,25},{9,1},{17,9},{25,17},{2,26},{10... | collective-permute-start | bytes 1179656 | tf_op jit(solution)/shard_map/ppermute | solution.py:64
  127.3 23.9 %collective-permute-start.33 = (bf16[4,3,128,128]{3,2,1,0:T(8,128)(2,1)S(1)}, bf16[4,3,128,128]{3,2,1,0:T(8,128)(2,1)S(1)}, u32[]{:S(2)}, u32[]{:S(2)}) collective-permute-start(bf16[4,3,128,128]{3,2,1,0:T(8,128)(2,1)S(1)} %get-tuple-element.75.refs_1_.refs_3_), channel_id=1, source_target_pairs={{0,64},{32,96},{64,0},{96,32},{1,65},{33,97},{65,1},{97,33},{2,66}... | collective-permute-start | bytes 1179656 | tf_op jit(solution)/shard_map/ppermute | solution.py:64
  128.3 22.8 %collective-permute-start.32 = (bf16[4,3,128,128]{3,2,1,0:T(8,128)(2,1)S(1)}, bf16[4,3,128,128]{3,2,1,0:T(8,128)(2,1)S(1)}, u32[]{:S(2)}, u32[]{:S(2)}) collective-permute-start(bf16[4,3,128,128]{3,2,1,0:T(8,128)(2,1)S(1)} %get-tuple-element.75.refs_1_.refs_3_), channel_id=1, source_target_pairs={{0,32},{32,64},{64,96},{96,0},{1,33},{33,65},{65,97},{97,1},{2,34}... | collective-permute-start | bytes 1179656 | tf_op jit(solution)/shard_map/ppermute | solution.py:64
  131.9 19.3 %collective-permute-start.31 = (bf16[4,3,128,128]{3,2,1,0:T(8,128)(2,1)S(1)}, bf16[4,3,128,128]{3,2,1,0:T(8,128)(2,1)S(1)}, u32[]{:S(2)}, u32[]{:S(2)}) collective-permute-start(bf16[4,3,128,128]{3,2,1,0:T(8,128)(2,1)S(1)} %get-tuple-element.75.refs_1_.refs_3_), channel_id=1, source_target_pairs={{0,96},{32,0},{64,32},{96,64},{1,97},{33,1},{65,33},{97,65},{2,98}... | collective-permute-start | bytes 1179656 | tf_op jit(solution)/shard_map/ppermute | solution.py:64
  136.7 15.3 %collective-permute-start.38 = (bf16[5,4,3,128,128]{4,3,2,1,0:T(8,128)(2,1)S(1)}, bf16[5,4,3,128,128]{4,3,2,1,0:T(8,128)(2,1)}, u32[]{:S(2)}, u32[]{:S(2)}) collective-permute-start(bf16[5,4,3,128,128]{4,3,2,1,0:T(8,128)(2,1)S(1)} %shard_map.121.refs_0_.refs_1_), channel_id=1, source_target_pairs={{0,4},{4,0},{1,5},{5,1},{2,6},{6,2},{3,7},{7,3},{8,12},{12,8},{9,1... | collective-permute-start | bytes 5898248 | tf_op jit(solution)/shard_map/ppermute | solution.py:64
  151.3 8.2 %collective-permute-start.37 = (bf16[4,4,3,128,128]{4,3,2,1,0:T(8,128)(2,1)S(1)}, bf16[4,4,3,128,128]{4,3,2,1,0:T(8,128)(2,1)}, u32[]{:S(2)}, u32[]{:S(2)}) collective-permute-start(bf16[4,4,3,128,128]{4,3,2,1,0:T(8,128)(2,1)S(1)} %shard_map.123.refs_2_), channel_id=1, source_target_pairs={{0,4},{4,0},{1,5},{5,1},{2,6},{6,2},{3,7},{7,3},{8,12},{12,8},{9,1... | collective-permute-start | bytes 4718600 | tf_op jit(solution)/shard_map/ppermute | solution.py:64
  152.1 1.0 copy-start.1

commit v6 on v5

--- a/solution.py
+++ b/solution.py
@@ -68,7 +68,7 @@
     return jax.ShapeDtypeStruct(dims, kind)
 
 
-def bucket_kernel(rows_far, dest_far, out, rows, dest_row, sems):
+def bucket_kernel(rows_far, dest_far, unused, out, rows, dest_row, sems):
     loads = [
         pltpu.make_async_copy(rows_far, rows, sems.at[0]),
         pltpu.make_async_copy(dest_far, dest_row, sems.at[1]),
@@ -86,7 +86,10 @@
     hot = jnp.where(lax.broadcasted_iota(jnp.int32, (256, 128), 0) == slot, 1.0, 0.0)
     used = jnp.max(hot, axis=1, keepdims=True)
     moved = dot(hot.astype(bf16), rows[...]) + (1.0 - used) * UNUSED
-    out[...] = moved.astype(bf16).reshape(16, 16, 128)
+    bucket = moved.astype(bf16).reshape(16, 16, 128)
+    for frame in range(4):
+        for core in range(2):
+            out[frame, :, core] = bucket
 
 
 def prepare_kernel(place, w, w_out, head_t, w_t, mix, mix_t, held, out_rows, turned, sems, leave):
@@ -112,28 +115,21 @@
         store.wait()
 
 
-def sides_kernel(time, before, after, arrived, top, bottom, both, spread):
-    column = lax.broadcasted_iota(jnp.int32, (16, 128), 1)
+def sides_kernel(time, before, across, after, unused, both):
+    both[:128] = before[...]
+    both[128:256] = after[...]
+    both[256:384] = across[...]
+    column = lax.broadcasted_iota(jnp.int32, (16, 2048), 1)
     digits = jnp.where(column == 0, time[0] // 32, jnp.where(column == 1, time[0] % 32, 0))
-    top[...] = before[:64]
-    bottom[...] = after[64:]
-    both[0] = before[...]
-    both[1] = after[...]
-    for k in range(8):
-        spread[k, :256] = arrived[...]
-        spread[k, 256:] = digits.astype(f32).astype(bf16)
-
-
-def fetch_kernel(place, arrived, pairs, moments):
+    both[384:] = digits.astype(f32).astype(bf16)
+
+
+def fetch_kernel(place, arrived, pairs):
     frame, core = place[0], place[1]
     slots = 512
-
-    def order_of(i):
-        return ((i % 256) // 16) * 32 + (i // 256) * 16 + i % 16
-
     before = jnp.where(
-        order_of(lax.broadcasted_iota(jnp.int32, (slots, slots), 0))
-        < order_of(lax.broadcasted_iota(jnp.int32, (slots, slots), 1)),
+        lax.broadcasted_iota(jnp.int32, (slots, slots), 0)
+        < lax.broadcasted_iota(jnp.int32, (slots, slots), 1),
         1.0,
         0.0,
     ).astype(bf16)
@@ -143,8 +139,7 @@
     first = jnp.where(lax.broadcasted_iota(jnp.int32, (16, 128), 1) == 0, 1.0, 0.0).astype(bf16)
     rows, values = [], jnp.zeros((8, slots), f32)
     for i, r in enumerate(ORDER):
-        from_frame = (frame + 4 - r) % 4
-        rows.append(jnp.concatenate([arrived[from_frame, :256], arrived[4 + from_frame, :256]], axis=0))
+        rows.append(arrived[(frame + 4 - r) % 4])
         values = jnp.where(which // 2 == i, dot(first, rows[i], NT)[:8], values)
     mine = jnp.where((values < 32.0) & (half == clip), 1.0, 0.0)
     doubled = jnp.concatenate([mine, mine], axis=0).astype(bf16)
@@ -153,40 +148,43 @@
     for b in range(8):
         pick = jnp.where(rank[b : b + 1] == line, 1.0, 0.0).astype(bf16)
         pairs[b] = dot(pick, rows[b // 2]).astype(bf16)
-    for other in range(2):
-        digits = arrived[(core + other - 2 * core * other) * 4 + frame, 256:].astype(f32)
-        time = digits[:, 0:1] * 32.0 + digits[:, 1:2]
-        moments[other] = jnp.broadcast_to((time + 0.5) / TIMESTEPS, (16, 128))
 
 
 def lanes(i, other):
     return slice((2 * i + other) * 128, (2 * i + other) * 128 + 128)
 
 
-def forward_kernel(moments, *refs):
-    act_own, act_theirs, sides, sides_theirs, top, top_theirs, bottom, bottom_theirs = refs[:8]
-    pairs, w_embed, gain, w_t_far, head_t, mix_t = refs[8:14]
-    normed_far, proj_far, probs, part_own, part_other = refs[14:19]
-    act, w_t, normed, proj, rest, sems, arrive = refs[19:]
+def forward_kernel(act_own, act_theirs, sides, sides_theirs, *refs):
+    pairs, w_embed, gain, w_t_far, head_t, mix_t = refs[:6]
+    normed_far, proj_far, probs, part_own, part_other = refs[6:11]
+    act, w_t, normed, proj, rest, digits, sems, arrive = refs[11:]
     attended = proj.at[768:1024]
-    whole, low, high = pl.ds(0, 128), pl.ds(0, 64), pl.ds(64, 64)
-    moves = [(act_own, 0, whole), (act_theirs, 1, whole)]
-    for side in range(2):
-        moves += [(sides.at[side], 2 + 2 * side, whole), (sides_theirs.at[side], 3 + 2 * side, whole)]
-    moves += [(top, 6, low), (bottom, 6, high), (top_theirs, 7, low), (bottom_theirs, 7, high)]
-    loads = [[] for _ in range(8)]
-    for k, (source, b, rows) in enumerate(moves):
-        loads[b].append(pltpu.make_async_copy(source, act.at[b, rows], arrive.at[k]))
-        loads[b][-1].start()
+    loads = []
+    for i in range(4):
+        for other, (first, later) in enumerate(((act_own, sides), (act_theirs, sides_theirs))):
+            source = first if i == 0 else later.at[pl.ds((i - 1) * 128, 128)]
+            loads.append(pltpu.make_async_copy(source, act.at[2 * i + other], arrive.at[2 * i + other]))
+            loads[-1].start()
+    times = [
+        pltpu.make_async_copy(source.at[pl.ds(384, 16), pl.ds(0, 128)], digits.at[k], arrive.at[8 + k])
+        for k, source in enumerate((sides, sides_theirs))
+    ]
+    for time in times:
+        time.start()
     weights = pltpu.make_async_copy(w_t_far, w_t, sems.at[0])
     weights.start()
+    moments = []
+    for k, time in enumerate(times):
+        time.wait()
+        pair_of = digits[k].astype(f32)
+        index = pair_of[0:1, 0:1] * 32.0 + pair_of[0:1, 1:2]
+        moments.append(jnp.broadcast_to((index + 0.5) / TIMESTEPS, (128, 64)))
     for b in range(8):
         pair = pairs[b].astype(f32)
-        t = moments[b % 2, 0:1, :64]
+        t = moments[b % 2]
         noised = ((1.0 - t) * pair[:, :64] + t * pair[:, 64:]).astype(bf16)
         added = dot(noised, w_embed[...])
-        for load in loads[b]:
-            load.wait()
+        loads[b].wait()
         hidden = act[b].astype(f32) + added
         scale = lax.rsqrt(jnp.mean(hidden * hidden, axis=1, keepdims=True) + 1e-06)
         normed[b * 128 : b * 128 + 128] = (hidden * scale * gain[...]).astype(bf16)
@@ -343,12 +341,13 @@
     count = len(tags)
     sources, refs = refs[:arrays], refs[arrays + aliased :]
     if with_out:
-        head_t, out, token, grad_out, held, ready, done, sems, whole, sent, factors = refs
-        fetched = []
+        head_far, out, token, grad_out, held, ready, done, sems, whole, sent, factors, head_t = refs
+        fetched = [pltpu.make_async_copy(head_far, head_t, sent.at[3])]
+        fetched[0].start()
         for k, core in ((0, 1 - place[2]), (1, place[2])):
             target = factors.at[pl.ds(core * 2, 2)]
             fetched.append(pltpu.make_async_copy(sources[k].at[4, 0, 0:2], target, sent.at[1 + k]))
-            fetched[k].start()
+            fetched[k + 1].start()
     else:
         out, token, held, ready, done, sems = refs
     token[...] = jnp.zeros((8, 128), f32)
@@ -406,10 +405,11 @@
     if product:
         out_shape.append(shape((512, 2048), f32))
         out_specs.append(HBM)
-        scratch += [pltpu.VMEM((512, 2048), f32), dma((3,)), pltpu.VMEM((4, 128, 128), bf16)]
+        scratch += [pltpu.VMEM((512, 2048), f32), dma((4,)), pltpu.VMEM((4, 128, 128), bf16)]
+        scratch.append(pltpu.VMEM((64, 2048), bf16))
     return pl.pallas_call(
         functools.partial(assemble_kernel, tags, len(arrays), len(given), bool(product)),
-        in_specs=[SMEM] + [ANY] * len(arrays) + [HBM] * len(given) + [VMEM] * len(product),
+        in_specs=[SMEM] + [ANY] * len(arrays) + [HBM] * (len(given) + len(product)),
         out_specs=out_specs,
         out_shape=out_shape,
         scratch_shapes=scratch,
@@ -446,23 +446,8 @@
     square = (SMEM, jnp.stack([x, y, core]))
     dma = pltpu.SemaphoreType.DMA
 
-    before, after = shift(act, "frame", 1), shift(act, "frame", 3)
+    before, after, across = (shift(act, "frame", o) for o in (1, 3, 2))
     act_theirs = shift(act, "core", 1)
-    (sent,) = call(
-        bucket_kernel, near(shape((16, 16, 128), bf16)), *far(cache_rows, row_dest.reshape(1, 128)),
-        scratch=[pltpu.VMEM((128, 128), bf16), pltpu.VMEM((1, 128), jnp.int32), dma((2,))],
-        mib=LARGE,
-    )
-    arrived = lax.all_to_all(sent, ("y", "x"), 0, 0, tiled=True).reshape(256, 128)
-    half_act = shape((64, 2048), bf16)
-    top, bottom, sides, spread = call(
-        sides_kernel,
-        near(half_act, half_act, shape((2, 128, 2048), bf16), shape((8, 272, 128), bf16)),
-        (SMEM, time_index), *near(before, after, arrived),
-    )
-    top, bottom = shift(top, "frame", 1), shift(bottom, "frame", 3)
-    sides_theirs = shift(sides, "core", 1)
-    arrived = lax.all_to_all(spread, ("core", "frame"), 0, 0, tiled=True)
     head_t = w_head.T
     w_t, mix, mix_t = call(
         prepare_kernel,
@@ -477,15 +462,25 @@
         ],
         mib=LARGE,
     )
-    pairs, moments = call(
-        fetch_kernel, near(shape((8, 128, 128), bf16), shape((2, 16, 128), f32)), here, *near(arrived)
-    )
+    (sent,) = call(
+        bucket_kernel, near(shape((4, 16, 2, 16, 128), bf16)),
+        *far(cache_rows, row_dest.reshape(1, 128)), (ANY, mix),
+        scratch=[pltpu.VMEM((128, 128), bf16), pltpu.VMEM((1, 128), jnp.int32), dma((2,))],
+        mib=LARGE,
+    )
+    arrived = lax.all_to_all(
+        sent.reshape(128, 16, 128), ("frame", "y", "x", "core"), 0, 0, tiled=True
+    ).reshape(4, 512, 128)
+    (sides,) = call(
+        sides_kernel, near(shape((400, 2048), bf16)), (SMEM, time_index), *near(before, across, after), (ANY, arrived)
+    )
+    sides_theirs = shift(sides, "core", 1)
+    (pairs,) = call(fetch_kernel, near(shape((8, 128, 128), bf16)), here, *near(arrived))
     normed, proj, probs, part_own, part_other = call(
         forward_kernel,
         far(shape((1024, 2048), bf16), shape((1024, 1024), bf16))
         + near(shape((4, 16, 128), f32), shape((64, 512), f32), shape((64, 512), f32)),
-        *near(moments),
-        *far(act, act_theirs, sides, sides_theirs, top, shift(top, "core", 1), bottom, shift(bottom, "core", 1)),
+        *((ANY, a) for a in (act, act_theirs, sides, sides_theirs)),
         *near(pairs, w_embed, norm_gain.reshape(1, 2048)), *far(w_t), *near(head_t, mix_t),
         scratch=[
             pltpu.VMEM((8, 128, 2048), bf16),
@@ -493,6 +488,7 @@
             pltpu.VMEM((1024, 2048), bf16),
             pltpu.VMEM((1024, 1024), bf16),
             pltpu.VMEM((64, 128), f32),
+            pltpu.VMEM((2, 16, 128), bf16),
             dma((4,)),
             dma((10,)),
         ],

time: 165 us -> 167 us (1.012)
  waiting for transfers between devices: 47.8 us -> 51.3 us
    all_to_all x2 -> x1, waiting for transfers between devices: 7.64 us -> 13 us  [shards(): lax.all_to_all(sent.reshape(128, 16, 128), ('frame', 'y', 'x', 'core'), 0...]
    all_to_all x2 -> x1, starting transfers between devices: 11 us -> 8.04 us  [shards(): lax.all_to_all(sent.reshape(128, 16, 128), ('frame', 'y', 'x', 'core'), 0...]
    ppermute x39 -> x36, starting transfers between devices: 55.7 us -> 57.7 us  [shift(): lax.ppermute(value, axis, [(i, (i + offset) % size) for i in range(size)])]
    ppermute x39 -> x36, waiting for transfers between devices: 40.2 us -> 38.3 us  [shift(): lax.ppermute(value, axis, [(i, (i + offset) % size) for i in range(size)])]
  transfers between devices with their start and end apart: 41 -> 37, of which waited for: 20 -> 18; matrix products, arithmetic and copies ran while one was open for 0% -> 0% of each run, Pallas kernels for 10% -> 10%
where the time goes in v6:
time: 167 us
  starting transfers between devices  65.7 us (39%)
  waiting for transfers between devices  51.3 us (31%)
  Pallas kernels  42.2 us (25%)
  between operations  3.42 us (2%)
  local copies, waits for them, and re-layouts  3.27 us (2%)
    ppermute x36, starting transfers between devices, shift(): lax.ppermute(value, axis, [(i, (i + offset) % size) for i in range(size)])  57.7 us
    ppermute x36, waiting for transfers between devices, shift(): lax.ppermute(value, axis, [(i, (i + offset) % size) for i in range(size)])  38.3 us
    pallas_call x11, Pallas kernels, call(): pl.pallas_call(kernel, in_specs=[spec for spec, _ in operands], out_specs...  28.2 us
    pallas_call x3, Pallas kernels, assemble(): pl.pallas_call(functools.partial(assemble_kernel, tags, len(arrays), len(...  14 us
    all_to_all x1, waiting for transfers between devices, shards(): lax.all_to_all(sent.reshape(128, 16, 128), ('frame', 'y', 'x', 'core'), 0...  13 us
    all_to_all x1, starting transfers between devices, shards(): lax.all_to_all(sent.reshape(128, 16, 128), ('frame', 'y', 'x', 'core'), 0...  8.04 us
  transfers between devices with their start and end apart: 37, of which 18 were waited for; matrix products, arithmetic and copies ran while one was open for 0% of the time, Pallas kernels for 10%

profile of v6, /device:TPU:1, one launch (start us, length us, event | category | flops | bytes accessed | tf_op | source)
XLA Modules:
  0.0 166.8 jit_solution(15561056618312701527)
XLA Ops:
  0.6 4.5 %collective-permute-start.2 = (bf16[128,2048]{1,0:T(8,128)(2,1)}, bf16[128,2048]{1,0:T(8,128)(2,1)S(1)}, u32[]{:S(2)}, u32[]{:S(2)}) collective-permute-start(bf16[128,2048]{1,0:T(8,128)(2,1)} %act_own.1), channel_id=1, source_target_pairs={{0,2},{1,3},{2,0},{3,1},{4,6},{5,7},{6,4},{7,5},{8,10},{9,11},{10,... | collective-permute-start | bytes 1572872 | tf_op jit(solution)/shard_map/ppermute | solution.py:64
  5.9 1.9 %collective-permute-start.3 = (bf16[128,2048]{1,0:T(8,128)(2,1)}, bf16[128,2048]{1,0:T(8,128)(2,1)S(1)}, u32[]{:S(2)}, u32[]{:S(2)}) collective-permute-start(bf16[128,2048]{1,0:T(8,128)(2,1)} %act_own.1), channel_id=1, source_target_pairs={{0,3},{1,0},{2,1},{3,2},{4,7},{5,4},{6,5},{7,6},{8,11},{9,8},{10,9... | collective-permute-start | bytes 1572872 | tf_op jit(solution)/shard_map/ppermute | solution.py:64
  7.9 0.9 copy-done.1
  8.8 3.7 %shard_map.112 = (bf16[768,2048]{1,0:T(8,128)(2,1)}, f32[256,64]{1,0:T(8,128)S(1)}, f32[64,256]{1,0:T(8,128)S(1)}) custom-call(s32[2]{0:T(128)S(1)} %pad_add_fusion.place, bf16[3,2048,512]{2,1,0:T(8,128)(2,1)} %w.1, bf16[512,2048]{1,0:T(8,128)(2,1)} %w_out.1, bf16[64,2048]{1,0:T(8,128)(2,1)S(1)} %bitcast.12), custom_call_target="tpu_custom_call" | custom-call | bytes 1024 | tf_op jit(solution)/shard_map/pallas_call | solution.py:423
  12.6 1.1 shard_map.113
  13.7 8.0 %all-to-all-start = ((bf16[128,16,128]{2,1,0:T(8,128)(2,1)}), bf16[128,16,128]{2,1,0:T(8,128)(2,1)S(1)}, u32[]{:S(2)}, u32[]{:S(2)}) async-start(bf16[128,16,128]{2,1,0:T(8,128)(2,1)} %bitcast.4), calls=%async_computation | async-start | bytes 1048576 | tf_op jit(solution)/shard_map/all_to_all | solution.py:471
  22.5 13.0 %all-to-all-done = bf16[128,16,128]{2,1,0:T(8,128)(2,1)S(1)} async-done(((bf16[128,16,128]{2,1,0:T(8,128)(2,1)}), bf16[128,16,128]{2,1,0:T(8,128)(2,1)S(1)}, u32[]{:S(2)}, u32[]{:S(2)}) %all-to-all-start) | async-done | bytes 524320 | tf_op jit(solution)/shard_map/all_to_all | solution.py:471
  35.7 1.0 collective-permute-start.4
  36.7 1.3 shard_map.115.refs_0_
  38.1 2.4 %collective-permute-done.act_theirs = bf16[128,2048]{1,0:T(8,128)(2,1)S(1)} collective-permute-done((bf16[128,2048]{1,0:T(8,128)(2,1)S(1)}, bf16[128,2048]{1,0:T(8,128)(2,1)S(1)}, u32[]{:S(2)}, u32[]{:S(2)}) %collective-permute-start) | collective-permute-done | bytes 524320 | tf_op jit(solution)/shard_map/ppermute | solution.py:64
  41.8 11.6 %shard_map.116 = (bf16[1024,2048]{1,0:T(8,128)(2,1)}, bf16[1024,1024]{1,0:T(8,128)(2,1)}, f32[4,16,128]{2,1,0:T(8,128)S(1)}, f32[64,512]{1,0:T(8,128)S(1)}, f32[64,512]{1,0:T(8,128)S(1)}) custom-call(bf16[128,2048]{1,0:T(8,128)(2,1)S(1)} %copy-done.4, bf16[128,2048]{1,0:T(8,128)(2,1)} %copy-done.10, bf16[400,2048]{1,0:T(8,128)(2,1)} %copy-done, ...), custom_call_target="tpu_custom_call" | custom-call | bytes 1024 | tf_op jit(solution)/shard_map/pallas_call | solution.py:423
  54.1 1.0 collective-permute-done.5
  55.1 1.9 %collective-permute-start.8 = (f32[64,512]{1,0:T(8,128)S(1)}, f32[64,512]{1,0:T(8,128)S(1)}, u32[]{:S(2)}, u32[]{:S(2)}) collective-permute-start(f32[64,512]{1,0:T(8,128)S(1)} %add.39), channel_id=1, source_target_pairs={{0,3},{1,0},{2,1},{3,2},{4,7},{5,4},{6,5},{7,6},{8,11},{9,8},{10,9... | collective-permute-start | bytes 393224 | tf_op jit(solution)/shard_map/ppermute | solution.py:64
  57.7 2.2 %collective-permute-done.8 = f32[64,512]{1,0:T(8,128)S(1)} collective-permute-done((f32[64,512]{1,0:T(8,128)S(1)}, f32[64,512]{1,0:T(8,128)S(1)}, u32[]{:S(2)}, u32[]{:S(2)}) %collective-permute-start.8) | collective-permute-done | bytes 131104 | tf_op jit(solution)/shard_map/ppermute | solution.py:64
  59.9 3.1 %collective-permute-done.7 = f32[64,512]{1,0:T(8,128)S(1)} collective-permute-done((f32[64,512]{1,0:T(8,128)S(1)}, f32[64,512]{1,0:T(8,128)S(1)}, u32[]{:S(2)}, u32[]{:S(2)}) %collective-permute-start.7) | collective-permute-done | bytes 131104 | tf_op jit(solution)/shard_map/ppermute | solution.py:64
  63.0 3.5 %collective-permute-done.6 = f32[64,512]{1,0:T(8,128)S(1)} collective-permute-done((f32[64,512]{1,0:T(8,128)S(1)}, f32[64,512]{1,0:T(8,128)S(1)}, u32[]{:S(2)}, u32[]{:S(2)}) %collective-permute-start.6) | collective-permute-done | bytes 131104 | tf_op jit(solution)/shard_map/ppermute | solution.py:64
  68.9 8.4 %shard_map.117 = (bf16[400,512]{1,0:T(8,128)(2,1)S(1)}, bf16[400,512]{1,0:T(8,128)(2,1)S(1)}, bf16[400,512]{1,0:T(8,128)(2,1)S(1)}, bf16[400,512]{1,0:T(8,128)(2...) custom-call(s32[3]{0:T(128)S(1)} %pad_add_fusion.1.place, ...), custom_call_target="tpu_custom_call" | custom-call | bytes 1024 | tf_op jit(solution)/shard_map/pallas_call | solution.py:423
  77.3 2.7 %collective-permute-start.10 = (bf16[400,512]{1,0:T(8,128)(2,1)S(1)}, bf16[400,512]{1,0:T(8,128)(2,1)S(1)}, u32[]{:S(2)}, u32[]{:S(2)}) collective-permute-start(bf16[400,512]{1,0:T(8,128)(2,1)S(1)} %get-tuple-element.45), channel_id=1, source_target_pairs={{0,16},{8,24},{16,0},{24,8},{1,17},{9,25},{17,1},{25,9},{2,18},{10... | collective-permute-start | bytes 1228808 | tf_op jit(solution)/shard_map/ppermute | solution.py:64
  80.0 2.9 %collective-permute-start.11 = (bf16[400,512]{1,0:T(8,128)(2,1)S(1)}, bf16[400,512]{1,0:T(8,128)(2,1)S(1)}, u32[]{:S(2)}, u32[]{:S(2)}) collective-permute-start(bf16[400,512]{1,0:T(8,128)(2,1)S(1)} %get-tuple-element.46), channel_id=1, source_target_pairs={{0,64},{32,96},{64,0},{96,32},{1,65},{33,97},{65,1},{97,33},{2,66}... | collective-permute-start | bytes 1228808 | tf_op jit(solution)/shard_map/ppermute | solution.py:64
  83.6 2.4 %collective-permute-start.14 = (bf16[400,512]{1,0:T(8,128)(2,1)S(1)}, bf16[400,512]{1,0:T(8,128)(2,1)S(1)}, u32[]{:S(2)}, u32[]{:S(2)}) collective-permute-start(bf16[400,512]{1,0:T(8,128)(2,1)S(1)} %get-tuple-element.49), channel_id=1, source_target_pairs={{0,24},{8,0},{16,8},{24,16},{1,25},{9,1},{17,9},{25,17},{2,26},{10... | collective-permute-start | bytes 1228808 | tf_op jit(solution)/shard_map/ppermute | solution.py:64
  86.0 3.6 %collective-permute-done.10.refs_0_ = bf16[400,512]{1,0:T(8,128)(2,1)S(1)} collective-permute-done((bf16[400,512]{1,0:T(8,128)(2,1)S(1)}, bf16[400,512]{1,0:T(8,128)(2,1)S(1)}, u32[]{:S(2)}, u32[]{:S(2)}) %collective-permute-start.10) | collective-permute-done | bytes 409632 | tf_op jit(solution)/shard_map/ppermute | solution.py:64
  89.6 2.6 %collective-permute-start.15 = (bf16[400,512]{1,0:T(8,128)(2,1)S(1)}, bf16[400,512]{1,0:T(8,128)(2,1)S(1)}, u32[]{:S(2)}, u32[]{:S(2)}) collective-permute-start(bf16[400,512]{1,0:T(8,128)(2,1)S(1)} %get-tuple-element.50), channel_id=1, source_target_pairs={{0,96},{32,0},{64,32},{96,64},{1,97},{33,1},{65,33},{97,65},{2,98}... | collective-permute-start | bytes 1228808 | tf_op jit(solution)/shard_map/ppermute | solution.py:64
  92.2 6.8 %collective-permute-done.12.refs_2_ = bf16[400,512]{1,0:T(8,128)(2,1)S(1)} collective-permute-done((bf16[400,512]{1,0:T(8,128)(2,1)S(1)}, bf16[400,512]{1,0:T(8,128)(2,1)S(1)}, u32[]{:S(2)}, u32[]{:S(2)}) %collective-permute-start.12) | collective-permute-done | bytes 409632 | tf_op jit(solution)/shard_map/ppermute | solution.py:64
  99.0 2.6 %collective-permute-done.13.refs_3_ = bf16[400,512]{1,0:T(8,128)(2,1)S(1)} collective-permute-done((bf16[400,512]{1,0:T(8,128)(2,1)S(1)}, bf16[400,512]{1,0:T(8,128)(2,1)S(1)}, u32[]{:S(2)}, u32[]{:S(2)}) %collective-permute-start.13) | collective-permute-done | bytes 409632 | tf_op jit(solution)/shard_map/ppermute | solution.py:64
  101.7 1.5 shard_map.118
  103.1 2.0 %collective-permute-start.16 = (bf16[448,128]{1,0:T(8,128)(2,1)S(1)}, bf16[448,128]{1,0:T(8,128)(2,1)S(1)}, u32[]{:S(2)}, u32[]{:S(2)}) collective-permute-start(bf16[448,128]{1,0:T(8,128)(2,1)S(1)} %get-tuple-element.53), channel_id=1, source_target_pairs={{0,64},{32,96},{64,0},{96,32},{1,65},{33,97},{65,1},{97,33},{2,66}... | collective-permute-start | bytes 344072 | tf_op jit(solution)/shard_map/ppermute | solution.py:64
  105.1 1.2 collective-permute-start.17
  106.4 0.9 collective-permute-start.18
  107.6 2.6 %collective-permute-start.20 = (bf16[448,128]{1,0:T(8,128)(2,1)S(1)}, bf16[448,128]{1,0:T(8,128)(2,1)S(1)}, u32[]{:S(2)}, u32[]{:S(2)}) collective-permute-start(bf16[448,128]{1,0:T(8,128)(2,1)S(1)} %get-tuple-element.57), channel_id=1, source_target_pairs={{0,96},{32,0},{64,32},{96,64},{1,97},{33,1},{65,33},{97,65},{2,98}... | collective-permute-start | bytes 344072 | tf_op jit(solution)/shard_map/ppermute | solution.py:64
  110.2 1.5 collective-permute-start.21
  111.7 1.9 %collective-permute-done.19.refs_3_ = bf16[448,128]{1,0:T(8,128)(2,1)S(1)} collective-permute-done((bf16[448,128]{1,0:T(8,128)(2,1)S(1)}, bf16[448,128]{1,0:T(8,128)(2,1)S(1)}, u32[]{:S(2)}, u32[]{:S(2)}) %collective-permute-start.19) | collective-permute-done | bytes 114720 | tf_op jit(solution)/shard_map/ppermute | solution.py:64
  114.5 1.4 collective-permute-start.24
  116.0 1.3 collective-permute-start.22
  117.2 1.6 collective-permute-start.27
  118.8 1.8 %collective-permute-start.25 = (bf16[3,128,128]{2,1,0:T(8,128)(2,1)S(1)}, bf16[3,128,128]{2,1,0:T(8,128)(2,1)S(1)}, u32[]{:S(2)}, u32[]{:S(2)}) collective-permute-start(bf16[3,128,128]{2,1,0:T(8,128)(2,1)S(1)} %get-tuple-element.62.refs_7_), channel_id=1, source_target_pairs={{0,8},{8,16},{16,24},{24,0},{1,9},{9,17},{17,25},{25,1},{2,10},{10... | collective-permute-start | bytes 294920 | tf_op jit(solution)/shard_map/ppermute | solution.py:64
  120.6 1.3 collective-permute-start.23
  122.2 1.6 collective-permute-done.25.refs_3_
  124.4 1.1 collective-permute-start.33
  125.5 2.1 %collective-permute-start.32 = (bf16[4,3,128,128]{3,2,1,0:T(8,128)(2,1)S(1)}, bf16[4,3,128,128]{3,2,1,0:T(8,128)(2,1)S(1)}, u32[]{:S(2)}, u32[]{:S(2)}) collective-permute-start(bf16[4,3,128,128]{3,2,1,0:T(8,128)(2,1)S(1)} %get-tuple-element.64.line), channel_id=1, source_target_pairs={{0,8},{8,16},{16,24},{24,0},{1,9},{9,17},{17,25},{25,1},{2,10},{10... | collective-permute-start | bytes 1179656 | tf_op jit(solution)/shard_map/ppermute | solution.py:64
  128.2 1.1 collective-permute-start.30
  129.9 3.8 %collective-permute-done.33.c = bf16[4,3,128,128]{3,2,1,0:T(8,128)(2,1)S(1)} collective-permute-done((bf16[4,3,128,128]{3,2,1,0:T(8,128)(2,1)S(1)}, bf16[4,3,128,128]{3,2,1,0:T(8,128)(2,1)S(1)}, u32[]{:S(2)}, u32[]{:S(2)}) %collective-permute-start.33) | collective-permute-done | bytes 393248 | tf_op jit(solution)/shard_map/ppermute | solution.py:64
  133.7 1.0 collective-permute-start.28
  134.7 3.0 %collective-permute-done.32.b = bf16[4,3,128,128]{3,2,1,0:T(8,128)(2,1)S(1)} collective-permute-done((bf16[4,3,128,128]{3,2,1,0:T(8,128)(2,1)S(1)}, bf16[4,3,128,128]{3,2,1,0:T(8,128)(2,1)S(1)}, u32[]{:S(2)}, u32[]{:S(2)}) %collective-permute-start.32) | collective-permute-done | bytes 393248 | tf_op jit(solution)/shard_map/ppermute | solution.py:64
  138.3 11.3 %collective-permute-start.35 = (bf16[5,4,3,128,128]{4,3,2,1,0:T(8,128)(2,1)S(1)}, bf16[5,4,3,128,128]{4,3,2,1,0:T(8,128)(2,1)}, u32[]{:S(2)}, u32[]{:S(2)}) collective-permute-start(bf16[5,4,3,128,128]{4,3,2,1,0:T(8,128)(2,1)S(1)} %shard_map.121.refs_0_.refs_1_), channel_id=1, source_target_pairs={{0,4},{4,0},{1,5},{5,1},{2,6},{6,2},{3,7},{7,3},{8,12},{12,8},{9,1... | collective-permute-start | bytes 5898248 | tf_op jit(solution)/shard_map/ppermute | solution.py:64
  149.6 3.5 %shard_map.122 = (f32[3,2048,512]{2,1,0:T(8,128)}, f32[8,128]{1,0:T(8,128)S(1)}) custom-call(s32[3]{0:T(128)S(1)} %pad_add_fusion.1.place, bf16[5,4,3,128,128]{4,3,2,1,0:T(8,128)(2,1)S(1)} %shard_map.121.refs_0_.refs_1_, bf16[4,3,128,128]{3,2,1,0:T(8,128)(2,1)S(1)} %get-tuple-element.63.refs_1_.refs_3_), custom_call_target="tpu_custom_call" | custom-call | bytes 1024 | tf_op jit(solution)/shard_map/pallas_call | solution.py:410
  154.2 0.9 copy-done.3
  155.2 6.5 %shard_map.124 = (f32[3,2048,512]{2,1,0:T(8,128)}, f32[8,128]{1,0:T(8,128)}, f32[512,2048]{1,0:T(8,128)}) custom-call(s32[3]{0:T(128)S(1)} %pad_add_fusion.1.place, bf16[5,4,3,128,128]{4,3,2,1,0:T(8,128)(2,1)} %collective-permute-done.35.refs_0_, bf16[5,4,3,128,128]{4,3,2,1,0:T(8,128)(2,1)S(1)} %shard_map.121.refs_0_.refs_1_, ...), custom_call_target="tpu_custom_call", output_to_operand_aliasing={{0}: (4, {})} | custom-call | bytes 1024 | tf_op jit(solution)/shard_map/pallas_call | solution.py:410
  161.7 3.9 %shard_map.125 = (f32[3,2048,512]{2,1,0:T(8,128)}, f32[8,128]{1,0:T(8,128)}) custom-call(s32[3]{0:T(128)S(1)} %pad_add_fusion.1.place, bf16[4,4,3,128,128]{4,3,2,1,0:T(8,128)(2,1)} %collective-permute-done.34.refs_0_, f32[3,2048,512]{2,1,0:T(8,128)} %get-tuple-element.68.refs_1_), custom_call_target="tpu_custom_call", output_to_operand_aliasing={{0}: (2, {})} | custom-call | bytes 1024 | tf_op jit(solution)/shard_map/pallas_call | solution.py:410
  (67 shorter events, 11.1 us)
Async XLA Ops:
  0.6 34.9 %collective-permute-start.2 = (bf16[128,2048]{1,0:T(8,128)(2,1)}, bf16[128,2048]{1,0:T(8,128)(2,1)S(1)}, u32[]{:S(2)}, u32[]{:S(2)}) collective-permute-start(bf16[128,2048]{1,0:T(8,128)(2,1)} %act_own.1), channel_id=1, source_target_pairs={{0,2},{1,3},{2,0},{3,1},{4,6},{5,7},{6,4},{7,5},{8,10},{9,11},{10,... | collective-permute-start | bytes 1572872 | tf_op jit(solution)/shard_map/ppermute | solution.py:64
  5.1 30.4 %collective-permute-start.1 = (bf16[128,2048]{1,0:T(8,128)(2,1)}, bf16[128,2048]{1,0:T(8,128)(2,1)S(1)}, u32[]{:S(2)}, u32[]{:S(2)}) collective-permute-start(bf16[128,2048]{1,0:T(8,128)(2,1)} %act_own.1), channel_id=1, source_target_pairs={{0,1},{1,2},{2,3},{3,0},{4,5},{5,6},{6,7},{7,4},{8,9},{9,10},{10,1... | collective-permute-start | bytes 1572872 | tf_op jit(solution)/shard_map/ppermute | solution.py:64
  5.9 29.6 %collective-permute-start.3 = (bf16[128,2048]{1,0:T(8,128)(2,1)}, bf16[128,2048]{1,0:T(8,128)(2,1)S(1)}, u32[]{:S(2)}, u32[]{:S(2)}) collective-permute-start(bf16[128,2048]{1,0:T(8,128)(2,1)} %act_own.1), channel_id=1, source_target_pairs={{0,3},{1,0},{2,1},{3,2},{4,7},{5,4},{6,5},{7,6},{8,11},{9,8},{10,9... | collective-permute-start | bytes 1572872 | tf_op jit(solution)/shard_map/ppermute | solution.py:64
  7.9 0.9 copy-start.1
  8.8 3.7 %copy-start.6 = (bf16[128,128]{1,0:T(8,128)(2,1)S(1)}, bf16[128,128]{1,0:T(8,128)(2,1)}, u32[]{:S(2)}) copy-start(bf16[128,128]{1,0:T(8,128)(2,1)} %rows_far.1) | copy-start | bytes 98308
  8.8 3.7 %copy-start.8 = (s32[128]{0:T(128)S(1)}, s32[128]{0:T(128)}, u32[]{:S(2)}) copy-start(s32[128]{0:T(128)} %param.11) | copy-start | bytes 1540
  13.7 21.8 %all-to-all-start = ((bf16[128,16,128]{2,1,0:T(8,128)(2,1)}), bf16[128,16,128]{2,1,0:T(8,128)(2,1)S(1)}, u32[]{:S(2)}, u32[]{:S(2)}) async-start(bf16[128,16,128]{2,1,0:T(8,128)(2,1)} %bitcast.4), calls=%async_computation | async-start | bytes 1048576 | tf_op jit(solution)/shard_map/all_to_all | solution.py:471
  21.8 14.9 %copy-start.4 = (bf16[128,2048]{1,0:T(8,128)(2,1)S(1)}, bf16[128,2048]{1,0:T(8,128)(2,1)}, u32[]{:S(2)}) copy-start(bf16[128,2048]{1,0:T(8,128)(2,1)} %act_own.1) | copy-start | bytes 1572868
  35.5 6.3 %copy-start.2 = (bf16[2048,64]{0,1:T(8,128)(2,1)S(1)}, bf16[2048,64]{0,1:T(8,128)(2,1)}, u32[]{:S(2)}) copy-start(bf16[2048,64]{0,1:T(8,128)(2,1)} %param.17) | copy-start | bytes 786436
  35.5 6.3 %copy-start.5 = (bf16[64,2048]{1,0:T(8,128)(2,1)S(1)}, bf16[64,2048]{1,0:T(8,128)(2,1)}, u32[]{:S(2)}) copy-start(bf16[64,2048]{1,0:T(8,128)(2,1)} %refs_1_.1) | copy-start | bytes 786436
  35.5 6.3 %copy-start.7 = (f32[2048]{0:T(1024)S(1)}, f32[2048]{0:T(1024)}, u32[]{:S(2)}) copy-start(f32[2048]{0:T(1024)} %param.14) | copy-start | bytes 24580
  35.7 4.9 %copy-start = (bf16[400,2048]{1,0:T(8,128)(2,1)}, bf16[400,2048]{1,0:T(8,128)(2,1)S(1)}, u32[]{:S(2)}) copy-start(bf16[400,2048]{1,0:T(8,128)(2,1)S(1)} %shard_map.114.sides) | copy-start | bytes 4915204
  35.7 4.8 %collective-permute-start.4 = (bf16[400,2048]{1,0:T(8,128)(2,1)S(1)}, bf16[400,2048]{1,0:T(8,128)(2,1)S(1)}, u32[]{:S(2)}, u32[]{:S(2)}) collective-permute-start(bf16[400,2048]{1,0:T(8,128)(2,1)S(1)} %shard_map.114.sides), channel_id=1, source_target_pairs={{0,4},{4,0},{1,5},{5,1},{2,6},{6,2},{3,7},{7,3},{8,12},{12,8},{9,1... | collective-permute-start | bytes 4915208 | tf_op jit(solution)/shard_map/ppermute | solution.py:64
  36.6 3.9 %collective-permute-start = (bf16[128,2048]{1,0:T(8,128)(2,1)S(1)}, bf16[128,2048]{1,0:T(8,128)(2,1)S(1)}, u32[]{:S(2)}, u32[]{:S(2)}) collective-permute-start(bf16[128,2048]{1,0:T(8,128)(2,1)S(1)} %copy-done.4), channel_id=1, source_target_pairs={{0,4},{4,0},{1,5},{5,1},{2,6},{6,2},{3,7},{7,3},{8,12},{12,8},{9,1... | collective-permute-start | bytes 1572872 | tf_op jit(solution)/shard_map/ppermute | solution.py:64
  40.5 0.8 copy-start.10
  40.5 1.3 copy-start.9
  53.4 1.6 collective-permute-start.5
  55.1 4.8 %collective-permute-start.8 = (f32[64,512]{1,0:T(8,128)S(1)}, f32[64,512]{1,0:T(8,128)S(1)}, u32[]{:S(2)}, u32[]{:S(2)}) collective-permute-start(f32[64,512]{1,0:T(8,128)S(1)} %add.39), channel_id=1, source_target_pairs={{0,3},{1,0},{2,1},{3,2},{4,7},{5,4},{6,5},{7,6},{8,11},{9,8},{10,9... | collective-permute-start | bytes 393224 | tf_op jit(solution)/shard_map/ppermute | solution.py:64
  57.0 6.0 %collective-permute-start.7 = (f32[64,512]{1,0:T(8,128)S(1)}, f32[64,512]{1,0:T(8,128)S(1)}, u32[]{:S(2)}, u32[]{:S(2)}) collective-permute-start(f32[64,512]{1,0:T(8,128)S(1)} %add.39), channel_id=1, source_target_pairs={{0,2},{1,3},{2,0},{3,1},{4,6},{5,7},{6,4},{7,5},{8,10},{9,11},{10,... | collective-permute-start | bytes 393224 | tf_op jit(solution)/shard_map/ppermute | solution.py:64
  57.1 9.3 %collective-permute-start.6 = (f32[64,512]{1,0:T(8,128)S(1)}, f32[64,512]{1,0:T(8,128)S(1)}, u32[]{:S(2)}, u32[]{:S(2)}) collective-permute-start(f32[64,512]{1,0:T(8,128)S(1)} %add.39), channel_id=1, source_target_pairs={{0,1},{1,2},{2,3},{3,0},{4,5},{5,6},{6,7},{7,4},{8,9},{9,10},{10,1... | collective-permute-start | bytes 393224 | tf_op jit(solution)/shard_map/ppermute | solution.py:64
  67.2 1.7 %collective-permute-start.9 = (f32[64,512]{1,0:T(8,128)S(1)}, f32[64,512]{1,0:T(8,128)S(1)}, u32[]{:S(2)}, u32[]{:S(2)}) collective-permute-start(f32[64,512]{1,0:T(8,128)S(1)} %pad_maximum_fusion.error_own), channel_id=1, source_target_pairs={{0,4},{4,0},{1,5},{5,1},{2,6},{6,2},{3,7},{7,3},{8,12},{12,8},{9,1... | collective-permute-start | bytes 393224 | tf_op jit(solution)/shard_map/ppermute | solution.py:64
  77.3 12.3 %collective-permute-start.10 = (bf16[400,512]{1,0:T(8,128)(2,1)S(1)}, bf16[400,512]{1,0:T(8,128)(2,1)S(1)}, u32[]{:S(2)}, u32[]{:S(2)}) collective-permute-start(bf16[400,512]{1,0:T(8,128)(2,1)S(1)} %get-tuple-element.45), channel_id=1, source_target_pairs={{0,16},{8,24},{16,0},{24,8},{1,17},{9,25},{17,1},{25,9},{2,18},{10... | collective-permute-start | bytes 1228808 | tf_op jit(solution)/shard_map/ppermute | solution.py:64
  80.0 12.2 %collective-permute-start.11 = (bf16[400,512]{1,0:T(8,128)(2,1)S(1)}, bf16[400,512]{1,0:T(8,128)(2,1)S(1)}, u32[]{:S(2)}, u32[]{:S(2)}) collective-permute-start(bf16[400,512]{1,0:T(8,128)(2,1)S(1)} %get-tuple-element.46), channel_id=1, source_target_pairs={{0,64},{32,96},{64,0},{96,32},{1,65},{33,97},{65,1},{97,33},{2,66}... | collective-permute-start | bytes 1228808 | tf_op jit(solution)/shard_map/ppermute | solution.py:64
  82.9 16.1 %collective-permute-start.12 = (bf16[400,512]{1,0:T(8,128)(2,1)S(1)}, bf16[400,512]{1,0:T(8,128)(2,1)S(1)}, u32[]{:S(2)}, u32[]{:S(2)}) collective-permute-start(bf16[400,512]{1,0:T(8,128)(2,1)S(1)} %get-tuple-element.47), channel_id=1, source_target_pairs={{0,8},{8,16},{16,24},{24,0},{1,9},{9,17},{17,25},{25,1},{2,10},{10... | collective-permute-start | bytes 1228808 | tf_op jit(solution)/shard_map/ppermute | solution.py:64
  83.2 18.4 %collective-permute-start.13 = (bf16[400,512]{1,0:T(8,128)(2,1)S(1)}, bf16[400,512]{1,0:T(8,128)(2,1)S(1)}, u32[]{:S(2)}, u32[]{:S(2)}) collective-permute-start(bf16[400,512]{1,0:T(8,128)(2,1)S(1)} %get-tuple-element.48), channel_id=1, source_target_pairs={{0,32},{32,64},{64,96},{96,0},{1,33},{33,65},{65,97},{97,1},{2,34}... | collective-permute-start | bytes 1228808 | tf_op jit(solution)/shard_map/ppermute | solution.py:64
  83.6 18.0 %collective-permute-start.14 = (bf16[400,512]{1,0:T(8,128)(2,1)S(1)}, bf16[400,512]{1,0:T(8,128)(2,1)S(1)}, u32[]{:S(2)}, u32[]{:S(2)}) collective-permute-start(bf16[400,512]{1,0:T(8,128)(2,1)S(1)} %get-tuple-element.49), channel_id=1, source_target_pairs={{0,24},{8,0},{16,8},{24,16},{1,25},{9,1},{17,9},{25,17},{2,26},{10... | collective-permute-start | bytes 1228808 | tf_op jit(solution)/shard_map/ppermute | solution.py:64
  89.6 12.1 %collective-permute-start.15 = (bf16[400,512]{1,0:T(8,128)(2,1)S(1)}, bf16[400,512]{1,0:T(8,128)(2,1)S(1)}, u32[]{:S(2)}, u32[]{:S(2)}) collective-permute-start(bf16[400,512]{1,0:T(8,128)(2,1)S(1)} %get-tuple-element.50), channel_id=1, source_target_pairs={{0,96},{32,0},{64,32},{96,64},{1,97},{33,1},{65,33},{97,65},{2,98}... | collective-permute-start | bytes 1228808 | tf_op jit(solution)/shard_map/ppermute | solution.py:64
  103.1 7.1 %collective-permute-start.16 = (bf16[448,128]{1,0:T(8,128)(2,1)S(1)}, bf16[448,128]{1,0:T(8,128)(2,1)S(1)}, u32[]{:S(2)}, u32[]{:S(2)}) collective-permute-start(bf16[448,128]{1,0:T(8,128)(2,1)S(1)} %get-tuple-element.53), channel_id=1, source_target_pairs={{0,64},{32,96},{64,0},{96,32},{1,65},{33,97},{65,1},{97,33},{2,66}... | collective-permute-start | bytes 344072 | tf_op jit(solution)/shard_map/ppermute | solution.py:64
  105.1 6.6 %collective-permute-start.17 = (bf16[448,128]{1,0:T(8,128)(2,1)S(1)}, bf16[448,128]{1,0:T(8,128)(2,1)S(1)}, u32[]{:S(2)}, u32[]{:S(2)}) collective-permute-start(bf16[448,128]{1,0:T(8,128)(2,1)S(1)} %get-tuple-element.54), channel_id=1, source_target_pairs={{0,16},{8,24},{16,0},{24,8},{1,17},{9,25},{17,1},{25,9},{2,18},{10... | collective-permute-start | bytes 344072 | tf_op jit(solution)/shard_map/ppermute | solution.py:64
  106.4 5.4 %collective-permute-start.18 = (bf16[448,128]{1,0:T(8,128)(2,1)S(1)}, bf16[448,128]{1,0:T(8,128)(2,1)S(1)}, u32[]{:S(2)}, u32[]{:S(2)}) collective-permute-start(bf16[448,128]{1,0:T(8,128)(2,1)S(1)} %get-tuple-element.55), channel_id=1, source_target_pairs={{0,32},{32,64},{64,96},{96,0},{1,33},{33,65},{65,97},{97,1},{2,34}... | collective-permute-start | bytes 344072 | tf_op jit(solution)/shard_map/ppermute | solution.py:64
  107.3 6.4 %collective-permute-start.19 = (bf16[448,128]{1,0:T(8,128)(2,1)S(1)}, bf16[448,128]{1,0:T(8,128)(2,1)S(1)}, u32[]{:S(2)}, u32[]{:S(2)}) collective-permute-start(bf16[448,128]{1,0:T(8,128)(2,1)S(1)} %get-tuple-element.56), channel_id=1, source_target_pairs={{0,8},{8,16},{16,24},{24,0},{1,9},{9,17},{17,25},{25,1},{2,10},{10... | collective-permute-start | bytes 344072 | tf_op jit(solution)/shard_map/ppermute | solution.py:64
  107.6 6.1 %collective-permute-start.20 = (bf16[448,128]{1,0:T(8,128)(2,1)S(1)}, bf16[448,128]{1,0:T(8,128)(2,1)S(1)}, u32[]{:S(2)}, u32[]{:S(2)}) collective-permute-start(bf16[448,128]{1,0:T(8,128)(2,1)S(1)} %get-tuple-element.57), channel_id=1, source_target_pairs={{0,96},{32,0},{64,32},{96,64},{1,97},{33,1},{65,33},{97,65},{2,98}... | collective-permute-start | bytes 344072 | tf_op jit(solution)/shard_map/ppermute | solution.py:64
  110.2 3.9 %collective-permute-start.21 = (bf16[448,128]{1,0:T(8,128)(2,1)S(1)}, bf16[448,128]{1,0:T(8,128)(2,1)S(1)}, u32[]{:S(2)}, u32[]{:S(2)}) collective-permute-start(bf16[448,128]{1,0:T(8,128)(2,1)S(1)} %get-tuple-element.58), channel_id=1, source_target_pairs={{0,24},{8,0},{16,8},{24,16},{1,25},{9,1},{17,9},{25,17},{2,26},{10... | collective-permute-start | bytes 344072 | tf_op jit(solution)/shard_map/ppermute | solution.py:64
  114.4 6.2 %collective-permute-start.26 = (bf16[3,128,128]{2,1,0:T(8,128)(2,1)S(1)}, bf16[3,128,128]{2,1,0:T(8,128)(2,1)S(1)}, u32[]{:S(2)}, u32[]{:S(2)}) collective-permute-start(bf16[3,128,128]{2,1,0:T(8,128)(2,1)S(1)} %get-tuple-element.61.refs_6_), channel_id=1, source_target_pairs={{0,64},{32,96},{64,0},{96,32},{1,65},{33,97},{65,1},{97,33},{2,66}... | collective-permute-start | bytes 294920 | tf_op jit(solution)/shard_map/ppermute | solution.py:64
  114.5 7.4 %collective-permute-start.24 = (bf16[3,128,128]{2,1,0:T(8,128)(2,1)S(1)}, bf16[3,128,128]{2,1,0:T(8,128)(2,1)S(1)}, u32[]{:S(2)}, u32[]{:S(2)}) collective-permute-start(bf16[3,128,128]{2,1,0:T(8,128)(2,1)S(1)} %get-tuple-element.61.refs_6_), channel_id=1, source_target_pairs={{0,32},{32,64},{64,96},{96,0},{1,33},{33,65},{65,97},{97,1},{2,34}... | collective-permute-start | bytes 294920 | tf_op jit(solution)/shard_map/ppermute | solution.py:64
  116.0 6.0 %collective-permute-start.22 = (bf16[3,128,128]{2,1,0:T(8,128)(2,1)S(1)}, bf16[3,128,128]{2,1,0:T(8,128)(2,1)S(1)}, u32[]{:S(2)}, u32[]{:S(2)}) collective-permute-start(bf16[3,128,128]{2,1,0:T(8,128)(2,1)S(1)} %get-tuple-element.61.refs_6_), channel_id=1, source_target_pairs={{0,96},{32,0},{64,32},{96,64},{1,97},{33,1},{65,33},{97,65},{2,98}... | collective-permute-start | bytes 294920 | tf_op jit(solution)/shard_map/ppermute | solution.py:64
  117.2 5.0 %collective-permute-start.27 = (bf16[3,128,128]{2,1,0:T(8,128)(2,1)S(1)}, bf16[3,128,128]{2,1,0:T(8,128)(2,1)S(1)}, u32[]{:S(2)}, u32[]{:S(2)}) collective-permute-start(bf16[3,128,128]{2,1,0:T(8,128)(2,1)S(1)} %get-tuple-element.62.refs_7_), channel_id=1, source_target_pairs={{0,16},{8,24},{16,0},{24,8},{1,17},{9,25},{17,1},{25,9},{2,18},{10... | collective-permute-start | bytes 294920 | tf_op jit(solution)/shard_map/ppermute | solution.py:64
  118.8 5.0 %collective-permute-start.25 = (bf16[3,128,128]{2,1,0:T(8,128)(2,1)S(1)}, bf16[3,128,128]{2,1,0:T(8,128)(2,1)S(1)}, u32[]{:S(2)}, u32[]{:S(2)}) collective-permute-start(bf16[3,128,128]{2,1,0:T(8,128)(2,1)S(1)} %get-tuple-element.62.refs_7_), channel_id=1, source_target_pairs={{0,8},{8,16},{16,24},{24,0},{1,9},{9,17},{17,25},{25,1},{2,10},{10... | collective-permute-start | bytes 294920 | tf_op jit(solution)/shard_map/ppermute | solution.py:64
  120.6 3.8 %collective-permute-start.23 = (bf16[3,128,128]{2,1,0:T(8,128)(2,1)S(1)}, bf16[3,128,128]{2,1,0:T(8,128)(2,1)S(1)}, u32[]{:S(2)}, u32[]{:S(2)}) collective-permute-start(bf16[3,128,128]{2,1,0:T(8,128)(2,1)S(1)} %get-tuple-element.62.refs_7_), channel_id=1, source_target_pairs={{0,24},{8,0},{16,8},{24,16},{1,25},{9,1},{17,9},{25,17},{2,26},{10... | collective-permute-start | bytes 294920 | tf_op jit(solution)/shard_map/ppermute | solution.py:64
  124.4 9.2 %collective-permute-start.33 = (bf16[4,3,128,128]{3,2,1,0:T(8,128)(2,1)S(1)}, bf16[4,3,128,128]{3,2,1,0:T(8,128)(2,1)S(1)}, u32[]{:S(2)}, u32[]{:S(2)}) collective-permute-start(bf16[4,3,128,128]{3,2,1,0:T(8,128)(2,1)S(1)} %get-tuple-element.64.line), channel_id=1, source_target_pairs={{0,16},{8,24},{16,0},{24,8},{1,17},{9,25},{17,1},{25,9},{2,18},{10... | collective-permute-start | bytes 1179656 | tf_op jit(solution)/shard_map/ppermute | solution.py:64
  125.5 12.1 %collective-permute-start.32 = (bf16[4,3,128,128]{3,2,1,0:T(8,128)(2,1)S(1)}, bf16[4,3,128,128]{3,2,1,0:T(8,128)(2,1)S(1)}, u32[]{:S(2)}, u32[]{:S(2)}) collective-permute-start(bf16[4,3,128,128]{3,2,1,0:T(8,128)(2,1)S(1)} %get-tuple-element.64.line), channel_id=1, source_target_pairs={{0,8},{8,16},{16,24},{24,0},{1,9},{9,17},{17,25},{25,1},{2,10},{10... | collective-permute-start | bytes 1179656 | tf_op jit(solution)/shard_map/ppermute | solution.py:64
  127.6 10.5 %collective-permute-start.31 = (bf16[4,3,128,128]{3,2,1,0:T(8,128)(2,1)S(1)}, bf16[4,3,128,128]{3,2,1,0:T(8,128)(2,1)S(1)}, u32[]{:S(2)}, u32[]{:S(2)}) collective-permute-start(bf16[4,3,128,128]{3,2,1,0:T(8,128)(2,1)S(1)} %get-tuple-element.64.line), channel_id=1, source_target_pairs={{0,24},{8,0},{16,8},{24,16},{1,25},{9,1},{17,9},{25,17},{2,26},{10... | collective-permute-start | bytes 1179656 | tf_op jit(solution)/shard_map/ppermute | solution.py:64
  128.2 24.9 %collective-permute-start.30 = (bf16[4,3,128,128]{3,2,1,0:T(8,128)(2,1)S(1)}, bf16[4,3,128,128]{3,2,1,0:T(8,128)(2,1)S(1)}, u32[]{:S(2)}, u32[]{:S(2)}) collective-permute-start(bf16[4,3,128,128]{3,2,1,0:T(8,128)(2,1)S(1)} %get-tuple-element.63.refs_1_.refs_3_), channel_id=1, source_target_pairs={{0,64},{32,96},{64,0},{96,32},{1,65},{33,97},{65,1},{97,33},{2,66}... | collective-permute-start | bytes 1179656 | tf_op jit(solution)/shard_map/ppermute | solution.py:64
  129.3 23.8 %collective-permute-start.29 = (bf16[4,3,128,128]{3,2,1,0:T(8,128)(2,1)S(1)}, bf16[4,3,128,128]{3,2,1,0:T(8,128)(2,1)S(1)}, u32[]{:S(2)}, u32[]{:S(2)}) collective-permute-start(bf16[4,3,128,128]{3,2,1,0:T(8,128)(2,1)S(1)} %get-tuple-element.63.refs_1_.refs_3_), channel_id=1, source_target_pairs={{0,32},{32,64},{64,96},{96,0},{1,33},{33,65},{65,97},{97,1},{2,34}... | collective-permute-start | bytes 1179656 | tf_op jit(solution)/shard_map/ppermute | solution.py:64
  133.7 19.5 %collective-permute-start.28 = (bf16[4,3,128,128]{3,2,1,0:T(8,128)(2,1)S(1)}, bf16[4,3,128,128]{3,2,1,0:T(8,128)(2,1)S(1)}, u32[]{:S(2)}, u32[]{:S(2)}) collective-permute-start(bf16[4,3,128,128]{3,2,1,0:T(8,128)(2,1)S(1)} %get-tuple-element.63.refs_1_.refs_3_), channel_id=1, source_target_pairs={{0,96},{32,0},{64,32},{96,64},{1,97},{33,1},{65,33},{97,65},{2,98}... | collective-permute-start | bytes 1179656 | tf_op jit(solution)/shard_map/ppermute | solution.py:64
  138.3 15.9 %collective-permute-start.35 = (bf16[5,4,3,128,128]{4,3,2,1,0:T(8,128)(2,1)S(1)}, bf16[5,4,3,128,128]{4,3,2,1,0:T(8,128)(2,1)}, u32[]{:S(2)}, u32[]{:S(2)}) collective-permute-start(bf16[5,4,3,128,128]{4,3,2,1,0:T(8,128)(2,1)S(1)} %shard_map.121.refs_0_.refs_1_), channel_id=1, source_target_pairs={{0,4},{4,0},{1,5},{5,1},{2,6},{6,2},{3,7},{7,3},{8,12},{12,8},{9,1... | collective-permute-start | bytes 5898248 | tf_op jit(solution)/shard_map/ppermute | solution.py:64
  153.3 8.5 %collective-permute-start.34 = (bf16[4,4,3,128,128]{4,3,2,1,0:T(8,128)(2,1)S(1)}, bf16[4,4,3,128,128]{4,3,2,1,0:T(8,128)(2,1)}, u32[]{:S(2)}, u32[]{:S(2)}) collective-permute-start(bf16[4,4,3,128,128]{4,3,2,1,0:T(8,128)(2,1)S(1)} %shard_map.123.refs_2_), channel_id=1, source_target_pairs={{0,4},{4,0},{1,5},{5,1},{2,6},{6,2},{3,7},{7,3},{8,12},{12,8},{9,1... | collective-permute-start | bytes 4718600 | tf_op jit(solution)/shard_map/ppermute | solution.py:64
  154.2 1.0 copy-start.3

commit v7 on v6

--- a/solution.py
+++ b/solution.py
@@ -232,6 +232,19 @@
             part[:, f * 128 : f * 128 + 128] = value[:, lanes(f, other)] + added
     for copy in leave:
         copy.wait()
+
+
+def error_kernel(own, three, one, two, error, loss):
+    heard = (own, one, two, three)
+    for i, r in enumerate(ORDER):
+        total = heard[0][:, i * 128 : i * 128 + 128]
+        for o in range(1, 4):
+            spot = SPOT[(r - o) % 4]
+            total = total + heard[o][:, spot * 128 : spot * 128 + 128]
+        error[:, i * 128 : i * 128 + 128] = total
+        if r == 0:
+            rows = jnp.sum(total * total, axis=1, keepdims=True)
+            loss[...] = jnp.sum(rows, axis=0, keepdims=True) / total.size
 
 
 def gradient_piece(delta, normed, factor, h, block, out):
@@ -496,18 +509,10 @@
     )
 
     clip_part = part_own + shift(part_other, "core", 1)
-    heard = {0: clip_part, **{o: shift(clip_part, "frame", o) for o in (2, 1, 3)}}
-    error_own = jnp.concatenate(
-        [
-            sum(
-                heard[o][:, SPOT[(r - o) % 4] * 128 : SPOT[(r - o) % 4] * 128 + 128]
-                for o in range(4)
-            )
-            for r in ORDER
-        ],
-        axis=1,
-    )
-    frame_loss = jnp.mean(error_own[:, :128] * error_own[:, :128]).reshape(1, 1)
+    error_own, frame_loss = call(
+        error_kernel, near(shape((64, 512), f32), shape((1, 1), f32)),
+        *near(clip_part, *(shift(clip_part, "frame", o) for o in (3, 1, 2))),
+    )
     error_other = shift(error_own, "core", 1)
 
     piece = shape((400, 512), bf16)

time: 167 us -> 162 us (0.970)
  waiting for transfers between devices: 51.3 us -> 48.3 us
  between operations: 3.42 us -> 1.75 us
    ppermute x36, waiting for transfers between devices: 38.3 us -> 35.3 us  [shift(): lax.ppermute(value, axis, [(i, (i + offset) % size) for i in range(size)])]
    pallas_call x11 -> x12, Pallas kernels: 28.2 us -> 28.9 us  [call(): pl.pallas_call(kernel, in_specs=[spec for spec, _ in operands], out_specs...]
  transfers between devices with their start and end apart: 37 -> 37, of which waited for: 18 -> 17; matrix products, arithmetic and copies ran while one was open for 0% -> 0% of each run, Pallas kernels for 10% -> 11%
where the time goes in v7:
time: 162 us
  starting transfers between devices  66.3 us (41%)
  waiting for transfers between devices  48.3 us (30%)
  Pallas kernels  43.2 us (27%)
  local copies, waits for them, and re-layouts  2.32 us (1%)
  between operations  1.75 us (1%)
    ppermute x36, starting transfers between devices, shift(): lax.ppermute(value, axis, [(i, (i + offset) % size) for i in range(size)])  58.3 us
    ppermute x36, waiting for transfers between devices, shift(): lax.ppermute(value, axis, [(i, (i + offset) % size) for i in range(size)])  35.3 us
    pallas_call x12, Pallas kernels, call(): pl.pallas_call(kernel, in_specs=[spec for spec, _ in operands], out_specs...  28.9 us
    pallas_call x3, Pallas kernels, assemble(): pl.pallas_call(functools.partial(assemble_kernel, tags, len(arrays), len(...  14.4 us
    all_to_all x1, waiting for transfers between devices, shards(): lax.all_to_all(sent.reshape(128, 16, 128), ('frame', 'y', 'x', 'core'), 0...  13 us
    all_to_all x1, starting transfers between devices, shards(): lax.all_to_all(sent.reshape(128, 16, 128), ('frame', 'y', 'x', 'core'), 0...  8.04 us
  transfers between devices with their start and end apart: 37, of which 17 were waited for; matrix products, arithmetic and copies ran while one was open for 0% of the time, Pallas kernels for 11%

profile of v7, /device:TPU:1, one launch (start us, length us, event | category | flops | bytes accessed | tf_op | source)
XLA Modules:
  0.0 162.1 jit_solution(5356437848019972298)
XLA Ops:
  0.6 4.5 %collective-permute-start.2 = (bf16[128,2048]{1,0:T(8,128)(2,1)}, bf16[128,2048]{1,0:T(8,128)(2,1)S(1)}, u32[]{:S(2)}, u32[]{:S(2)}) collective-permute-start(bf16[128,2048]{1,0:T(8,128)(2,1)} %act_own.1), channel_id=1, source_target_pairs={{0,2},{1,3},{2,0},{3,1},{4,6},{5,7},{6,4},{7,5},{8,10},{9,11},{10,... | collective-permute-start | bytes 1572872 | tf_op jit(solution)/shard_map/ppermute | solution.py:64
  5.9 1.9 %collective-permute-start.3 = (bf16[128,2048]{1,0:T(8,128)(2,1)}, bf16[128,2048]{1,0:T(8,128)(2,1)S(1)}, u32[]{:S(2)}, u32[]{:S(2)}) collective-permute-start(bf16[128,2048]{1,0:T(8,128)(2,1)} %act_own.1), channel_id=1, source_target_pairs={{0,3},{1,0},{2,1},{3,2},{4,7},{5,4},{6,5},{7,6},{8,11},{9,8},{10,9... | collective-permute-start | bytes 1572872 | tf_op jit(solution)/shard_map/ppermute | solution.py:64
  7.9 0.9 copy-done.1
  8.8 3.7 %shard_map.112 = (bf16[768,2048]{1,0:T(8,128)(2,1)}, f32[256,64]{1,0:T(8,128)S(1)}, f32[64,256]{1,0:T(8,128)S(1)}) custom-call(s32[2]{0:T(128)S(1)} %pad_add_fusion.place, bf16[3,2048,512]{2,1,0:T(8,128)(2,1)} %w.1, bf16[512,2048]{1,0:T(8,128)(2,1)} %w_out.1, bf16[64,2048]{1,0:T(8,128)(2,1)S(1)} %bitcast.11), custom_call_target="tpu_custom_call" | custom-call | bytes 1024 | tf_op jit(solution)/shard_map/pallas_call | solution.py:436
  12.6 1.1 shard_map.113
  13.7 8.0 %all-to-all-start = ((bf16[128,16,128]{2,1,0:T(8,128)(2,1)}), bf16[128,16,128]{2,1,0:T(8,128)(2,1)S(1)}, u32[]{:S(2)}, u32[]{:S(2)}) async-start(bf16[128,16,128]{2,1,0:T(8,128)(2,1)} %bitcast.4), calls=%async_computation | async-start | bytes 1048576 | tf_op jit(solution)/shard_map/all_to_all | solution.py:484
  22.5 13.0 %all-to-all-done = bf16[128,16,128]{2,1,0:T(8,128)(2,1)S(1)} async-done(((bf16[128,16,128]{2,1,0:T(8,128)(2,1)}), bf16[128,16,128]{2,1,0:T(8,128)(2,1)S(1)}, u32[]{:S(2)}, u32[]{:S(2)}) %all-to-all-start) | async-done | bytes 524320 | tf_op jit(solution)/shard_map/all_to_all | solution.py:484
  35.7 1.0 collective-permute-start.4
  36.7 1.3 shard_map.115.refs_0_
  38.1 2.4 %collective-permute-done.act_theirs = bf16[128,2048]{1,0:T(8,128)(2,1)S(1)} collective-permute-done((bf16[128,2048]{1,0:T(8,128)(2,1)S(1)}, bf16[128,2048]{1,0:T(8,128)(2,1)S(1)}, u32[]{:S(2)}, u32[]{:S(2)}) %collective-permute-start) | collective-permute-done | bytes 524320 | tf_op jit(solution)/shard_map/ppermute | solution.py:64
  41.8 11.6 %shard_map.116 = (bf16[1024,2048]{1,0:T(8,128)(2,1)}, bf16[1024,1024]{1,0:T(8,128)(2,1)}, f32[4,16,128]{2,1,0:T(8,128)S(1)}, f32[64,512]{1,0:T(8,128)S(1)}, f32[64,512]{1,0:T(8,128)S(1)}) custom-call(bf16[128,2048]{1,0:T(8,128)(2,1)S(1)} %copy-done.3, bf16[128,2048]{1,0:T(8,128)(2,1)} %copy-done.9, bf16[400,2048]{1,0:T(8,128)(2,1)} %copy-done, ...), custom_call_target="tpu_custom_call" | custom-call | bytes 1024 | tf_op jit(solution)/shard_map/pallas_call | solution.py:436
  54.0 1.0 collective-permute-done.5
  55.1 1.8 %collective-permute-start.8 = (f32[64,512]{1,0:T(8,128)S(1)}, f32[64,512]{1,0:T(8,128)S(1)}, u32[]{:S(2)}, u32[]{:S(2)}) collective-permute-start(f32[64,512]{1,0:T(8,128)S(1)} %add.3.own), channel_id=1, source_target_pairs={{0,2},{1,3},{2,0},{3,1},{4,6},{5,7},{6,4},{7,5},{8,10},{9,11},{10,... | collective-permute-start | bytes 393224 | tf_op jit(solution)/shard_map/ppermute | solution.py:64
  57.6 1.9 %collective-permute-start.6 = (f32[64,512]{1,0:T(8,128)S(1)}, f32[64,512]{1,0:T(8,128)S(1)}, u32[]{:S(2)}, u32[]{:S(2)}) collective-permute-start(f32[64,512]{1,0:T(8,128)S(1)} %add.3.own), channel_id=1, source_target_pairs={{0,3},{1,0},{2,1},{3,2},{4,7},{5,4},{6,5},{7,6},{8,11},{9,8},{10,9... | collective-permute-start | bytes 393224 | tf_op jit(solution)/shard_map/ppermute | solution.py:64
  59.5 1.9 %collective-permute-done.8.two = f32[64,512]{1,0:T(8,128)S(1)} collective-permute-done((f32[64,512]{1,0:T(8,128)S(1)}, f32[64,512]{1,0:T(8,128)S(1)}, u32[]{:S(2)}, u32[]{:S(2)}) %collective-permute-start.8) | collective-permute-done | bytes 131104 | tf_op jit(solution)/shard_map/ppermute | solution.py:64
  61.4 3.3 %collective-permute-done.7.one = f32[64,512]{1,0:T(8,128)S(1)} collective-permute-done((f32[64,512]{1,0:T(8,128)S(1)}, f32[64,512]{1,0:T(8,128)S(1)}, u32[]{:S(2)}, u32[]{:S(2)}) %collective-permute-start.7) | collective-permute-done | bytes 131104 | tf_op jit(solution)/shard_map/ppermute | solution.py:64
  66.1 0.9 collective-permute-done.9.error_other
  67.0 8.4 %shard_map.118 = (bf16[400,512]{1,0:T(8,128)(2,1)S(1)}, bf16[400,512]{1,0:T(8,128)(2,1)S(1)}, bf16[400,512]{1,0:T(8,128)(2,1)S(1)}, bf16[400,512]{1,0:T(8,128)(2...) custom-call(s32[3]{0:T(128)S(1)} %pad_add_fusion.1.place, ...), custom_call_target="tpu_custom_call" | custom-call | bytes 1024 | tf_op jit(solution)/shard_map/pallas_call | solution.py:436
  75.4 2.3 %collective-permute-start.10 = (bf16[400,512]{1,0:T(8,128)(2,1)S(1)}, bf16[400,512]{1,0:T(8,128)(2,1)S(1)}, u32[]{:S(2)}, u32[]{:S(2)}) collective-permute-start(bf16[400,512]{1,0:T(8,128)(2,1)S(1)} %get-tuple-element.49), channel_id=1, source_target_pairs={{0,16},{8,24},{16,0},{24,8},{1,17},{9,25},{17,1},{25,9},{2,18},{10... | collective-permute-start | bytes 1228808 | tf_op jit(solution)/shard_map/ppermute | solution.py:64
  77.7 2.9 %collective-permute-start.11 = (bf16[400,512]{1,0:T(8,128)(2,1)S(1)}, bf16[400,512]{1,0:T(8,128)(2,1)S(1)}, u32[]{:S(2)}, u32[]{:S(2)}) collective-permute-start(bf16[400,512]{1,0:T(8,128)(2,1)S(1)} %get-tuple-element.50), channel_id=1, source_target_pairs={{0,64},{32,96},{64,0},{96,32},{1,65},{33,97},{65,1},{97,33},{2,66}... | collective-permute-start | bytes 1228808 | tf_op jit(solution)/shard_map/ppermute | solution.py:64
  81.3 2.4 %collective-permute-start.14 = (bf16[400,512]{1,0:T(8,128)(2,1)S(1)}, bf16[400,512]{1,0:T(8,128)(2,1)S(1)}, u32[]{:S(2)}, u32[]{:S(2)}) collective-permute-start(bf16[400,512]{1,0:T(8,128)(2,1)S(1)} %get-tuple-element.53), channel_id=1, source_target_pairs={{0,24},{8,0},{16,8},{24,16},{1,25},{9,1},{17,9},{25,17},{2,26},{10... | collective-permute-start | bytes 1228808 | tf_op jit(solution)/shard_map/ppermute | solution.py:64
  83.6 4.1 %collective-permute-done.10.refs_0_ = bf16[400,512]{1,0:T(8,128)(2,1)S(1)} collective-permute-done((bf16[400,512]{1,0:T(8,128)(2,1)S(1)}, bf16[400,512]{1,0:T(8,128)(2,1)S(1)}, u32[]{:S(2)}, u32[]{:S(2)}) %collective-permute-start.10) | collective-permute-done | bytes 409632 | tf_op jit(solution)/shard_map/ppermute | solution.py:64
  87.7 2.2 %collective-permute-start.15 = (bf16[400,512]{1,0:T(8,128)(2,1)S(1)}, bf16[400,512]{1,0:T(8,128)(2,1)S(1)}, u32[]{:S(2)}, u32[]{:S(2)}) collective-permute-start(bf16[400,512]{1,0:T(8,128)(2,1)S(1)} %get-tuple-element.54), channel_id=1, source_target_pairs={{0,96},{32,0},{64,32},{96,64},{1,97},{33,1},{65,33},{97,65},{2,98}... | collective-permute-start | bytes 1228808 | tf_op jit(solution)/shard_map/ppermute | solution.py:64
  89.9 7.2 %collective-permute-done.12.refs_2_ = bf16[400,512]{1,0:T(8,128)(2,1)S(1)} collective-permute-done((bf16[400,512]{1,0:T(8,128)(2,1)S(1)}, bf16[400,512]{1,0:T(8,128)(2,1)S(1)}, u32[]{:S(2)}, u32[]{:S(2)}) %collective-permute-start.12) | collective-permute-done | bytes 409632 | tf_op jit(solution)/shard_map/ppermute | solution.py:64
  97.2 2.2 %collective-permute-done.13.refs_3_ = bf16[400,512]{1,0:T(8,128)(2,1)S(1)} collective-permute-done((bf16[400,512]{1,0:T(8,128)(2,1)S(1)}, bf16[400,512]{1,0:T(8,128)(2,1)S(1)}, u32[]{:S(2)}, u32[]{:S(2)}) %collective-permute-start.13) | collective-permute-done | bytes 409632 | tf_op jit(solution)/shard_map/ppermute | solution.py:64
  99.4 1.5 shard_map.119
  100.8 2.0 %collective-permute-start.16 = (bf16[448,128]{1,0:T(8,128)(2,1)S(1)}, bf16[448,128]{1,0:T(8,128)(2,1)S(1)}, u32[]{:S(2)}, u32[]{:S(2)}) collective-permute-start(bf16[448,128]{1,0:T(8,128)(2,1)S(1)} %get-tuple-element.57), channel_id=1, source_target_pairs={{0,64},{32,96},{64,0},{96,32},{1,65},{33,97},{65,1},{97,33},{2,66}... | collective-permute-start | bytes 344072 | tf_op jit(solution)/shard_map/ppermute | solution.py:64
  102.8 1.3 collective-permute-start.17
  104.1 0.9 collective-permute-start.18
  105.3 2.7 %collective-permute-start.20 = (bf16[448,128]{1,0:T(8,128)(2,1)S(1)}, bf16[448,128]{1,0:T(8,128)(2,1)S(1)}, u32[]{:S(2)}, u32[]{:S(2)}) collective-permute-start(bf16[448,128]{1,0:T(8,128)(2,1)S(1)} %get-tuple-element.61), channel_id=1, source_target_pairs={{0,96},{32,0},{64,32},{96,64},{1,97},{33,1},{65,33},{97,65},{2,98}... | collective-permute-start | bytes 344072 | tf_op jit(solution)/shard_map/ppermute | solution.py:64
  107.9 1.5 collective-permute-start.21
  109.4 1.9 %collective-permute-done.19.refs_3_ = bf16[448,128]{1,0:T(8,128)(2,1)S(1)} collective-permute-done((bf16[448,128]{1,0:T(8,128)(2,1)S(1)}, bf16[448,128]{1,0:T(8,128)(2,1)S(1)}, u32[]{:S(2)}, u32[]{:S(2)}) %collective-permute-start.19) | collective-permute-done | bytes 114720 | tf_op jit(solution)/shard_map/ppermute | solution.py:64
  112.2 1.4 collective-permute-start.24
  113.6 1.3 collective-permute-start.22
  114.9 1.6 collective-permute-start.27
  116.5 1.8 %collective-permute-start.25 = (bf16[3,128,128]{2,1,0:T(8,128)(2,1)S(1)}, bf16[3,128,128]{2,1,0:T(8,128)(2,1)S(1)}, u32[]{:S(2)}, u32[]{:S(2)}) collective-permute-start(bf16[3,128,128]{2,1,0:T(8,128)(2,1)S(1)} %get-tuple-element.66.refs_7_), channel_id=1, source_target_pairs={{0,8},{8,16},{16,24},{24,0},{1,9},{9,17},{17,25},{25,1},{2,10},{10... | collective-permute-start | bytes 294920 | tf_op jit(solution)/shard_map/ppermute | solution.py:64
  118.3 1.3 collective-permute-start.23
  119.9 1.6 collective-permute-done.25.refs_3_
  122.1 1.1 collective-permute-start.33
  123.2 2.1 %collective-permute-start.32 = (bf16[4,3,128,128]{3,2,1,0:T(8,128)(2,1)S(1)}, bf16[4,3,128,128]{3,2,1,0:T(8,128)(2,1)S(1)}, u32[]{:S(2)}, u32[]{:S(2)}) collective-permute-start(bf16[4,3,128,128]{3,2,1,0:T(8,128)(2,1)S(1)} %get-tuple-element.68.line), channel_id=1, source_target_pairs={{0,8},{8,16},{16,24},{24,0},{1,9},{9,17},{17,25},{25,1},{2,10},{10... | collective-permute-start | bytes 1179656 | tf_op jit(solution)/shard_map/ppermute | solution.py:64
  125.9 1.1 collective-permute-start.30
  127.5 3.9 %collective-permute-done.33.c = bf16[4,3,128,128]{3,2,1,0:T(8,128)(2,1)S(1)} collective-permute-done((bf16[4,3,128,128]{3,2,1,0:T(8,128)(2,1)S(1)}, bf16[4,3,128,128]{3,2,1,0:T(8,128)(2,1)S(1)}, u32[]{:S(2)}, u32[]{:S(2)}) %collective-permute-start.33) | collective-permute-done | bytes 393248 | tf_op jit(solution)/shard_map/ppermute | solution.py:64
  131.4 0.9 collective-permute-start.28
  132.3 3.0 %collective-permute-done.32.b = bf16[4,3,128,128]{3,2,1,0:T(8,128)(2,1)S(1)} collective-permute-done((bf16[4,3,128,128]{3,2,1,0:T(8,128)(2,1)S(1)}, bf16[4,3,128,128]{3,2,1,0:T(8,128)(2,1)S(1)}, u32[]{:S(2)}, u32[]{:S(2)}) %collective-permute-start.32) | collective-permute-done | bytes 393248 | tf_op jit(solution)/shard_map/ppermute | solution.py:64
  135.9 11.3 %collective-permute-start.35 = (bf16[5,4,3,128,128]{4,3,2,1,0:T(8,128)(2,1)S(1)}, bf16[5,4,3,128,128]{4,3,2,1,0:T(8,128)(2,1)S(1)}, u32[]{:S(2)}, u32[]{:S(2)}) collective-permute-start(bf16[5,4,3,128,128]{4,3,2,1,0:T(8,128)(2,1)S(1)} %shard_map.122.refs_0_.refs_1_), channel_id=1, source_target_pairs={{0,4},{4,0},{1,5},{5,1},{2,6},{6,2},{3,7},{7,3},{8,12},{12,8},{9,1... | collective-permute-start | bytes 5898248 | tf_op jit(solution)/shard_map/ppermute | solution.py:64
  147.2 3.5 %shard_map.123 = (f32[3,2048,512]{2,1,0:T(8,128)}, f32[8,128]{1,0:T(8,128)S(1)}) custom-call(s32[3]{0:T(128)S(1)} %pad_add_fusion.1.place, bf16[5,4,3,128,128]{4,3,2,1,0:T(8,128)(2,1)S(1)} %shard_map.122.refs_0_.refs_1_, bf16[4,3,128,128]{3,2,1,0:T(8,128)(2,1)S(1)} %get-tuple-element.67.refs_1_.refs_3_), custom_call_target="tpu_custom_call" | custom-call | bytes 1024 | tf_op jit(solution)/shard_map/pallas_call | solution.py:423
  151.1 7.2 %shard_map.125 = (f32[3,2048,512]{2,1,0:T(8,128)}, f32[8,128]{1,0:T(8,128)}, f32[512,2048]{1,0:T(8,128)}) custom-call(s32[3]{0:T(128)S(1)} %pad_add_fusion.1.place, bf16[5,4,3,128,128]{4,3,2,1,0:T(8,128)(2,1)S(1)} %collective-permute-done.35.refs_0_, bf16[5,4,3,128,128]{4,3,2,1,0:T(8,128)(2,1)S(1)} %shard_map.122.refs_0_.refs_1_, ...), custom_call_target="tpu_custom_call", output_to_operand_aliasing={{0}: (4, {})} | custom-call | bytes 1024 | tf_op jit(solution)/shard_map/pallas_call | solution.py:423
  158.3 3.7 %shard_map.126 = (f32[3,2048,512]{2,1,0:T(8,128)}, f32[8,128]{1,0:T(8,128)}) custom-call(s32[3]{0:T(128)S(1)} %pad_add_fusion.1.place, bf16[4,4,3,128,128]{4,3,2,1,0:T(8,128)(2,1)S(1)} %collective-permute-done.34.refs_0_, f32[3,2048,512]{2,1,0:T(8,128)} %get-tuple-element.72.refs_1_), custom_call_target="tpu_custom_call", output_to_operand_aliasing={{0}: (2, {})} | custom-call | bytes 1024 | tf_op jit(solution)/shard_map/pallas_call | solution.py:423
  (64 shorter events, 9.9 us)
Async XLA Ops:
  0.6 34.9 %collective-permute-start.2 = (bf16[128,2048]{1,0:T(8,128)(2,1)}, bf16[128,2048]{1,0:T(8,128)(2,1)S(1)}, u32[]{:S(2)}, u32[]{:S(2)}) collective-permute-start(bf16[128,2048]{1,0:T(8,128)(2,1)} %act_own.1), channel_id=1, source_target_pairs={{0,2},{1,3},{2,0},{3,1},{4,6},{5,7},{6,4},{7,5},{8,10},{9,11},{10,... | collective-permute-start | bytes 1572872 | tf_op jit(solution)/shard_map/ppermute | solution.py:64
  5.1 30.4 %collective-permute-start.1 = (bf16[128,2048]{1,0:T(8,128)(2,1)}, bf16[128,2048]{1,0:T(8,128)(2,1)S(1)}, u32[]{:S(2)}, u32[]{:S(2)}) collective-permute-start(bf16[128,2048]{1,0:T(8,128)(2,1)} %act_own.1), channel_id=1, source_target_pairs={{0,1},{1,2},{2,3},{3,0},{4,5},{5,6},{6,7},{7,4},{8,9},{9,10},{10,1... | collective-permute-start | bytes 1572872 | tf_op jit(solution)/shard_map/ppermute | solution.py:64
  5.9 29.6 %collective-permute-start.3 = (bf16[128,2048]{1,0:T(8,128)(2,1)}, bf16[128,2048]{1,0:T(8,128)(2,1)S(1)}, u32[]{:S(2)}, u32[]{:S(2)}) collective-permute-start(bf16[128,2048]{1,0:T(8,128)(2,1)} %act_own.1), channel_id=1, source_target_pairs={{0,3},{1,0},{2,1},{3,2},{4,7},{5,4},{6,5},{7,6},{8,11},{9,8},{10,9... | collective-permute-start | bytes 1572872 | tf_op jit(solution)/shard_map/ppermute | solution.py:64
  7.9 0.9 copy-start.1
  8.8 3.7 %copy-start.5 = (bf16[128,128]{1,0:T(8,128)(2,1)S(1)}, bf16[128,128]{1,0:T(8,128)(2,1)}, u32[]{:S(2)}) copy-start(bf16[128,128]{1,0:T(8,128)(2,1)} %rows_far.1) | copy-start | bytes 98308
  8.8 3.7 %copy-start.7 = (s32[128]{0:T(128)S(1)}, s32[128]{0:T(128)}, u32[]{:S(2)}) copy-start(s32[128]{0:T(128)} %param.11) | copy-start | bytes 1540
  13.7 21.8 %all-to-all-start = ((bf16[128,16,128]{2,1,0:T(8,128)(2,1)}), bf16[128,16,128]{2,1,0:T(8,128)(2,1)S(1)}, u32[]{:S(2)}, u32[]{:S(2)}) async-start(bf16[128,16,128]{2,1,0:T(8,128)(2,1)} %bitcast.4), calls=%async_computation | async-start | bytes 1048576 | tf_op jit(solution)/shard_map/all_to_all | solution.py:484
  21.8 14.9 %copy-start.3 = (bf16[128,2048]{1,0:T(8,128)(2,1)S(1)}, bf16[128,2048]{1,0:T(8,128)(2,1)}, u32[]{:S(2)}) copy-start(bf16[128,2048]{1,0:T(8,128)(2,1)} %act_own.1) | copy-start | bytes 1572868
  35.5 6.3 %copy-start.2 = (bf16[2048,64]{0,1:T(8,128)(2,1)S(1)}, bf16[2048,64]{0,1:T(8,128)(2,1)}, u32[]{:S(2)}) copy-start(bf16[2048,64]{0,1:T(8,128)(2,1)} %param.17) | copy-start | bytes 786436
  35.5 6.3 %copy-start.4 = (bf16[64,2048]{1,0:T(8,128)(2,1)S(1)}, bf16[64,2048]{1,0:T(8,128)(2,1)}, u32[]{:S(2)}) copy-start(bf16[64,2048]{1,0:T(8,128)(2,1)} %refs_1_.1) | copy-start | bytes 786436
  35.5 6.3 %copy-start.6 = (f32[2048]{0:T(1024)S(1)}, f32[2048]{0:T(1024)}, u32[]{:S(2)}) copy-start(f32[2048]{0:T(1024)} %param.14) | copy-start | bytes 24580
  35.7 4.9 %copy-start = (bf16[400,2048]{1,0:T(8,128)(2,1)}, bf16[400,2048]{1,0:T(8,128)(2,1)S(1)}, u32[]{:S(2)}) copy-start(bf16[400,2048]{1,0:T(8,128)(2,1)S(1)} %shard_map.114.sides) | copy-start | bytes 4915204
  35.7 4.8 %collective-permute-start.4 = (bf16[400,2048]{1,0:T(8,128)(2,1)S(1)}, bf16[400,2048]{1,0:T(8,128)(2,1)S(1)}, u32[]{:S(2)}, u32[]{:S(2)}) collective-permute-start(bf16[400,2048]{1,0:T(8,128)(2,1)S(1)} %shard_map.114.sides), channel_id=1, source_target_pairs={{0,4},{4,0},{1,5},{5,1},{2,6},{6,2},{3,7},{7,3},{8,12},{12,8},{9,1... | collective-permute-start | bytes 4915208 | tf_op jit(solution)/shard_map/ppermute | solution.py:64
  36.6 3.9 %collective-permute-start = (bf16[128,2048]{1,0:T(8,128)(2,1)S(1)}, bf16[128,2048]{1,0:T(8,128)(2,1)S(1)}, u32[]{:S(2)}, u32[]{:S(2)}) collective-permute-start(bf16[128,2048]{1,0:T(8,128)(2,1)S(1)} %copy-done.3), channel_id=1, source_target_pairs={{0,4},{4,0},{1,5},{5,1},{2,6},{6,2},{3,7},{7,3},{8,12},{12,8},{9,1... | collective-permute-start | bytes 1572872 | tf_op jit(solution)/shard_map/ppermute | solution.py:64
  40.5 0.8 copy-start.9
  40.5 1.3 copy-start.8
  53.4 1.6 collective-permute-start.5
  55.1 6.3 %collective-permute-start.8 = (f32[64,512]{1,0:T(8,128)S(1)}, f32[64,512]{1,0:T(8,128)S(1)}, u32[]{:S(2)}, u32[]{:S(2)}) collective-permute-start(f32[64,512]{1,0:T(8,128)S(1)} %add.3.own), channel_id=1, source_target_pairs={{0,2},{1,3},{2,0},{3,1},{4,6},{5,7},{6,4},{7,5},{8,10},{9,11},{10,... | collective-permute-start | bytes 393224 | tf_op jit(solution)/shard_map/ppermute | solution.py:64
  56.9 7.9 %collective-permute-start.7 = (f32[64,512]{1,0:T(8,128)S(1)}, f32[64,512]{1,0:T(8,128)S(1)}, u32[]{:S(2)}, u32[]{:S(2)}) collective-permute-start(f32[64,512]{1,0:T(8,128)S(1)} %add.3.own), channel_id=1, source_target_pairs={{0,1},{1,2},{2,3},{3,0},{4,5},{5,6},{6,7},{7,4},{8,9},{9,10},{10,1... | collective-permute-start | bytes 393224 | tf_op jit(solution)/shard_map/ppermute | solution.py:64
  57.6 7.2 %collective-permute-start.6 = (f32[64,512]{1,0:T(8,128)S(1)}, f32[64,512]{1,0:T(8,128)S(1)}, u32[]{:S(2)}, u32[]{:S(2)}) collective-permute-start(f32[64,512]{1,0:T(8,128)S(1)} %add.3.own), channel_id=1, source_target_pairs={{0,3},{1,0},{2,1},{3,2},{4,7},{5,4},{6,5},{7,6},{8,11},{9,8},{10,9... | collective-permute-start | bytes 393224 | tf_op jit(solution)/shard_map/ppermute | solution.py:64
  65.4 1.6 collective-permute-start.9
  75.4 12.3 %collective-permute-start.10 = (bf16[400,512]{1,0:T(8,128)(2,1)S(1)}, bf16[400,512]{1,0:T(8,128)(2,1)S(1)}, u32[]{:S(2)}, u32[]{:S(2)}) collective-permute-start(bf16[400,512]{1,0:T(8,128)(2,1)S(1)} %get-tuple-element.49), channel_id=1, source_target_pairs={{0,16},{8,24},{16,0},{24,8},{1,17},{9,25},{17,1},{25,9},{2,18},{10... | collective-permute-start | bytes 1228808 | tf_op jit(solution)/shard_map/ppermute | solution.py:64
  77.7 12.2 %collective-permute-start.11 = (bf16[400,512]{1,0:T(8,128)(2,1)S(1)}, bf16[400,512]{1,0:T(8,128)(2,1)S(1)}, u32[]{:S(2)}, u32[]{:S(2)}) collective-permute-start(bf16[400,512]{1,0:T(8,128)(2,1)S(1)} %get-tuple-element.50), channel_id=1, source_target_pairs={{0,64},{32,96},{64,0},{96,32},{1,65},{33,97},{65,1},{97,33},{2,66}... | collective-permute-start | bytes 1228808 | tf_op jit(solution)/shard_map/ppermute | solution.py:64
  80.6 16.6 %collective-permute-start.12 = (bf16[400,512]{1,0:T(8,128)(2,1)S(1)}, bf16[400,512]{1,0:T(8,128)(2,1)S(1)}, u32[]{:S(2)}, u32[]{:S(2)}) collective-permute-start(bf16[400,512]{1,0:T(8,128)(2,1)S(1)} %get-tuple-element.51), channel_id=1, source_target_pairs={{0,8},{8,16},{16,24},{24,0},{1,9},{9,17},{17,25},{25,1},{2,10},{10... | collective-permute-start | bytes 1228808 | tf_op jit(solution)/shard_map/ppermute | solution.py:64
  80.9 18.5 %collective-permute-start.13 = (bf16[400,512]{1,0:T(8,128)(2,1)S(1)}, bf16[400,512]{1,0:T(8,128)(2,1)S(1)}, u32[]{:S(2)}, u32[]{:S(2)}) collective-permute-start(bf16[400,512]{1,0:T(8,128)(2,1)S(1)} %get-tuple-element.52), channel_id=1, source_target_pairs={{0,32},{32,64},{64,96},{96,0},{1,33},{33,65},{65,97},{97,1},{2,34}... | collective-permute-start | bytes 1228808 | tf_op jit(solution)/shard_map/ppermute | solution.py:64
  81.3 18.1 %collective-permute-start.14 = (bf16[400,512]{1,0:T(8,128)(2,1)S(1)}, bf16[400,512]{1,0:T(8,128)(2,1)S(1)}, u32[]{:S(2)}, u32[]{:S(2)}) collective-permute-start(bf16[400,512]{1,0:T(8,128)(2,1)S(1)} %get-tuple-element.53), channel_id=1, source_target_pairs={{0,24},{8,0},{16,8},{24,16},{1,25},{9,1},{17,9},{25,17},{2,26},{10... | collective-permute-start | bytes 1228808 | tf_op jit(solution)/shard_map/ppermute | solution.py:64
  87.7 11.6 %collective-permute-start.15 = (bf16[400,512]{1,0:T(8,128)(2,1)S(1)}, bf16[400,512]{1,0:T(8,128)(2,1)S(1)}, u32[]{:S(2)}, u32[]{:S(2)}) collective-permute-start(bf16[400,512]{1,0:T(8,128)(2,1)S(1)} %get-tuple-element.54), channel_id=1, source_target_pairs={{0,96},{32,0},{64,32},{96,64},{1,97},{33,1},{65,33},{97,65},{2,98}... | collective-permute-start | bytes 1228808 | tf_op jit(solution)/shard_map/ppermute | solution.py:64
  100.8 7.1 %collective-permute-start.16 = (bf16[448,128]{1,0:T(8,128)(2,1)S(1)}, bf16[448,128]{1,0:T(8,128)(2,1)S(1)}, u32[]{:S(2)}, u32[]{:S(2)}) collective-permute-start(bf16[448,128]{1,0:T(8,128)(2,1)S(1)} %get-tuple-element.57), channel_id=1, source_target_pairs={{0,64},{32,96},{64,0},{96,32},{1,65},{33,97},{65,1},{97,33},{2,66}... | collective-permute-start | bytes 344072 | tf_op jit(solution)/shard_map/ppermute | solution.py:64
  102.8 6.6 %collective-permute-start.17 = (bf16[448,128]{1,0:T(8,128)(2,1)S(1)}, bf16[448,128]{1,0:T(8,128)(2,1)S(1)}, u32[]{:S(2)}, u32[]{:S(2)}) collective-permute-start(bf16[448,128]{1,0:T(8,128)(2,1)S(1)} %get-tuple-element.58), channel_id=1, source_target_pairs={{0,16},{8,24},{16,0},{24,8},{1,17},{9,25},{17,1},{25,9},{2,18},{10... | collective-permute-start | bytes 344072 | tf_op jit(solution)/shard_map/ppermute | solution.py:64
  104.1 5.4 %collective-permute-start.18 = (bf16[448,128]{1,0:T(8,128)(2,1)S(1)}, bf16[448,128]{1,0:T(8,128)(2,1)S(1)}, u32[]{:S(2)}, u32[]{:S(2)}) collective-permute-start(bf16[448,128]{1,0:T(8,128)(2,1)S(1)} %get-tuple-element.59), channel_id=1, source_target_pairs={{0,32},{32,64},{64,96},{96,0},{1,33},{33,65},{65,97},{97,1},{2,34}... | collective-permute-start | bytes 344072 | tf_op jit(solution)/shard_map/ppermute | solution.py:64
  104.9 6.4 %collective-permute-start.19 = (bf16[448,128]{1,0:T(8,128)(2,1)S(1)}, bf16[448,128]{1,0:T(8,128)(2,1)S(1)}, u32[]{:S(2)}, u32[]{:S(2)}) collective-permute-start(bf16[448,128]{1,0:T(8,128)(2,1)S(1)} %get-tuple-element.60), channel_id=1, source_target_pairs={{0,8},{8,16},{16,24},{24,0},{1,9},{9,17},{17,25},{25,1},{2,10},{10... | collective-permute-start | bytes 344072 | tf_op jit(solution)/shard_map/ppermute | solution.py:64
  105.3 6.1 %collective-permute-start.20 = (bf16[448,128]{1,0:T(8,128)(2,1)S(1)}, bf16[448,128]{1,0:T(8,128)(2,1)S(1)}, u32[]{:S(2)}, u32[]{:S(2)}) collective-permute-start(bf16[448,128]{1,0:T(8,128)(2,1)S(1)} %get-tuple-element.61), channel_id=1, source_target_pairs={{0,96},{32,0},{64,32},{96,64},{1,97},{33,1},{65,33},{97,65},{2,98}... | collective-permute-start | bytes 344072 | tf_op jit(solution)/shard_map/ppermute | solution.py:64
  107.9 3.9 %collective-permute-start.21 = (bf16[448,128]{1,0:T(8,128)(2,1)S(1)}, bf16[448,128]{1,0:T(8,128)(2,1)S(1)}, u32[]{:S(2)}, u32[]{:S(2)}) collective-permute-start(bf16[448,128]{1,0:T(8,128)(2,1)S(1)} %get-tuple-element.62), channel_id=1, source_target_pairs={{0,24},{8,0},{16,8},{24,16},{1,25},{9,1},{17,9},{25,17},{2,26},{10... | collective-permute-start | bytes 344072 | tf_op jit(solution)/shard_map/ppermute | solution.py:64
  112.1 6.2 %collective-permute-start.26 = (bf16[3,128,128]{2,1,0:T(8,128)(2,1)S(1)}, bf16[3,128,128]{2,1,0:T(8,128)(2,1)S(1)}, u32[]{:S(2)}, u32[]{:S(2)}) collective-permute-start(bf16[3,128,128]{2,1,0:T(8,128)(2,1)S(1)} %get-tuple-element.65.refs_6_), channel_id=1, source_target_pairs={{0,64},{32,96},{64,0},{96,32},{1,65},{33,97},{65,1},{97,33},{2,66}... | collective-permute-start | bytes 294920 | tf_op jit(solution)/shard_map/ppermute | solution.py:64
  112.2 7.4 %collective-permute-start.24 = (bf16[3,128,128]{2,1,0:T(8,128)(2,1)S(1)}, bf16[3,128,128]{2,1,0:T(8,128)(2,1)S(1)}, u32[]{:S(2)}, u32[]{:S(2)}) collective-permute-start(bf16[3,128,128]{2,1,0:T(8,128)(2,1)S(1)} %get-tuple-element.65.refs_6_), channel_id=1, source_target_pairs={{0,32},{32,64},{64,96},{96,0},{1,33},{33,65},{65,97},{97,1},{2,34}... | collective-permute-start | bytes 294920 | tf_op jit(solution)/shard_map/ppermute | solution.py:64
  113.6 6.0 %collective-permute-start.22 = (bf16[3,128,128]{2,1,0:T(8,128)(2,1)S(1)}, bf16[3,128,128]{2,1,0:T(8,128)(2,1)S(1)}, u32[]{:S(2)}, u32[]{:S(2)}) collective-permute-start(bf16[3,128,128]{2,1,0:T(8,128)(2,1)S(1)} %get-tuple-element.65.refs_6_), channel_id=1, source_target_pairs={{0,96},{32,0},{64,32},{96,64},{1,97},{33,1},{65,33},{97,65},{2,98}... | collective-permute-start | bytes 294920 | tf_op jit(solution)/shard_map/ppermute | solution.py:64
  114.9 5.0 %collective-permute-start.27 = (bf16[3,128,128]{2,1,0:T(8,128)(2,1)S(1)}, bf16[3,128,128]{2,1,0:T(8,128)(2,1)S(1)}, u32[]{:S(2)}, u32[]{:S(2)}) collective-permute-start(bf16[3,128,128]{2,1,0:T(8,128)(2,1)S(1)} %get-tuple-element.66.refs_7_), channel_id=1, source_target_pairs={{0,16},{8,24},{16,0},{24,8},{1,17},{9,25},{17,1},{25,9},{2,18},{10... | collective-permute-start | bytes 294920 | tf_op jit(solution)/shard_map/ppermute | solution.py:64
  116.5 5.0 %collective-permute-start.25 = (bf16[3,128,128]{2,1,0:T(8,128)(2,1)S(1)}, bf16[3,128,128]{2,1,0:T(8,128)(2,1)S(1)}, u32[]{:S(2)}, u32[]{:S(2)}) collective-permute-start(bf16[3,128,128]{2,1,0:T(8,128)(2,1)S(1)} %get-tuple-element.66.refs_7_), channel_id=1, source_target_pairs={{0,8},{8,16},{16,24},{24,0},{1,9},{9,17},{17,25},{25,1},{2,10},{10... | collective-permute-start | bytes 294920 | tf_op jit(solution)/shard_map/ppermute | solution.py:64
  118.3 3.8 %collective-permute-start.23 = (bf16[3,128,128]{2,1,0:T(8,128)(2,1)S(1)}, bf16[3,128,128]{2,1,0:T(8,128)(2,1)S(1)}, u32[]{:S(2)}, u32[]{:S(2)}) collective-permute-start(bf16[3,128,128]{2,1,0:T(8,128)(2,1)S(1)} %get-tuple-element.66.refs_7_), channel_id=1, source_target_pairs={{0,24},{8,0},{16,8},{24,16},{1,25},{9,1},{17,9},{25,17},{2,26},{10... | collective-permute-start | bytes 294920 | tf_op jit(solution)/shard_map/ppermute | solution.py:64
  122.1 9.3 %collective-permute-start.33 = (bf16[4,3,128,128]{3,2,1,0:T(8,128)(2,1)S(1)}, bf16[4,3,128,128]{3,2,1,0:T(8,128)(2,1)S(1)}, u32[]{:S(2)}, u32[]{:S(2)}) collective-permute-start(bf16[4,3,128,128]{3,2,1,0:T(8,128)(2,1)S(1)} %get-tuple-element.68.line), channel_id=1, source_target_pairs={{0,16},{8,24},{16,0},{24,8},{1,17},{9,25},{17,1},{25,9},{2,18},{10... | collective-permute-start | bytes 1179656 | tf_op jit(solution)/shard_map/ppermute | solution.py:64
  123.2 12.1 %collective-permute-start.32 = (bf16[4,3,128,128]{3,2,1,0:T(8,128)(2,1)S(1)}, bf16[4,3,128,128]{3,2,1,0:T(8,128)(2,1)S(1)}, u32[]{:S(2)}, u32[]{:S(2)}) collective-permute-start(bf16[4,3,128,128]{3,2,1,0:T(8,128)(2,1)S(1)} %get-tuple-element.68.line), channel_id=1, source_target_pairs={{0,8},{8,16},{16,24},{24,0},{1,9},{9,17},{17,25},{25,1},{2,10},{10... | collective-permute-start | bytes 1179656 | tf_op jit(solution)/shard_map/ppermute | solution.py:64
  125.3 10.4 %collective-permute-start.31 = (bf16[4,3,128,128]{3,2,1,0:T(8,128)(2,1)S(1)}, bf16[4,3,128,128]{3,2,1,0:T(8,128)(2,1)S(1)}, u32[]{:S(2)}, u32[]{:S(2)}) collective-permute-start(bf16[4,3,128,128]{3,2,1,0:T(8,128)(2,1)S(1)} %get-tuple-element.68.line), channel_id=1, source_target_pairs={{0,24},{8,0},{16,8},{24,16},{1,25},{9,1},{17,9},{25,17},{2,26},{10... | collective-permute-start | bytes 1179656 | tf_op jit(solution)/shard_map/ppermute | solution.py:64
  125.9 24.8 %collective-permute-start.30 = (bf16[4,3,128,128]{3,2,1,0:T(8,128)(2,1)S(1)}, bf16[4,3,128,128]{3,2,1,0:T(8,128)(2,1)S(1)}, u32[]{:S(2)}, u32[]{:S(2)}) collective-permute-start(bf16[4,3,128,128]{3,2,1,0:T(8,128)(2,1)S(1)} %get-tuple-element.67.refs_1_.refs_3_), channel_id=1, source_target_pairs={{0,64},{32,96},{64,0},{96,32},{1,65},{33,97},{65,1},{97,33},{2,66}... | collective-permute-start | bytes 1179656 | tf_op jit(solution)/shard_map/ppermute | solution.py:64
  127.0 23.7 %collective-permute-start.29 = (bf16[4,3,128,128]{3,2,1,0:T(8,128)(2,1)S(1)}, bf16[4,3,128,128]{3,2,1,0:T(8,128)(2,1)S(1)}, u32[]{:S(2)}, u32[]{:S(2)}) collective-permute-start(bf16[4,3,128,128]{3,2,1,0:T(8,128)(2,1)S(1)} %get-tuple-element.67.refs_1_.refs_3_), channel_id=1, source_target_pairs={{0,32},{32,64},{64,96},{96,0},{1,33},{33,65},{65,97},{97,1},{2,34}... | collective-permute-start | bytes 1179656 | tf_op jit(solution)/shard_map/ppermute | solution.py:64
  131.4 19.4 %collective-permute-start.28 = (bf16[4,3,128,128]{3,2,1,0:T(8,128)(2,1)S(1)}, bf16[4,3,128,128]{3,2,1,0:T(8,128)(2,1)S(1)}, u32[]{:S(2)}, u32[]{:S(2)}) collective-permute-start(bf16[4,3,128,128]{3,2,1,0:T(8,128)(2,1)S(1)} %get-tuple-element.67.refs_1_.refs_3_), channel_id=1, source_target_pairs={{0,96},{32,0},{64,32},{96,64},{1,97},{33,1},{65,33},{97,65},{2,98}... | collective-permute-start | bytes 1179656 | tf_op jit(solution)/shard_map/ppermute | solution.py:64
  135.9 15.2 %collective-permute-start.35 = (bf16[5,4,3,128,128]{4,3,2,1,0:T(8,128)(2,1)S(1)}, bf16[5,4,3,128,128]{4,3,2,1,0:T(8,128)(2,1)S(1)}, u32[]{:S(2)}, u32[]{:S(2)}) collective-permute-start(bf16[5,4,3,128,128]{4,3,2,1,0:T(8,128)(2,1)S(1)} %shard_map.122.refs_0_.refs_1_), channel_id=1, source_target_pairs={{0,4},{4,0},{1,5},{5,1},{2,6},{6,2},{3,7},{7,3},{8,12},{12,8},{9,1... | collective-permute-start | bytes 5898248 | tf_op jit(solution)/shard_map/ppermute | solution.py:64
  150.9 7.4 %collective-permute-start.34 = (bf16[4,4,3,128,128]{4,3,2,1,0:T(8,128)(2,1)S(1)}, bf16[4,4,3,128,128]{4,3,2,1,0:T(8,128)(2,1)S(1)}, u32[]{:S(2)}, u32[]{:S(2)}) collective-permute-start(bf16[4,4,3,128,128]{4,3,2,1,0:T(8,128)(2,1)S(1)} %shard_map.124.refs_2_), channel_id=1, source_target_pairs={{0,4},{4,0},{1,5},{5,1},{2,6},{6,2},{3,7},{7,3},{8,12},{12,8},{9,1... | collective-permute-start | bytes 4718600 | tf_op jit(solution)/shard_map/ppermute | solution.py:64

commit v8 on v7

--- a/solution.py
+++ b/solution.py
@@ -68,7 +68,7 @@
     return jax.ShapeDtypeStruct(dims, kind)
 
 
-def bucket_kernel(rows_far, dest_far, unused, out, rows, dest_row, sems):
+def bucket_kernel(rows_far, dest_far, out, rows, dest_row, sems):
     loads = [
         pltpu.make_async_copy(rows_far, rows, sems.at[0]),
         pltpu.make_async_copy(dest_far, dest_row, sems.at[1]),
@@ -477,7 +477,7 @@
     )
     (sent,) = call(
         bucket_kernel, near(shape((4, 16, 2, 16, 128), bf16)),
-        *far(cache_rows, row_dest.reshape(1, 128)), (ANY, mix),
+        *far(cache_rows, row_dest.reshape(1, 128)),
         scratch=[pltpu.VMEM((128, 128), bf16), pltpu.VMEM((1, 128), jnp.int32), dma((2,))],
         mib=LARGE,
     )

time: 162 us -> 166 us (1.025)
  local copies, waits for them, and re-layouts: 2.32 us -> 5.1 us
  starting transfers between devices: 66.3 us -> 68.1 us
    ppermute x36, waiting for transfers between devices: 35.3 us -> 31.5 us  [shift(): lax.ppermute(value, axis, [(i, (i + offset) % size) for i in range(size)])]
    all_to_all x1, waiting for transfers between devices: 13 us -> 16.2 us  [shards(): lax.all_to_all(sent.reshape(128, 16, 128), ('frame', 'y', 'x', 'core'), 0...]
    unnamed x20 -> x22, local copies, waits for them, and re-layouts: 2.32 us -> 5.1 us
    ppermute x36, starting transfers between devices: 58.3 us -> 60 us  [shift(): lax.ppermute(value, axis, [(i, (i + offset) % size) for i in range(size)])]
  transfers between devices with their start and end apart: 37 -> 37, of which waited for: 17 -> 16; matrix products, arithmetic and copies ran while one was open for 0% -> 0% of each run, Pallas kernels for 11% -> 10%
where the time goes in v8:
time: 166 us
  starting transfers between devices  68.1 us (41%)
  waiting for transfers between devices  47.7 us (29%)
  Pallas kernels  43.3 us (26%)
  local copies, waits for them, and re-layouts  5.1 us (3%)
  between operations  1.76 us (1%)
    ppermute x36, starting transfers between devices, shift(): lax.ppermute(value, axis, [(i, (i + offset) % size) for i in range(size)])  60 us
    ppermute x36, waiting for transfers between devices, shift(): lax.ppermute(value, axis, [(i, (i + offset) % size) for i in range(size)])  31.5 us
    pallas_call x12, Pallas kernels, call(): pl.pallas_call(kernel, in_specs=[spec for spec, _ in operands], out_specs...  29 us
    all_to_all x1, waiting for transfers between devices, shards(): lax.all_to_all(sent.reshape(128, 16, 128), ('frame', 'y', 'x', 'core'), 0...  16.2 us
    pallas_call x3, Pallas kernels, assemble(): pl.pallas_call(functools.partial(assemble_kernel, tags, len(arrays), len(...  14.4 us
    all_to_all x1, starting transfers between devices, shards(): lax.all_to_all(sent.reshape(128, 16, 128), ('frame', 'y', 'x', 'core'), 0...  8.04 us
    unnamed x22, local copies, waits for them, and re-layouts  5.1 us
  transfers between devices with their start and end apart: 37, of which 16 were waited for; matrix products, arithmetic and copies ran while one was open for 0% of the time, Pallas kernels for 10%

profile of v8, /device:TPU:1, one launch (start us, length us, event | category | flops | bytes accessed | tf_op | source)
XLA Modules:
  0.0 166.1 jit_solution(13084239269182226766)
XLA Ops:
  0.6 4.5 %collective-permute-start.2 = (bf16[128,2048]{1,0:T(8,128)(2,1)}, bf16[128,2048]{1,0:T(8,128)(2,1)S(1)}, u32[]{:S(2)}, u32[]{:S(2)}) collective-permute-start(bf16[128,2048]{1,0:T(8,128)(2,1)} %act_own.1), channel_id=1, source_target_pairs={{0,2},{1,3},{2,0},{3,1},{4,6},{5,7},{6,4},{7,5},{8,10},{9,11},{10,... | collective-permute-start | bytes 1572872 | tf_op jit(solution)/shard_map/ppermute | solution.py:64
  5.9 1.9 %collective-permute-start.3 = (bf16[128,2048]{1,0:T(8,128)(2,1)}, bf16[128,2048]{1,0:T(8,128)(2,1)S(1)}, u32[]{:S(2)}, u32[]{:S(2)}) collective-permute-start(bf16[128,2048]{1,0:T(8,128)(2,1)} %act_own.1), channel_id=1, source_target_pairs={{0,3},{1,0},{2,1},{3,2},{4,7},{5,4},{6,5},{7,6},{8,11},{9,8},{10,9... | collective-permute-start | bytes 1572872 | tf_op jit(solution)/shard_map/ppermute | solution.py:64
  9.2 1.1 shard_map.112
  10.3 8.0 %all-to-all-start = ((bf16[128,16,128]{2,1,0:T(8,128)(2,1)}), bf16[128,16,128]{2,1,0:T(8,128)(2,1)S(1)}, u32[]{:S(2)}, u32[]{:S(2)}) async-start(bf16[128,16,128]{2,1,0:T(8,128)(2,1)} %bitcast.1), calls=%async_computation | async-start | bytes 1048576 | tf_op jit(solution)/shard_map/all_to_all | solution.py:484
  19.1 16.2 %all-to-all-done = bf16[128,16,128]{2,1,0:T(8,128)(2,1)S(1)} async-done(((bf16[128,16,128]{2,1,0:T(8,128)(2,1)}), bf16[128,16,128]{2,1,0:T(8,128)(2,1)S(1)}, u32[]{:S(2)}, u32[]{:S(2)}) %all-to-all-start) | async-done | bytes 524320 | tf_op jit(solution)/shard_map/all_to_all | solution.py:484
  36.9 1.0 copy-done.4
  38.0 1.0 copy-done.6
  39.8 3.7 %shard_map.115 = (bf16[768,2048]{1,0:T(8,128)(2,1)}, f32[256,64]{1,0:T(8,128)S(1)}, f32[64,256]{1,0:T(8,128)S(1)}) custom-call(s32[2]{0:T(128)S(1)} %pad_add_fusion.place, bf16[3,2048,512]{2,1,0:T(8,128)(2,1)} %w.1, bf16[512,2048]{1,0:T(8,128)(2,1)} %w_out.1, bf16[64,2048]{1,0:T(8,128)(2,1)S(1)} %bitcast.11), custom_call_target="tpu_custom_call" | custom-call | bytes 1024 | tf_op jit(solution)/shard_map/pallas_call | solution.py:436
  43.5 1.3 shard_map.114.refs_0_
  44.9 11.7 %shard_map.116 = (bf16[1024,2048]{1,0:T(8,128)(2,1)}, bf16[1024,1024]{1,0:T(8,128)(2,1)}, f32[4,16,128]{2,1,0:T(8,128)S(1)}, f32[64,512]{1,0:T(8,128)S(1)}, f32[64,512]{1,0:T(8,128)S(1)}) custom-call(bf16[128,2048]{1,0:T(8,128)(2,1)S(1)} %copy-done.2, bf16[128,2048]{1,0:T(8,128)(2,1)} %collective-permute-done.act_theirs, bf16[400,2048]{1,0:T(8,128)(2,1)} %copy-done, ...), custom_call_target="tpu_custom_call" | custom-call | bytes 1024 | tf_op jit(solution)/shard_map/pallas_call | solution.py:436
  57.2 1.0 collective-permute-done.5
  58.3 2.4 %collective-permute-start.8 = (f32[64,512]{1,0:T(8,128)S(1)}, f32[64,512]{1,0:T(8,128)S(1)}, u32[]{:S(2)}, u32[]{:S(2)}) collective-permute-start(f32[64,512]{1,0:T(8,128)S(1)} %add.3.own), channel_id=1, source_target_pairs={{0,2},{1,3},{2,0},{3,1},{4,6},{5,7},{6,4},{7,5},{8,10},{9,11},{10,... | collective-permute-start | bytes 393224 | tf_op jit(solution)/shard_map/ppermute | solution.py:64
  61.4 1.9 %collective-permute-start.6 = (f32[64,512]{1,0:T(8,128)S(1)}, f32[64,512]{1,0:T(8,128)S(1)}, u32[]{:S(2)}, u32[]{:S(2)}) collective-permute-start(f32[64,512]{1,0:T(8,128)S(1)} %add.3.own), channel_id=1, source_target_pairs={{0,3},{1,0},{2,1},{3,2},{4,7},{5,4},{6,5},{7,6},{8,11},{9,8},{10,9... | collective-permute-start | bytes 393224 | tf_op jit(solution)/shard_map/ppermute | solution.py:64
  63.3 1.2 collective-permute-done.8.two
  64.6 3.0 %collective-permute-done.7.one = f32[64,512]{1,0:T(8,128)S(1)} collective-permute-done((f32[64,512]{1,0:T(8,128)S(1)}, f32[64,512]{1,0:T(8,128)S(1)}, u32[]{:S(2)}, u32[]{:S(2)}) %collective-permute-start.7) | collective-permute-done | bytes 131104 | tf_op jit(solution)/shard_map/ppermute | solution.py:64
  68.2 1.1 collective-permute-start.9
  69.4 0.9 collective-permute-done.9.error_other
  70.3 8.4 %shard_map.118 = (bf16[400,512]{1,0:T(8,128)(2,1)S(1)}, bf16[400,512]{1,0:T(8,128)(2,1)S(1)}, bf16[400,512]{1,0:T(8,128)(2,1)S(1)}, bf16[400,512]{1,0:T(8,128)(2...) custom-call(s32[3]{0:T(128)S(1)} %pad_add_fusion.1.place, ...), custom_call_target="tpu_custom_call" | custom-call | bytes 1024 | tf_op jit(solution)/shard_map/pallas_call | solution.py:436
  78.7 2.8 %collective-permute-start.10 = (bf16[400,512]{1,0:T(8,128)(2,1)S(1)}, bf16[400,512]{1,0:T(8,128)(2,1)S(1)}, u32[]{:S(2)}, u32[]{:S(2)}) collective-permute-start(bf16[400,512]{1,0:T(8,128)(2,1)S(1)} %get-tuple-element.49), channel_id=1, source_target_pairs={{0,16},{8,24},{16,0},{24,8},{1,17},{9,25},{17,1},{25,9},{2,18},{10... | collective-permute-start | bytes 1228808 | tf_op jit(solution)/shard_map/ppermute | solution.py:64
  81.5 2.9 %collective-permute-start.11 = (bf16[400,512]{1,0:T(8,128)(2,1)S(1)}, bf16[400,512]{1,0:T(8,128)(2,1)S(1)}, u32[]{:S(2)}, u32[]{:S(2)}) collective-permute-start(bf16[400,512]{1,0:T(8,128)(2,1)S(1)} %get-tuple-element.50), channel_id=1, source_target_pairs={{0,64},{32,96},{64,0},{96,32},{1,65},{33,97},{65,1},{97,33},{2,66}... | collective-permute-start | bytes 1228808 | tf_op jit(solution)/shard_map/ppermute | solution.py:64
  85.2 2.4 %collective-permute-start.14 = (bf16[400,512]{1,0:T(8,128)(2,1)S(1)}, bf16[400,512]{1,0:T(8,128)(2,1)S(1)}, u32[]{:S(2)}, u32[]{:S(2)}) collective-permute-start(bf16[400,512]{1,0:T(8,128)(2,1)S(1)} %get-tuple-element.53), channel_id=1, source_target_pairs={{0,24},{8,0},{16,8},{24,16},{1,25},{9,1},{17,9},{25,17},{2,26},{10... | collective-permute-start | bytes 1228808 | tf_op jit(solution)/shard_map/ppermute | solution.py:64
  87.5 3.5 %collective-permute-done.10.refs_0_ = bf16[400,512]{1,0:T(8,128)(2,1)S(1)} collective-permute-done((bf16[400,512]{1,0:T(8,128)(2,1)S(1)}, bf16[400,512]{1,0:T(8,128)(2,1)S(1)}, u32[]{:S(2)}, u32[]{:S(2)}) %collective-permute-start.10) | collective-permute-done | bytes 409632 | tf_op jit(solution)/shard_map/ppermute | solution.py:64
  91.0 2.7 %collective-permute-start.15 = (bf16[400,512]{1,0:T(8,128)(2,1)S(1)}, bf16[400,512]{1,0:T(8,128)(2,1)S(1)}, u32[]{:S(2)}, u32[]{:S(2)}) collective-permute-start(bf16[400,512]{1,0:T(8,128)(2,1)S(1)} %get-tuple-element.54), channel_id=1, source_target_pairs={{0,96},{32,0},{64,32},{96,64},{1,97},{33,1},{65,33},{97,65},{2,98}... | collective-permute-start | bytes 1228808 | tf_op jit(solution)/shard_map/ppermute | solution.py:64
  93.7 6.7 %collective-permute-done.12.refs_2_ = bf16[400,512]{1,0:T(8,128)(2,1)S(1)} collective-permute-done((bf16[400,512]{1,0:T(8,128)(2,1)S(1)}, bf16[400,512]{1,0:T(8,128)(2,1)S(1)}, u32[]{:S(2)}, u32[]{:S(2)}) %collective-permute-start.12) | collective-permute-done | bytes 409632 | tf_op jit(solution)/shard_map/ppermute | solution.py:64
  100.5 2.7 %collective-permute-done.13.refs_3_ = bf16[400,512]{1,0:T(8,128)(2,1)S(1)} collective-permute-done((bf16[400,512]{1,0:T(8,128)(2,1)S(1)}, bf16[400,512]{1,0:T(8,128)(2,1)S(1)}, u32[]{:S(2)}, u32[]{:S(2)}) %collective-permute-start.13) | collective-permute-done | bytes 409632 | tf_op jit(solution)/shard_map/ppermute | solution.py:64
  103.2 1.5 shard_map.119
  104.7 2.0 %collective-permute-start.16 = (bf16[448,128]{1,0:T(8,128)(2,1)S(1)}, bf16[448,128]{1,0:T(8,128)(2,1)S(1)}, u32[]{:S(2)}, u32[]{:S(2)}) collective-permute-start(bf16[448,128]{1,0:T(8,128)(2,1)S(1)} %get-tuple-element.57), channel_id=1, source_target_pairs={{0,64},{32,96},{64,0},{96,32},{1,65},{33,97},{65,1},{97,33},{2,66}... | collective-permute-start | bytes 344072 | tf_op jit(solution)/shard_map/ppermute | solution.py:64
  106.7 1.2 collective-permute-start.17
  107.9 1.0 collective-permute-start.18
  109.1 2.7 %collective-permute-start.20 = (bf16[448,128]{1,0:T(8,128)(2,1)S(1)}, bf16[448,128]{1,0:T(8,128)(2,1)S(1)}, u32[]{:S(2)}, u32[]{:S(2)}) collective-permute-start(bf16[448,128]{1,0:T(8,128)(2,1)S(1)} %get-tuple-element.61), channel_id=1, source_target_pairs={{0,96},{32,0},{64,32},{96,64},{1,97},{33,1},{65,33},{97,65},{2,98}... | collective-permute-start | bytes 344072 | tf_op jit(solution)/shard_map/ppermute | solution.py:64
  111.8 1.4 collective-permute-start.21
  113.2 2.0 %collective-permute-done.19.refs_3_ = bf16[448,128]{1,0:T(8,128)(2,1)S(1)} collective-permute-done((bf16[448,128]{1,0:T(8,128)(2,1)S(1)}, bf16[448,128]{1,0:T(8,128)(2,1)S(1)}, u32[]{:S(2)}, u32[]{:S(2)}) %collective-permute-start.19) | collective-permute-done | bytes 114720 | tf_op jit(solution)/shard_map/ppermute | solution.py:64
  116.1 1.4 collective-permute-start.24
  117.5 1.3 collective-permute-start.22
  118.8 1.6 collective-permute-start.27
  120.4 1.8 %collective-permute-start.25 = (bf16[3,128,128]{2,1,0:T(8,128)(2,1)S(1)}, bf16[3,128,128]{2,1,0:T(8,128)(2,1)S(1)}, u32[]{:S(2)}, u32[]{:S(2)}) collective-permute-start(bf16[3,128,128]{2,1,0:T(8,128)(2,1)S(1)} %get-tuple-element.66.refs_7_), channel_id=1, source_target_pairs={{0,8},{8,16},{16,24},{24,0},{1,9},{9,17},{17,25},{25,1},{2,10},{10... | collective-permute-start | bytes 294920 | tf_op jit(solution)/shard_map/ppermute | solution.py:64
  122.2 1.3 collective-permute-start.23
  123.7 1.6 collective-permute-done.25.refs_3_
  126.0 1.1 collective-permute-start.33
  127.0 2.1 %collective-permute-start.32 = (bf16[4,3,128,128]{3,2,1,0:T(8,128)(2,1)S(1)}, bf16[4,3,128,128]{3,2,1,0:T(8,128)(2,1)S(1)}, u32[]{:S(2)}, u32[]{:S(2)}) collective-permute-start(bf16[4,3,128,128]{3,2,1,0:T(8,128)(2,1)S(1)} %get-tuple-element.68.line), channel_id=1, source_target_pairs={{0,8},{8,16},{16,24},{24,0},{1,9},{9,17},{17,25},{25,1},{2,10},{10... | collective-permute-start | bytes 1179656 | tf_op jit(solution)/shard_map/ppermute | solution.py:64
  129.7 1.1 collective-permute-start.30
  131.4 3.9 %collective-permute-done.33.c = bf16[4,3,128,128]{3,2,1,0:T(8,128)(2,1)S(1)} collective-permute-done((bf16[4,3,128,128]{3,2,1,0:T(8,128)(2,1)S(1)}, bf16[4,3,128,128]{3,2,1,0:T(8,128)(2,1)S(1)}, u32[]{:S(2)}, u32[]{:S(2)}) %collective-permute-start.33) | collective-permute-done | bytes 393248 | tf_op jit(solution)/shard_map/ppermute | solution.py:64
  135.2 1.0 collective-permute-start.28
  136.2 3.1 %collective-permute-done.32.b = bf16[4,3,128,128]{3,2,1,0:T(8,128)(2,1)S(1)} collective-permute-done((bf16[4,3,128,128]{3,2,1,0:T(8,128)(2,1)S(1)}, bf16[4,3,128,128]{3,2,1,0:T(8,128)(2,1)S(1)}, u32[]{:S(2)}, u32[]{:S(2)}) %collective-permute-start.32) | collective-permute-done | bytes 393248 | tf_op jit(solution)/shard_map/ppermute | solution.py:64
  139.8 11.3 %collective-permute-start.35 = (bf16[5,4,3,128,128]{4,3,2,1,0:T(8,128)(2,1)S(1)}, bf16[5,4,3,128,128]{4,3,2,1,0:T(8,128)(2,1)S(1)}, u32[]{:S(2)}, u32[]{:S(2)}) collective-permute-start(bf16[5,4,3,128,128]{4,3,2,1,0:T(8,128)(2,1)S(1)} %shard_map.122.refs_0_.refs_1_), channel_id=1, source_target_pairs={{0,4},{4,0},{1,5},{5,1},{2,6},{6,2},{3,7},{7,3},{8,12},{12,8},{9,1... | collective-permute-start | bytes 5898248 | tf_op jit(solution)/shard_map/ppermute | solution.py:64
  151.1 3.5 %shard_map.123 = (f32[3,2048,512]{2,1,0:T(8,128)}, f32[8,128]{1,0:T(8,128)S(1)}) custom-call(s32[3]{0:T(128)S(1)} %pad_add_fusion.1.place, bf16[5,4,3,128,128]{4,3,2,1,0:T(8,128)(2,1)S(1)} %shard_map.122.refs_0_.refs_1_, bf16[4,3,128,128]{3,2,1,0:T(8,128)(2,1)S(1)} %get-tuple-element.67.refs_1_.refs_3_), custom_call_target="tpu_custom_call" | custom-call | bytes 1024 | tf_op jit(solution)/shard_map/pallas_call | solution.py:423
  155.1 7.2 %shard_map.125 = (f32[3,2048,512]{2,1,0:T(8,128)}, f32[8,128]{1,0:T(8,128)}, f32[512,2048]{1,0:T(8,128)}) custom-call(s32[3]{0:T(128)S(1)} %pad_add_fusion.1.place, bf16[5,4,3,128,128]{4,3,2,1,0:T(8,128)(2,1)S(1)} %collective-permute-done.35.refs_0_, bf16[5,4,3,128,128]{4,3,2,1,0:T(8,128)(2,1)S(1)} %shard_map.122.refs_0_.refs_1_, ...), custom_call_target="tpu_custom_call", output_to_operand_aliasing={{0}: (4, {})} | custom-call | bytes 1024 | tf_op jit(solution)/shard_map/pallas_call | solution.py:423
  162.3 3.7 %shard_map.126 = (f32[3,2048,512]{2,1,0:T(8,128)}, f32[8,128]{1,0:T(8,128)}) custom-call(s32[3]{0:T(128)S(1)} %pad_add_fusion.1.place, bf16[4,4,3,128,128]{4,3,2,1,0:T(8,128)(2,1)S(1)} %collective-permute-done.34.refs_0_, f32[3,2048,512]{2,1,0:T(8,128)} %get-tuple-element.72.refs_1_), custom_call_target="tpu_custom_call", output_to_operand_aliasing={{0}: (2, {})} | custom-call | bytes 1024 | tf_op jit(solution)/shard_map/pallas_call | solution.py:423
  (66 shorter events, 11.5 us)
Async XLA Ops:
  0.6 34.7 %collective-permute-start.2 = (bf16[128,2048]{1,0:T(8,128)(2,1)}, bf16[128,2048]{1,0:T(8,128)(2,1)S(1)}, u32[]{:S(2)}, u32[]{:S(2)}) collective-permute-start(bf16[128,2048]{1,0:T(8,128)(2,1)} %act_own.1), channel_id=1, source_target_pairs={{0,2},{1,3},{2,0},{3,1},{4,6},{5,7},{6,4},{7,5},{8,10},{9,11},{10,... | collective-permute-start | bytes 1572872 | tf_op jit(solution)/shard_map/ppermute | solution.py:64
  5.1 30.2 %collective-permute-start.1 = (bf16[128,2048]{1,0:T(8,128)(2,1)}, bf16[128,2048]{1,0:T(8,128)(2,1)S(1)}, u32[]{:S(2)}, u32[]{:S(2)}) collective-permute-start(bf16[128,2048]{1,0:T(8,128)(2,1)} %act_own.1), channel_id=1, source_target_pairs={{0,1},{1,2},{2,3},{3,0},{4,5},{5,6},{6,7},{7,4},{8,9},{9,10},{10,1... | collective-permute-start | bytes 1572872 | tf_op jit(solution)/shard_map/ppermute | solution.py:64
  5.9 30.3 %collective-permute-start.3 = (bf16[128,2048]{1,0:T(8,128)(2,1)}, bf16[128,2048]{1,0:T(8,128)(2,1)S(1)}, u32[]{:S(2)}, u32[]{:S(2)}) collective-permute-start(bf16[128,2048]{1,0:T(8,128)(2,1)} %act_own.1), channel_id=1, source_target_pairs={{0,3},{1,0},{2,1},{3,2},{4,7},{5,4},{6,5},{7,6},{8,11},{9,8},{10,9... | collective-permute-start | bytes 1572872 | tf_op jit(solution)/shard_map/ppermute | solution.py:64
  7.8 0.8 copy-start.8
  8.6 0.7 copy-start.10
  10.3 25.0 %all-to-all-start = ((bf16[128,16,128]{2,1,0:T(8,128)(2,1)}), bf16[128,16,128]{2,1,0:T(8,128)(2,1)S(1)}, u32[]{:S(2)}, u32[]{:S(2)}) async-start(bf16[128,16,128]{2,1,0:T(8,128)(2,1)} %bitcast.1), calls=%async_computation | async-start | bytes 1048576 | tf_op jit(solution)/shard_map/all_to_all | solution.py:484
  18.4 21.2 %copy-start.2 = (bf16[128,2048]{1,0:T(8,128)(2,1)S(1)}, bf16[128,2048]{1,0:T(8,128)(2,1)}, u32[]{:S(2)}) copy-start(bf16[128,2048]{1,0:T(8,128)(2,1)} %act_own.1) | copy-start | bytes 1572868
  18.4 21.4 %copy-start.1 = (bf16[2048,64]{0,1:T(8,128)(2,1)S(1)}, bf16[2048,64]{0,1:T(8,128)(2,1)}, u32[]{:S(2)}) copy-start(bf16[2048,64]{0,1:T(8,128)(2,1)} %param.17) | copy-start | bytes 786436
  35.3 0.8 copy-start.3
  36.1 0.8 copy-start.5
  36.9 1.0 copy-start.4
  38.0 1.0 copy-start.6
  39.1 4.4 %copy-start = (bf16[400,2048]{1,0:T(8,128)(2,1)}, bf16[400,2048]{1,0:T(8,128)(2,1)S(1)}, u32[]{:S(2)}) copy-start(bf16[400,2048]{1,0:T(8,128)(2,1)S(1)} %shard_map.113.sides) | copy-start | bytes 4915204
  39.1 5.7 %collective-permute-start.4 = (bf16[400,2048]{1,0:T(8,128)(2,1)S(1)}, bf16[400,2048]{1,0:T(8,128)(2,1)}, u32[]{:S(2)}, u32[]{:S(2)}) collective-permute-start(bf16[400,2048]{1,0:T(8,128)(2,1)S(1)} %shard_map.113.sides), channel_id=1, source_target_pairs={{0,4},{4,0},{1,5},{5,1},{2,6},{6,2},{3,7},{7,3},{8,12},{12,8},{9,1... | collective-permute-start | bytes 4915208 | tf_op jit(solution)/shard_map/ppermute | solution.py:64
  39.6 5.3 %collective-permute-start = (bf16[128,2048]{1,0:T(8,128)(2,1)S(1)}, bf16[128,2048]{1,0:T(8,128)(2,1)}, u32[]{:S(2)}, u32[]{:S(2)}) collective-permute-start(bf16[128,2048]{1,0:T(8,128)(2,1)S(1)} %copy-done.2), channel_id=1, source_target_pairs={{0,4},{4,0},{1,5},{5,1},{2,6},{6,2},{3,7},{7,3},{8,12},{12,8},{9,1... | collective-permute-start | bytes 1572872 | tf_op jit(solution)/shard_map/ppermute | solution.py:64
  39.8 5.1 %copy-start.7 = (bf16[64,2048]{1,0:T(8,128)(2,1)S(1)}, bf16[64,2048]{1,0:T(8,128)(2,1)}, u32[]{:S(2)}) copy-start(bf16[64,2048]{1,0:T(8,128)(2,1)} %refs_1_.1) | copy-start | bytes 786436
  39.8 5.1 %copy-start.9 = (f32[2048]{0:T(1024)S(1)}, f32[2048]{0:T(1024)}, u32[]{:S(2)}) copy-start(f32[2048]{0:T(1024)} %param.14) | copy-start | bytes 24580
  56.6 1.6 collective-permute-start.5
  58.3 6.3 %collective-permute-start.8 = (f32[64,512]{1,0:T(8,128)S(1)}, f32[64,512]{1,0:T(8,128)S(1)}, u32[]{:S(2)}, u32[]{:S(2)}) collective-permute-start(f32[64,512]{1,0:T(8,128)S(1)} %add.3.own), channel_id=1, source_target_pairs={{0,2},{1,3},{2,0},{3,1},{4,6},{5,7},{6,4},{7,5},{8,10},{9,11},{10,... | collective-permute-start | bytes 393224 | tf_op jit(solution)/shard_map/ppermute | solution.py:64
  60.7 6.9 %collective-permute-start.7 = (f32[64,512]{1,0:T(8,128)S(1)}, f32[64,512]{1,0:T(8,128)S(1)}, u32[]{:S(2)}, u32[]{:S(2)}) collective-permute-start(f32[64,512]{1,0:T(8,128)S(1)} %add.3.own), channel_id=1, source_target_pairs={{0,1},{1,2},{2,3},{3,0},{4,5},{5,6},{6,7},{7,4},{8,9},{9,10},{10,1... | collective-permute-start | bytes 393224 | tf_op jit(solution)/shard_map/ppermute | solution.py:64
  61.4 6.2 %collective-permute-start.6 = (f32[64,512]{1,0:T(8,128)S(1)}, f32[64,512]{1,0:T(8,128)S(1)}, u32[]{:S(2)}, u32[]{:S(2)}) collective-permute-start(f32[64,512]{1,0:T(8,128)S(1)} %add.3.own), channel_id=1, source_target_pairs={{0,3},{1,0},{2,1},{3,2},{4,7},{5,4},{6,5},{7,6},{8,11},{9,8},{10,9... | collective-permute-start | bytes 393224 | tf_op jit(solution)/shard_map/ppermute | solution.py:64
  68.2 2.1 %collective-permute-start.9 = (f32[64,512]{1,0:T(8,128)S(1)}, f32[64,512]{1,0:T(8,128)S(1)}, u32[]{:S(2)}, u32[]{:S(2)}) collective-permute-start(f32[64,512]{1,0:T(8,128)S(1)} %get-tuple-element.44.error_own), channel_id=1, source_target_pairs={{0,4},{4,0},{1,5},{5,1},{2,6},{6,2},{3,7},{7,3},{8,12},{12,8},{9,1... | collective-permute-start | bytes 393224 | tf_op jit(solution)/shard_map/ppermute | solution.py:64
  78.7 12.3 %collective-permute-start.10 = (bf16[400,512]{1,0:T(8,128)(2,1)S(1)}, bf16[400,512]{1,0:T(8,128)(2,1)S(1)}, u32[]{:S(2)}, u32[]{:S(2)}) collective-permute-start(bf16[400,512]{1,0:T(8,128)(2,1)S(1)} %get-tuple-element.49), channel_id=1, source_target_pairs={{0,16},{8,24},{16,0},{24,8},{1,17},{9,25},{17,1},{25,9},{2,18},{10... | collective-permute-start | bytes 1228808 | tf_op jit(solution)/shard_map/ppermute | solution.py:64
  81.5 12.2 %collective-permute-start.11 = (bf16[400,512]{1,0:T(8,128)(2,1)S(1)}, bf16[400,512]{1,0:T(8,128)(2,1)S(1)}, u32[]{:S(2)}, u32[]{:S(2)}) collective-permute-start(bf16[400,512]{1,0:T(8,128)(2,1)S(1)} %get-tuple-element.50), channel_id=1, source_target_pairs={{0,64},{32,96},{64,0},{96,32},{1,65},{33,97},{65,1},{97,33},{2,66}... | collective-permute-start | bytes 1228808 | tf_op jit(solution)/shard_map/ppermute | solution.py:64
  84.5 16.0 %collective-permute-start.12 = (bf16[400,512]{1,0:T(8,128)(2,1)S(1)}, bf16[400,512]{1,0:T(8,128)(2,1)S(1)}, u32[]{:S(2)}, u32[]{:S(2)}) collective-permute-start(bf16[400,512]{1,0:T(8,128)(2,1)S(1)} %get-tuple-element.51), channel_id=1, source_target_pairs={{0,8},{8,16},{16,24},{24,0},{1,9},{9,17},{17,25},{25,1},{2,10},{10... | collective-permute-start | bytes 1228808 | tf_op jit(solution)/shard_map/ppermute | solution.py:64
  84.8 18.5 %collective-permute-start.13 = (bf16[400,512]{1,0:T(8,128)(2,1)S(1)}, bf16[400,512]{1,0:T(8,128)(2,1)S(1)}, u32[]{:S(2)}, u32[]{:S(2)}) collective-permute-start(bf16[400,512]{1,0:T(8,128)(2,1)S(1)} %get-tuple-element.52), channel_id=1, source_target_pairs={{0,32},{32,64},{64,96},{96,0},{1,33},{33,65},{65,97},{97,1},{2,34}... | collective-permute-start | bytes 1228808 | tf_op jit(solution)/shard_map/ppermute | solution.py:64
  85.2 18.1 %collective-permute-start.14 = (bf16[400,512]{1,0:T(8,128)(2,1)S(1)}, bf16[400,512]{1,0:T(8,128)(2,1)S(1)}, u32[]{:S(2)}, u32[]{:S(2)}) collective-permute-start(bf16[400,512]{1,0:T(8,128)(2,1)S(1)} %get-tuple-element.53), channel_id=1, source_target_pairs={{0,24},{8,0},{16,8},{24,16},{1,25},{9,1},{17,9},{25,17},{2,26},{10... | collective-permute-start | bytes 1228808 | tf_op jit(solution)/shard_map/ppermute | solution.py:64
  91.0 12.2 %collective-permute-start.15 = (bf16[400,512]{1,0:T(8,128)(2,1)S(1)}, bf16[400,512]{1,0:T(8,128)(2,1)S(1)}, u32[]{:S(2)}, u32[]{:S(2)}) collective-permute-start(bf16[400,512]{1,0:T(8,128)(2,1)S(1)} %get-tuple-element.54), channel_id=1, source_target_pairs={{0,96},{32,0},{64,32},{96,64},{1,97},{33,1},{65,33},{97,65},{2,98}... | collective-permute-start | bytes 1228808 | tf_op jit(solution)/shard_map/ppermute | solution.py:64
  104.7 7.1 %collective-permute-start.16 = (bf16[448,128]{1,0:T(8,128)(2,1)S(1)}, bf16[448,128]{1,0:T(8,128)(2,1)S(1)}, u32[]{:S(2)}, u32[]{:S(2)}) collective-permute-start(bf16[448,128]{1,0:T(8,128)(2,1)S(1)} %get-tuple-element.57), channel_id=1, source_target_pairs={{0,64},{32,96},{64,0},{96,32},{1,65},{33,97},{65,1},{97,33},{2,66}... | collective-permute-start | bytes 344072 | tf_op jit(solution)/shard_map/ppermute | solution.py:64
  106.7 6.6 %collective-permute-start.17 = (bf16[448,128]{1,0:T(8,128)(2,1)S(1)}, bf16[448,128]{1,0:T(8,128)(2,1)S(1)}, u32[]{:S(2)}, u32[]{:S(2)}) collective-permute-start(bf16[448,128]{1,0:T(8,128)(2,1)S(1)} %get-tuple-element.58), channel_id=1, source_target_pairs={{0,16},{8,24},{16,0},{24,8},{1,17},{9,25},{17,1},{25,9},{2,18},{10... | collective-permute-start | bytes 344072 | tf_op jit(solution)/shard_map/ppermute | solution.py:64
  107.9 5.4 %collective-permute-start.18 = (bf16[448,128]{1,0:T(8,128)(2,1)S(1)}, bf16[448,128]{1,0:T(8,128)(2,1)S(1)}, u32[]{:S(2)}, u32[]{:S(2)}) collective-permute-start(bf16[448,128]{1,0:T(8,128)(2,1)S(1)} %get-tuple-element.59), channel_id=1, source_target_pairs={{0,32},{32,64},{64,96},{96,0},{1,33},{33,65},{65,97},{97,1},{2,34}... | collective-permute-start | bytes 344072 | tf_op jit(solution)/shard_map/ppermute | solution.py:64
  108.8 6.4 %collective-permute-start.19 = (bf16[448,128]{1,0:T(8,128)(2,1)S(1)}, bf16[448,128]{1,0:T(8,128)(2,1)S(1)}, u32[]{:S(2)}, u32[]{:S(2)}) collective-permute-start(bf16[448,128]{1,0:T(8,128)(2,1)S(1)} %get-tuple-element.60), channel_id=1, source_target_pairs={{0,8},{8,16},{16,24},{24,0},{1,9},{9,17},{17,25},{25,1},{2,10},{10... | collective-permute-start | bytes 344072 | tf_op jit(solution)/shard_map/ppermute | solution.py:64
  109.1 6.1 %collective-permute-start.20 = (bf16[448,128]{1,0:T(8,128)(2,1)S(1)}, bf16[448,128]{1,0:T(8,128)(2,1)S(1)}, u32[]{:S(2)}, u32[]{:S(2)}) collective-permute-start(bf16[448,128]{1,0:T(8,128)(2,1)S(1)} %get-tuple-element.61), channel_id=1, source_target_pairs={{0,96},{32,0},{64,32},{96,64},{1,97},{33,1},{65,33},{97,65},{2,98}... | collective-permute-start | bytes 344072 | tf_op jit(solution)/shard_map/ppermute | solution.py:64
  111.8 3.9 %collective-permute-start.21 = (bf16[448,128]{1,0:T(8,128)(2,1)S(1)}, bf16[448,128]{1,0:T(8,128)(2,1)S(1)}, u32[]{:S(2)}, u32[]{:S(2)}) collective-permute-start(bf16[448,128]{1,0:T(8,128)(2,1)S(1)} %get-tuple-element.62), channel_id=1, source_target_pairs={{0,24},{8,0},{16,8},{24,16},{1,25},{9,1},{17,9},{25,17},{2,26},{10... | collective-permute-start | bytes 344072 | tf_op jit(solution)/shard_map/ppermute | solution.py:64
  115.9 6.2 %collective-permute-start.26 = (bf16[3,128,128]{2,1,0:T(8,128)(2,1)S(1)}, bf16[3,128,128]{2,1,0:T(8,128)(2,1)S(1)}, u32[]{:S(2)}, u32[]{:S(2)}) collective-permute-start(bf16[3,128,128]{2,1,0:T(8,128)(2,1)S(1)} %get-tuple-element.65.refs_6_), channel_id=1, source_target_pairs={{0,64},{32,96},{64,0},{96,32},{1,65},{33,97},{65,1},{97,33},{2,66}... | collective-permute-start | bytes 294920 | tf_op jit(solution)/shard_map/ppermute | solution.py:64
  116.1 7.4 %collective-permute-start.24 = (bf16[3,128,128]{2,1,0:T(8,128)(2,1)S(1)}, bf16[3,128,128]{2,1,0:T(8,128)(2,1)S(1)}, u32[]{:S(2)}, u32[]{:S(2)}) collective-permute-start(bf16[3,128,128]{2,1,0:T(8,128)(2,1)S(1)} %get-tuple-element.65.refs_6_), channel_id=1, source_target_pairs={{0,32},{32,64},{64,96},{96,0},{1,33},{33,65},{65,97},{97,1},{2,34}... | collective-permute-start | bytes 294920 | tf_op jit(solution)/shard_map/ppermute | solution.py:64
  117.5 5.9 %collective-permute-start.22 = (bf16[3,128,128]{2,1,0:T(8,128)(2,1)S(1)}, bf16[3,128,128]{2,1,0:T(8,128)(2,1)S(1)}, u32[]{:S(2)}, u32[]{:S(2)}) collective-permute-start(bf16[3,128,128]{2,1,0:T(8,128)(2,1)S(1)} %get-tuple-element.65.refs_6_), channel_id=1, source_target_pairs={{0,96},{32,0},{64,32},{96,64},{1,97},{33,1},{65,33},{97,65},{2,98}... | collective-permute-start | bytes 294920 | tf_op jit(solution)/shard_map/ppermute | solution.py:64
  118.8 5.0 %collective-permute-start.27 = (bf16[3,128,128]{2,1,0:T(8,128)(2,1)S(1)}, bf16[3,128,128]{2,1,0:T(8,128)(2,1)S(1)}, u32[]{:S(2)}, u32[]{:S(2)}) collective-permute-start(bf16[3,128,128]{2,1,0:T(8,128)(2,1)S(1)} %get-tuple-element.66.refs_7_), channel_id=1, source_target_pairs={{0,16},{8,24},{16,0},{24,8},{1,17},{9,25},{17,1},{25,9},{2,18},{10... | collective-permute-start | bytes 294920 | tf_op jit(solution)/shard_map/ppermute | solution.py:64
  120.4 5.0 %collective-permute-start.25 = (bf16[3,128,128]{2,1,0:T(8,128)(2,1)S(1)}, bf16[3,128,128]{2,1,0:T(8,128)(2,1)S(1)}, u32[]{:S(2)}, u32[]{:S(2)}) collective-permute-start(bf16[3,128,128]{2,1,0:T(8,128)(2,1)S(1)} %get-tuple-element.66.refs_7_), channel_id=1, source_target_pairs={{0,8},{8,16},{16,24},{24,0},{1,9},{9,17},{17,25},{25,1},{2,10},{10... | collective-permute-start | bytes 294920 | tf_op jit(solution)/shard_map/ppermute | solution.py:64
  122.2 3.8 %collective-permute-start.23 = (bf16[3,128,128]{2,1,0:T(8,128)(2,1)S(1)}, bf16[3,128,128]{2,1,0:T(8,128)(2,1)S(1)}, u32[]{:S(2)}, u32[]{:S(2)}) collective-permute-start(bf16[3,128,128]{2,1,0:T(8,128)(2,1)S(1)} %get-tuple-element.66.refs_7_), channel_id=1, source_target_pairs={{0,24},{8,0},{16,8},{24,16},{1,25},{9,1},{17,9},{25,17},{2,26},{10... | collective-permute-start | bytes 294920 | tf_op jit(solution)/shard_map/ppermute | solution.py:64
  126.0 9.3 %collective-permute-start.33 = (bf16[4,3,128,128]{3,2,1,0:T(8,128)(2,1)S(1)}, bf16[4,3,128,128]{3,2,1,0:T(8,128)(2,1)S(1)}, u32[]{:S(2)}, u32[]{:S(2)}) collective-permute-start(bf16[4,3,128,128]{3,2,1,0:T(8,128)(2,1)S(1)} %get-tuple-element.68.line), channel_id=1, source_target_pairs={{0,16},{8,24},{16,0},{24,8},{1,17},{9,25},{17,1},{25,9},{2,18},{10... | collective-permute-start | bytes 1179656 | tf_op jit(solution)/shard_map/ppermute | solution.py:64
  127.0 12.2 %collective-permute-start.32 = (bf16[4,3,128,128]{3,2,1,0:T(8,128)(2,1)S(1)}, bf16[4,3,128,128]{3,2,1,0:T(8,128)(2,1)S(1)}, u32[]{:S(2)}, u32[]{:S(2)}) collective-permute-start(bf16[4,3,128,128]{3,2,1,0:T(8,128)(2,1)S(1)} %get-tuple-element.68.line), channel_id=1, source_target_pairs={{0,8},{8,16},{16,24},{24,0},{1,9},{9,17},{17,25},{25,1},{2,10},{10... | collective-permute-start | bytes 1179656 | tf_op jit(solution)/shard_map/ppermute | solution.py:64
  129.1 10.5 %collective-permute-start.31 = (bf16[4,3,128,128]{3,2,1,0:T(8,128)(2,1)S(1)}, bf16[4,3,128,128]{3,2,1,0:T(8,128)(2,1)S(1)}, u32[]{:S(2)}, u32[]{:S(2)}) collective-permute-start(bf16[4,3,128,128]{3,2,1,0:T(8,128)(2,1)S(1)} %get-tuple-element.68.line), channel_id=1, source_target_pairs={{0,24},{8,0},{16,8},{24,16},{1,25},{9,1},{17,9},{25,17},{2,26},{10... | collective-permute-start | bytes 1179656 | tf_op jit(solution)/shard_map/ppermute | solution.py:64
  129.7 24.9 %collective-permute-start.30 = (bf16[4,3,128,128]{3,2,1,0:T(8,128)(2,1)S(1)}, bf16[4,3,128,128]{3,2,1,0:T(8,128)(2,1)S(1)}, u32[]{:S(2)}, u32[]{:S(2)}) collective-permute-start(bf16[4,3,128,128]{3,2,1,0:T(8,128)(2,1)S(1)} %get-tuple-element.67.refs_1_.refs_3_), channel_id=1, source_target_pairs={{0,64},{32,96},{64,0},{96,32},{1,65},{33,97},{65,1},{97,33},{2,66}... | collective-permute-start | bytes 1179656 | tf_op jit(solution)/shard_map/ppermute | solution.py:64
  130.9 23.8 %collective-permute-start.29 = (bf16[4,3,128,128]{3,2,1,0:T(8,128)(2,1)S(1)}, bf16[4,3,128,128]{3,2,1,0:T(8,128)(2,1)S(1)}, u32[]{:S(2)}, u32[]{:S(2)}) collective-permute-start(bf16[4,3,128,128]{3,2,1,0:T(8,128)(2,1)S(1)} %get-tuple-element.67.refs_1_.refs_3_), channel_id=1, source_target_pairs={{0,32},{32,64},{64,96},{96,0},{1,33},{33,65},{65,97},{97,1},{2,34}... | collective-permute-start | bytes 1179656 | tf_op jit(solution)/shard_map/ppermute | solution.py:64
  135.2 19.4 %collective-permute-start.28 = (bf16[4,3,128,128]{3,2,1,0:T(8,128)(2,1)S(1)}, bf16[4,3,128,128]{3,2,1,0:T(8,128)(2,1)S(1)}, u32[]{:S(2)}, u32[]{:S(2)}) collective-permute-start(bf16[4,3,128,128]{3,2,1,0:T(8,128)(2,1)S(1)} %get-tuple-element.67.refs_1_.refs_3_), channel_id=1, source_target_pairs={{0,96},{32,0},{64,32},{96,64},{1,97},{33,1},{65,33},{97,65},{2,98}... | collective-permute-start | bytes 1179656 | tf_op jit(solution)/shard_map/ppermute | solution.py:64
  139.8 15.3 %collective-permute-start.35 = (bf16[5,4,3,128,128]{4,3,2,1,0:T(8,128)(2,1)S(1)}, bf16[5,4,3,128,128]{4,3,2,1,0:T(8,128)(2,1)S(1)}, u32[]{:S(2)}, u32[]{:S(2)}) collective-permute-start(bf16[5,4,3,128,128]{4,3,2,1,0:T(8,128)(2,1)S(1)} %shard_map.122.refs_0_.refs_1_), channel_id=1, source_target_pairs={{0,4},{4,0},{1,5},{5,1},{2,6},{6,2},{3,7},{7,3},{8,12},{12,8},{9,1... | collective-permute-start | bytes 5898248 | tf_op jit(solution)/shard_map/ppermute | solution.py:64
  154.8 7.5 %collective-permute-start.34 = (bf16[4,4,3,128,128]{4,3,2,1,0:T(8,128)(2,1)S(1)}, bf16[4,4,3,128,128]{4,3,2,1,0:T(8,128)(2,1)S(1)}, u32[]{:S(2)}, u32[]{:S(2)}) collective-permute-start(bf16[4,4,3,128,128]{4,3,2,1,0:T(8,128)(2,1)S(1)} %shard_map.124.refs_2_), channel_id=1, source_target_pairs={{0,4},{4,0},{1,5},{5,1},{2,6},{6,2},{3,7},{7,3},{8,12},{12,8},{9,1... | collective-permute-start | bytes 4718600 | tf_op jit(solution)/shard_map/ppermute | solution.py:64
